TPU v7x, 256 devices: a whole 4x4x8 slice. The times are simulated.
256 devices in a mesh: dp: 4 (over x_lo, core), tile: 64 (over y, x_hi, z).
Axes of the slice: x: 4 (x_hi: 2, x_lo: 2; x = x_hi * 2 + x_lo), y: 4, z: 8, core: 2. Of those that a mesh axis runs over, the one named last changes fastest.
Arguments:
- activations: bfloat16 [4, 512, 8192], P('dp', None, 'tile'), may hold values from -6 to 6
- gradients: bfloat16 [4, 512, 8192], P('dp', None, 'tile'), may hold values from -6 to 6
- basis_in: float32 [8192, 8192], P(None, 'tile'), may hold values from -0.0625 to 0.0625
- basis_out: float32 [8192, 8192], P(None, 'tile'), may hold values from -0.0625 to 0.0625
Outputs:
- eigenvalues: float32 [8192, 8192], P('tile', 'dp')
All inputs are finite; a program needn't handle non-finite values.
Results may differ from a plain program's by a relative error of at most 0.0035.
Values may be sent and summed in bfloat16 or wider, within the bound.
No kernel may reach another device: no remote copies, remote signals or barrier semaphores. Data moves between devices by JAX's collectives and lax.ppermute only.
A program may use at most 64 MiB of HBM per device.

v0:
```python
import jax
import jax.numpy as jnp
from jax import lax
from jax.sharding import PartitionSpec as P


def body(activations, gradients, basis_in, basis_out):
    seqs_here = activations.shape[0]
    tok_count = activations.shape[1]
    groups = lax.axis_size("dp")
    scale = jnp.float32(1.0 / (tok_count * seqs_here * groups))
    whole_acts, whole_grads = (
        lax.all_gather(activations, "tile", axis=2, tiled=True),
        lax.all_gather(gradients, "tile", axis=2, tiled=True),
    )
    acts_rot = jnp.einsum(
        "stf,fk->stk", whole_acts.astype(jnp.float32), basis_in, precision=lax.Precision.HIGHEST
    )
    grads_rot = jnp.einsum(
        "stf,fk->stk", whole_grads.astype(jnp.float32), basis_out, precision=lax.Precision.HIGHEST
    )
    rot_acts = acts_rot.astype(jnp.bfloat16)
    rot_grads = grads_rot.astype(jnp.bfloat16)
    products = jnp.einsum(
        "sti,stj->sij",
        rot_grads,
        lax.all_gather(rot_acts, "tile", axis=2, tiled=True),
        preferred_element_type=jnp.float32,
    )
    partial_sums = jnp.sum(products * products, axis=0) * scale
    return lax.psum_scatter(partial_sums, "dp", scatter_dimension=1, tiled=True)


def solution(mesh):
    return jax.shard_map(
        body,
        mesh=mesh,
        in_specs=(P("dp", None, "tile"), P("dp", None, "tile"), P(None, "tile"), P(None, "tile")),
        out_specs=P("tile", "dp"),
        check_vma=False,
    )
```

profile of v0, /device:TPU:2, one launch (start us, length us, event | category | flops | bytes accessed | tf_op | source)
XLA Modules:
  0.0 581.7 jit_solution(5302137179107013484)
XLA Ops:
  6.5 0.0 all-gather.7.cloned.1.call-start
  6.5 0.7 all-gather.7.cloned.1.call-update
  7.3 0.0 all-gather.5.cloned.1.call-start
  7.3 0.7 all-gather.5.cloned.1.call-update
  8.0 0.0 all-gather.9.cloned.1.call-start
  8.1 175.4 %all-gather.7.cloned.1.call-done = bf16[1,512,8192]{2,1,0:T(8,128)(2,1)} async-done(((bf16[1,512,128]{2,1,0:T(8,128)(2,1)}), bf16[1,512,8192]{2,1,0:T(8,128)(2,1)}) %all-gather.7.cloned.1.call-update) | async-done | bytes 8388624 | tf_op jit(solution)/shard_map/all_gather | solution.py:13
  183.4 10.4 %fusion.8 = bf16[512,128]{1,0:T(8,128)(2,1)} fusion(f32[8192,128]{1,0:T(8,128)} %param.6, bf16[1,512,8192]{2,1,0:T(8,128)(2,1)} %all-gather.7.cloned.1.call-done), kind=kOutput, calls=%fused_computation.7 | convolution fusion | flops 6442516480 | bytes 12713984 | tf_op jit(solution)/shard_map/stf,fk->stk/dot_general | solution.py:16
  193.8 0.0 all-gather.9.cloned.1.call-update
  193.9 0.0 reduce-scatter.2.cloned.1.call-start
  193.9 160.0 %all-gather.5.cloned.1.call-done = bf16[1,512,8192]{2,1,0:T(8,128)(2,1)} async-done(((bf16[1,512,128]{2,1,0:T(8,128)(2,1)}), bf16[1,512,8192]{2,1,0:T(8,128)(2,1)}) %all-gather.5.cloned.1.call-update) | async-done | bytes 8388624 | tf_op jit(solution)/shard_map/all_gather | solution.py:14
  353.9 9.8 %fusion.5 = bf16[512,128]{1,0:T(8,128)(2,1)S(1)} fusion(f32[8192,128]{1,0:T(8,128)} %param.7, bf16[1,512,8192]{2,1,0:T(8,128)(2,1)} %all-gather.5.cloned.1.call-done), kind=kOutput, calls=%fused_computation.6 | convolution fusion | flops 6442516480 | bytes 12713984 | tf_op jit(solution)/shard_map/stf,fk->stk/dot_general | solution.py:19
  363.7 160.7 %all-gather.9.cloned.1.call-done = bf16[512,8192]{1,0:T(8,128)(2,1)} async-done(((bf16[512,128]{1,0:T(8,128)(2,1)}), bf16[512,8192]{1,0:T(8,128)(2,1)}) %all-gather.9.cloned.1.call-update) | async-done | bytes 8388624 | tf_op jit(solution)/shard_map/all_gather | solution.py:27
  524.5 6.8 %fusion = f32[128,8192]{1,0:T(8,128)} fusion(bf16[512,128]{1,0:T(8,128)(2,1)S(1)} %fusion.5, bf16[512,8192]{1,0:T(8,128)(2,1)} %all-gather.9.cloned.1.call-done), kind=kOutput, calls=%fused_computation.1 | convolution fusion | flops 1075838976 | bytes 12713984 | tf_op jit(solution)/shard_map/sti,stj->sij/dot_general | solution.py:24
  531.3 0.0 reduce-scatter.2.cloned.1.call-update
  531.3 43.8 %reduce-scatter.2.cloned.1.call-done = f32[128,2048]{1,0:T(8,128)} async-done(((f32[128,8192]{1,0:T(8,128)}), f32[128,2048]{1,0:T(8,128)}) %reduce-scatter.2.cloned.1.call-update) | async-done | bytes 1048592 | tf_op jit(solution)/shard_map/reduce_scatter | solution.py:31
Async XLA Ops:
  6.5 176.9 %all-gather.7.cloned.1.call-start = ((), (), s32[]{:S(2)}) async-start(), calls=%async_computation.2 | async-start | bytes 8519680 | tf_op jit(solution)/shard_map/all_gather | solution.py:13
  7.3 346.7 %all-gather.5.cloned.1.call-start = ((), (), s32[]{:S(2)}) async-start(), calls=%async_computation.1 | async-start | bytes 8519680 | tf_op jit(solution)/shard_map/all_gather | solution.py:14
  8.0 516.5 %all-gather.9.cloned.1.call-start = ((), (), s32[]{:S(2)}) async-start(), calls=%async_computation.4 | async-start | bytes 8519680 | tf_op jit(solution)/shard_map/all_gather | solution.py:27
  193.9 381.3 %reduce-scatter.2.cloned.1.call-start = ((), (), s32[]{:S(2)}) async-start(), calls=%async_computation.3 | async-start | bytes 5242880 | tf_op jit(solution)/shard_map/reduce_scatter | solution.py:31
Sparse Core Ops, SparseCore 0:
  10.8 172.6 all-gather.6
  186.8 167.0 all-gather.4
  357.4 167.0 all-gather.8
  531.4 43.6 reduce-scatter.1
where the time goes:
time: 585 us; the launch traced here: 582 us
  waiting for transfers between devices  541 us (92%)
  matrix products  27 us (5%)
  between operations  13.1 us (2%)
    all_gather x1, waiting for transfers between devices, body(): lax.all_gather(activations, 'tile', axis=2, tiled=True)  175 us
    all_gather x1, waiting for transfers between devices, body(): lax.all_gather(rot_acts, 'tile', axis=2, tiled=True)  161 us
    all_gather x1, waiting for transfers between devices, body(): lax.all_gather(gradients, 'tile', axis=2, tiled=True)  160 us
    reduce_scatter x1, waiting for transfers between devices, body(): return lax.psum_scatter(partial_sums, 'dp', scatter_dimension=1, tiled=True)  43.8 us
  transfers between devices with their start and end apart: 4, of which 4 were waited for; matrix products, arithmetic and copies ran while one was open for 3% of the time, Pallas kernels for 0%

commit v1 on v0

v1 whole, which is shorter than its diff:
```python
import functools

import jax
import jax.numpy as jnp
from jax import lax
from jax.experimental import pallas as pl
from jax.experimental.pallas import tpu as pltpu
from jax.sharding import Mesh, PartitionSpec as P

AXES = ("xl", "c", "y", "xh", "z")
SIZES = (2, 2, 4, 2, 8)
DP = ("xl", "c")
TILE = ("y", "xh", "z")
TOK = 512
COLS = 128
F32 = jnp.float32
BF16 = jnp.bfloat16
VMEM_LIMIT = 48 * 1024 * 1024
OFFSETS = (0, -1, 1, -2, 2, -3, 3, -4)


def shift(x, axis, by):
    n = lax.axis_size(axis)
    return lax.ppermute(x, axis, [(i, (i + by) % n) for i in range(n)])


def gather_z(x):
    blocks = [x]
    up = down = x
    for step in range(1, 4):
        up = shift(up, "z", 1)
        down = shift(down, "z", -1)
        blocks += [up, down]
    blocks.append(shift(up, "z", 1))
    return blocks


def whole(shape):
    return pl.BlockSpec(shape, lambda *_: (0,) * len(shape))


def rotate_kernel(z_ref, *refs):
    blocks, (own_ref, other_ref, out_ref, lhs, rhs) = refs[:8], refs[8:]

    @pl.when(pl.program_id(0) == 0)
    def _():
        for k, block in enumerate(blocks):
            lhs[:, k * 256 : (k + 1) * 256] = block[...]

    for k, offset in enumerate(OFFSETS):
        at = lax.rem(z_ref[0] + 8 + offset, 8) * COLS
        for half, ref in enumerate((own_ref, other_ref)):
            exact = ref[0, pl.ds(pl.multiple_of(at, COLS), COLS), :]
            high = exact.astype(BF16)
            low = (exact - high.astype(F32)).astype(BF16)
            row = k * 256 + half * COLS
            rhs[row : row + COLS, :COLS] = high
            rhs[row : row + COLS, COLS:] = low
    both = jnp.dot(lhs[...], rhs[...], preferred_element_type=F32)
    out_ref[0] = (both[:, :COLS] + both[:, COLS:]).T


def rotate(z, blocks, own, other):
    slab = pl.BlockSpec((1, 1024, COLS), lambda g: (g, 0, 0))
    return pl.pallas_call(
        rotate_kernel,
        grid=(4,),
        out_shape=jax.ShapeDtypeStruct((4, COLS, TOK), F32),
        in_specs=[pl.BlockSpec(memory_space=pltpu.SMEM)]
        + [whole((TOK, 256))] * 8
        + [slab, slab],
        out_specs=pl.BlockSpec((1, COLS, TOK), lambda g: (g, 0, 0)),
        scratch_shapes=[pltpu.VMEM((TOK, 2048), BF16), pltpu.VMEM((2048, 256), BF16)],
        compiler_params=pltpu.CompilerParams(vmem_limit_bytes=VMEM_LIMIT),
        cost_estimate=pl.CostEstimate(
            flops=4 * TOK * 2048 * 512, bytes_accessed=7 << 20, transcendentals=0
        ),
    )(z, *blocks, own, other)


def product_kernel(scale, at_ref, *refs):
    acts, grads, out_ref, right = refs[:8], refs[8:16], refs[16], refs[17]
    z, xh, y, xl, c = (at_ref[i] for i in range(5))
    for k, offset in enumerate(OFFSETS):
        for half in range(2):
            place = (xh if half == 0 else 1 - xh) * 8 + lax.rem(z + 8 + offset, 8)
            for s in range(4):
                right[s, pl.ds(pl.multiple_of(place * 32, 32), 32), :] = acts[k][half, s]
    for step in range(4):
        total = None
        for core in range(2):
            for side in range(2):
                s = (xl if side == 0 else 1 - xl) * 2 + (c if core == 0 else 1 - c)
                part = lax.dot_general(
                    grads[core * 4 + step][side],
                    right[s],
                    (((1,), (1,)), ((), ())),
                    preferred_element_type=F32,
                )
                total = part * part if total is None else total + part * part
        out_ref[lax.rem(y + step, 4)] = total * scale


def products(at, acts, grads, scale):
    return pl.pallas_call(
        functools.partial(product_kernel, scale),
        out_shape=jax.ShapeDtypeStruct((4, COLS, 512), F32),
        in_specs=[pl.BlockSpec(memory_space=pltpu.SMEM)]
        + [pl.BlockSpec(memory_space=pltpu.VMEM)] * 16,
        out_specs=pl.BlockSpec(memory_space=pltpu.VMEM),
        scratch_shapes=[pltpu.VMEM((4, 512, TOK), BF16)],
        compiler_params=pltpu.CompilerParams(vmem_limit_bytes=VMEM_LIMIT),
        cost_estimate=pl.CostEstimate(
            flops=2 * 4 * 512 * 512 * TOK, bytes_accessed=5 << 20, transcendentals=0
        ),
    )(at, *acts, *grads)


def weave_kernel(in_ref, out_ref):
    for tile in range(4):
        lanes = slice(tile * 32, tile * 32 + 32)
        out_ref[:, tile * COLS : (tile + 1) * COLS] = jnp.concatenate(
            [in_ref[q, :, lanes] for q in range(4)], axis=1
        )


def weave(parts):
    return pl.pallas_call(
        weave_kernel,
        grid=(4,),
        out_shape=jax.ShapeDtypeStruct((COLS, 2048), F32),
        in_specs=[pl.BlockSpec((4, COLS, 128), lambda g: (0, 0, g))],
        out_specs=pl.BlockSpec((COLS, 512), lambda g: (0, g)),
        compiler_params=pltpu.CompilerParams(vmem_limit_bytes=VMEM_LIMIT),
    )(parts)


def spread_basis(basis):
    halves = basis.reshape(4, 2, 1024, COLS)
    mine = lax.dynamic_index_in_dim(halves, lax.axis_index("c"), 1, keepdims=False)
    own = lax.all_to_all(mine, "y", 0, 0)
    return own, shift(own, "c", 1)


def gather_rows(x):
    x = x[0]
    other = shift(x, "xh", 1)
    same = lax.axis_index("xh") == lax.axis_index("c")
    pair = jnp.concatenate(
        [jnp.where(same, x, other), jnp.where(same, other, x)], axis=1
    )
    return gather_z(pair)


def body(activations, gradients, basis_in, basis_out):
    z, xh, y, xl, c = (lax.axis_index(a) for a in ("z", "xh", "y", "xl", "c"))
    at = jnp.stack([z, xh, y, xl, c]).astype(jnp.int32)

    act_blocks = gather_rows(activations)
    own_in, other_in = spread_basis(basis_in)
    acts_part = rotate(at, act_blocks, own_in, other_in)
    acts_in = lax.all_to_all(acts_part.reshape(16, 32, TOK), ("xl", "c", "y"), 0, 0)
    acts = jnp.sum(acts_in.reshape(4, 4, 32, TOK), axis=1).astype(BF16)
    acts_pair = jnp.stack([acts, shift(acts, "xh", 1)])
    rot_acts = gather_z(acts_pair)

    grad_blocks = gather_rows(gradients)
    own_out, other_out = spread_basis(basis_out)
    grads_part = rotate(at, grad_blocks, own_out, other_out)
    grads_in = lax.all_to_all(grads_part, "y", 0, 0)
    grads = jnp.sum(grads_in, axis=0).astype(BF16)
    sides = jnp.stack([grads, shift(grads, "xl", 1)])
    along = [sides] + [shift(sides, "y", -step) for step in range(1, 4)]
    rot_grads = along + [shift(block, "c", 1) for block in along]

    scale = 1.0 / (TOK * 4)
    part = products(at, rot_acts, rot_grads, scale)
    return weave(lax.all_to_all(part, "y", 0, 0))


def solution(mesh):
    fine = Mesh(mesh.devices.reshape(SIZES), AXES)
    return jax.shard_map(
        body,
        mesh=fine,
        in_specs=(P(DP, None, TILE), P(DP, None, TILE), P(None, TILE), P(None, TILE)),
        out_specs=P(TILE, DP),
        check_vma=False,
    )
```

time: 585 us -> 217 us (0.37)
  waiting for transfers between devices: 541 us -> 109 us
  starting transfers between devices: 0.12 us -> 56 us
  matrix products: 27 us -> 0 us
  blocking collectives: 0 us -> 20.5 us
  Pallas kernels: 0 us -> 18.1 us
  between operations: 13.1 us -> 0.18 us
  local copies, waits for them, and re-layouts: 0 us -> 10.1 us
    all_gather x3 -> x0, waiting for transfers between devices: 496 us -> none  [the longest x1 175 us: body(): lax.all_gather(activations, 'tile', axis=2, tiled=True)]
    ppermute x0 -> x34, waiting for transfers between devices: none -> 64.7 us  [shift(): return lax.ppermute(x, axis, [(i, (i + by) % n) for i in range(n)])]
    all_to_all x0 -> x4, waiting for transfers between devices: none -> 44.7 us  [the longest x2 39 us: spread_basis(): own = lax.all_to_all(mine, 'y', 0, 0)]
    reduce_scatter x1 -> x0, waiting for transfers between devices: 43.8 us -> none  [body(): return lax.psum_scatter(partial_sums, 'dp', scatter_dimension=1, tiled=True)]
    ppermute x0 -> x34, starting transfers between devices: none -> 39.1 us  [shift(): return lax.ppermute(x, axis, [(i, (i + by) % n) for i in range(n)])]
    dot_general x3 -> x0, matrix products: 27 us -> none  [the longest x1 10.4 us: body(): jnp.einsum('stf,fk->stk', whole_acts.astype(jnp.float32), basis_in, preci...]
    all_to_all x0 -> x1, blocking collectives: none -> 20.5 us  [body(): return weave(lax.all_to_all(part, 'y', 0, 0))]
    pallas_call x0 -> x4, Pallas kernels: none -> 18.1 us  [the longest x2 12.3 us: rotate(): pl.pallas_call(rotate_kernel, grid=(4,), out_shape=jax.ShapeDtypeStruct((...]
  transfers between devices with their start and end apart: 4 -> 38, of which waited for: 4 -> 21; matrix products, arithmetic and copies ran while one was open for 3% -> 2% of each run, Pallas kernels for 0% -> 6%
where the time goes in v1:
time: 217 us; the launch traced here: 216 us
  waiting for transfers between devices  109 us (50%)
  starting transfers between devices  56 us (26%)
  blocking collectives  20.5 us (9%)
  Pallas kernels  18.1 us (8%)
  local copies, waits for them, and re-layouts  10.1 us (5%)
    ppermute x34, waiting for transfers between devices, shift(): return lax.ppermute(x, axis, [(i, (i + by) % n) for i in range(n)])  64.7 us
    ppermute x34, starting transfers between devices, shift(): return lax.ppermute(x, axis, [(i, (i + by) % n) for i in range(n)])  39.1 us
    all_to_all x2, waiting for transfers between devices, spread_basis(): own = lax.all_to_all(mine, 'y', 0, 0)  39 us
    all_to_all x1, blocking collectives, body(): return weave(lax.all_to_all(part, 'y', 0, 0))  20.5 us
    pallas_call x2, Pallas kernels, rotate(): pl.pallas_call(rotate_kernel, grid=(4,), out_shape=jax.ShapeDtypeStruct((...  12.3 us
    all_to_all x2, starting transfers between devices, spread_basis(): own = lax.all_to_all(mine, 'y', 0, 0)  8.07 us
    squeeze x2, local copies, waits for them, and re-layouts, spread_basis(): lax.dynamic_index_in_dim(halves, lax.axis_index('c'), 1, keepdims=False)  6.13 us
    all_to_all x1, waiting for transfers between devices, body(): grads_in = lax.all_to_all(grads_part, 'y', 0, 0)  5.69 us
  transfers between devices with their start and end apart: 38, of which 21 were waited for; matrix products, arithmetic and copies ran while one was open for 2% of the time, Pallas kernels for 6%

profile of v1, /device:TPU:2, one launch (start us, length us, event | category | flops | bytes accessed | tf_op | source)
XLA Modules:
  0.0 215.9 jit_solution(11857507413502140205)
XLA Ops:
  0.0 3.0 %dynamic-slice_bitcast_fusion.1 = f32[4,1024,128]{2,1,0:T(8,128)} fusion(f32[4,2,1024,128]{3,2,1,0:T(8,128)} %bitcast.28, s32[]{:T(128)S(6)} %select_n.28), kind=kLoop, calls=%fused_computation.1 | loop fusion | bytes 4194308 | tf_op jit(solution)/shard_map/jit(dynamic_index_in_dim)/squeeze | solution.py:140
  3.0 4.5 %all-to-all-start = ((f32[4,1024,128]{2,1,0:T(8,128)}), f32[4,1024,128]{2,1,0:T(8,128)S(1)}, u32[]{:S(2)}, u32[]{:S(2)}) async-start(f32[4,1024,128]{2,1,0:T(8,128)} %dynamic-slice_bitcast_fusion.1), calls=%async_computation | async-start | bytes 4194304 | tf_op jit(solution)/shard_map/all_to_all | solution.py:141
  7.5 3.1 %dynamic-slice_bitcast_fusion = f32[4,1024,128]{2,1,0:T(8,128)} fusion(f32[4,2,1024,128]{3,2,1,0:T(8,128)} %bitcast.29, s32[]{:T(128)S(6)} %select_n.28), kind=kLoop, calls=%fused_computation | loop fusion | bytes 4194308 | tf_op jit(solution)/shard_map/jit(dynamic_index_in_dim)/squeeze | solution.py:140
  10.6 23.2 %all-to-all-done.refs_8_ = f32[4,1024,128]{2,1,0:T(8,128)S(1)} async-done(((f32[4,1024,128]{2,1,0:T(8,128)}), f32[4,1024,128]{2,1,0:T(8,128)S(1)}, u32[]{:S(2)}, u32[]{:S(2)}) %all-to-all-start) | async-done | bytes 2097184 | tf_op jit(solution)/shard_map/all_to_all | solution.py:141
  33.8 1.3 copy-done
  35.2 3.6 %all-to-all-start.2 = ((f32[4,1024,128]{2,1,0:T(8,128)}), f32[4,1024,128]{2,1,0:T(8,128)S(1)}, u32[]{:S(2)}, u32[]{:S(2)}) async-start(f32[4,1024,128]{2,1,0:T(8,128)} %dynamic-slice_bitcast_fusion), calls=%async_computation.2 | async-start | bytes 4194304 | tf_op jit(solution)/shard_map/all_to_all | solution.py:141
  38.8 0.1 collective-permute-start.8
  38.9 2.2 %collective-permute-start = (bf16[512,128]{1,0:T(8,128)(2,1)S(1)}, bf16[512,128]{1,0:T(8,128)(2,1)S(1)}, u32[]{:S(2)}, u32[]{:S(2)}) collective-permute-start(bf16[512,128]{1,0:T(8,128)(2,1)S(1)} %bitcast.32), channel_id=1, source_target_pairs={{0,8},{8,0},{1,9},{9,1},{2,10},{10,2},{3,11},{11,3},{4,12},{12,4},... | collective-permute-start | bytes 393224 | tf_op jit(solution)/shard_map/ppermute | solution.py:24
  41.1 5.2 %collective-permute-done = bf16[512,128]{1,0:T(8,128)(2,1)S(1)} collective-permute-done((bf16[512,128]{1,0:T(8,128)(2,1)S(1)}, bf16[512,128]{1,0:T(8,128)(2,1)S(1)}, u32[]{:S(2)}, u32[]{:S(2)}) %collective-permute-start) | collective-permute-done | bytes 131104 | tf_op jit(solution)/shard_map/ppermute | solution.py:24
  46.4 2.0 collective-permute-start.1
  48.4 15.8 %all-to-all-done.2.refs_8_ = f32[4,1024,128]{2,1,0:T(8,128)S(1)} async-done(((f32[4,1024,128]{2,1,0:T(8,128)}), f32[4,1024,128]{2,1,0:T(8,128)S(1)}, u32[]{:S(2)}, u32[]{:S(2)}) %all-to-all-start.2) | async-done | bytes 2097184 | tf_op jit(solution)/shard_map/all_to_all | solution.py:141
  64.2 0.0 collective-permute-start.25
  64.2 5.9 %collective-permute-start.2 = (bf16[512,256]{1,0:T(8,128)(2,1)S(1)}, bf16[512,256]{1,0:T(8,128)(2,1)S(1)}, u32[]{:S(2)}, u32[]{:S(2)}) collective-permute-start(bf16[512,256]{1,0:T(8,128)(2,1)S(1)} %pad_maximum_fusion.refs_0_), channel_id=1, source_target_pairs={{0,7},{1,0},{2,1},{3,2},{4,3},{5,4},{6,5},{7,6},{8,15},{9,8},{10,9... | collective-permute-start | bytes 786440 | tf_op jit(solution)/shard_map/ppermute | solution.py:24
  70.0 2.2 %collective-permute-start.17 = (bf16[512,128]{1,0:T(8,128)(2,1)S(1)}, bf16[512,128]{1,0:T(8,128)(2,1)S(1)}, u32[]{:S(2)}, u32[]{:S(2)}) collective-permute-start(bf16[512,128]{1,0:T(8,128)(2,1)S(1)} %bitcast.33), channel_id=1, source_target_pairs={{0,8},{8,0},{1,9},{9,1},{2,10},{10,2},{3,11},{11,3},{4,12},{12,4},... | collective-permute-start | bytes 393224 | tf_op jit(solution)/shard_map/ppermute | solution.py:24
  72.2 4.0 %collective-permute-done.2.refs_2_ = bf16[512,256]{1,0:T(8,128)(2,1)S(1)} collective-permute-done((bf16[512,256]{1,0:T(8,128)(2,1)S(1)}, bf16[512,256]{1,0:T(8,128)(2,1)S(1)}, u32[]{:S(2)}, u32[]{:S(2)}) %collective-permute-start.2) | collective-permute-done | bytes 262176 | tf_op jit(solution)/shard_map/ppermute | solution.py:24
  76.3 3.7 %collective-permute-start.4 = (bf16[512,256]{1,0:T(8,128)(2,1)S(1)}, bf16[512,256]{1,0:T(8,128)(2,1)}, u32[]{:S(2)}, u32[]{:S(2)}) collective-permute-start(bf16[512,256]{1,0:T(8,128)(2,1)S(1)} %collective-permute-done.2.refs_2_), channel_id=1, source_target_pairs={{0,7},{1,0},{2,1},{3,2},{4,3},{5,4},{6,5},{7,6},{8,15},{9,8},{10,9... | collective-permute-start | bytes 786440 | tf_op jit(solution)/shard_map/ppermute | solution.py:24
  80.0 0.1 collective-permute-start.18
  80.1 5.3 %collective-permute-done.4.refs_4_ = bf16[512,256]{1,0:T(8,128)(2,1)} collective-permute-done((bf16[512,256]{1,0:T(8,128)(2,1)S(1)}, bf16[512,256]{1,0:T(8,128)(2,1)}, u32[]{:S(2)}, u32[]{:S(2)}) %collective-permute-start.4) | collective-permute-done | bytes 262176 | tf_op jit(solution)/shard_map/ppermute | solution.py:24
  85.4 3.8 %collective-permute-start.6 = (bf16[512,256]{1,0:T(8,128)(2,1)}, bf16[512,256]{1,0:T(8,128)(2,1)}, u32[]{:S(2)}, u32[]{:S(2)}) collective-permute-start(bf16[512,256]{1,0:T(8,128)(2,1)} %collective-permute-done.4.refs_4_), channel_id=1, source_target_pairs={{0,7},{1,0},{2,1},{3,2},{4,3},{5,4},{6,5},{7,6},{8,15},{9,8},{10,9... | collective-permute-start | bytes 786440 | tf_op jit(solution)/shard_map/ppermute | solution.py:24
  89.2 1.3 collective-permute-done.5.refs_5_
  90.5 0.1 stack.37.z_ref.at_ref
  90.6 5.4 %collective-permute-done.18.refs_1_ = bf16[512,256]{1,0:T(8,128)(2,1)S(1)} collective-permute-done((bf16[512,256]{1,0:T(8,128)(2,1)S(1)}, bf16[512,256]{1,0:T(8,128)(2,1)S(1)}, u32[]{:S(2)}, u32[]{:S(2)}) %collective-permute-start.18) | collective-permute-done | bytes 262176 | tf_op jit(solution)/shard_map/ppermute | solution.py:24
  96.0 2.0 collective-permute-start.20
  98.1 3.7 %collective-permute-done.7.refs_7_ = bf16[512,256]{1,0:T(8,128)(2,1)} collective-permute-done((bf16[512,256]{1,0:T(8,128)(2,1)}, bf16[512,256]{1,0:T(8,128)(2,1)}, u32[]{:S(2)}, u32[]{:S(2)}) %collective-permute-start.7) | collective-permute-done | bytes 262176 | tf_op jit(solution)/shard_map/ppermute | solution.py:24
  101.8 1.6 copy-done.1
  103.3 0.9 copy-done.3
  104.3 6.2 %shard_map.46 = f32[4,128,512]{2,1,0:T(8,128)} custom-call(s32[5]{0:T(128)S(1)} %stack.37.z_ref.at_ref, bf16[512,256]{1,0:T(8,128)(2,1)S(1)} %pad_maximum_fusion.refs_0_, bf16[512,256]{1,0:T(8,128)(2,1)S(1)} %collective-permute-done.1.refs_1_, bf16[512,256]{1,0:T(8,128)(2,1)S(1)} %collective-permute-done.2.refs_2_, bf16[512,256]{1,0:T(8,128)(2,1)S(1)} %copy-done.3, ...), custom_call_target="tpu_custom_call" | custom-call | flops 2147483648 | bytes 7340032 | tf_op jit(solution)/shard_map/pallas_call | solution.py:65
  110.5 4.7 %all-to-all-start.1 = ((f32[16,32,512]{2,1,0:T(8,128)}), f32[16,32,512]{2,1,0:T(8,128)}, u32[]{:S(2)}, u32[]{:S(2)}) async-start(f32[16,32,512]{2,1,0:T(8,128)} %bitcast.8), calls=%async_computation.1 | async-start | bytes 2097152 | tf_op jit(solution)/shard_map/all_to_all | solution.py:162
  115.2 0.3 collective-permute-start.21
  115.4 2.0 collective-permute-start.22
  117.5 6.5 %collective-permute-done.21.refs_4_ = bf16[512,256]{1,0:T(8,128)(2,1)S(1)} collective-permute-done((bf16[512,256]{1,0:T(8,128)(2,1)}, bf16[512,256]{1,0:T(8,128)(2,1)S(1)}, u32[]{:S(2)}, u32[]{:S(2)}) %collective-permute-start.21) | collective-permute-done | bytes 262176 | tf_op jit(solution)/shard_map/ppermute | solution.py:24
  124.0 1.5 collective-permute-start.23
  125.5 0.5 collective-permute-start.24
  126.0 5.6 %collective-permute-done.23.refs_6_ = bf16[512,256]{1,0:T(8,128)(2,1)S(1)} collective-permute-done((bf16[512,256]{1,0:T(8,128)(2,1)S(1)}, bf16[512,256]{1,0:T(8,128)(2,1)S(1)}, u32[]{:S(2)}, u32[]{:S(2)}) %collective-permute-start.23) | collective-permute-done | bytes 262176 | tf_op jit(solution)/shard_map/ppermute | solution.py:24
  131.6 2.7 %collective-permute-done.24.refs_7_ = bf16[512,256]{1,0:T(8,128)(2,1)S(1)} collective-permute-done((bf16[512,256]{1,0:T(8,128)(2,1)S(1)}, bf16[512,256]{1,0:T(8,128)(2,1)S(1)}, u32[]{:S(2)}, u32[]{:S(2)}) %collective-permute-start.24) | collective-permute-done | bytes 262176 | tf_op jit(solution)/shard_map/ppermute | solution.py:24
  134.4 6.1 %shard_map.47 = f32[4,128,512]{2,1,0:T(8,128)} custom-call(s32[5]{0:T(128)S(1)} %stack.37.z_ref.at_ref, bf16[512,256]{1,0:T(8,128)(2,1)S(1)} %pad_maximum_fusion.2.refs_0_, bf16[512,256]{1,0:T(8,128)(2,1)S(1)} %collective-permute-done.18.refs_1_, bf16[512,256]{1,0:T(8,128)(2,1)} %collective-permute-done.19.refs_2_, ...), custom_call_target="tpu_custom_call" | custom-call | flops 2147483648 | bytes 7340032 | tf_op jit(solution)/shard_map/pallas_call | solution.py:65
  140.5 4.1 %all-to-all-start.3 = ((f32[4,128,512]{2,1,0:T(8,128)}), f32[4,128,512]{2,1,0:T(8,128)S(1)}, u32[]{:S(2)}, u32[]{:S(2)}) async-start(f32[4,128,512]{2,1,0:T(8,128)} %shard_map.47), calls=%async_computation.3 | async-start | bytes 2097152 | tf_op jit(solution)/shard_map/all_to_all | solution.py:170
  144.6 1.3 bitcast_reduce_fusion
  145.9 2.5 %collective-permute-start.9 = (bf16[4,32,512]{2,1,0:T(8,128)(2,1)S(1)}, bf16[4,32,512]{2,1,0:T(8,128)(2,1)S(1)}, u32[]{:S(2)}, u32[]{:S(2)}) collective-permute-start(bf16[4,32,512]{2,1,0:T(8,128)(2,1)S(1)} %bitcast_reduce_fusion), channel_id=1, source_target_pairs={{0,8},{8,0},{1,9},{9,1},{2,10},{10,2},{3,11},{11,3},{4,12},{12,4},... | collective-permute-start | bytes 393224 | tf_op jit(solution)/shard_map/ppermute | solution.py:24
  148.4 4.1 %collective-permute-done.9 = bf16[4,32,512]{2,1,0:T(8,128)(2,1)S(1)} collective-permute-done((bf16[4,32,512]{2,1,0:T(8,128)(2,1)S(1)}, bf16[4,32,512]{2,1,0:T(8,128)(2,1)S(1)}, u32[]{:S(2)}, u32[]{:S(2)}) %collective-permute-start.9) | collective-permute-done | bytes 131104 | tf_op jit(solution)/shard_map/ppermute | solution.py:24
  152.5 0.1 collective-permute-start.10
  152.6 5.7 %all-to-all-done.3 = f32[4,128,512]{2,1,0:T(8,128)S(1)} async-done(((f32[4,128,512]{2,1,0:T(8,128)}), f32[4,128,512]{2,1,0:T(8,128)S(1)}, u32[]{:S(2)}, u32[]{:S(2)}) %all-to-all-start.3) | async-done | bytes 1048608 | tf_op jit(solution)/shard_map/all_to_all | solution.py:170
  158.3 0.1 reduce_sum.19
  158.4 0.6 collective-permute-start.26
  159.0 4.5 %collective-permute-done.26 = bf16[128,512]{1,0:T(8,128)(2,1)S(1)} collective-permute-done((bf16[128,512]{1,0:T(8,128)(2,1)S(1)}, bf16[128,512]{1,0:T(8,128)(2,1)S(1)}, u32[]{:S(2)}, u32[]{:S(2)}) %collective-permute-start.26) | collective-permute-done | bytes 131104 | tf_op jit(solution)/shard_map/ppermute | solution.py:24
  163.5 1.2 collective-permute-start.27
  164.7 0.6 collective-permute-start.11
  165.3 1.4 collective-permute-start.12
  166.8 1.5 collective-permute-start.28
  168.2 2.4 %collective-permute-done.27.refs_9_ = bf16[2,128,512]{2,1,0:T(8,128)(2,1)S(1)} collective-permute-done((bf16[2,128,512]{2,1,0:T(8,128)(2,1)S(1)}, bf16[2,128,512]{2,1,0:T(8,128)(2,1)S(1)}, u32[]{:S(2)}, u32[]{:S(2)}) %collective-permute-start.27) | collective-permute-done | bytes 262176 | tf_op jit(solution)/shard_map/ppermute | solution.py:24
  170.7 0.4 collective-permute-done.11.refs_2_
  171.1 1.8 collective-permute-start.13
  172.9 0.0 collective-permute-done.12.refs_3_
  172.9 0.2 collective-permute-start.14
  173.1 1.6 collective-permute-done.28.refs_10_
  174.7 2.7 %collective-permute-done.29.refs_11_ = bf16[2,128,512]{2,1,0:T(8,128)(2,1)S(1)} collective-permute-done((bf16[2,128,512]{2,1,0:T(8,128)(2,1)S(1)}, bf16[2,128,512]{2,1,0:T(8,128)(2,1)S(1)}, u32[]{:S(2)}, u32[]{:S(2)}) %collective-permute-start.29) | collective-permute-done | bytes 262176 | tf_op jit(solution)/shard_map/ppermute | solution.py:24
  177.5 0.5 collective-permute-start.33
  178.0 1.4 collective-permute-done.13.refs_4_
  179.4 2.4 %collective-permute-start.15 = (bf16[2,4,32,512]{3,2,1,0:T(8,128)(2,1)S(1)}, bf16[2,4,32,512]{3,2,1,0:T(8,128)(2,1)S(1)}, u32[]{:S(2)}, u32[]{:S(2)}) collective-permute-start(bf16[2,4,32,512]{3,2,1,0:T(8,128)(2,1)S(1)} %collective-permute-done.13.refs_4_), channel_id=1, source_target_pairs={{0,7},{1,0},{2,1},{3,2},{4,3},{5,4},{6,5},{7,6},{8,15},{9,8},{10,9... | collective-permute-start | bytes 786440 | tf_op jit(solution)/shard_map/ppermute | solution.py:24
  181.8 5.1 %collective-permute-done.15.refs_6_ = bf16[2,4,32,512]{3,2,1,0:T(8,128)(2,1)S(1)} collective-permute-done((bf16[2,4,32,512]{3,2,1,0:T(8,128)(2,1)S(1)}, bf16[2,4,32,512]{3,2,1,0:T(8,128)(2,1)S(1)}, u32[]{:S(2)}, u32[]{:S(2)}) %collective-permute-start.15) | collective-permute-done | bytes 262176 | tf_op jit(solution)/shard_map/ppermute | solution.py:24
  186.9 2.7 %collective-permute-done.16.refs_7_ = bf16[2,4,32,512]{3,2,1,0:T(8,128)(2,1)S(1)} collective-permute-done((bf16[2,4,32,512]{3,2,1,0:T(8,128)(2,1)S(1)}, bf16[2,4,32,512]{3,2,1,0:T(8,128)(2,1)S(1)}, u32[]{:S(2)}, u32[]{:S(2)}) %collective-permute-start.16) | collective-permute-done | bytes 262176 | tf_op jit(solution)/shard_map/ppermute | solution.py:24
  189.5 3.5 %shard_map.48 = f32[4,128,512]{2,1,0:T(8,128)S(1)} custom-call(s32[5]{0:T(128)S(1)} %stack.37.z_ref.at_ref, bf16[2,4,32,512]{3,2,1,0:T(8,128)(2,1)S(1)} %pad_maximum_fusion.1.refs_0_, bf16[2,4,32,512]{3,2,1,0:T(8,128)(2,1)S(1)} %collective-permute-done.10.refs_1_, bf16[2,4,32,512]{3,2,1,0:T(8,128)(2,1)S(1)} %collective-permute-done.11.refs_2_, ...), custom_call_target="tpu_custom_call" | custom-call | flops 1073741824 | bytes 5242880 | tf_op jit(solution)/shard_map/pallas_call | solution.py:105
  193.0 20.5 %all_to_all.25.in_ref = f32[4,128,512]{2,1,0:T(8,128)S(1)} all-to-all(f32[4,128,512]{2,1,0:T(8,128)S(1)} %shard_map.48), channel_id=1, replica_groups=mesh['xl'=2,'c'=2,'y'=4,'xh'=2,'z'=8] {'y'}, dimensions={0} | all-to-all | bytes 2097152 | tf_op jit(solution)/shard_map/all_to_all | solution.py:178
  213.6 2.4 %shard_map.49 = f32[128,2048]{1,0:T(8,128)} custom-call(f32[4,128,512]{2,1,0:T(8,128)S(1)} %all_to_all.25.in_ref), custom_call_target="tpu_custom_call" | custom-call | tf_op jit(solution)/shard_map/pallas_call | solution.py:128
  (40 shorter events, 0.2 us)
Async XLA Ops:
  3.0 30.8 %all-to-all-start = ((f32[4,1024,128]{2,1,0:T(8,128)}), f32[4,1024,128]{2,1,0:T(8,128)S(1)}, u32[]{:S(2)}, u32[]{:S(2)}) async-start(f32[4,1024,128]{2,1,0:T(8,128)} %dynamic-slice_bitcast_fusion.1), calls=%async_computation | async-start | bytes 4194304 | tf_op jit(solution)/shard_map/all_to_all | solution.py:141
  10.6 28.3 %copy-start.4 = (bf16[1,512,128]{2,1,0:T(8,128)(2,1)S(1)}, bf16[1,512,128]{2,1,0:T(8,128)(2,1)}, u32[]{:S(2)}) copy-start(bf16[1,512,128]{2,1,0:T(8,128)(2,1)} %param.4) | copy-start | bytes 393220
  10.6 59.4 %copy-start.5 = (bf16[1,512,128]{2,1,0:T(8,128)(2,1)S(1)}, bf16[1,512,128]{2,1,0:T(8,128)(2,1)}, u32[]{:S(2)}) copy-start(bf16[1,512,128]{2,1,0:T(8,128)(2,1)} %param.5) | copy-start | bytes 393220
  33.8 1.3 copy-start
  35.2 29.0 %all-to-all-start.2 = ((f32[4,1024,128]{2,1,0:T(8,128)}), f32[4,1024,128]{2,1,0:T(8,128)S(1)}, u32[]{:S(2)}, u32[]{:S(2)}) async-start(f32[4,1024,128]{2,1,0:T(8,128)} %dynamic-slice_bitcast_fusion), calls=%async_computation.2 | async-start | bytes 4194304 | tf_op jit(solution)/shard_map/all_to_all | solution.py:141
  38.8 63.0 %collective-permute-start.8 = (f32[4,1024,128]{2,1,0:T(8,128)}, f32[4,1024,128]{2,1,0:T(8,128)}, u32[]{:S(2)}, u32[]{:S(2)}) collective-permute-start(f32[4,1024,128]{2,1,0:T(8,128)} %copy-done), channel_id=1, source_target_pairs={{0,64},{64,0},{1,65},{65,1},{2,66},{66,2},{3,67},{67,3},{4,68},{68... | collective-permute-start | bytes 6291464 | tf_op jit(solution)/shard_map/ppermute | solution.py:24
  38.9 7.4 %collective-permute-start = (bf16[512,128]{1,0:T(8,128)(2,1)S(1)}, bf16[512,128]{1,0:T(8,128)(2,1)S(1)}, u32[]{:S(2)}, u32[]{:S(2)}) collective-permute-start(bf16[512,128]{1,0:T(8,128)(2,1)S(1)} %bitcast.32), channel_id=1, source_target_pairs={{0,8},{8,0},{1,9},{9,1},{2,10},{10,2},{3,11},{11,3},{4,12},{12,4},... | collective-permute-start | bytes 393224 | tf_op jit(solution)/shard_map/ppermute | solution.py:24
  46.4 23.6 %collective-permute-start.1 = (bf16[512,256]{1,0:T(8,128)(2,1)S(1)}, bf16[512,256]{1,0:T(8,128)(2,1)S(1)}, u32[]{:S(2)}, u32[]{:S(2)}) collective-permute-start(bf16[512,256]{1,0:T(8,128)(2,1)S(1)} %pad_maximum_fusion.refs_0_), channel_id=1, source_target_pairs={{0,1},{1,2},{2,3},{3,4},{4,5},{5,6},{6,7},{7,0},{8,9},{9,10},{10,1... | collective-permute-start | bytes 786440 | tf_op jit(solution)/shard_map/ppermute | solution.py:24
  64.2 70.2 %collective-permute-start.25 = (f32[4,1024,128]{2,1,0:T(8,128)S(1)}, f32[4,1024,128]{2,1,0:T(8,128)}, u32[]{:S(2)}, u32[]{:S(2)}) collective-permute-start(f32[4,1024,128]{2,1,0:T(8,128)S(1)} %all-to-all-done.2.refs_8_), channel_id=1, source_target_pairs={{0,64},{64,0},{1,65},{65,1},{2,66},{66,2},{3,67},{67,3},{4,68},{68... | collective-permute-start | bytes 6291464 | tf_op jit(solution)/shard_map/ppermute | solution.py:24
  64.2 12.1 %collective-permute-start.2 = (bf16[512,256]{1,0:T(8,128)(2,1)S(1)}, bf16[512,256]{1,0:T(8,128)(2,1)S(1)}, u32[]{:S(2)}, u32[]{:S(2)}) collective-permute-start(bf16[512,256]{1,0:T(8,128)(2,1)S(1)} %pad_maximum_fusion.refs_0_), channel_id=1, source_target_pairs={{0,7},{1,0},{2,1},{3,2},{4,3},{5,4},{6,5},{7,6},{8,15},{9,8},{10,9... | collective-permute-start | bytes 786440 | tf_op jit(solution)/shard_map/ppermute | solution.py:24
  70.0 9.9 %collective-permute-start.3 = (bf16[512,256]{1,0:T(8,128)(2,1)S(1)}, bf16[512,256]{1,0:T(8,128)(2,1)S(1)}, u32[]{:S(2)}, u32[]{:S(2)}) collective-permute-start(bf16[512,256]{1,0:T(8,128)(2,1)S(1)} %collective-permute-done.1.refs_1_), channel_id=1, source_target_pairs={{0,1},{1,2},{2,3},{3,4},{4,5},{5,6},{6,7},{7,0},{8,9},{9,10},{10,1... | collective-permute-start | bytes 786440 | tf_op jit(solution)/shard_map/ppermute | solution.py:24
  70.0 9.9 %collective-permute-start.17 = (bf16[512,128]{1,0:T(8,128)(2,1)S(1)}, bf16[512,128]{1,0:T(8,128)(2,1)S(1)}, u32[]{:S(2)}, u32[]{:S(2)}) collective-permute-start(bf16[512,128]{1,0:T(8,128)(2,1)S(1)} %bitcast.33), channel_id=1, source_target_pairs={{0,8},{8,0},{1,9},{9,1},{2,10},{10,2},{3,11},{11,3},{4,12},{12,4},... | collective-permute-start | bytes 393224 | tf_op jit(solution)/shard_map/ppermute | solution.py:24
  76.3 9.1 %collective-permute-start.4 = (bf16[512,256]{1,0:T(8,128)(2,1)S(1)}, bf16[512,256]{1,0:T(8,128)(2,1)}, u32[]{:S(2)}, u32[]{:S(2)}) collective-permute-start(bf16[512,256]{1,0:T(8,128)(2,1)S(1)} %collective-permute-done.2.refs_2_), channel_id=1, source_target_pairs={{0,7},{1,0},{2,1},{3,2},{4,3},{5,4},{6,5},{7,6},{8,15},{9,8},{10,9... | collective-permute-start | bytes 786440 | tf_op jit(solution)/shard_map/ppermute | solution.py:24
  80.0 5.5 %copy-start.2 = (bf16[512,256]{1,0:T(8,128)(2,1)}, bf16[512,256]{1,0:T(8,128)(2,1)S(1)}, u32[]{:S(2)}) copy-start(bf16[512,256]{1,0:T(8,128)(2,1)S(1)} %collective-permute-done.3.refs_3_) | copy-start | bytes 786436
  80.0 10.6 %collective-permute-start.5 = (bf16[512,256]{1,0:T(8,128)(2,1)S(1)}, bf16[512,256]{1,0:T(8,128)(2,1)}, u32[]{:S(2)}, u32[]{:S(2)}) collective-permute-start(bf16[512,256]{1,0:T(8,128)(2,1)S(1)} %collective-permute-done.3.refs_3_), channel_id=1, source_target_pairs={{0,1},{1,2},{2,3},{3,4},{4,5},{5,6},{6,7},{7,0},{8,9},{9,10},{10,1... | collective-permute-start | bytes 786440 | tf_op jit(solution)/shard_map/ppermute | solution.py:24
  80.0 16.0 %collective-permute-start.18 = (bf16[512,256]{1,0:T(8,128)(2,1)S(1)}, bf16[512,256]{1,0:T(8,128)(2,1)S(1)}, u32[]{:S(2)}, u32[]{:S(2)}) collective-permute-start(bf16[512,256]{1,0:T(8,128)(2,1)S(1)} %pad_maximum_fusion.2.refs_0_), channel_id=1, source_target_pairs={{0,1},{1,2},{2,3},{3,4},{4,5},{5,6},{6,7},{7,0},{8,9},{9,10},{10,1... | collective-permute-start | bytes 786440 | tf_op jit(solution)/shard_map/ppermute | solution.py:24
  85.4 10.6 %collective-permute-start.6 = (bf16[512,256]{1,0:T(8,128)(2,1)}, bf16[512,256]{1,0:T(8,128)(2,1)}, u32[]{:S(2)}, u32[]{:S(2)}) collective-permute-start(bf16[512,256]{1,0:T(8,128)(2,1)} %collective-permute-done.4.refs_4_), channel_id=1, source_target_pairs={{0,7},{1,0},{2,1},{3,2},{4,3},{5,4},{6,5},{7,6},{8,15},{9,8},{10,9... | collective-permute-start | bytes 786440 | tf_op jit(solution)/shard_map/ppermute | solution.py:24
  90.5 11.2 %collective-permute-start.7 = (bf16[512,256]{1,0:T(8,128)(2,1)}, bf16[512,256]{1,0:T(8,128)(2,1)}, u32[]{:S(2)}, u32[]{:S(2)}) collective-permute-start(bf16[512,256]{1,0:T(8,128)(2,1)} %collective-permute-done.5.refs_5_), channel_id=1, source_target_pairs={{0,1},{1,2},{2,3},{3,4},{4,5},{5,6},{6,7},{7,0},{8,9},{9,10},{10,1... | collective-permute-start | bytes 786440 | tf_op jit(solution)/shard_map/ppermute | solution.py:24
  96.0 19.1 %collective-permute-start.19 = (bf16[512,256]{1,0:T(8,128)(2,1)S(1)}, bf16[512,256]{1,0:T(8,128)(2,1)}, u32[]{:S(2)}, u32[]{:S(2)}) collective-permute-start(bf16[512,256]{1,0:T(8,128)(2,1)S(1)} %pad_maximum_fusion.2.refs_0_), channel_id=1, source_target_pairs={{0,7},{1,0},{2,1},{3,2},{4,3},{5,4},{6,5},{7,6},{8,15},{9,8},{10,9... | collective-permute-start | bytes 786440 | tf_op jit(solution)/shard_map/ppermute | solution.py:24
  96.0 19.4 %collective-permute-start.20 = (bf16[512,256]{1,0:T(8,128)(2,1)S(1)}, bf16[512,256]{1,0:T(8,128)(2,1)}, u32[]{:S(2)}, u32[]{:S(2)}) collective-permute-start(bf16[512,256]{1,0:T(8,128)(2,1)S(1)} %collective-permute-done.18.refs_1_), channel_id=1, source_target_pairs={{0,1},{1,2},{2,3},{3,4},{4,5},{5,6},{6,7},{7,0},{8,9},{9,10},{10,1... | collective-permute-start | bytes 786440 | tf_op jit(solution)/shard_map/ppermute | solution.py:24
  101.8 1.6 copy-start.1
  103.3 0.9 copy-start.3
  110.5 30.0 %all-to-all-start.1 = ((f32[16,32,512]{2,1,0:T(8,128)}), f32[16,32,512]{2,1,0:T(8,128)}, u32[]{:S(2)}, u32[]{:S(2)}) async-start(f32[16,32,512]{2,1,0:T(8,128)} %bitcast.8), calls=%async_computation.1 | async-start | bytes 2097152 | tf_op jit(solution)/shard_map/all_to_all | solution.py:162
  115.2 8.8 %collective-permute-start.21 = (bf16[512,256]{1,0:T(8,128)(2,1)}, bf16[512,256]{1,0:T(8,128)(2,1)S(1)}, u32[]{:S(2)}, u32[]{:S(2)}) collective-permute-start(bf16[512,256]{1,0:T(8,128)(2,1)} %collective-permute-done.19.refs_2_), channel_id=1, source_target_pairs={{0,7},{1,0},{2,1},{3,2},{4,3},{5,4},{6,5},{7,6},{8,15},{9,8},{10,9... | collective-permute-start | bytes 786440 | tf_op jit(solution)/shard_map/ppermute | solution.py:24
  115.4 10.1 %collective-permute-start.22 = (bf16[512,256]{1,0:T(8,128)(2,1)}, bf16[512,256]{1,0:T(8,128)(2,1)S(1)}, u32[]{:S(2)}, u32[]{:S(2)}) collective-permute-start(bf16[512,256]{1,0:T(8,128)(2,1)} %collective-permute-done.20.refs_3_), channel_id=1, source_target_pairs={{0,1},{1,2},{2,3},{3,4},{4,5},{5,6},{6,7},{7,0},{8,9},{9,10},{10,1... | collective-permute-start | bytes 786440 | tf_op jit(solution)/shard_map/ppermute | solution.py:24
  124.0 7.6 %collective-permute-start.23 = (bf16[512,256]{1,0:T(8,128)(2,1)S(1)}, bf16[512,256]{1,0:T(8,128)(2,1)S(1)}, u32[]{:S(2)}, u32[]{:S(2)}) collective-permute-start(bf16[512,256]{1,0:T(8,128)(2,1)S(1)} %collective-permute-done.21.refs_4_), channel_id=1, source_target_pairs={{0,7},{1,0},{2,1},{3,2},{4,3},{5,4},{6,5},{7,6},{8,15},{9,8},{10,9... | collective-permute-start | bytes 786440 | tf_op jit(solution)/shard_map/ppermute | solution.py:24
  125.5 8.9 %collective-permute-start.24 = (bf16[512,256]{1,0:T(8,128)(2,1)S(1)}, bf16[512,256]{1,0:T(8,128)(2,1)S(1)}, u32[]{:S(2)}, u32[]{:S(2)}) collective-permute-start(bf16[512,256]{1,0:T(8,128)(2,1)S(1)} %collective-permute-done.22.refs_5_), channel_id=1, source_target_pairs={{0,1},{1,2},{2,3},{3,4},{4,5},{5,6},{6,7},{7,0},{8,9},{9,10},{10,1... | collective-permute-start | bytes 786440 | tf_op jit(solution)/shard_map/ppermute | solution.py:24
  140.5 17.8 %all-to-all-start.3 = ((f32[4,128,512]{2,1,0:T(8,128)}), f32[4,128,512]{2,1,0:T(8,128)S(1)}, u32[]{:S(2)}, u32[]{:S(2)}) async-start(f32[4,128,512]{2,1,0:T(8,128)} %shard_map.47), calls=%async_computation.3 | async-start | bytes 2097152 | tf_op jit(solution)/shard_map/all_to_all | solution.py:170
  145.9 6.6 %collective-permute-start.9 = (bf16[4,32,512]{2,1,0:T(8,128)(2,1)S(1)}, bf16[4,32,512]{2,1,0:T(8,128)(2,1)S(1)}, u32[]{:S(2)}, u32[]{:S(2)}) collective-permute-start(bf16[4,32,512]{2,1,0:T(8,128)(2,1)S(1)} %bitcast_reduce_fusion), channel_id=1, source_target_pairs={{0,8},{8,0},{1,9},{9,1},{2,10},{10,2},{3,11},{11,3},{4,12},{12,4},... | collective-permute-start | bytes 393224 | tf_op jit(solution)/shard_map/ppermute | solution.py:24
  152.5 12.8 %collective-permute-start.10 = (bf16[2,4,32,512]{3,2,1,0:T(8,128)(2,1)S(1)}, bf16[2,4,32,512]{3,2,1,0:T(8,128)(2,1)S(1)}, u32[]{:S(2)}, u32[]{:S(2)}) collective-permute-start(bf16[2,4,32,512]{3,2,1,0:T(8,128)(2,1)S(1)} %pad_maximum_fusion.1.refs_0_), channel_id=1, source_target_pairs={{0,1},{1,2},{2,3},{3,4},{4,5},{5,6},{6,7},{7,0},{8,9},{9,10},{10,1... | collective-permute-start | bytes 786440 | tf_op jit(solution)/shard_map/ppermute | solution.py:24
  158.4 5.1 %collective-permute-start.26 = (bf16[128,512]{1,0:T(8,128)(2,1)S(1)}, bf16[128,512]{1,0:T(8,128)(2,1)S(1)}, u32[]{:S(2)}, u32[]{:S(2)}) collective-permute-start(bf16[128,512]{1,0:T(8,128)(2,1)S(1)} %reduce_sum.19), channel_id=1, source_target_pairs={{0,128},{128,0},{1,129},{129,1},{2,130},{130,2},{3,131},{131,3},{4... | collective-permute-start | bytes 393224 | tf_op jit(solution)/shard_map/ppermute | solution.py:24
  163.5 7.2 %collective-permute-start.27 = (bf16[2,128,512]{2,1,0:T(8,128)(2,1)S(1)}, bf16[2,128,512]{2,1,0:T(8,128)(2,1)S(1)}, u32[]{:S(2)}, u32[]{:S(2)}) collective-permute-start(bf16[2,128,512]{2,1,0:T(8,128)(2,1)S(1)} %pad_maximum_fusion.3.refs_8_), channel_id=1, source_target_pairs={{0,48},{16,0},{32,16},{48,32},{1,49},{17,1},{33,17},{49,33},{2,50}... | collective-permute-start | bytes 786440 | tf_op jit(solution)/shard_map/ppermute | solution.py:24
  164.7 6.4 %collective-permute-start.11 = (bf16[2,4,32,512]{3,2,1,0:T(8,128)(2,1)S(1)}, bf16[2,4,32,512]{3,2,1,0:T(8,128)(2,1)S(1)}, u32[]{:S(2)}, u32[]{:S(2)}) collective-permute-start(bf16[2,4,32,512]{3,2,1,0:T(8,128)(2,1)S(1)} %pad_maximum_fusion.1.refs_0_), channel_id=1, source_target_pairs={{0,7},{1,0},{2,1},{3,2},{4,3},{5,4},{6,5},{7,6},{8,15},{9,8},{10,9... | collective-permute-start | bytes 786440 | tf_op jit(solution)/shard_map/ppermute | solution.py:24
  165.3 7.6 %collective-permute-start.12 = (bf16[2,4,32,512]{3,2,1,0:T(8,128)(2,1)S(1)}, bf16[2,4,32,512]{3,2,1,0:T(8,128)(2,1)S(1)}, u32[]{:S(2)}, u32[]{:S(2)}) collective-permute-start(bf16[2,4,32,512]{3,2,1,0:T(8,128)(2,1)S(1)} %collective-permute-done.10.refs_1_), channel_id=1, source_target_pairs={{0,1},{1,2},{2,3},{3,4},{4,5},{5,6},{6,7},{7,0},{8,9},{9,10},{10,1... | collective-permute-start | bytes 786440 | tf_op jit(solution)/shard_map/ppermute | solution.py:24
  166.8 8.0 %collective-permute-start.28 = (bf16[2,128,512]{2,1,0:T(8,128)(2,1)S(1)}, bf16[2,128,512]{2,1,0:T(8,128)(2,1)S(1)}, u32[]{:S(2)}, u32[]{:S(2)}) collective-permute-start(bf16[2,128,512]{2,1,0:T(8,128)(2,1)S(1)} %pad_maximum_fusion.3.refs_8_), channel_id=1, source_target_pairs={{0,32},{16,48},{32,0},{48,16},{1,33},{17,49},{33,1},{49,17},{2,34}... | collective-permute-start | bytes 786440 | tf_op jit(solution)/shard_map/ppermute | solution.py:24
  168.2 9.2 %collective-permute-start.29 = (bf16[2,128,512]{2,1,0:T(8,128)(2,1)S(1)}, bf16[2,128,512]{2,1,0:T(8,128)(2,1)S(1)}, u32[]{:S(2)}, u32[]{:S(2)}) collective-permute-start(bf16[2,128,512]{2,1,0:T(8,128)(2,1)S(1)} %pad_maximum_fusion.3.refs_8_), channel_id=1, source_target_pairs={{0,16},{16,32},{32,48},{48,0},{1,17},{17,33},{33,49},{49,1},{2,18}... | collective-permute-start | bytes 786440 | tf_op jit(solution)/shard_map/ppermute | solution.py:24
  170.7 6.8 %collective-permute-start.30 = (bf16[2,128,512]{2,1,0:T(8,128)(2,1)S(1)}, bf16[2,128,512]{2,1,0:T(8,128)(2,1)S(1)}, u32[]{:S(2)}, u32[]{:S(2)}) collective-permute-start(bf16[2,128,512]{2,1,0:T(8,128)(2,1)S(1)} %pad_maximum_fusion.3.refs_8_), channel_id=1, source_target_pairs={{0,64},{64,0},{1,65},{65,1},{2,66},{66,2},{3,67},{67,3},{4,68},{68... | collective-permute-start | bytes 786440 | tf_op jit(solution)/shard_map/ppermute | solution.py:24
  171.1 8.3 %collective-permute-start.13 = (bf16[2,4,32,512]{3,2,1,0:T(8,128)(2,1)S(1)}, bf16[2,4,32,512]{3,2,1,0:T(8,128)(2,1)S(1)}, u32[]{:S(2)}, u32[]{:S(2)}) collective-permute-start(bf16[2,4,32,512]{3,2,1,0:T(8,128)(2,1)S(1)} %collective-permute-done.11.refs_2_), channel_id=1, source_target_pairs={{0,7},{1,0},{2,1},{3,2},{4,3},{5,4},{6,5},{7,6},{8,15},{9,8},{10,9... | collective-permute-start | bytes 786440 | tf_op jit(solution)/shard_map/ppermute | solution.py:24
  172.9 8.8 %collective-permute-start.14 = (bf16[2,4,32,512]{3,2,1,0:T(8,128)(2,1)S(1)}, bf16[2,4,32,512]{3,2,1,0:T(8,128)(2,1)S(1)}, u32[]{:S(2)}, u32[]{:S(2)}) collective-permute-start(bf16[2,4,32,512]{3,2,1,0:T(8,128)(2,1)S(1)} %collective-permute-done.12.refs_3_), channel_id=1, source_target_pairs={{0,1},{1,2},{2,3},{3,4},{4,5},{5,6},{6,7},{7,0},{8,9},{9,10},{10,1... | collective-permute-start | bytes 786440 | tf_op jit(solution)/shard_map/ppermute | solution.py:24
  174.7 7.0 %collective-permute-start.31 = (bf16[2,128,512]{2,1,0:T(8,128)(2,1)S(1)}, bf16[2,128,512]{2,1,0:T(8,128)(2,1)S(1)}, u32[]{:S(2)}, u32[]{:S(2)}) collective-permute-start(bf16[2,128,512]{2,1,0:T(8,128)(2,1)S(1)} %collective-permute-done.27.refs_9_), channel_id=1, source_target_pairs={{0,64},{64,0},{1,65},{65,1},{2,66},{66,2},{3,67},{67,3},{4,68},{68... | collective-permute-start | bytes 786440 | tf_op jit(solution)/shard_map/ppermute | solution.py:24
  177.4 4.3 %collective-permute-start.32 = (bf16[2,128,512]{2,1,0:T(8,128)(2,1)S(1)}, bf16[2,128,512]{2,1,0:T(8,128)(2,1)S(1)}, u32[]{:S(2)}, u32[]{:S(2)}) collective-permute-start(bf16[2,128,512]{2,1,0:T(8,128)(2,1)S(1)} %collective-permute-done.28.refs_10_), channel_id=1, source_target_pairs={{0,64},{64,0},{1,65},{65,1},{2,66},{66,2},{3,67},{67,3},{4,68},{68... | collective-permute-start | bytes 786440 | tf_op jit(solution)/shard_map/ppermute | solution.py:24
  177.5 4.3 %collective-permute-start.33 = (bf16[2,128,512]{2,1,0:T(8,128)(2,1)S(1)}, bf16[2,128,512]{2,1,0:T(8,128)(2,1)S(1)}, u32[]{:S(2)}, u32[]{:S(2)}) collective-permute-start(bf16[2,128,512]{2,1,0:T(8,128)(2,1)S(1)} %collective-permute-done.29.refs_11_), channel_id=1, source_target_pairs={{0,64},{64,0},{1,65},{65,1},{2,66},{66,2},{3,67},{67,3},{4,68},{68... | collective-permute-start | bytes 786440 | tf_op jit(solution)/shard_map/ppermute | solution.py:24
  179.4 7.5 %collective-permute-start.15 = (bf16[2,4,32,512]{3,2,1,0:T(8,128)(2,1)S(1)}, bf16[2,4,32,512]{3,2,1,0:T(8,128)(2,1)S(1)}, u32[]{:S(2)}, u32[]{:S(2)}) collective-permute-start(bf16[2,4,32,512]{3,2,1,0:T(8,128)(2,1)S(1)} %collective-permute-done.13.refs_4_), channel_id=1, source_target_pairs={{0,7},{1,0},{2,1},{3,2},{4,3},{5,4},{6,5},{7,6},{8,15},{9,8},{10,9... | collective-permute-start | bytes 786440 | tf_op jit(solution)/shard_map/ppermute | solution.py:24
  181.8 7.8 %collective-permute-start.16 = (bf16[2,4,32,512]{3,2,1,0:T(8,128)(2,1)S(1)}, bf16[2,4,32,512]{3,2,1,0:T(8,128)(2,1)S(1)}, u32[]{:S(2)}, u32[]{:S(2)}) collective-permute-start(bf16[2,4,32,512]{3,2,1,0:T(8,128)(2,1)S(1)} %collective-permute-done.14.refs_5_), channel_id=1, source_target_pairs={{0,1},{1,2},{2,3},{3,4},{4,5},{5,6},{6,7},{7,0},{8,9},{9,10},{10,1... | collective-permute-start | bytes 786440 | tf_op jit(solution)/shard_map/ppermute | solution.py:24

commit v2 on v1

v2 whole, which is shorter than its diff:
```python
import functools

import jax
import jax.numpy as jnp
from jax import lax
from jax.experimental import pallas as pl
from jax.experimental.pallas import tpu as pltpu
from jax.sharding import Mesh, PartitionSpec as P

AXES = ("xl", "c", "y", "xh", "z")
SIZES = (2, 2, 4, 2, 8)
DP = ("xl", "c")
TILE = ("y", "xh", "z")
TOK = 512
COLS = 128
F32 = jnp.float32
BF16 = jnp.bfloat16
VMEM_LIMIT = 48 * 1024 * 1024
PARAMS = pltpu.CompilerParams(vmem_limit_bytes=VMEM_LIMIT)


def shift(x, axis, by):
    n = lax.axis_size(axis)
    return lax.ppermute(x, axis, [(i, (i + by) % n) for i in range(n)])


def after(x, *others):
    return lax.optimization_barrier((x, *others))[0]


def whole(shape):
    return pl.BlockSpec(shape, lambda *_: (0,) * len(shape))


def split_kernel(core_ref, in_ref, out_ref):
    exact = in_ref[...]
    high = exact.astype(BF16)
    out_ref[0, :, :COLS] = high
    out_ref[0, :, COLS:] = (exact - high.astype(F32)).astype(BF16)


def split_basis(core, basis):
    return pl.pallas_call(
        split_kernel,
        grid_spec=pltpu.PrefetchScalarGridSpec(
            num_scalar_prefetch=1,
            grid=(4,),
            in_specs=[pl.BlockSpec((1024, COLS), lambda g, core: (g * 2 + core[0], 0))],
            out_specs=pl.BlockSpec((1, 1024, 256), lambda g, core: (g, 0, 0)),
        ),
        out_shape=jax.ShapeDtypeStruct((4, 1024, 256), BF16),
        compiler_params=PARAMS,
        cost_estimate=pl.CostEstimate(
            flops=1 << 20, bytes_accessed=4 << 20, transcendentals=0
        ),
    )(core, basis)


def rotate_kernel(places, at_ref, *refs):
    blocks, (own_ref, other_ref, out_ref, lhs) = refs[: len(places)], refs[len(places) :]

    @pl.when(pl.program_id(0) == 0)
    def _():
        z, xh, c = at_ref[0], at_ref[1], at_ref[4]
        turned = lax.rem(xh + c, 2)
        for block, parts in zip(blocks, places):
            for i, (offset, side) in enumerate(parts):
                half = turned if side == 0 else 1 - turned
                at = (half * 8 + lax.rem(z + 8 + offset, 8)) * COLS
                lhs[:, pl.ds(pl.multiple_of(at, COLS), COLS)] = block[i]

    both = jnp.dot(lhs[:, :1024], own_ref[0], preferred_element_type=F32)
    both += jnp.dot(lhs[:, 1024:], other_ref[0], preferred_element_type=F32)
    out_ref[0] = (both[:, :COLS] + both[:, COLS:]).T


def rotate(at, blocks, places, own, other):
    slab = pl.BlockSpec((1, 1024, 256), lambda g: (g, 0, 0))
    return pl.pallas_call(
        functools.partial(rotate_kernel, places),
        grid=(4,),
        out_shape=jax.ShapeDtypeStruct((4, COLS, TOK), F32),
        in_specs=[pl.BlockSpec(memory_space=pltpu.SMEM)]
        + [whole(b.shape) for b in blocks]
        + [slab, slab],
        out_specs=pl.BlockSpec((1, COLS, TOK), lambda g: (g, 0, 0)),
        scratch_shapes=[pltpu.VMEM((TOK, 2048), BF16)],
        compiler_params=PARAMS,
        cost_estimate=pl.CostEstimate(
            flops=4 * TOK * 2048 * 512, bytes_accessed=7 << 20, transcendentals=0
        ),
    )(at, *blocks, own, other)


def product_kernel(scale, places, at_ref, *refs):
    n = len(places)
    acts, grads, out_ref, right = refs[:n], refs[n : n + 2], refs[n + 2], refs[n + 3]
    z, xh, y, xl, c = (at_ref[i] for i in range(5))
    for block, parts in zip(acts, places):
        for i, (offset, side) in enumerate(parts):
            place = (xh if side == 0 else 1 - xh) * 8 + lax.rem(z + 8 + offset, 8)
            for s in range(4):
                right[s, pl.ds(pl.multiple_of(place * 32, 32), 32), :] = block[i, s]
    for row in range(4):
        total = None
        for core in range(2):
            for side in range(2):
                s = side * 2 + (c if core == 0 else 1 - c)
                part = lax.dot_general(
                    grads[core][side, row],
                    right[s],
                    (((1,), (1,)), ((), ())),
                    preferred_element_type=F32,
                )
                total = part * part if total is None else total + part * part
        out_ref[row] = total * scale


def products(at, acts, places, grads, scale):
    return pl.pallas_call(
        functools.partial(product_kernel, scale, places),
        out_shape=jax.ShapeDtypeStruct((4, COLS, 512), F32),
        in_specs=[pl.BlockSpec(memory_space=pltpu.SMEM)]
        + [pl.BlockSpec(memory_space=pltpu.VMEM)] * (len(acts) + 2),
        out_specs=pl.BlockSpec(memory_space=pltpu.VMEM),
        scratch_shapes=[pltpu.VMEM((4, 512, TOK), BF16)],
        compiler_params=PARAMS,
        cost_estimate=pl.CostEstimate(
            flops=2 * 4 * 512 * 512 * TOK, bytes_accessed=5 << 20, transcendentals=0
        ),
    )(at, *acts, *grads)


def weave_kernel(in_ref, out_ref):
    for tile in range(4):
        lanes = slice(tile * 32, tile * 32 + 32)
        out_ref[:, tile * COLS : (tile + 1) * COLS] = jnp.concatenate(
            [in_ref[q, :, lanes] for q in range(4)], axis=1
        )


def weave(parts):
    return pl.pallas_call(
        weave_kernel,
        grid=(4,),
        out_shape=jax.ShapeDtypeStruct((COLS, 2048), F32),
        in_specs=[pl.BlockSpec((4, COLS, 128), lambda g: (0, 0, g))],
        out_specs=pl.BlockSpec((COLS, 512), lambda g: (0, g)),
        compiler_params=PARAMS,
    )(parts)


def sync(*arrays):
    return lax.optimization_barrier(arrays)


def ring_step(up, down):
    return shift(up, "z", 1), shift(down, "z", -1)


PAIR = ((0, 0), (0, 1))


def both_sides(offset):
    return ((offset, 0), (offset, 1))


def body(activations, gradients, basis_in, basis_out):
    z, xh, y, xl, c = (lax.axis_index(a) for a in ("z", "xh", "y", "xl", "c"))
    at = jnp.stack([z, xh, y, xl, c]).astype(jnp.int32)
    core = c.astype(jnp.int32).reshape(1)

    own_in = lax.all_to_all(split_basis(core, basis_in), "y", 0, 0)
    acts_other = shift(activations, "xh", 1)
    g_up1, g_down1 = ring_step(gradients, gradients)
    acts_other, g_up1, g_down1, basis_out = sync(acts_other, g_up1, g_down1, basis_out)

    a0 = jnp.concatenate([activations, acts_other])
    g_near = jnp.concatenate([gradients, g_up1, g_down1])
    a_up1, a_down1 = ring_step(a0, a0)
    g_near_other = shift(g_near, "xh", 1)
    g_up2, g_down2 = ring_step(g_up1, g_down1)
    mine_out = split_basis(core, basis_out)
    a_up1, a_down1, g_near_other, g_up2, g_down2, mine_out = sync(
        a_up1, a_down1, g_near_other, g_up2, g_down2, mine_out
    )

    a_up2, a_down2 = ring_step(a_up1, a_down1)
    g_two = jnp.concatenate([g_up2, g_down2])
    g_two_other = shift(g_two, "xh", 1)
    g_up3, g_down3 = ring_step(g_up2, g_down2)
    a_up2, a_down2, g_two_other, g_up3, g_down3, mine_out, own_in = sync(
        a_up2, a_down2, g_two_other, g_up3, g_down3, mine_out, own_in
    )

    own_out = lax.all_to_all(mine_out, "y", 0, 0)
    a_up3, a_down3 = ring_step(a_up2, a_down2)
    g_three = jnp.concatenate([g_up3, g_down3])
    g_three_other = shift(g_three, "xh", 1)
    g_up4 = shift(g_up3, "z", 1)
    other_in = shift(own_in, "c", 1)
    a_up3, a_down3, g_three_other, g_up4, other_in = sync(
        a_up3, a_down3, g_three_other, g_up4, other_in
    )

    a_up4, a_down4 = ring_step(a_up3[:1], a_down3[1:])
    g_four_other = shift(g_up4, "xh", 1)
    act_blocks = [a0, a_up1, a_down1, a_up2, a_down2, a_up3, a_down3, a_up4, a_down4]
    act_places = [both_sides(o) for o in (0, -1, 1, -2, 2, -3, 3)] + [((-4, 0),), ((4, 1),)]
    acts_part = rotate(at, act_blocks, act_places, own_in, other_in)
    acts_in = lax.all_to_all(acts_part.reshape(16, 32, TOK), ("xl", "c", "y"), 0, 0)

    grad_blocks = [g_near, g_near_other, g_two, g_two_other, g_three, g_three_other, g_up4, g_four_other]
    grad_places = []
    for offsets in ((0, -1, 1), (-2, 2), (-3, 3), (-4,)):
        grad_places += [tuple((o, 0) for o in offsets), tuple((o, 1) for o in offsets)]
    other_out = shift(after(own_out, acts_part), "c", 1)
    grads_part = rotate(at, grad_blocks, grad_places, own_out, other_out)
    grads_in = lax.all_to_all(grads_part, "y", 0, 0)

    acts = jnp.sum(acts_in.reshape(4, 4, 32, TOK), axis=1).astype(BF16)[None]
    r0 = jnp.concatenate([acts, shift(acts, "xh", 1)])
    r_up1, r_down1 = sync(*ring_step(r0, r0))
    r_up2, r_down2, grads_in = sync(*ring_step(r_up1, r_down1), grads_in)
    grads = jnp.sum(grads_in, axis=0).astype(BF16)
    copies = jnp.broadcast_to(grads, (8, COLS, TOK))
    rot_own = lax.all_to_all(copies, ("xl", "y"), 0, 0).reshape(2, 4, COLS, TOK)
    r_up3, r_down3, rot_own = sync(*ring_step(r_up2, r_down2), rot_own)
    r_up4, r_down4 = ring_step(r_up3[:1], r_down3[1:])
    rot_grads = [rot_own, shift(rot_own, "c", 1)]
    rot_acts = [r0, r_up1, r_down1, r_up2, r_down2, r_up3, r_down3, r_up4, r_down4]

    scale = 1.0 / (TOK * 4)
    part = products(at, rot_acts, act_places, rot_grads, scale)
    return weave(lax.all_to_all(part, "y", 0, 0))


def solution(mesh):
    fine = Mesh(mesh.devices.reshape(SIZES), AXES)
    return jax.shard_map(
        body,
        mesh=fine,
        in_specs=(P(DP, None, TILE), P(DP, None, TILE), P(None, TILE), P(None, TILE)),
        out_specs=P(TILE, DP),
        check_vma=False,
    )
```

time: 217 us -> 195 us (0.90)
  waiting for transfers between devices: 109 us -> 68.3 us
  starting transfers between devices: 56 us -> 72.4 us
  Pallas kernels: 18.1 us -> 26.1 us
  blocking collectives: 20.5 us -> 17.4 us
    all_to_all x2 -> x3, waiting for transfers between devices: 39 us -> 2.6 us  [the longest x1 2.59 us: body(): rot_own = lax.all_to_all(copies, ('xl', 'y'), 0, 0).reshape(2, 4, COLS, TOK)]
    pallas_call x3 -> x5, Pallas kernels: 15.8 us -> 23.8 us  [the longest x2 12.4 us: rotate(): pl.pallas_call(functools.partial(rotate_kernel, places), grid=(4,), out_s...]
    ppermute x34 -> x32, starting transfers between devices: 39.1 us -> 47 us  [shift(): return lax.ppermute(x, axis, [(i, (i + by) % n) for i in range(n)])]
    all_to_all x2 -> x3, starting transfers between devices: 8.07 us -> 15 us  [the longest x1 5.97 us: body(): rot_own = lax.all_to_all(copies, ('xl', 'y'), 0, 0).reshape(2, 4, COLS, TOK)]
    squeeze x2 -> x0, local copies, waits for them, and re-layouts: 6.13 us -> none  [spread_basis(): lax.dynamic_index_in_dim(halves, lax.axis_index('c'), 1, keepdims=False)]
    all_to_all x1, waiting for transfers between devices: 5.69 us -> 0.01 us  [body(): grads_in = lax.all_to_all(grads_part, 'y', 0, 0)]
    all_to_all x1, blocking collectives: 20.5 us -> 17.4 us  [body(): return weave(lax.all_to_all(part, 'y', 0, 0))]
    unnamed x12 -> x39, local copies, waits for them, and re-layouts: 3.87 us -> 5.78 us
  transfers between devices with their start and end apart: 38 -> 37, of which waited for: 21 -> 15; matrix products, arithmetic and copies ran while one was open for 2% -> 2% of each run, Pallas kernels for 6% -> 8%
where the time goes in v2:
time: 195 us; the launch traced here: 194 us
  starting transfers between devices  72.4 us (37%)
  waiting for transfers between devices  68.3 us (35%)
  Pallas kernels  26.1 us (13%)
  blocking collectives  17.4 us (9%)
  local copies, waits for them, and re-layouts  8.35 us (4%)
    ppermute x32, waiting for transfers between devices, shift(): return lax.ppermute(x, axis, [(i, (i + by) % n) for i in range(n)])  65.7 us
    ppermute x32, starting transfers between devices, shift(): return lax.ppermute(x, axis, [(i, (i + by) % n) for i in range(n)])  47 us
    all_to_all x1, blocking collectives, body(): return weave(lax.all_to_all(part, 'y', 0, 0))  17.4 us
    pallas_call x2, Pallas kernels, rotate(): pl.pallas_call(functools.partial(rotate_kernel, places), grid=(4,), out_s...  12.4 us
    pallas_call x2, Pallas kernels, split_basis(): pl.pallas_call(split_kernel, grid_spec=pltpu.PrefetchScalarGridSpec(num_s...  7.85 us
    all_to_all x1, starting transfers between devices, body(): lax.all_to_all(acts_part.reshape(16, 32, TOK), ('xl', 'c', 'y'), 0, 0)  6.13 us
    all_to_all x1, starting transfers between devices, body(): rot_own = lax.all_to_all(copies, ('xl', 'y'), 0, 0).reshape(2, 4, COLS, TOK)  5.97 us
    unnamed x39, local copies, waits for them, and re-layouts  5.78 us
  transfers between devices with their start and end apart: 37, of which 15 were waited for; matrix products, arithmetic and copies ran while one was open for 2% of the time, Pallas kernels for 8%

profile of v2, /device:TPU:2, one launch (start us, length us, event | category | flops | bytes accessed | tf_op | source)
XLA Modules:
  0.0 194.3 jit_solution(13543877953816939946)
XLA Ops:
  0.0 3.9 %shard_map.47 = bf16[4,1024,256]{2,1,0:T(8,128)(2,1)} custom-call(s32[1]{0:T(128)} %bitcast.4.core_ref, f32[8192,128]{1,0:T(8,128)} %in_ref.2), custom_call_target="tpu_custom_call" | custom-call | flops 1048576 | bytes 4194304 | tf_op jit(solution)/shard_map/pallas_call | solution.py:43
  3.9 4.6 %all-to-all-start = ((bf16[4,1024,256]{2,1,0:T(8,128)(2,1)}), bf16[4,1024,256]{2,1,0:T(8,128)(2,1)S(1)}, u32[]{:S(2)}, u32[]{:S(2)}) async-start(bf16[4,1024,256]{2,1,0:T(8,128)(2,1)} %shard_map.47), calls=%async_computation | async-start | bytes 4194304 | tf_op jit(solution)/shard_map/all_to_all | solution.py:173
  8.5 2.1 %collective-permute-start = (bf16[1,512,128]{2,1,0:T(8,128)(2,1)S(1)}, bf16[1,512,128]{2,1,0:T(8,128)(2,1)S(1)}, u32[]{:S(2)}, u32[]{:S(2)}) collective-permute-start(bf16[1,512,128]{2,1,0:T(8,128)(2,1)S(1)} %copy-done.15), channel_id=1, source_target_pairs={{0,8},{8,0},{1,9},{9,1},{2,10},{10,2},{3,11},{11,3},{4,12},{12,4},... | collective-permute-start | bytes 393224 | tf_op jit(solution)/shard_map/ppermute | solution.py:24
  10.7 1.9 collective-permute-start.1
  12.6 3.9 %collective-permute-start.2 = (bf16[1,512,128]{2,1,0:T(8,128)(2,1)S(1)}, bf16[1,512,128]{2,1,0:T(8,128)(2,1)S(1)}, u32[]{:S(2)}, u32[]{:S(2)}) collective-permute-start(bf16[1,512,128]{2,1,0:T(8,128)(2,1)S(1)} %copy-done.14), channel_id=1, source_target_pairs={{0,7},{1,0},{2,1},{3,2},{4,3},{5,4},{6,5},{7,6},{8,15},{9,8},{10,9... | collective-permute-start | bytes 393224 | tf_op jit(solution)/shard_map/ppermute | solution.py:24
  16.6 2.9 %collective-permute-done.1 = bf16[1,512,128]{2,1,0:T(8,128)(2,1)S(1)} collective-permute-done((bf16[1,512,128]{2,1,0:T(8,128)(2,1)S(1)}, bf16[1,512,128]{2,1,0:T(8,128)(2,1)S(1)}, u32[]{:S(2)}, u32[]{:S(2)}) %collective-permute-start.1) | collective-permute-done | bytes 131104 | tf_op jit(solution)/shard_map/ppermute | solution.py:24
  19.5 1.5 collective-permute-start.5
  21.1 3.3 %collective-permute-start.4 = (bf16[2,512,128]{2,1,0:T(8,128)(2,1)S(1)}, bf16[2,512,128]{2,1,0:T(8,128)(2,1)S(1)}, u32[]{:S(2)}, u32[]{:S(2)}) collective-permute-start(bf16[2,512,128]{2,1,0:T(8,128)(2,1)S(1)} %constant_dynamic-update-slice_fusion.refs_0_), channel_id=1, source_target_pairs={{0,7},{1,0},{2,1},{3,2},{4,3},{5,4},{6,5},{7,6},{8,15},{9,8},{10,9... | collective-permute-start | bytes 786440 | tf_op jit(solution)/shard_map/ppermute | solution.py:24
  24.4 3.3 %collective-permute-start.7 = (bf16[1,512,128]{2,1,0:T(8,128)(2,1)S(1)}, bf16[1,512,128]{2,1,0:T(8,128)(2,1)S(1)}, u32[]{:S(2)}, u32[]{:S(2)}) collective-permute-start(bf16[1,512,128]{2,1,0:T(8,128)(2,1)S(1)} %collective-permute-done.2), channel_id=1, source_target_pairs={{0,7},{1,0},{2,1},{3,2},{4,3},{5,4},{6,5},{7,6},{8,15},{9,8},{10,9... | collective-permute-start | bytes 393224 | tf_op jit(solution)/shard_map/ppermute | solution.py:24
  27.6 3.9 %shard_map.46 = bf16[4,1024,256]{2,1,0:T(8,128)(2,1)} custom-call(s32[1]{0:T(128)} %bitcast.4.core_ref, f32[8192,128]{1,0:T(8,128)} %in_ref.1), custom_call_target="tpu_custom_call" | custom-call | flops 1048576 | bytes 4194304 | tf_op jit(solution)/shard_map/pallas_call | solution.py:43
  31.6 2.9 %collective-permute-done.6 = bf16[1,512,128]{2,1,0:T(8,128)(2,1)S(1)} collective-permute-done((bf16[1,512,128]{2,1,0:T(8,128)(2,1)S(1)}, bf16[1,512,128]{2,1,0:T(8,128)(2,1)S(1)}, u32[]{:S(2)}, u32[]{:S(2)}) %collective-permute-start.6) | collective-permute-done | bytes 131104 | tf_op jit(solution)/shard_map/ppermute | solution.py:24
  34.5 2.2 %collective-permute-start.10 = (bf16[2,512,128]{2,1,0:T(8,128)(2,1)S(1)}, bf16[2,512,128]{2,1,0:T(8,128)(2,1)S(1)}, u32[]{:S(2)}, u32[]{:S(2)}) collective-permute-start(bf16[2,512,128]{2,1,0:T(8,128)(2,1)S(1)} %constant_dynamic-update-slice_fusion.5.refs_2_), channel_id=1, source_target_pairs={{0,8},{8,0},{1,9},{9,1},{2,10},{10,2},{3,11},{11,3},{4,12},{12,4},... | collective-permute-start | bytes 786440 | tf_op jit(solution)/shard_map/ppermute | solution.py:24
  36.8 0.7 copy-done.8
  37.5 3.2 %collective-permute-start.9 = (bf16[2,512,128]{2,1,0:T(8,128)(2,1)S(1)}, bf16[2,512,128]{2,1,0:T(8,128)(2,1)S(1)}, u32[]{:S(2)}, u32[]{:S(2)}) collective-permute-start(bf16[2,512,128]{2,1,0:T(8,128)(2,1)S(1)} %collective-permute-done.4.refs_2_), channel_id=1, source_target_pairs={{0,7},{1,0},{2,1},{3,2},{4,3},{5,4},{6,5},{7,6},{8,15},{9,8},{10,9... | collective-permute-start | bytes 786440 | tf_op jit(solution)/shard_map/ppermute | solution.py:24
  40.7 0.7 copy-done.4
  41.4 3.2 %collective-permute-start.12 = (bf16[1,512,128]{2,1,0:T(8,128)(2,1)S(1)}, bf16[1,512,128]{2,1,0:T(8,128)(2,1)S(1)}, u32[]{:S(2)}, u32[]{:S(2)}) collective-permute-start(bf16[1,512,128]{2,1,0:T(8,128)(2,1)S(1)} %collective-permute-done.7), channel_id=1, source_target_pairs={{0,7},{1,0},{2,1},{3,2},{4,3},{5,4},{6,5},{7,6},{8,15},{9,8},{10,9... | collective-permute-start | bytes 393224 | tf_op jit(solution)/shard_map/ppermute | solution.py:24
  44.6 2.9 %collective-permute-done.11 = bf16[1,512,128]{2,1,0:T(8,128)(2,1)S(1)} collective-permute-done((bf16[1,512,128]{2,1,0:T(8,128)(2,1)S(1)}, bf16[1,512,128]{2,1,0:T(8,128)(2,1)S(1)}, u32[]{:S(2)}, u32[]{:S(2)}) %collective-permute-start.11) | collective-permute-done | bytes 131104 | tf_op jit(solution)/shard_map/ppermute | solution.py:24
  47.7 0.1 collective-permute-start.17
  47.8 0.7 copy-done.10
  48.4 4.4 %all-to-all-start.2 = ((bf16[4,1024,256]{2,1,0:T(8,128)(2,1)}), bf16[4,1024,256]{2,1,0:T(8,128)(2,1)}, u32[]{:S(2)}, u32[]{:S(2)}) async-start(bf16[4,1024,256]{2,1,0:T(8,128)(2,1)} %shard_map.46), calls=%async_computation.2 | async-start | bytes 4194304 | tf_op jit(solution)/shard_map/all_to_all | solution.py:196
  52.9 1.6 collective-permute-start.15
  54.5 3.2 %collective-permute-start.14 = (bf16[2,512,128]{2,1,0:T(8,128)(2,1)}, bf16[2,512,128]{2,1,0:T(8,128)(2,1)S(1)}, u32[]{:S(2)}, u32[]{:S(2)}) collective-permute-start(bf16[2,512,128]{2,1,0:T(8,128)(2,1)} %copy-done.10), channel_id=1, source_target_pairs={{0,7},{1,0},{2,1},{3,2},{4,3},{5,4},{6,5},{7,6},{8,15},{9,8},{10,9... | collective-permute-start | bytes 786440 | tf_op jit(solution)/shard_map/ppermute | solution.py:24
  57.7 8.9 %collective-permute-done.16.refs_6_ = bf16[1,512,128]{2,1,0:T(8,128)(2,1)S(1)} collective-permute-done((bf16[1,512,128]{2,1,0:T(8,128)(2,1)}, bf16[1,512,128]{2,1,0:T(8,128)(2,1)S(1)}, u32[]{:S(2)}, u32[]{:S(2)}) %collective-permute-start.16) | collective-permute-done | bytes 131104 | tf_op jit(solution)/shard_map/ppermute | solution.py:24
  66.7 0.8 copy-done.12
  67.5 0.7 slice.12
  68.1 0.7 slice.13
  68.8 1.7 collective-permute-start.19
  70.5 0.3 collective-permute-start.18
  70.8 0.1 stack.23.at_ref
  70.9 3.2 %collective-permute-done.19.refs_8_ = bf16[1,512,128]{2,1,0:T(8,128)(2,1)} collective-permute-done((bf16[1,512,128]{2,1,0:T(8,128)(2,1)}, bf16[1,512,128]{2,1,0:T(8,128)(2,1)}, u32[]{:S(2)}, u32[]{:S(2)}) %collective-permute-start.19) | collective-permute-done | bytes 131104 | tf_op jit(solution)/shard_map/ppermute | solution.py:24
  74.1 3.0 %collective-permute-done.18.refs_7_ = bf16[1,512,128]{2,1,0:T(8,128)(2,1)} collective-permute-done((bf16[1,512,128]{2,1,0:T(8,128)(2,1)}, bf16[1,512,128]{2,1,0:T(8,128)(2,1)}, u32[]{:S(2)}, u32[]{:S(2)}) %collective-permute-start.18) | collective-permute-done | bytes 131104 | tf_op jit(solution)/shard_map/ppermute | solution.py:24
  77.0 0.9 copy-done.5
  78.0 0.9 copy-done.9
  78.9 0.9 copy-done.11
  79.9 6.1 %shard_map.48 = f32[4,128,512]{2,1,0:T(8,128)} custom-call(s32[5]{0:T(128)S(1)} %stack.23.at_ref, bf16[2,512,128]{2,1,0:T(8,128)(2,1)S(1)} %constant_dynamic-update-slice_fusion.refs_0_, bf16[2,512,128]{2,1,0:T(8,128)(2,1)S(1)} %copy-done.9, bf16[2,512,128]{2,1,0:T(8,128)(2,1)S(1)} %copy-done.5, bf16[2,512,128]{2,1,0:T(8,128)(2,1)} %collective-permute-done.8.refs_3_, ...), custom_call_target="tpu_custom_call" | custom-call | flops 2147483648 | bytes 7340032 | tf_op jit(solution)/shard_map/pallas_call | solution.py:79
  86.0 0.1 collective-permute-start.26
  86.1 6.1 %all-to-all-start.1 = ((f32[16,32,512]{2,1,0:T(8,128)}), f32[16,32,512]{2,1,0:T(8,128)}, u32[]{:S(2)}, u32[]{:S(2)}) async-start(f32[16,32,512]{2,1,0:T(8,128)} %bitcast.5), calls=%async_computation.1 | async-start | bytes 2097152 | tf_op jit(solution)/shard_map/all_to_all | solution.py:211
  92.2 2.1 %collective-permute-start.25 = (bf16[1,512,128]{2,1,0:T(8,128)(2,1)S(1)}, bf16[1,512,128]{2,1,0:T(8,128)(2,1)S(1)}, u32[]{:S(2)}, u32[]{:S(2)}) collective-permute-start(bf16[1,512,128]{2,1,0:T(8,128)(2,1)S(1)} %collective-permute-done.16.refs_6_), channel_id=1, source_target_pairs={{0,8},{8,0},{1,9},{9,1},{2,10},{10,2},{3,11},{11,3},{4,12},{12,4},... | collective-permute-start | bytes 393224 | tf_op jit(solution)/shard_map/ppermute | solution.py:24
  94.3 15.3 %collective-permute-done.25.refs_7_ = bf16[1,512,128]{2,1,0:T(8,128)(2,1)S(1)} collective-permute-done((bf16[1,512,128]{2,1,0:T(8,128)(2,1)S(1)}, bf16[1,512,128]{2,1,0:T(8,128)(2,1)S(1)}, u32[]{:S(2)}, u32[]{:S(2)}) %collective-permute-start.25) | collective-permute-done | bytes 131104 | tf_op jit(solution)/shard_map/ppermute | solution.py:24
  109.7 6.3 %shard_map.49 = f32[4,128,512]{2,1,0:T(8,128)} custom-call(s32[5]{0:T(128)S(1)} %stack.23.at_ref, bf16[3,512,128]{2,1,0:T(8,128)(2,1)S(1)} %copy-done.1, bf16[3,512,128]{2,1,0:T(8,128)(2,1)S(1)} %copy-done.3, bf16[2,512,128]{2,1,0:T(8,128)(2,1)S(1)} %constant_dynamic-update-slice_fusion.5.refs_2_, bf16[2,512,128]{2,1,0:T(8,128)(2,1)S(1)} %copy-done.7, ...), custom_call_target="tpu_custom_call" | custom-call | flops 2147483648 | bytes 7340032 | tf_op jit(solution)/shard_map/pallas_call | solution.py:79
  116.0 4.2 %all-to-all-start.3 = ((f32[4,128,512]{2,1,0:T(8,128)}), f32[4,128,512]{2,1,0:T(8,128)S(1)}, u32[]{:S(2)}, u32[]{:S(2)}) async-start(f32[4,128,512]{2,1,0:T(8,128)} %shard_map.49), calls=%async_computation.3 | async-start | bytes 2097152 | tf_op jit(solution)/shard_map/all_to_all | solution.py:219
  120.2 1.3 bitcast_reduce_fusion
  121.5 1.5 collective-permute-start.20
  123.1 5.0 %collective-permute-done.20 = bf16[1,4,32,512]{3,2,1,0:T(8,128)(2,1)S(1)} collective-permute-done((bf16[1,4,32,512]{3,2,1,0:T(8,128)(2,1)S(1)}, bf16[1,4,32,512]{3,2,1,0:T(8,128)(2,1)S(1)}, u32[]{:S(2)}, u32[]{:S(2)}) %collective-permute-start.20) | collective-permute-done | bytes 131104 | tf_op jit(solution)/shard_map/ppermute | solution.py:24
  128.1 0.1 collective-permute-start.22
  128.2 2.0 %collective-permute-start.21 = (bf16[2,4,32,512]{3,2,1,0:T(8,128)(2,1)S(1)}, bf16[2,4,32,512]{3,2,1,0:T(8,128)(2,1)S(1)}, u32[]{:S(2)}, u32[]{:S(2)}) collective-permute-start(bf16[2,4,32,512]{3,2,1,0:T(8,128)(2,1)S(1)} %pad_maximum_fusion.refs_0_), channel_id=1, source_target_pairs={{0,1},{1,2},{2,3},{3,4},{4,5},{5,6},{6,7},{7,0},{8,9},{9,10},{10,1... | collective-permute-start | bytes 786440 | tf_op jit(solution)/shard_map/ppermute | solution.py:24
  130.2 4.7 %collective-permute-done.22.refs_2_ = bf16[2,4,32,512]{3,2,1,0:T(8,128)(2,1)S(1)} collective-permute-done((bf16[2,4,32,512]{3,2,1,0:T(8,128)(2,1)S(1)}, bf16[2,4,32,512]{3,2,1,0:T(8,128)(2,1)S(1)}, u32[]{:S(2)}, u32[]{:S(2)}) %collective-permute-start.22) | collective-permute-done | bytes 262176 | tf_op jit(solution)/shard_map/ppermute | solution.py:24
  134.9 1.3 collective-permute-done.21.refs_1_
  136.2 0.4 collective-permute-start.23
  136.7 2.8 %collective-permute-start.24 = (bf16[2,4,32,512]{3,2,1,0:T(8,128)(2,1)S(1)}, bf16[2,4,32,512]{3,2,1,0:T(8,128)(2,1)S(1)}, u32[]{:S(2)}, u32[]{:S(2)}) collective-permute-start(bf16[2,4,32,512]{3,2,1,0:T(8,128)(2,1)S(1)} %collective-permute-done.22.refs_2_), channel_id=1, source_target_pairs={{0,7},{1,0},{2,1},{3,2},{4,3},{5,4},{6,5},{7,6},{8,15},{9,8},{10,9... | collective-permute-start | bytes 786440 | tf_op jit(solution)/shard_map/ppermute | solution.py:24
  139.5 4.3 %collective-permute-done.23.refs_3_ = bf16[2,4,32,512]{3,2,1,0:T(8,128)(2,1)S(1)} collective-permute-done((bf16[2,4,32,512]{3,2,1,0:T(8,128)(2,1)S(1)}, bf16[2,4,32,512]{3,2,1,0:T(8,128)(2,1)S(1)}, u32[]{:S(2)}, u32[]{:S(2)}) %collective-permute-start.23) | collective-permute-done | bytes 262176 | tf_op jit(solution)/shard_map/ppermute | solution.py:24
  143.8 0.1 reduce_sum.19
  143.9 1.1 broadcast_in_dim.4
  145.0 6.0 %all-to-all-start.4 = ((bf16[8,128,512]{2,1,0:T(8,128)(2,1)}), bf16[8,128,512]{2,1,0:T(8,128)(2,1)S(1)}, u32[]{:S(2)}, u32[]{:S(2)}) async-start(bf16[8,128,512]{2,1,0:T(8,128)(2,1)} %broadcast_in_dim.4), calls=%async_computation.4 | async-start | bytes 2097152 | tf_op jit(solution)/shard_map/all_to_all | solution.py:227
  150.9 0.0 collective-permute-start.27
  150.9 3.2 %collective-permute-start.28 = (bf16[2,4,32,512]{3,2,1,0:T(8,128)(2,1)S(1)}, bf16[2,4,32,512]{3,2,1,0:T(8,128)(2,1)S(1)}, u32[]{:S(2)}, u32[]{:S(2)}) collective-permute-start(bf16[2,4,32,512]{3,2,1,0:T(8,128)(2,1)S(1)} %collective-permute-done.24.refs_4_), channel_id=1, source_target_pairs={{0,7},{1,0},{2,1},{3,2},{4,3},{5,4},{6,5},{7,6},{8,15},{9,8},{10,9... | collective-permute-start | bytes 786440 | tf_op jit(solution)/shard_map/ppermute | solution.py:24
  154.2 4.3 %collective-permute-done.27.refs_5_ = bf16[2,4,32,512]{3,2,1,0:T(8,128)(2,1)S(1)} collective-permute-done((bf16[2,4,32,512]{3,2,1,0:T(8,128)(2,1)S(1)}, bf16[2,4,32,512]{3,2,1,0:T(8,128)(2,1)S(1)}, u32[]{:S(2)}, u32[]{:S(2)}) %collective-permute-start.27) | collective-permute-done | bytes 262176 | tf_op jit(solution)/shard_map/ppermute | solution.py:24
  158.5 2.6 %all-to-all-done.4 = bf16[8,128,512]{2,1,0:T(8,128)(2,1)S(1)} async-done(((bf16[8,128,512]{2,1,0:T(8,128)(2,1)}), bf16[8,128,512]{2,1,0:T(8,128)(2,1)S(1)}, u32[]{:S(2)}, u32[]{:S(2)}) %all-to-all-start.4) | async-done | bytes 1048608 | tf_op jit(solution)/shard_map/all_to_all | solution.py:227
  161.2 3.1 %collective-permute-start.30 = (bf16[1,4,32,512]{3,2,1,0:T(8,128)(2,1)S(1)}, bf16[1,4,32,512]{3,2,1,0:T(8,128)(2,1)S(1)}, u32[]{:S(2)}, u32[]{:S(2)}) collective-permute-start(bf16[1,4,32,512]{3,2,1,0:T(8,128)(2,1)S(1)} %slice.15), channel_id=1, source_target_pairs={{0,7},{1,0},{2,1},{3,2},{4,3},{5,4},{6,5},{7,6},{8,15},{9,8},{10,9... | collective-permute-start | bytes 393224 | tf_op jit(solution)/shard_map/ppermute | solution.py:24
  164.3 3.4 %collective-permute-done.30.refs_8_ = bf16[1,4,32,512]{3,2,1,0:T(8,128)(2,1)S(1)} collective-permute-done((bf16[1,4,32,512]{3,2,1,0:T(8,128)(2,1)S(1)}, bf16[1,4,32,512]{3,2,1,0:T(8,128)(2,1)S(1)}, u32[]{:S(2)}, u32[]{:S(2)}) %collective-permute-start.30) | collective-permute-done | bytes 131104 | tf_op jit(solution)/shard_map/ppermute | solution.py:24
  167.7 3.4 %collective-permute-done.29.refs_7_ = bf16[1,4,32,512]{3,2,1,0:T(8,128)(2,1)S(1)} collective-permute-done((bf16[1,4,32,512]{3,2,1,0:T(8,128)(2,1)S(1)}, bf16[1,4,32,512]{3,2,1,0:T(8,128)(2,1)S(1)}, u32[]{:S(2)}, u32[]{:S(2)}) %collective-permute-start.29) | collective-permute-done | bytes 131104 | tf_op jit(solution)/shard_map/ppermute | solution.py:24
  171.1 3.5 %shard_map.50 = f32[4,128,512]{2,1,0:T(8,128)S(1)} custom-call(s32[5]{0:T(128)S(1)} %stack.23.at_ref, bf16[2,4,32,512]{3,2,1,0:T(8,128)(2,1)S(1)} %pad_maximum_fusion.refs_0_, bf16[2,4,32,512]{3,2,1,0:T(8,128)(2,1)S(1)} %collective-permute-done.21.refs_1_, bf16[2,4,32,512]{3,2,1,0:T(8,128)(2,1)S(1)} %collective-permute-done.22.refs_2_, ...), custom_call_target="tpu_custom_call" | custom-call | flops 1073741824 | bytes 5242880 | tf_op jit(solution)/shard_map/pallas_call | solution.py:120
  174.6 17.4 %all_to_all.30.in_ref = f32[4,128,512]{2,1,0:T(8,128)S(1)} all-to-all(f32[4,128,512]{2,1,0:T(8,128)S(1)} %shard_map.50), channel_id=1, replica_groups=mesh['xl'=2,'c'=2,'y'=4,'xh'=2,'z'=8] {'y'}, dimensions={0} | all-to-all | bytes 2097152 | tf_op jit(solution)/shard_map/all_to_all | solution.py:235
  192.0 2.4 %shard_map.51 = f32[128,2048]{1,0:T(8,128)} custom-call(f32[4,128,512]{2,1,0:T(8,128)S(1)} %all_to_all.30.in_ref), custom_call_target="tpu_custom_call" | custom-call | tf_op jit(solution)/shard_map/pallas_call | solution.py:143
  (69 shorter events, 0.3 us)
Async XLA Ops:
  3.9 4.6 %copy-start.15 = (bf16[1,512,128]{2,1,0:T(8,128)(2,1)S(1)}, bf16[1,512,128]{2,1,0:T(8,128)(2,1)}, u32[]{:S(2)}) copy-start(bf16[1,512,128]{2,1,0:T(8,128)(2,1)} %param.4) | copy-start | bytes 393220
  3.9 6.7 %copy-start.14 = (bf16[1,512,128]{2,1,0:T(8,128)(2,1)S(1)}, bf16[1,512,128]{2,1,0:T(8,128)(2,1)}, u32[]{:S(2)}) copy-start(bf16[1,512,128]{2,1,0:T(8,128)(2,1)} %param.5) | copy-start | bytes 393220
  3.9 43.7 %all-to-all-start = ((bf16[4,1024,256]{2,1,0:T(8,128)(2,1)}), bf16[4,1024,256]{2,1,0:T(8,128)(2,1)S(1)}, u32[]{:S(2)}, u32[]{:S(2)}) async-start(bf16[4,1024,256]{2,1,0:T(8,128)(2,1)} %shard_map.47), calls=%async_computation | async-start | bytes 4194304 | tf_op jit(solution)/shard_map/all_to_all | solution.py:173
  8.5 8.0 %collective-permute-start = (bf16[1,512,128]{2,1,0:T(8,128)(2,1)S(1)}, bf16[1,512,128]{2,1,0:T(8,128)(2,1)S(1)}, u32[]{:S(2)}, u32[]{:S(2)}) collective-permute-start(bf16[1,512,128]{2,1,0:T(8,128)(2,1)S(1)} %copy-done.15), channel_id=1, source_target_pairs={{0,8},{8,0},{1,9},{9,1},{2,10},{10,2},{3,11},{11,3},{4,12},{12,4},... | collective-permute-start | bytes 393224 | tf_op jit(solution)/shard_map/ppermute | solution.py:24
  10.7 8.8 %collective-permute-start.1 = (bf16[1,512,128]{2,1,0:T(8,128)(2,1)S(1)}, bf16[1,512,128]{2,1,0:T(8,128)(2,1)S(1)}, u32[]{:S(2)}, u32[]{:S(2)}) collective-permute-start(bf16[1,512,128]{2,1,0:T(8,128)(2,1)S(1)} %copy-done.14), channel_id=1, source_target_pairs={{0,1},{1,2},{2,3},{3,4},{4,5},{5,6},{6,7},{7,0},{8,9},{9,10},{10,1... | collective-permute-start | bytes 393224 | tf_op jit(solution)/shard_map/ppermute | solution.py:24
  12.6 6.9 %collective-permute-start.2 = (bf16[1,512,128]{2,1,0:T(8,128)(2,1)S(1)}, bf16[1,512,128]{2,1,0:T(8,128)(2,1)S(1)}, u32[]{:S(2)}, u32[]{:S(2)}) collective-permute-start(bf16[1,512,128]{2,1,0:T(8,128)(2,1)S(1)} %copy-done.14), channel_id=1, source_target_pairs={{0,7},{1,0},{2,1},{3,2},{4,3},{5,4},{6,5},{7,6},{8,15},{9,8},{10,9... | collective-permute-start | bytes 393224 | tf_op jit(solution)/shard_map/ppermute | solution.py:24
  19.5 12.0 %copy-start = (bf16[3,512,128]{2,1,0:T(8,128)(2,1)}, bf16[3,512,128]{2,1,0:T(8,128)(2,1)S(1)}, u32[]{:S(2)}) copy-start(bf16[3,512,128]{2,1,0:T(8,128)(2,1)S(1)} %constant_dynamic-update-slice_fusion.2.refs_0_) | copy-start | bytes 1179652
  19.5 14.9 %collective-permute-start.5 = (bf16[3,512,128]{2,1,0:T(8,128)(2,1)S(1)}, bf16[3,512,128]{2,1,0:T(8,128)(2,1)S(1)}, u32[]{:S(2)}, u32[]{:S(2)}) collective-permute-start(bf16[3,512,128]{2,1,0:T(8,128)(2,1)S(1)} %constant_dynamic-update-slice_fusion.2.refs_0_), channel_id=1, source_target_pairs={{0,8},{8,0},{1,9},{9,1},{2,10},{10,2},{3,11},{11,3},{4,12},{12,4},... | collective-permute-start | bytes 1179656 | tf_op jit(solution)/shard_map/ppermute | solution.py:24
  21.1 13.4 %collective-permute-start.4 = (bf16[2,512,128]{2,1,0:T(8,128)(2,1)S(1)}, bf16[2,512,128]{2,1,0:T(8,128)(2,1)S(1)}, u32[]{:S(2)}, u32[]{:S(2)}) collective-permute-start(bf16[2,512,128]{2,1,0:T(8,128)(2,1)S(1)} %constant_dynamic-update-slice_fusion.refs_0_), channel_id=1, source_target_pairs={{0,7},{1,0},{2,1},{3,2},{4,3},{5,4},{6,5},{7,6},{8,15},{9,8},{10,9... | collective-permute-start | bytes 786440 | tf_op jit(solution)/shard_map/ppermute | solution.py:24
  24.4 10.1 %collective-permute-start.3 = (bf16[2,512,128]{2,1,0:T(8,128)(2,1)S(1)}, bf16[2,512,128]{2,1,0:T(8,128)(2,1)S(1)}, u32[]{:S(2)}, u32[]{:S(2)}) collective-permute-start(bf16[2,512,128]{2,1,0:T(8,128)(2,1)S(1)} %constant_dynamic-update-slice_fusion.refs_0_), channel_id=1, source_target_pairs={{0,1},{1,2},{2,3},{3,4},{4,5},{5,6},{6,7},{7,0},{8,9},{9,10},{10,1... | collective-permute-start | bytes 786440 | tf_op jit(solution)/shard_map/ppermute | solution.py:24
  24.4 10.1 %collective-permute-start.6 = (bf16[1,512,128]{2,1,0:T(8,128)(2,1)S(1)}, bf16[1,512,128]{2,1,0:T(8,128)(2,1)S(1)}, u32[]{:S(2)}, u32[]{:S(2)}) collective-permute-start(bf16[1,512,128]{2,1,0:T(8,128)(2,1)S(1)} %collective-permute-done.1), channel_id=1, source_target_pairs={{0,1},{1,2},{2,3},{3,4},{4,5},{5,6},{6,7},{7,0},{8,9},{9,10},{10,1... | collective-permute-start | bytes 393224 | tf_op jit(solution)/shard_map/ppermute | solution.py:24
  24.4 10.1 %collective-permute-start.7 = (bf16[1,512,128]{2,1,0:T(8,128)(2,1)S(1)}, bf16[1,512,128]{2,1,0:T(8,128)(2,1)S(1)}, u32[]{:S(2)}, u32[]{:S(2)}) collective-permute-start(bf16[1,512,128]{2,1,0:T(8,128)(2,1)S(1)} %collective-permute-done.2), channel_id=1, source_target_pairs={{0,7},{1,0},{2,1},{3,2},{4,3},{5,4},{6,5},{7,6},{8,15},{9,8},{10,9... | collective-permute-start | bytes 393224 | tf_op jit(solution)/shard_map/ppermute | solution.py:24
  34.5 13.1 %copy-start.2 = (bf16[3,512,128]{2,1,0:T(8,128)(2,1)}, bf16[3,512,128]{2,1,0:T(8,128)(2,1)S(1)}, u32[]{:S(2)}) copy-start(bf16[3,512,128]{2,1,0:T(8,128)(2,1)S(1)} %collective-permute-done.5.refs_1_) | copy-start | bytes 1179652
  34.5 13.0 %collective-permute-start.10 = (bf16[2,512,128]{2,1,0:T(8,128)(2,1)S(1)}, bf16[2,512,128]{2,1,0:T(8,128)(2,1)S(1)}, u32[]{:S(2)}, u32[]{:S(2)}) collective-permute-start(bf16[2,512,128]{2,1,0:T(8,128)(2,1)S(1)} %constant_dynamic-update-slice_fusion.5.refs_2_), channel_id=1, source_target_pairs={{0,8},{8,0},{1,9},{9,1},{2,10},{10,2},{3,11},{11,3},{4,12},{12,4},... | collective-permute-start | bytes 786440 | tf_op jit(solution)/shard_map/ppermute | solution.py:24
  36.8 10.8 %collective-permute-start.8 = (bf16[2,512,128]{2,1,0:T(8,128)(2,1)S(1)}, bf16[2,512,128]{2,1,0:T(8,128)(2,1)}, u32[]{:S(2)}, u32[]{:S(2)}) collective-permute-start(bf16[2,512,128]{2,1,0:T(8,128)(2,1)S(1)} %collective-permute-done.3.refs_1_), channel_id=1, source_target_pairs={{0,1},{1,2},{2,3},{3,4},{4,5},{5,6},{6,7},{7,0},{8,9},{9,10},{10,1... | collective-permute-start | bytes 786440 | tf_op jit(solution)/shard_map/ppermute | solution.py:24
  36.8 0.7 copy-start.8
  37.5 10.2 %collective-permute-start.9 = (bf16[2,512,128]{2,1,0:T(8,128)(2,1)S(1)}, bf16[2,512,128]{2,1,0:T(8,128)(2,1)S(1)}, u32[]{:S(2)}, u32[]{:S(2)}) collective-permute-start(bf16[2,512,128]{2,1,0:T(8,128)(2,1)S(1)} %collective-permute-done.4.refs_2_), channel_id=1, source_target_pairs={{0,7},{1,0},{2,1},{3,2},{4,3},{5,4},{6,5},{7,6},{8,15},{9,8},{10,9... | collective-permute-start | bytes 786440 | tf_op jit(solution)/shard_map/ppermute | solution.py:24
  40.7 0.7 copy-start.4
  41.4 6.2 %collective-permute-start.11 = (bf16[1,512,128]{2,1,0:T(8,128)(2,1)S(1)}, bf16[1,512,128]{2,1,0:T(8,128)(2,1)S(1)}, u32[]{:S(2)}, u32[]{:S(2)}) collective-permute-start(bf16[1,512,128]{2,1,0:T(8,128)(2,1)S(1)} %collective-permute-done.6), channel_id=1, source_target_pairs={{0,1},{1,2},{2,3},{3,4},{4,5},{5,6},{6,7},{7,0},{8,9},{9,10},{10,1... | collective-permute-start | bytes 393224 | tf_op jit(solution)/shard_map/ppermute | solution.py:24
  41.4 6.2 %collective-permute-start.12 = (bf16[1,512,128]{2,1,0:T(8,128)(2,1)S(1)}, bf16[1,512,128]{2,1,0:T(8,128)(2,1)S(1)}, u32[]{:S(2)}, u32[]{:S(2)}) collective-permute-start(bf16[1,512,128]{2,1,0:T(8,128)(2,1)S(1)} %collective-permute-done.7), channel_id=1, source_target_pairs={{0,7},{1,0},{2,1},{3,2},{4,3},{5,4},{6,5},{7,6},{8,15},{9,8},{10,9... | collective-permute-start | bytes 393224 | tf_op jit(solution)/shard_map/ppermute | solution.py:24
  47.6 5.3 %copy-start.16 = (bf16[1,512,128]{2,1,0:T(8,128)(2,1)}, bf16[1,512,128]{2,1,0:T(8,128)(2,1)S(1)}, u32[]{:S(2)}) copy-start(bf16[1,512,128]{2,1,0:T(8,128)(2,1)S(1)} %collective-permute-done.11) | copy-start | bytes 393220
  47.6 5.3 %copy-start.6 = (bf16[2,512,128]{2,1,0:T(8,128)(2,1)}, bf16[2,512,128]{2,1,0:T(8,128)(2,1)S(1)}, u32[]{:S(2)}) copy-start(bf16[2,512,128]{2,1,0:T(8,128)(2,1)S(1)} %collective-permute-done.10.refs_3_) | copy-start | bytes 786436
  47.6 0.8 copy-start.10
  47.7 19.8 %collective-permute-start.17 = (bf16[4,1024,256]{2,1,0:T(8,128)(2,1)S(1)}, bf16[4,1024,256]{2,1,0:T(8,128)(2,1)}, u32[]{:S(2)}, u32[]{:S(2)}) collective-permute-start(bf16[4,1024,256]{2,1,0:T(8,128)(2,1)S(1)} %all-to-all-done.refs_9_), channel_id=1, source_target_pairs={{0,64},{64,0},{1,65},{65,1},{2,66},{66,2},{3,67},{67,3},{4,68},{68... | collective-permute-start | bytes 6291464 | tf_op jit(solution)/shard_map/ppermute | solution.py:24
  48.4 37.6 %all-to-all-start.2 = ((bf16[4,1024,256]{2,1,0:T(8,128)(2,1)}), bf16[4,1024,256]{2,1,0:T(8,128)(2,1)}, u32[]{:S(2)}, u32[]{:S(2)}) async-start(bf16[4,1024,256]{2,1,0:T(8,128)(2,1)} %shard_map.46), calls=%async_computation.2 | async-start | bytes 4194304 | tf_op jit(solution)/shard_map/all_to_all | solution.py:196
  52.9 13.7 %collective-permute-start.15 = (bf16[2,512,128]{2,1,0:T(8,128)(2,1)S(1)}, bf16[2,512,128]{2,1,0:T(8,128)(2,1)S(1)}, u32[]{:S(2)}, u32[]{:S(2)}) collective-permute-start(bf16[2,512,128]{2,1,0:T(8,128)(2,1)S(1)} %constant_dynamic-update-slice_fusion.7.refs_4_), channel_id=1, source_target_pairs={{0,8},{8,0},{1,9},{9,1},{2,10},{10,2},{3,11},{11,3},{4,12},{12,4},... | collective-permute-start | bytes 786440 | tf_op jit(solution)/shard_map/ppermute | solution.py:24
  54.5 13.0 %collective-permute-start.13 = (bf16[2,512,128]{2,1,0:T(8,128)(2,1)}, bf16[2,512,128]{2,1,0:T(8,128)(2,1)S(1)}, u32[]{:S(2)}, u32[]{:S(2)}) collective-permute-start(bf16[2,512,128]{2,1,0:T(8,128)(2,1)} %collective-permute-done.8.refs_3_), channel_id=1, source_target_pairs={{0,1},{1,2},{2,3},{3,4},{4,5},{5,6},{6,7},{7,0},{8,9},{9,10},{10,1... | collective-permute-start | bytes 786440 | tf_op jit(solution)/shard_map/ppermute | solution.py:24
  54.5 13.0 %collective-permute-start.14 = (bf16[2,512,128]{2,1,0:T(8,128)(2,1)}, bf16[2,512,128]{2,1,0:T(8,128)(2,1)S(1)}, u32[]{:S(2)}, u32[]{:S(2)}) collective-permute-start(bf16[2,512,128]{2,1,0:T(8,128)(2,1)} %copy-done.10), channel_id=1, source_target_pairs={{0,7},{1,0},{2,1},{3,2},{4,3},{5,4},{6,5},{7,6},{8,15},{9,8},{10,9... | collective-permute-start | bytes 786440 | tf_op jit(solution)/shard_map/ppermute | solution.py:24
  57.7 9.0 %collective-permute-start.16 = (bf16[1,512,128]{2,1,0:T(8,128)(2,1)}, bf16[1,512,128]{2,1,0:T(8,128)(2,1)S(1)}, u32[]{:S(2)}, u32[]{:S(2)}) collective-permute-start(bf16[1,512,128]{2,1,0:T(8,128)(2,1)} %copy-done.16), channel_id=1, source_target_pairs={{0,1},{1,2},{2,3},{3,4},{4,5},{5,6},{6,7},{7,0},{8,9},{9,10},{10,1... | collective-permute-start | bytes 393224 | tf_op jit(solution)/shard_map/ppermute | solution.py:24
  66.7 0.8 copy-start.12
  68.8 5.3 %collective-permute-start.19 = (bf16[1,512,128]{2,1,0:T(8,128)(2,1)}, bf16[1,512,128]{2,1,0:T(8,128)(2,1)}, u32[]{:S(2)}, u32[]{:S(2)}) collective-permute-start(bf16[1,512,128]{2,1,0:T(8,128)(2,1)} %slice.13), channel_id=1, source_target_pairs={{0,7},{1,0},{2,1},{3,2},{4,3},{5,4},{6,5},{7,6},{8,15},{9,8},{10,9... | collective-permute-start | bytes 393224 | tf_op jit(solution)/shard_map/ppermute | solution.py:24
  70.5 6.5 %collective-permute-start.18 = (bf16[1,512,128]{2,1,0:T(8,128)(2,1)}, bf16[1,512,128]{2,1,0:T(8,128)(2,1)}, u32[]{:S(2)}, u32[]{:S(2)}) collective-permute-start(bf16[1,512,128]{2,1,0:T(8,128)(2,1)} %slice.12), channel_id=1, source_target_pairs={{0,1},{1,2},{2,3},{3,4},{4,5},{5,6},{6,7},{7,0},{8,9},{9,10},{10,1... | collective-permute-start | bytes 393224 | tf_op jit(solution)/shard_map/ppermute | solution.py:24
  77.0 1.0 copy-start.5
  78.0 0.9 copy-start.9
  78.9 0.9 copy-start.11
  86.0 23.6 %copy-start.1 = (bf16[3,512,128]{2,1,0:T(8,128)(2,1)S(1)}, bf16[3,512,128]{2,1,0:T(8,128)(2,1)}, u32[]{:S(2)}) copy-start(bf16[3,512,128]{2,1,0:T(8,128)(2,1)} %copy-done) | copy-start | bytes 1179652
  86.0 23.6 %copy-start.3 = (bf16[3,512,128]{2,1,0:T(8,128)(2,1)S(1)}, bf16[3,512,128]{2,1,0:T(8,128)(2,1)}, u32[]{:S(2)}) copy-start(bf16[3,512,128]{2,1,0:T(8,128)(2,1)} %copy-done.2) | copy-start | bytes 1179652
  86.0 23.6 %copy-start.7 = (bf16[2,512,128]{2,1,0:T(8,128)(2,1)S(1)}, bf16[2,512,128]{2,1,0:T(8,128)(2,1)}, u32[]{:S(2)}) copy-start(bf16[2,512,128]{2,1,0:T(8,128)(2,1)} %copy-done.6) | copy-start | bytes 786436
  86.0 23.7 %copy-start.13 = (bf16[2,512,128]{2,1,0:T(8,128)(2,1)S(1)}, bf16[2,512,128]{2,1,0:T(8,128)(2,1)}, u32[]{:S(2)}) copy-start(bf16[2,512,128]{2,1,0:T(8,128)(2,1)} %copy-done.12) | copy-start | bytes 786436
  86.0 23.6 %collective-permute-start.26 = (bf16[4,1024,256]{2,1,0:T(8,128)(2,1)}, bf16[4,1024,256]{2,1,0:T(8,128)(2,1)}, u32[]{:S(2)}, u32[]{:S(2)}) collective-permute-start(bf16[4,1024,256]{2,1,0:T(8,128)(2,1)} %all-to-all-done.2.refs_8_), channel_id=1, source_target_pairs={{0,64},{64,0},{1,65},{65,1},{2,66},{66,2},{3,67},{67,3},{4,68},{68... | collective-permute-start | bytes 6291464 | tf_op jit(solution)/shard_map/ppermute | solution.py:24
  86.1 29.9 %all-to-all-start.1 = ((f32[16,32,512]{2,1,0:T(8,128)}), f32[16,32,512]{2,1,0:T(8,128)}, u32[]{:S(2)}, u32[]{:S(2)}) async-start(f32[16,32,512]{2,1,0:T(8,128)} %bitcast.5), calls=%async_computation.1 | async-start | bytes 2097152 | tf_op jit(solution)/shard_map/all_to_all | solution.py:211
  92.2 17.4 %collective-permute-start.25 = (bf16[1,512,128]{2,1,0:T(8,128)(2,1)S(1)}, bf16[1,512,128]{2,1,0:T(8,128)(2,1)S(1)}, u32[]{:S(2)}, u32[]{:S(2)}) collective-permute-start(bf16[1,512,128]{2,1,0:T(8,128)(2,1)S(1)} %collective-permute-done.16.refs_6_), channel_id=1, source_target_pairs={{0,8},{8,0},{1,9},{9,1},{2,10},{10,2},{3,11},{11,3},{4,12},{12,4},... | collective-permute-start | bytes 393224 | tf_op jit(solution)/shard_map/ppermute | solution.py:24
  116.0 27.8 %all-to-all-start.3 = ((f32[4,128,512]{2,1,0:T(8,128)}), f32[4,128,512]{2,1,0:T(8,128)S(1)}, u32[]{:S(2)}, u32[]{:S(2)}) async-start(f32[4,128,512]{2,1,0:T(8,128)} %shard_map.49), calls=%async_computation.3 | async-start | bytes 2097152 | tf_op jit(solution)/shard_map/all_to_all | solution.py:219
  121.5 6.6 %collective-permute-start.20 = (bf16[1,4,32,512]{3,2,1,0:T(8,128)(2,1)S(1)}, bf16[1,4,32,512]{3,2,1,0:T(8,128)(2,1)S(1)}, u32[]{:S(2)}, u32[]{:S(2)}) collective-permute-start(bf16[1,4,32,512]{3,2,1,0:T(8,128)(2,1)S(1)} %bitcast.14), channel_id=1, source_target_pairs={{0,8},{8,0},{1,9},{9,1},{2,10},{10,2},{3,11},{11,3},{4,12},{12,4},... | collective-permute-start | bytes 393224 | tf_op jit(solution)/shard_map/ppermute | solution.py:24
  128.1 6.8 %collective-permute-start.22 = (bf16[2,4,32,512]{3,2,1,0:T(8,128)(2,1)S(1)}, bf16[2,4,32,512]{3,2,1,0:T(8,128)(2,1)S(1)}, u32[]{:S(2)}, u32[]{:S(2)}) collective-permute-start(bf16[2,4,32,512]{3,2,1,0:T(8,128)(2,1)S(1)} %pad_maximum_fusion.refs_0_), channel_id=1, source_target_pairs={{0,7},{1,0},{2,1},{3,2},{4,3},{5,4},{6,5},{7,6},{8,15},{9,8},{10,9... | collective-permute-start | bytes 786440 | tf_op jit(solution)/shard_map/ppermute | solution.py:24
  128.2 8.0 %collective-permute-start.21 = (bf16[2,4,32,512]{3,2,1,0:T(8,128)(2,1)S(1)}, bf16[2,4,32,512]{3,2,1,0:T(8,128)(2,1)S(1)}, u32[]{:S(2)}, u32[]{:S(2)}) collective-permute-start(bf16[2,4,32,512]{3,2,1,0:T(8,128)(2,1)S(1)} %pad_maximum_fusion.refs_0_), channel_id=1, source_target_pairs={{0,1},{1,2},{2,3},{3,4},{4,5},{5,6},{6,7},{7,0},{8,9},{9,10},{10,1... | collective-permute-start | bytes 786440 | tf_op jit(solution)/shard_map/ppermute | solution.py:24
  136.2 7.6 %collective-permute-start.23 = (bf16[2,4,32,512]{3,2,1,0:T(8,128)(2,1)S(1)}, bf16[2,4,32,512]{3,2,1,0:T(8,128)(2,1)S(1)}, u32[]{:S(2)}, u32[]{:S(2)}) collective-permute-start(bf16[2,4,32,512]{3,2,1,0:T(8,128)(2,1)S(1)} %collective-permute-done.21.refs_1_), channel_id=1, source_target_pairs={{0,1},{1,2},{2,3},{3,4},{4,5},{5,6},{6,7},{7,0},{8,9},{9,10},{10,1... | collective-permute-start | bytes 786440 | tf_op jit(solution)/shard_map/ppermute | solution.py:24
  136.7 7.1 %collective-permute-start.24 = (bf16[2,4,32,512]{3,2,1,0:T(8,128)(2,1)S(1)}, bf16[2,4,32,512]{3,2,1,0:T(8,128)(2,1)S(1)}, u32[]{:S(2)}, u32[]{:S(2)}) collective-permute-start(bf16[2,4,32,512]{3,2,1,0:T(8,128)(2,1)S(1)} %collective-permute-done.22.refs_2_), channel_id=1, source_target_pairs={{0,7},{1,0},{2,1},{3,2},{4,3},{5,4},{6,5},{7,6},{8,15},{9,8},{10,9... | collective-permute-start | bytes 786440 | tf_op jit(solution)/shard_map/ppermute | solution.py:24
  145.0 16.2 %all-to-all-start.4 = ((bf16[8,128,512]{2,1,0:T(8,128)(2,1)}), bf16[8,128,512]{2,1,0:T(8,128)(2,1)S(1)}, u32[]{:S(2)}, u32[]{:S(2)}) async-start(bf16[8,128,512]{2,1,0:T(8,128)(2,1)} %broadcast_in_dim.4), calls=%async_computation.4 | async-start | bytes 2097152 | tf_op jit(solution)/shard_map/all_to_all | solution.py:227
  150.9 7.6 %collective-permute-start.27 = (bf16[2,4,32,512]{3,2,1,0:T(8,128)(2,1)S(1)}, bf16[2,4,32,512]{3,2,1,0:T(8,128)(2,1)S(1)}, u32[]{:S(2)}, u32[]{:S(2)}) collective-permute-start(bf16[2,4,32,512]{3,2,1,0:T(8,128)(2,1)S(1)} %collective-permute-done.23.refs_3_), channel_id=1, source_target_pairs={{0,1},{1,2},{2,3},{3,4},{4,5},{5,6},{6,7},{7,0},{8,9},{9,10},{10,1... | collective-permute-start | bytes 786440 | tf_op jit(solution)/shard_map/ppermute | solution.py:24
  150.9 7.6 %collective-permute-start.28 = (bf16[2,4,32,512]{3,2,1,0:T(8,128)(2,1)S(1)}, bf16[2,4,32,512]{3,2,1,0:T(8,128)(2,1)S(1)}, u32[]{:S(2)}, u32[]{:S(2)}) collective-permute-start(bf16[2,4,32,512]{3,2,1,0:T(8,128)(2,1)S(1)} %collective-permute-done.24.refs_4_), channel_id=1, source_target_pairs={{0,7},{1,0},{2,1},{3,2},{4,3},{5,4},{6,5},{7,6},{8,15},{9,8},{10,9... | collective-permute-start | bytes 786440 | tf_op jit(solution)/shard_map/ppermute | solution.py:24
  161.1 10.0 %collective-permute-start.31 = (bf16[2,4,128,512]{3,2,1,0:T(8,128)(2,1)S(1)}, bf16[2,4,128,512]{3,2,1,0:T(8,128)(2,1)S(1)}, u32[]{:S(2)}, u32[]{:S(2)}) collective-permute-start(bf16[2,4,128,512]{3,2,1,0:T(8,128)(2,1)S(1)} %bitcast.12), channel_id=1, source_target_pairs={{0,64},{64,0},{1,65},{65,1},{2,66},{66,2},{3,67},{67,3},{4,68},{68... | collective-permute-start | bytes 3145736 | tf_op jit(solution)/shard_map/ppermute | solution.py:24
  161.2 6.5 %collective-permute-start.30 = (bf16[1,4,32,512]{3,2,1,0:T(8,128)(2,1)S(1)}, bf16[1,4,32,512]{3,2,1,0:T(8,128)(2,1)S(1)}, u32[]{:S(2)}, u32[]{:S(2)}) collective-permute-start(bf16[1,4,32,512]{3,2,1,0:T(8,128)(2,1)S(1)} %slice.15), channel_id=1, source_target_pairs={{0,7},{1,0},{2,1},{3,2},{4,3},{5,4},{6,5},{7,6},{8,15},{9,8},{10,9... | collective-permute-start | bytes 393224 | tf_op jit(solution)/shard_map/ppermute | solution.py:24
  164.3 6.8 %collective-permute-start.29 = (bf16[1,4,32,512]{3,2,1,0:T(8,128)(2,1)S(1)}, bf16[1,4,32,512]{3,2,1,0:T(8,128)(2,1)S(1)}, u32[]{:S(2)}, u32[]{:S(2)}) collective-permute-start(bf16[1,4,32,512]{3,2,1,0:T(8,128)(2,1)S(1)} %slice.14), channel_id=1, source_target_pairs={{0,1},{1,2},{2,3},{3,4},{4,5},{5,6},{6,7},{7,0},{8,9},{9,10},{10,1... | collective-permute-start | bytes 393224 | tf_op jit(solution)/shard_map/ppermute | solution.py:24

commit v3 on v2

v3 whole, which is shorter than its diff:
```python
import functools

import jax
import jax.numpy as jnp
from jax import lax
from jax.experimental import pallas as pl
from jax.experimental.pallas import tpu as pltpu
from jax.sharding import Mesh, PartitionSpec as P

AXES = ("xl", "c", "y", "xh", "z")
SIZES = (2, 2, 4, 2, 8)
DP = ("xl", "c")
TILE = ("y", "xh", "z")
TOK = 512
COLS = 128
F32 = jnp.float32
BF16 = jnp.bfloat16
VMEM_LIMIT = 48 * 1024 * 1024
PARAMS = pltpu.CompilerParams(vmem_limit_bytes=VMEM_LIMIT)


def shift(x, axis, by):
    n = lax.axis_size(axis)
    return lax.ppermute(x, axis, [(i, (i + by) % n) for i in range(n)])


def after(x, *others):
    return lax.optimization_barrier((x, *others))[0]


def whole(shape):
    return pl.BlockSpec(shape, lambda *_: (0,) * len(shape))


def split_kernel(rows_ref, in_ref, own_ref, near_ref, far_ref):
    def put(out_ref):
        exact = in_ref[...]
        high = exact.astype(BF16)
        out_ref[:, :COLS] = high
        out_ref[:, COLS:] = (exact - high.astype(F32)).astype(BF16)

    step = pl.program_id(0)
    pl.when(step < 2)(lambda: put(own_ref))
    pl.when((step >= 2) & (step < 4))(lambda: put(near_ref))
    pl.when(step == 4)(lambda: put(far_ref))


def split_basis(rows, basis):
    return pl.pallas_call(
        split_kernel,
        grid_spec=pltpu.PrefetchScalarGridSpec(
            num_scalar_prefetch=1,
            grid=(5,),
            in_specs=[pl.BlockSpec((1024, COLS), lambda g, rows: (rows[g], 0))],
            out_specs=[
                pl.BlockSpec((1024, 256), lambda g, rows: (jnp.minimum(g, 1), 0)),
                pl.BlockSpec((1024, 256), lambda g, rows: (jnp.clip(g - 2, 0, 1), 0)),
                pl.BlockSpec((1024, 256), lambda g, rows: (0, 0)),
            ],
        ),
        out_shape=[jax.ShapeDtypeStruct((n, 256), BF16) for n in (2048, 2048, 1024)],
        compiler_params=PARAMS,
        cost_estimate=pl.CostEstimate(
            flops=1 << 20, bytes_accessed=5 << 20, transcendentals=0
        ),
    )(rows, basis)


def rotate_kernel(places, at_ref, *refs):
    blocks, refs = refs[: len(places)], refs[len(places) :]
    own_ref, near_ref, near_swapped, far_ref, far_swapped, out_ref, lhs = refs
    z, xh, y, c = at_ref[0], at_ref[1], at_ref[2], at_ref[4]
    for block, parts in zip(blocks, places):
        for i, (offset, side, token) in enumerate(parts):
            half = xh if side == 0 else 1 - xh
            at = (half * 8 + lax.rem(z + 8 + offset, 8)) * COLS
            rows = pl.ds(token, block.shape[1])
            lhs[rows, pl.ds(pl.multiple_of(at, COLS), COLS)] = block[i]

    def put(place, both):
        out_ref[lax.rem(place, 4)] = (both[:, :COLS] + both[:, COLS:]).T

    for offset, ref in ((4, own_ref), (3 + 2 * c, near_ref), (5 - 2 * c, near_swapped)):
        put(y + offset, jnp.dot(lhs[...], ref[...], preferred_element_type=F32))
    mine = lhs[:, pl.ds(pl.multiple_of(c * 1024, 1024), 1024)]
    rest = lhs[:, pl.ds(pl.multiple_of((1 - c) * 1024, 1024), 1024)]
    both = jnp.dot(mine, far_ref[...], preferred_element_type=F32)
    put(y + 2, both + jnp.dot(rest, far_swapped[...], preferred_element_type=F32))


def rotate(at, entries, slabs):
    blocks = [
        pl.BlockSpec((len(parts), *array.shape[1:]), lambda g, index=index: (index, 0, 0))
        for array, index, parts in entries
    ]
    return pl.pallas_call(
        functools.partial(rotate_kernel, [parts for _, _, parts in entries]),
        grid=(1,),
        out_shape=jax.ShapeDtypeStruct((4, COLS, TOK), F32),
        in_specs=[pl.BlockSpec(memory_space=pltpu.SMEM)]
        + blocks
        + [whole(slab.shape) for slab in slabs],
        out_specs=whole((4, COLS, TOK)),
        scratch_shapes=[pltpu.VMEM((TOK, 2048), BF16)],
        compiler_params=PARAMS,
        cost_estimate=pl.CostEstimate(
            flops=4 * TOK * 2048 * 512, bytes_accessed=7 << 20, transcendentals=0
        ),
    )(at, *[array for array, _, _ in entries], *slabs)


def product_kernel(scale, places, at_ref, *refs):
    n = len(places)
    acts, grads, out_ref, right = refs[:n], refs[n : n + 2], refs[n + 2], refs[n + 3]
    z, xh, y, xl, c = (at_ref[i] for i in range(5))
    for block, parts in zip(acts, places):
        for i, (offset, side) in enumerate(parts):
            place = (xh if side == 0 else 1 - xh) * 8 + lax.rem(z + 8 + offset, 8)
            for s in range(4):
                right[s, pl.ds(pl.multiple_of(place * 32, 32), 32), :] = block[i, s]
    for row in range(4):
        total = None
        for core in range(2):
            for side in range(2):
                s = side * 2 + (c if core == 0 else 1 - c)
                part = lax.dot_general(
                    grads[core][side, row],
                    right[s],
                    (((1,), (1,)), ((), ())),
                    preferred_element_type=F32,
                )
                total = part * part if total is None else total + part * part
        out_ref[row] = total * scale


def products(at, acts, places, grads, scale):
    return pl.pallas_call(
        functools.partial(product_kernel, scale, places),
        out_shape=jax.ShapeDtypeStruct((4, COLS, 512), F32),
        in_specs=[pl.BlockSpec(memory_space=pltpu.SMEM)]
        + [pl.BlockSpec(memory_space=pltpu.VMEM)] * (len(acts) + 2),
        out_specs=pl.BlockSpec(memory_space=pltpu.VMEM),
        scratch_shapes=[pltpu.VMEM((4, 512, TOK), BF16)],
        compiler_params=PARAMS,
        cost_estimate=pl.CostEstimate(
            flops=2 * 4 * 512 * 512 * TOK, bytes_accessed=5 << 20, transcendentals=0
        ),
    )(at, *acts, *grads)


def weave_kernel(in_ref, out_ref):
    for tile in range(4):
        lanes = slice(tile * 32, tile * 32 + 32)
        out_ref[:, tile * COLS : (tile + 1) * COLS] = jnp.concatenate(
            [in_ref[q, :, lanes] for q in range(4)], axis=1
        )


def weave(parts):
    return pl.pallas_call(
        weave_kernel,
        grid=(4,),
        out_shape=jax.ShapeDtypeStruct((COLS, 2048), F32),
        in_specs=[pl.BlockSpec((4, COLS, 128), lambda g: (0, 0, g))],
        out_specs=pl.BlockSpec((COLS, 512), lambda g: (0, g)),
        compiler_params=PARAMS,
    )(parts)


def sync(*arrays):
    return lax.optimization_barrier(arrays)


def ring_step(up, down):
    return shift(up, "z", 1), shift(down, "z", -1)


def shift_near(x):
    pairs = [(i, (i + 1) % 4) for i in range(4)] + [(4 + i, 4 + (i + 3) % 4) for i in range(4)]
    return lax.ppermute(x, ("c", "y"), pairs)


def body(activations, gradients, basis_in, basis_out):
    z, xh, y, xl, c = (lax.axis_index(a) for a in ("z", "xh", "y", "xl", "c"))
    at = jnp.stack([z, xh, y, xl, c]).astype(jnp.int32)
    near_y, far_y = (y + 1 + 2 * c) % 4, (y + 2) % 4
    rows = jnp.stack(
        [y * 2, y * 2 + 1, near_y * 2, near_y * 2 + 1, far_y * 2 + c]
    ).astype(jnp.int32)

    own_in, near_in, far_in = split_basis(rows, basis_in)
    acts_other, own_in, near_in, far_in, basis_out = sync(
        shift(activations, "xh", 1), own_in, near_in, far_in, basis_out
    )
    base = jnp.concatenate([activations, acts_other, gradients])
    own_out, near_out, far_out = split_basis(rows, basis_out)
    up1, down1, near_in, far_in, own_out, near_out, far_out = sync(
        *ring_step(base, base), shift_near(near_in), far_in, own_out, near_out, far_out
    )
    up2, down2, far_in, near_in2, near_out, far_out = sync(
        *ring_step(up1, down1), shift(far_in, "y", 2), shift(near_in, "c", 1), near_out, far_out
    )
    near = jnp.concatenate([a[2:] for a in (base, up1, down1, up2, down2)])
    up3, down3, near_out, far_in2, near_other, far_out = sync(
        *ring_step(up2, down2), shift_near(near_out), shift(far_in, "c", 1), shift(near, "xh", 1), far_out
    )
    up_end = jnp.concatenate([up3[0].reshape(2, 256, COLS), up3[2:, :256]])
    down_end = jnp.concatenate([down3[1].reshape(2, 256, COLS), down3[2:, 256:]])
    far_out = shift(far_out, "y", 2)
    up4, down4, near_out2 = sync(*ring_step(up_end, down_end), shift(near_out, "c", 1))
    ring = [(base, 0), (up1, -1), (down1, 1), (up2, -2), (down2, 2), (up3, -3), (down3, 3)]

    acts_entries = [(a, 0, ((o, 0, 0), (o, 1, 0))) for a, o in ring]
    acts_entries += [(up4, 0, ((-4, 0, 0), (-4, 0, 256))), (down4, 0, ((4, 1, 0), (4, 1, 256)))]
    acts_part = rotate(at, acts_entries, (own_in, near_in, near_in2, far_in, far_in2))
    acts_in = lax.all_to_all(acts_part.reshape(16, 32, TOK), ("xl", "c", "y"), 0, 0)

    end = jnp.concatenate([up4[2], down4[2]])[None]
    far_other = shift(jnp.concatenate([up3[2:], down3[2:], end]), "xh", 1)
    far_out2 = shift(after(far_out, acts_part), "c", 1)
    grads_entries = [(a, 2, ((o, 0, 0),)) for a, o in ring]
    grads_entries += [(up4, 2, ((-4, 0, 0),)), (down4, 2, ((4, 0, 256),))]
    grads_entries += [(near_other, 0, tuple((o, 1, 0) for o in (0, -1, 1, -2, 2)))]
    grads_entries += [(far_other, 0, tuple((o, 1, 0) for o in (-3, 3, 4)))]
    grads_part = rotate(at, grads_entries, (own_out, near_out, near_out2, far_out, far_out2))
    grads_in = lax.all_to_all(grads_part, "y", 0, 0)

    acts = jnp.sum(acts_in.reshape(4, 4, 32, TOK), axis=1).astype(BF16)[None]
    r0 = jnp.concatenate([acts, shift(acts, "xh", 1)])
    r_up1, r_down1 = sync(*ring_step(r0, r0))
    r_up2, r_down2, grads_in = sync(*ring_step(r_up1, r_down1), grads_in)
    grads = jnp.sum(grads_in, axis=0).astype(BF16)
    copies = jnp.broadcast_to(grads, (8, COLS, TOK))
    rot_own = lax.all_to_all(copies, ("xl", "y"), 0, 0).reshape(2, 4, COLS, TOK)
    r_up3, r_down3, rot_own = sync(*ring_step(r_up2, r_down2), rot_own)
    r_up4, r_down4 = ring_step(r_up3[:1], r_down3[1:])
    rot_grads = [rot_own, shift(rot_own, "c", 1)]
    rot_acts = [r0, r_up1, r_down1, r_up2, r_down2, r_up3, r_down3, r_up4, r_down4]
    rot_places = [((o, 0), (o, 1)) for _, o in ring] + [((-4, 0),), ((4, 1),)]

    scale = 1.0 / (TOK * 4)
    part = products(at, rot_acts, rot_places, rot_grads, scale)
    return weave(lax.all_to_all(part, "y", 0, 0))


def solution(mesh):
    fine = Mesh(mesh.devices.reshape(SIZES), AXES)
    return jax.shard_map(
        body,
        mesh=fine,
        in_specs=(P(DP, None, TILE), P(DP, None, TILE), P(None, TILE), P(None, TILE)),
        out_specs=P(TILE, DP),
        check_vma=False,
    )
```

time: 195 us -> 198 us (1.015)
  waiting for transfers between devices: 68.3 us -> 87.9 us
  starting transfers between devices: 72.4 us -> 56.1 us
    ppermute x32 -> x27, waiting for transfers between devices: 65.7 us -> 85.4 us  [shift(): return lax.ppermute(x, axis, [(i, (i + by) % n) for i in range(n)])]
    all_to_all x2 -> x0, starting transfers between devices: 9.04 us -> none  [the longest x1 4.59 us: body(): own_in = lax.all_to_all(split_basis(core, basis_in), 'y', 0, 0)]
    ppermute x32 -> x27, starting transfers between devices: 47 us -> 38.4 us  [shift(): return lax.ppermute(x, axis, [(i, (i + by) % n) for i in range(n)])]
    unnamed x39 -> x30, local copies, waits for them, and re-layouts: 5.78 us -> 5.2 us
  transfers between devices with their start and end apart: 37 -> 32, of which waited for: 15 -> 17; matrix products, arithmetic and copies ran while one was open for 2% -> 2% of each run, Pallas kernels for 8% -> 11%
where the time goes in v3:
time: 198 us
  waiting for transfers between devices  87.9 us (44%)
  starting transfers between devices  56.1 us (28%)
  Pallas kernels  26.7 us (13%)
  blocking collectives  17.4 us (9%)
  local copies, waits for them, and re-layouts  6.52 us (3%)
  other arithmetic  2.91 us (1%)
    ppermute x27, waiting for transfers between devices, shift(): return lax.ppermute(x, axis, [(i, (i + by) % n) for i in range(n)])  85.4 us
    ppermute x27, starting transfers between devices, shift(): return lax.ppermute(x, axis, [(i, (i + by) % n) for i in range(n)])  38.4 us
    all_to_all x1, blocking collectives, body(): return weave(lax.all_to_all(part, 'y', 0, 0))  17.4 us
    pallas_call x2, Pallas kernels, rotate(): pl.pallas_call(functools.partial(rotate_kernel, [parts for _, _, parts in...  11.9 us
    pallas_call x2, Pallas kernels, split_basis(): pl.pallas_call(split_kernel, grid_spec=pltpu.PrefetchScalarGridSpec(num_s...  8.95 us
    all_to_all x1, starting transfers between devices, body(): rot_own = lax.all_to_all(copies, ('xl', 'y'), 0, 0).reshape(2, 4, COLS, TOK)  6.2 us
    all_to_all x1, starting transfers between devices, body(): lax.all_to_all(acts_part.reshape(16, 32, TOK), ('xl', 'c', 'y'), 0, 0)  5.59 us
    unnamed x30, local copies, waits for them, and re-layouts  5.2 us
  transfers between devices with their start and end apart: 32, of which 17 were waited for; matrix products, arithmetic and copies ran while one was open for 2% of the time, Pallas kernels for 11%

profile of v3, /device:TPU:2, one launch (start us, length us, event | category | flops | bytes accessed | tf_op | source)
XLA Modules:
  0.0 197.7 jit_solution(13758438636592896299)
XLA Ops:
  0.0 2.1 %collective-permute-start = (bf16[1,512,128]{2,1,0:T(8,128)(2,1)}, bf16[1,512,128]{2,1,0:T(8,128)(2,1)S(1)}, u32[]{:S(2)}, u32[]{:S(2)}) collective-permute-start(bf16[1,512,128]{2,1,0:T(8,128)(2,1)} %param.4), channel_id=1, source_target_pairs={{0,8},{8,0},{1,9},{9,1},{2,10},{10,2},{3,11},{11,3},{4,12},{12,4},... | collective-permute-start | bytes 393224 | tf_op jit(solution)/shard_map/ppermute | solution.py:24
  2.1 0.1 stack.47.rows_ref
  2.2 4.1 %shard_map.46 = (bf16[2048,256]{1,0:T(8,128)(2,1)S(1)}, bf16[2048,256]{1,0:T(8,128)(2,1)S(1)}, bf16[1024,256]{1,0:T(8,128)(2,1)S(1)}) custom-call(s32[5]{0:T(128)S(1)} %stack.47.rows_ref, f32[8192,128]{1,0:T(8,128)} %in_ref.1), custom_call_target="tpu_custom_call" | custom-call | flops 1048576 | bytes 5242880 | tf_op jit(solution)/shard_map/pallas_call | solution.py:49
  6.3 0.0 copy-start.1
  6.3 1.0 copy-done.1
  7.3 1.6 collective-permute-start.3
  9.0 5.9 %collective-permute-start.2 = (bf16[3,512,128]{2,1,0:T(8,128)(2,1)S(1)}, bf16[3,512,128]{2,1,0:T(8,128)(2,1)S(1)}, u32[]{:S(2)}, u32[]{:S(2)}) collective-permute-start(bf16[3,512,128]{2,1,0:T(8,128)(2,1)S(1)} %get-tuple-element.94.refs_0_), channel_id=1, source_target_pairs={{0,7},{1,0},{2,1},{3,2},{4,3},{5,4},{6,5},{7,6},{8,15},{9,8},{10,9... | collective-permute-start | bytes 1179656 | tf_op jit(solution)/shard_map/ppermute | solution.py:24
  14.9 4.9 %shard_map.47 = (bf16[2048,256]{1,0:T(8,128)(2,1)S(1)}, bf16[2048,256]{1,0:T(8,128)(2,1)S(1)}, bf16[1024,256]{1,0:T(8,128)(2,1)}) custom-call(s32[5]{0:T(128)S(1)} %stack.47.rows_ref, f32[8192,128]{1,0:T(8,128)} %in_ref.2), custom_call_target="tpu_custom_call" | custom-call | flops 1048576 | bytes 5242880 | tf_op jit(solution)/shard_map/pallas_call | solution.py:49
  19.8 4.4 %collective-permute-done.2.refs_2_ = bf16[3,512,128]{2,1,0:T(8,128)(2,1)S(1)} collective-permute-done((bf16[3,512,128]{2,1,0:T(8,128)(2,1)S(1)}, bf16[3,512,128]{2,1,0:T(8,128)(2,1)S(1)}, u32[]{:S(2)}, u32[]{:S(2)}) %collective-permute-start.2) | collective-permute-done | bytes 393248 | tf_op jit(solution)/shard_map/ppermute | solution.py:24
  24.1 3.4 %collective-permute-done.1.refs_1_ = bf16[3,512,128]{2,1,0:T(8,128)(2,1)S(1)} collective-permute-done((bf16[3,512,128]{2,1,0:T(8,128)(2,1)S(1)}, bf16[3,512,128]{2,1,0:T(8,128)(2,1)S(1)}, u32[]{:S(2)}, u32[]{:S(2)}) %collective-permute-start.1) | collective-permute-done | bytes 393248 | tf_op jit(solution)/shard_map/ppermute | solution.py:24
  27.6 0.0 collective-permute-done.3.refs_10_
  27.6 0.7 collective-permute-start.6
  28.3 3.2 %collective-permute-start.5 = (bf16[3,512,128]{2,1,0:T(8,128)(2,1)S(1)}, bf16[3,512,128]{2,1,0:T(8,128)(2,1)S(1)}, u32[]{:S(2)}, u32[]{:S(2)}) collective-permute-start(bf16[3,512,128]{2,1,0:T(8,128)(2,1)S(1)} %collective-permute-done.2.refs_2_), channel_id=1, source_target_pairs={{0,7},{1,0},{2,1},{3,2},{4,3},{5,4},{6,5},{7,6},{8,15},{9,8},{10,9... | collective-permute-start | bytes 1179656 | tf_op jit(solution)/shard_map/ppermute | solution.py:24
  31.6 9.1 %collective-permute-done.4.refs_3_ = bf16[3,512,128]{2,1,0:T(8,128)(2,1)S(1)} collective-permute-done((bf16[3,512,128]{2,1,0:T(8,128)(2,1)S(1)}, bf16[3,512,128]{2,1,0:T(8,128)(2,1)S(1)}, u32[]{:S(2)}, u32[]{:S(2)}) %collective-permute-start.4) | collective-permute-done | bytes 393248 | tf_op jit(solution)/shard_map/ppermute | solution.py:24
  40.7 0.0 collective-permute-done.5.refs_4_
  40.7 2.8 %collective-permute-done.6.refs_12_ = bf16[1024,256]{1,0:T(8,128)(2,1)S(1)} collective-permute-done((bf16[1024,256]{1,0:T(8,128)(2,1)S(1)}, bf16[1024,256]{1,0:T(8,128)(2,1)S(1)}, u32[]{:S(2)}, u32[]{:S(2)}) %collective-permute-start.6) | collective-permute-done | bytes 524320 | tf_op jit(solution)/shard_map/ppermute | solution.py:24
  43.4 0.1 collective-permute-start.10
  43.6 0.9 copy-done.9
  44.5 1.5 collective-permute-start.12
  46.0 0.0 collective-permute-start.11
  46.0 0.0 collective-permute-start.8
  46.0 3.2 %collective-permute-start.9 = (bf16[3,512,128]{2,1,0:T(8,128)(2,1)S(1)}, bf16[3,512,128]{2,1,0:T(8,128)(2,1)S(1)}, u32[]{:S(2)}, u32[]{:S(2)}) collective-permute-start(bf16[3,512,128]{2,1,0:T(8,128)(2,1)S(1)} %collective-permute-done.5.refs_4_), channel_id=1, source_target_pairs={{0,7},{1,0},{2,1},{3,2},{4,3},{5,4},{6,5},{7,6},{8,15},{9,8},{10,9... | collective-permute-start | bytes 1179656 | tf_op jit(solution)/shard_map/ppermute | solution.py:24
  49.2 9.5 %collective-permute-done.8.refs_5_ = bf16[3,512,128]{2,1,0:T(8,128)(2,1)S(1)} collective-permute-done((bf16[3,512,128]{2,1,0:T(8,128)(2,1)S(1)}, bf16[3,512,128]{2,1,0:T(8,128)(2,1)S(1)}, u32[]{:S(2)}, u32[]{:S(2)}) %collective-permute-start.8) | collective-permute-done | bytes 393248 | tf_op jit(solution)/shard_map/ppermute | solution.py:24
  58.7 0.0 collective-permute-done.9.refs_6_
  58.7 3.6 %collective-permute-done.12.refs_9_ = bf16[5,512,128]{2,1,0:T(8,128)(2,1)S(1)} collective-permute-done((bf16[5,512,128]{2,1,0:T(8,128)(2,1)S(1)}, bf16[5,512,128]{2,1,0:T(8,128)(2,1)S(1)}, u32[]{:S(2)}, u32[]{:S(2)}) %collective-permute-start.12) | collective-permute-done | bytes 655392 | tf_op jit(solution)/shard_map/ppermute | solution.py:24
  62.4 0.7 collective-permute-start.22
  63.1 0.7 pad_maximum_fusion.2
  63.9 0.7 pad_maximum_fusion.3
  64.6 3.5 %collective-permute-start.14 = (bf16[3,256,128]{2,1,0:T(8,128)(2,1)}, bf16[3,256,128]{2,1,0:T(8,128)(2,1)S(1)}, u32[]{:S(2)}, u32[]{:S(2)}) collective-permute-start(bf16[3,256,128]{2,1,0:T(8,128)(2,1)} %pad_maximum_fusion.3), channel_id=1, source_target_pairs={{0,7},{1,0},{2,1},{3,2},{4,3},{5,4},{6,5},{7,6},{8,15},{9,8},{10,9... | collective-permute-start | bytes 589832 | tf_op jit(solution)/shard_map/ppermute | solution.py:24
  68.0 0.1 stack.41.at_ref
  68.1 4.1 %collective-permute-done.13.refs_7_ = bf16[3,256,128]{2,1,0:T(8,128)(2,1)S(1)} collective-permute-done((bf16[3,256,128]{2,1,0:T(8,128)(2,1)}, bf16[3,256,128]{2,1,0:T(8,128)(2,1)S(1)}, u32[]{:S(2)}, u32[]{:S(2)}) %collective-permute-start.13) | collective-permute-done | bytes 196640 | tf_op jit(solution)/shard_map/ppermute | solution.py:24
  72.3 0.4 collective-permute-done.14.refs_8_
  72.6 1.0 copy-done.5
  73.7 1.0 copy-done.7
  74.7 5.9 %shard_map.48 = f32[4,128,512]{2,1,0:T(8,128)} custom-call(s32[5]{0:T(128)S(1)} %stack.41.at_ref, bf16[3,512,128]{2,1,0:T(8,128)(2,1)S(1)} %get-tuple-element.94.refs_0_, bf16[3,512,128]{2,1,0:T(8,128)(2,1)S(1)} %collective-permute-done.1.refs_1_, bf16[3,512,128]{2,1,0:T(8,128)(2,1)S(1)} %collective-permute-done.2.refs_2_, ...), custom_call_target="tpu_custom_call" | custom-call | flops 2147483648 | bytes 7340032 | tf_op jit(solution)/shard_map/pallas_call | solution.py:96
  80.6 0.0 collective-permute-done.22.refs_14_
  80.6 5.6 %all-to-all-start = ((f32[16,32,512]{2,1,0:T(8,128)}), f32[16,32,512]{2,1,0:T(8,128)}, u32[]{:S(2)}, u32[]{:S(2)}) async-start(f32[16,32,512]{2,1,0:T(8,128)} %bitcast.12), calls=%async_computation | async-start | bytes 2097152 | tf_op jit(solution)/shard_map/all_to_all | solution.py:216
  86.2 0.1 collective-permute-start.23
  86.4 1.5 collective-permute-start.21
  87.9 20.6 %collective-permute-done.21.refs_10_ = bf16[3,512,128]{2,1,0:T(8,128)(2,1)S(1)} collective-permute-done((bf16[3,512,128]{2,1,0:T(8,128)(2,1)S(1)}, bf16[3,512,128]{2,1,0:T(8,128)(2,1)S(1)}, u32[]{:S(2)}, u32[]{:S(2)}) %collective-permute-start.21) | collective-permute-done | bytes 393248 | tf_op jit(solution)/shard_map/ppermute | solution.py:24
  108.5 0.0 collective-permute-done.23.refs_15_
  108.5 1.1 copy-done.3
  109.6 6.0 %shard_map.49 = f32[4,128,512]{2,1,0:T(8,128)} custom-call(s32[5]{0:T(128)S(1)} %stack.41.at_ref, bf16[3,512,128]{2,1,0:T(8,128)(2,1)S(1)} %get-tuple-element.94.refs_0_, bf16[3,512,128]{2,1,0:T(8,128)(2,1)S(1)} %collective-permute-done.1.refs_1_, bf16[3,512,128]{2,1,0:T(8,128)(2,1)S(1)} %collective-permute-done.2.refs_2_, ...), custom_call_target="tpu_custom_call" | custom-call | flops 2147483648 | bytes 7340032 | tf_op jit(solution)/shard_map/pallas_call | solution.py:96
  115.6 4.2 %all-to-all-start.1 = ((f32[4,128,512]{2,1,0:T(8,128)}), f32[4,128,512]{2,1,0:T(8,128)S(1)}, u32[]{:S(2)}, u32[]{:S(2)}) async-start(f32[4,128,512]{2,1,0:T(8,128)} %shard_map.49), calls=%async_computation.1 | async-start | bytes 2097152 | tf_op jit(solution)/shard_map/all_to_all | solution.py:226
  119.8 1.3 bitcast_reduce_fusion
  121.2 2.2 %collective-permute-start.16 = (bf16[1,4,32,512]{3,2,1,0:T(8,128)(2,1)S(1)}, bf16[1,4,32,512]{3,2,1,0:T(8,128)(2,1)S(1)}, u32[]{:S(2)}, u32[]{:S(2)}) collective-permute-start(bf16[1,4,32,512]{3,2,1,0:T(8,128)(2,1)S(1)} %bitcast.28), channel_id=1, source_target_pairs={{0,8},{8,0},{1,9},{9,1},{2,10},{10,2},{3,11},{11,3},{4,12},{12,4},... | collective-permute-start | bytes 393224 | tf_op jit(solution)/shard_map/ppermute | solution.py:24
  123.4 4.3 %collective-permute-done.16 = bf16[1,4,32,512]{3,2,1,0:T(8,128)(2,1)S(1)} collective-permute-done((bf16[1,4,32,512]{3,2,1,0:T(8,128)(2,1)S(1)}, bf16[1,4,32,512]{3,2,1,0:T(8,128)(2,1)S(1)}, u32[]{:S(2)}, u32[]{:S(2)}) %collective-permute-start.16) | collective-permute-done | bytes 131104 | tf_op jit(solution)/shard_map/ppermute | solution.py:24
  127.8 3.7 %collective-permute-start.18 = (bf16[2,4,32,512]{3,2,1,0:T(8,128)(2,1)S(1)}, bf16[2,4,32,512]{3,2,1,0:T(8,128)(2,1)S(1)}, u32[]{:S(2)}, u32[]{:S(2)}) collective-permute-start(bf16[2,4,32,512]{3,2,1,0:T(8,128)(2,1)S(1)} %pad_maximum_fusion.1.refs_0_), channel_id=1, source_target_pairs={{0,7},{1,0},{2,1},{3,2},{4,3},{5,4},{6,5},{7,6},{8,15},{9,8},{10,9... | collective-permute-start | bytes 786440 | tf_op jit(solution)/shard_map/ppermute | solution.py:24
  131.4 4.2 %collective-permute-done.18.refs_2_ = bf16[2,4,32,512]{3,2,1,0:T(8,128)(2,1)S(1)} collective-permute-done((bf16[2,4,32,512]{3,2,1,0:T(8,128)(2,1)S(1)}, bf16[2,4,32,512]{3,2,1,0:T(8,128)(2,1)S(1)}, u32[]{:S(2)}, u32[]{:S(2)}) %collective-permute-start.18) | collective-permute-done | bytes 262176 | tf_op jit(solution)/shard_map/ppermute | solution.py:24
  135.7 3.4 %collective-permute-done.17.refs_1_ = bf16[2,4,32,512]{3,2,1,0:T(8,128)(2,1)S(1)} collective-permute-done((bf16[2,4,32,512]{3,2,1,0:T(8,128)(2,1)S(1)}, bf16[2,4,32,512]{3,2,1,0:T(8,128)(2,1)S(1)}, u32[]{:S(2)}, u32[]{:S(2)}) %collective-permute-start.17) | collective-permute-done | bytes 262176 | tf_op jit(solution)/shard_map/ppermute | solution.py:24
  139.1 3.2 %collective-permute-start.20 = (bf16[2,4,32,512]{3,2,1,0:T(8,128)(2,1)S(1)}, bf16[2,4,32,512]{3,2,1,0:T(8,128)(2,1)S(1)}, u32[]{:S(2)}, u32[]{:S(2)}) collective-permute-start(bf16[2,4,32,512]{3,2,1,0:T(8,128)(2,1)S(1)} %collective-permute-done.18.refs_2_), channel_id=1, source_target_pairs={{0,7},{1,0},{2,1},{3,2},{4,3},{5,4},{6,5},{7,6},{8,15},{9,8},{10,9... | collective-permute-start | bytes 786440 | tf_op jit(solution)/shard_map/ppermute | solution.py:24
  142.3 4.3 %collective-permute-done.19.refs_3_ = bf16[2,4,32,512]{3,2,1,0:T(8,128)(2,1)S(1)} collective-permute-done((bf16[2,4,32,512]{3,2,1,0:T(8,128)(2,1)S(1)}, bf16[2,4,32,512]{3,2,1,0:T(8,128)(2,1)S(1)}, u32[]{:S(2)}, u32[]{:S(2)}) %collective-permute-start.19) | collective-permute-done | bytes 262176 | tf_op jit(solution)/shard_map/ppermute | solution.py:24
  146.7 0.1 reduce_sum.19
  146.7 1.1 broadcast_in_dim.8
  147.8 6.2 %all-to-all-start.2 = ((bf16[8,128,512]{2,1,0:T(8,128)(2,1)}), bf16[8,128,512]{2,1,0:T(8,128)(2,1)S(1)}, u32[]{:S(2)}, u32[]{:S(2)}) async-start(bf16[8,128,512]{2,1,0:T(8,128)(2,1)} %broadcast_in_dim.8), calls=%async_computation.2 | async-start | bytes 2097152 | tf_op jit(solution)/shard_map/all_to_all | solution.py:234
  154.0 3.2 %collective-permute-start.25 = (bf16[2,4,32,512]{3,2,1,0:T(8,128)(2,1)S(1)}, bf16[2,4,32,512]{3,2,1,0:T(8,128)(2,1)S(1)}, u32[]{:S(2)}, u32[]{:S(2)}) collective-permute-start(bf16[2,4,32,512]{3,2,1,0:T(8,128)(2,1)S(1)} %collective-permute-done.20.refs_4_), channel_id=1, source_target_pairs={{0,7},{1,0},{2,1},{3,2},{4,3},{5,4},{6,5},{7,6},{8,15},{9,8},{10,9... | collective-permute-start | bytes 786440 | tf_op jit(solution)/shard_map/ppermute | solution.py:24
  157.2 4.3 %collective-permute-done.24.refs_5_ = bf16[2,4,32,512]{3,2,1,0:T(8,128)(2,1)S(1)} collective-permute-done((bf16[2,4,32,512]{3,2,1,0:T(8,128)(2,1)S(1)}, bf16[2,4,32,512]{3,2,1,0:T(8,128)(2,1)S(1)}, u32[]{:S(2)}, u32[]{:S(2)}) %collective-permute-start.24) | collective-permute-done | bytes 262176 | tf_op jit(solution)/shard_map/ppermute | solution.py:24
  161.6 2.5 %all-to-all-done.2 = bf16[8,128,512]{2,1,0:T(8,128)(2,1)S(1)} async-done(((bf16[8,128,512]{2,1,0:T(8,128)(2,1)}), bf16[8,128,512]{2,1,0:T(8,128)(2,1)S(1)}, u32[]{:S(2)}, u32[]{:S(2)}) %all-to-all-start.2) | async-done | bytes 1048608 | tf_op jit(solution)/shard_map/all_to_all | solution.py:234
  164.1 3.5 %collective-permute-start.27 = (bf16[1,4,32,512]{3,2,1,0:T(8,128)(2,1)S(1)}, bf16[1,4,32,512]{3,2,1,0:T(8,128)(2,1)S(1)}, u32[]{:S(2)}, u32[]{:S(2)}) collective-permute-start(bf16[1,4,32,512]{3,2,1,0:T(8,128)(2,1)S(1)} %slice.55), channel_id=1, source_target_pairs={{0,7},{1,0},{2,1},{3,2},{4,3},{5,4},{6,5},{7,6},{8,15},{9,8},{10,9... | collective-permute-start | bytes 393224 | tf_op jit(solution)/shard_map/ppermute | solution.py:24
  167.6 3.4 %collective-permute-done.27.refs_8_ = bf16[1,4,32,512]{3,2,1,0:T(8,128)(2,1)S(1)} collective-permute-done((bf16[1,4,32,512]{3,2,1,0:T(8,128)(2,1)S(1)}, bf16[1,4,32,512]{3,2,1,0:T(8,128)(2,1)S(1)}, u32[]{:S(2)}, u32[]{:S(2)}) %collective-permute-start.27) | collective-permute-done | bytes 131104 | tf_op jit(solution)/shard_map/ppermute | solution.py:24
  171.0 3.4 %collective-permute-done.26.refs_7_ = bf16[1,4,32,512]{3,2,1,0:T(8,128)(2,1)S(1)} collective-permute-done((bf16[1,4,32,512]{3,2,1,0:T(8,128)(2,1)S(1)}, bf16[1,4,32,512]{3,2,1,0:T(8,128)(2,1)S(1)}, u32[]{:S(2)}, u32[]{:S(2)}) %collective-permute-start.26) | collective-permute-done | bytes 131104 | tf_op jit(solution)/shard_map/ppermute | solution.py:24
  174.5 3.5 %shard_map.50 = f32[4,128,512]{2,1,0:T(8,128)S(1)} custom-call(s32[5]{0:T(128)S(1)} %stack.41.at_ref, bf16[2,4,32,512]{3,2,1,0:T(8,128)(2,1)S(1)} %pad_maximum_fusion.1.refs_0_, bf16[2,4,32,512]{3,2,1,0:T(8,128)(2,1)S(1)} %collective-permute-done.17.refs_1_, bf16[2,4,32,512]{3,2,1,0:T(8,128)(2,1)S(1)} %collective-permute-done.18.refs_2_, ...), custom_call_target="tpu_custom_call" | custom-call | flops 1073741824 | bytes 5242880 | tf_op jit(solution)/shard_map/pallas_call | solution.py:137
  178.0 17.4 %all_to_all.20.in_ref = f32[4,128,512]{2,1,0:T(8,128)S(1)} all-to-all(f32[4,128,512]{2,1,0:T(8,128)S(1)} %shard_map.50), channel_id=1, replica_groups=mesh['xl'=2,'c'=2,'y'=4,'xh'=2,'z'=8] {'y'}, dimensions={0} | all-to-all | bytes 2097152 | tf_op jit(solution)/shard_map/all_to_all | solution.py:243
  195.3 2.4 %shard_map.51 = f32[128,2048]{1,0:T(8,128)} custom-call(f32[4,128,512]{2,1,0:T(8,128)S(1)} %all_to_all.20.in_ref), custom_call_target="tpu_custom_call" | custom-call | tf_op jit(solution)/shard_map/pallas_call | solution.py:160
  (55 shorter events, 0.4 us)
Async XLA Ops:
  0.0 8.9 %copy-start.11 = (bf16[1,512,128]{2,1,0:T(8,128)(2,1)S(1)}, bf16[1,512,128]{2,1,0:T(8,128)(2,1)}, u32[]{:S(2)}) copy-start(bf16[1,512,128]{2,1,0:T(8,128)(2,1)} %param.4) | copy-start | bytes 393220
  0.0 8.9 %copy-start.10 = (bf16[1,512,128]{2,1,0:T(8,128)(2,1)S(1)}, bf16[1,512,128]{2,1,0:T(8,128)(2,1)}, u32[]{:S(2)}) copy-start(bf16[1,512,128]{2,1,0:T(8,128)(2,1)} %param.5) | copy-start | bytes 393220
  0.0 7.3 %collective-permute-start = (bf16[1,512,128]{2,1,0:T(8,128)(2,1)}, bf16[1,512,128]{2,1,0:T(8,128)(2,1)S(1)}, u32[]{:S(2)}, u32[]{:S(2)}) collective-permute-start(bf16[1,512,128]{2,1,0:T(8,128)(2,1)} %param.4), channel_id=1, source_target_pairs={{0,8},{8,0},{1,9},{9,1},{2,10},{10,2},{3,11},{11,3},{4,12},{12,4},... | collective-permute-start | bytes 393224 | tf_op jit(solution)/shard_map/ppermute | solution.py:24
  6.3 1.0 copy-start.1
  7.3 20.3 %collective-permute-start.3 = (bf16[2048,256]{1,0:T(8,128)(2,1)S(1)}, bf16[2048,256]{1,0:T(8,128)(2,1)S(1)}, u32[]{:S(2)}, u32[]{:S(2)}) collective-permute-start(bf16[2048,256]{1,0:T(8,128)(2,1)S(1)} %get-tuple-element.51), channel_id=1, source_target_pairs={{0,16},{16,32},{32,48},{48,0},{64,112},{80,64},{96,80},{112,96},{1... | collective-permute-start | bytes 3145736 | tf_op jit(solution)/shard_map/ppermute | solution.py:180
  9.0 15.2 %collective-permute-start.2 = (bf16[3,512,128]{2,1,0:T(8,128)(2,1)S(1)}, bf16[3,512,128]{2,1,0:T(8,128)(2,1)S(1)}, u32[]{:S(2)}, u32[]{:S(2)}) collective-permute-start(bf16[3,512,128]{2,1,0:T(8,128)(2,1)S(1)} %get-tuple-element.94.refs_0_), channel_id=1, source_target_pairs={{0,7},{1,0},{2,1},{3,2},{4,3},{5,4},{6,5},{7,6},{8,15},{9,8},{10,9... | collective-permute-start | bytes 1179656 | tf_op jit(solution)/shard_map/ppermute | solution.py:24
  14.9 12.7 %collective-permute-start.1 = (bf16[3,512,128]{2,1,0:T(8,128)(2,1)S(1)}, bf16[3,512,128]{2,1,0:T(8,128)(2,1)S(1)}, u32[]{:S(2)}, u32[]{:S(2)}) collective-permute-start(bf16[3,512,128]{2,1,0:T(8,128)(2,1)S(1)} %get-tuple-element.94.refs_0_), channel_id=1, source_target_pairs={{0,1},{1,2},{2,3},{3,4},{4,5},{5,6},{6,7},{7,0},{8,9},{9,10},{10,1... | collective-permute-start | bytes 1179656 | tf_op jit(solution)/shard_map/ppermute | solution.py:24
  19.8 44.1 %copy-start = (bf16[2048,256]{1,0:T(8,128)(2,1)}, bf16[2048,256]{1,0:T(8,128)(2,1)S(1)}, u32[]{:S(2)}) copy-start(bf16[2048,256]{1,0:T(8,128)(2,1)S(1)} %get-tuple-element.79.refs_11_) | copy-start | bytes 3145732
  27.6 37.0 %copy-start.8 = (bf16[2048,256]{1,0:T(8,128)(2,1)}, bf16[2048,256]{1,0:T(8,128)(2,1)S(1)}, u32[]{:S(2)}) copy-start(bf16[2048,256]{1,0:T(8,128)(2,1)S(1)} %collective-permute-done.3.refs_10_) | copy-start | bytes 3145732
  27.6 15.9 %collective-permute-start.7 = (bf16[2048,256]{1,0:T(8,128)(2,1)S(1)}, bf16[2048,256]{1,0:T(8,128)(2,1)S(1)}, u32[]{:S(2)}, u32[]{:S(2)}) collective-permute-start(bf16[2048,256]{1,0:T(8,128)(2,1)S(1)} %collective-permute-done.3.refs_10_), channel_id=1, source_target_pairs={{0,64},{64,0},{1,65},{65,1},{2,66},{66,2},{3,67},{67,3},{4,68},{68... | collective-permute-start | bytes 3145736 | tf_op jit(solution)/shard_map/ppermute | solution.py:24
  27.6 15.9 %collective-permute-start.6 = (bf16[1024,256]{1,0:T(8,128)(2,1)S(1)}, bf16[1024,256]{1,0:T(8,128)(2,1)S(1)}, u32[]{:S(2)}, u32[]{:S(2)}) collective-permute-start(bf16[1024,256]{1,0:T(8,128)(2,1)S(1)} %get-tuple-element.59), channel_id=1, source_target_pairs={{0,32},{16,48},{32,0},{48,16},{1,33},{17,49},{33,1},{49,17},{2,34}... | collective-permute-start | bytes 1572872 | tf_op jit(solution)/shard_map/ppermute | solution.py:24
  28.3 12.4 %collective-permute-start.4 = (bf16[3,512,128]{2,1,0:T(8,128)(2,1)S(1)}, bf16[3,512,128]{2,1,0:T(8,128)(2,1)S(1)}, u32[]{:S(2)}, u32[]{:S(2)}) collective-permute-start(bf16[3,512,128]{2,1,0:T(8,128)(2,1)S(1)} %collective-permute-done.1.refs_1_), channel_id=1, source_target_pairs={{0,1},{1,2},{2,3},{3,4},{4,5},{5,6},{6,7},{7,0},{8,9},{9,10},{10,1... | collective-permute-start | bytes 1179656 | tf_op jit(solution)/shard_map/ppermute | solution.py:24
  28.3 12.4 %collective-permute-start.5 = (bf16[3,512,128]{2,1,0:T(8,128)(2,1)S(1)}, bf16[3,512,128]{2,1,0:T(8,128)(2,1)S(1)}, u32[]{:S(2)}, u32[]{:S(2)}) collective-permute-start(bf16[3,512,128]{2,1,0:T(8,128)(2,1)S(1)} %collective-permute-done.2.refs_2_), channel_id=1, source_target_pairs={{0,7},{1,0},{2,1},{3,2},{4,3},{5,4},{6,5},{7,6},{8,15},{9,8},{10,9... | collective-permute-start | bytes 1179656 | tf_op jit(solution)/shard_map/ppermute | solution.py:24
  43.4 21.1 %copy-start.4 = (bf16[1024,256]{1,0:T(8,128)(2,1)}, bf16[1024,256]{1,0:T(8,128)(2,1)S(1)}, u32[]{:S(2)}) copy-start(bf16[1024,256]{1,0:T(8,128)(2,1)S(1)} %collective-permute-done.6.refs_12_) | copy-start | bytes 1572868
  43.4 1.0 copy-start.9
  43.4 18.9 %collective-permute-start.10 = (bf16[2048,256]{1,0:T(8,128)(2,1)S(1)}, bf16[2048,256]{1,0:T(8,128)(2,1)}, u32[]{:S(2)}, u32[]{:S(2)}) collective-permute-start(bf16[2048,256]{1,0:T(8,128)(2,1)S(1)} %get-tuple-element.65), channel_id=1, source_target_pairs={{0,16},{16,32},{32,48},{48,0},{64,112},{80,64},{96,80},{112,96},{1... | collective-permute-start | bytes 3145736 | tf_op jit(solution)/shard_map/ppermute | solution.py:180
  44.5 17.9 %collective-permute-start.12 = (bf16[5,512,128]{2,1,0:T(8,128)(2,1)S(1)}, bf16[5,512,128]{2,1,0:T(8,128)(2,1)S(1)}, u32[]{:S(2)}, u32[]{:S(2)}) collective-permute-start(bf16[5,512,128]{2,1,0:T(8,128)(2,1)S(1)} %slice_dynamic-update-slice_fusion), channel_id=1, source_target_pairs={{0,8},{8,0},{1,9},{9,1},{2,10},{10,2},{3,11},{11,3},{4,12},{12,4},... | collective-permute-start | bytes 1966088 | tf_op jit(solution)/shard_map/ppermute | solution.py:24
  46.0 12.7 %collective-permute-start.11 = (bf16[1024,256]{1,0:T(8,128)(2,1)S(1)}, bf16[1024,256]{1,0:T(8,128)(2,1)S(1)}, u32[]{:S(2)}, u32[]{:S(2)}) collective-permute-start(bf16[1024,256]{1,0:T(8,128)(2,1)S(1)} %collective-permute-done.6.refs_12_), channel_id=1, source_target_pairs={{0,64},{64,0},{1,65},{65,1},{2,66},{66,2},{3,67},{67,3},{4,68},{68... | collective-permute-start | bytes 1572872 | tf_op jit(solution)/shard_map/ppermute | solution.py:24
  46.0 12.7 %collective-permute-start.8 = (bf16[3,512,128]{2,1,0:T(8,128)(2,1)S(1)}, bf16[3,512,128]{2,1,0:T(8,128)(2,1)S(1)}, u32[]{:S(2)}, u32[]{:S(2)}) collective-permute-start(bf16[3,512,128]{2,1,0:T(8,128)(2,1)S(1)} %collective-permute-done.4.refs_3_), channel_id=1, source_target_pairs={{0,1},{1,2},{2,3},{3,4},{4,5},{5,6},{6,7},{7,0},{8,9},{9,10},{10,1... | collective-permute-start | bytes 1179656 | tf_op jit(solution)/shard_map/ppermute | solution.py:24
  46.0 12.7 %collective-permute-start.9 = (bf16[3,512,128]{2,1,0:T(8,128)(2,1)S(1)}, bf16[3,512,128]{2,1,0:T(8,128)(2,1)S(1)}, u32[]{:S(2)}, u32[]{:S(2)}) collective-permute-start(bf16[3,512,128]{2,1,0:T(8,128)(2,1)S(1)} %collective-permute-done.5.refs_4_), channel_id=1, source_target_pairs={{0,7},{1,0},{2,1},{3,2},{4,3},{5,4},{6,5},{7,6},{8,15},{9,8},{10,9... | collective-permute-start | bytes 1179656 | tf_op jit(solution)/shard_map/ppermute | solution.py:24
  58.7 5.8 %copy-start.6 = (bf16[1024,256]{1,0:T(8,128)(2,1)}, bf16[1024,256]{1,0:T(8,128)(2,1)S(1)}, u32[]{:S(2)}) copy-start(bf16[1024,256]{1,0:T(8,128)(2,1)S(1)} %collective-permute-done.11.refs_13_) | copy-start | bytes 1572868
  62.4 2.2 %copy-start.2 = (bf16[5,512,128]{2,1,0:T(8,128)(2,1)}, bf16[5,512,128]{2,1,0:T(8,128)(2,1)S(1)}, u32[]{:S(2)}) copy-start(bf16[5,512,128]{2,1,0:T(8,128)(2,1)S(1)} %collective-permute-done.12.refs_9_) | copy-start | bytes 1966084
  62.4 10.3 %collective-permute-start.15 = (bf16[2048,256]{1,0:T(8,128)(2,1)}, bf16[2048,256]{1,0:T(8,128)(2,1)}, u32[]{:S(2)}, u32[]{:S(2)}) collective-permute-start(bf16[2048,256]{1,0:T(8,128)(2,1)} %collective-permute-done.10.refs_12_), channel_id=1, source_target_pairs={{0,64},{64,0},{1,65},{65,1},{2,66},{66,2},{3,67},{67,3},{4,68},{68... | collective-permute-start | bytes 3145736 | tf_op jit(solution)/shard_map/ppermute | solution.py:24
  62.4 18.2 %collective-permute-start.22 = (bf16[1024,256]{1,0:T(8,128)(2,1)}, bf16[1024,256]{1,0:T(8,128)(2,1)}, u32[]{:S(2)}, u32[]{:S(2)}) collective-permute-start(bf16[1024,256]{1,0:T(8,128)(2,1)} %get-tuple-element.81), channel_id=1, source_target_pairs={{0,32},{16,48},{32,0},{48,16},{1,33},{17,49},{33,1},{49,17},{2,34}... | collective-permute-start | bytes 1572872 | tf_op jit(solution)/shard_map/ppermute | solution.py:24
  63.8 8.4 %collective-permute-start.13 = (bf16[3,256,128]{2,1,0:T(8,128)(2,1)}, bf16[3,256,128]{2,1,0:T(8,128)(2,1)S(1)}, u32[]{:S(2)}, u32[]{:S(2)}) collective-permute-start(bf16[3,256,128]{2,1,0:T(8,128)(2,1)} %pad_maximum_fusion.2), channel_id=1, source_target_pairs={{0,1},{1,2},{2,3},{3,4},{4,5},{5,6},{6,7},{7,0},{8,9},{9,10},{10,1... | collective-permute-start | bytes 589832 | tf_op jit(solution)/shard_map/ppermute | solution.py:24
  64.6 8.1 %collective-permute-start.14 = (bf16[3,256,128]{2,1,0:T(8,128)(2,1)}, bf16[3,256,128]{2,1,0:T(8,128)(2,1)S(1)}, u32[]{:S(2)}, u32[]{:S(2)}) collective-permute-start(bf16[3,256,128]{2,1,0:T(8,128)(2,1)} %pad_maximum_fusion.3), channel_id=1, source_target_pairs={{0,7},{1,0},{2,1},{3,2},{4,3},{5,4},{6,5},{7,6},{8,15},{9,8},{10,9... | collective-permute-start | bytes 589832 | tf_op jit(solution)/shard_map/ppermute | solution.py:24
  72.6 1.0 copy-start.5
  73.7 1.0 copy-start.7
  80.6 35.0 %all-to-all-start = ((f32[16,32,512]{2,1,0:T(8,128)}), f32[16,32,512]{2,1,0:T(8,128)}, u32[]{:S(2)}, u32[]{:S(2)}) async-start(f32[16,32,512]{2,1,0:T(8,128)} %bitcast.12), calls=%async_computation | async-start | bytes 2097152 | tf_op jit(solution)/shard_map/all_to_all | solution.py:216
  86.2 22.3 %collective-permute-start.23 = (bf16[1024,256]{1,0:T(8,128)(2,1)}, bf16[1024,256]{1,0:T(8,128)(2,1)S(1)}, u32[]{:S(2)}, u32[]{:S(2)}) collective-permute-start(bf16[1024,256]{1,0:T(8,128)(2,1)} %collective-permute-done.22.refs_14_), channel_id=1, source_target_pairs={{0,64},{64,0},{1,65},{65,1},{2,66},{66,2},{3,67},{67,3},{4,68},{68... | collective-permute-start | bytes 1572872 | tf_op jit(solution)/shard_map/ppermute | solution.py:24
  86.4 22.1 %collective-permute-start.21 = (bf16[3,512,128]{2,1,0:T(8,128)(2,1)S(1)}, bf16[3,512,128]{2,1,0:T(8,128)(2,1)S(1)}, u32[]{:S(2)}, u32[]{:S(2)}) collective-permute-start(bf16[3,512,128]{2,1,0:T(8,128)(2,1)S(1)} %pad_maximum_fusion), channel_id=1, source_target_pairs={{0,8},{8,0},{1,9},{9,1},{2,10},{10,2},{3,11},{11,3},{4,12},{12,4},... | collective-permute-start | bytes 1179656 | tf_op jit(solution)/shard_map/ppermute | solution.py:24
  108.5 1.1 copy-start.3
  115.6 26.7 %all-to-all-start.1 = ((f32[4,128,512]{2,1,0:T(8,128)}), f32[4,128,512]{2,1,0:T(8,128)S(1)}, u32[]{:S(2)}, u32[]{:S(2)}) async-start(f32[4,128,512]{2,1,0:T(8,128)} %shard_map.49), calls=%async_computation.1 | async-start | bytes 2097152 | tf_op jit(solution)/shard_map/all_to_all | solution.py:226
  121.2 6.6 %collective-permute-start.16 = (bf16[1,4,32,512]{3,2,1,0:T(8,128)(2,1)S(1)}, bf16[1,4,32,512]{3,2,1,0:T(8,128)(2,1)S(1)}, u32[]{:S(2)}, u32[]{:S(2)}) collective-permute-start(bf16[1,4,32,512]{3,2,1,0:T(8,128)(2,1)S(1)} %bitcast.28), channel_id=1, source_target_pairs={{0,8},{8,0},{1,9},{9,1},{2,10},{10,2},{3,11},{11,3},{4,12},{12,4},... | collective-permute-start | bytes 393224 | tf_op jit(solution)/shard_map/ppermute | solution.py:24
  127.8 7.9 %collective-permute-start.18 = (bf16[2,4,32,512]{3,2,1,0:T(8,128)(2,1)S(1)}, bf16[2,4,32,512]{3,2,1,0:T(8,128)(2,1)S(1)}, u32[]{:S(2)}, u32[]{:S(2)}) collective-permute-start(bf16[2,4,32,512]{3,2,1,0:T(8,128)(2,1)S(1)} %pad_maximum_fusion.1.refs_0_), channel_id=1, source_target_pairs={{0,7},{1,0},{2,1},{3,2},{4,3},{5,4},{6,5},{7,6},{8,15},{9,8},{10,9... | collective-permute-start | bytes 786440 | tf_op jit(solution)/shard_map/ppermute | solution.py:24
  131.4 7.6 %collective-permute-start.17 = (bf16[2,4,32,512]{3,2,1,0:T(8,128)(2,1)S(1)}, bf16[2,4,32,512]{3,2,1,0:T(8,128)(2,1)S(1)}, u32[]{:S(2)}, u32[]{:S(2)}) collective-permute-start(bf16[2,4,32,512]{3,2,1,0:T(8,128)(2,1)S(1)} %pad_maximum_fusion.1.refs_0_), channel_id=1, source_target_pairs={{0,1},{1,2},{2,3},{3,4},{4,5},{5,6},{6,7},{7,0},{8,9},{9,10},{10,1... | collective-permute-start | bytes 786440 | tf_op jit(solution)/shard_map/ppermute | solution.py:24
  139.1 7.6 %collective-permute-start.19 = (bf16[2,4,32,512]{3,2,1,0:T(8,128)(2,1)S(1)}, bf16[2,4,32,512]{3,2,1,0:T(8,128)(2,1)S(1)}, u32[]{:S(2)}, u32[]{:S(2)}) collective-permute-start(bf16[2,4,32,512]{3,2,1,0:T(8,128)(2,1)S(1)} %collective-permute-done.17.refs_1_), channel_id=1, source_target_pairs={{0,1},{1,2},{2,3},{3,4},{4,5},{5,6},{6,7},{7,0},{8,9},{9,10},{10,1... | collective-permute-start | bytes 786440 | tf_op jit(solution)/shard_map/ppermute | solution.py:24
  139.1 7.6 %collective-permute-start.20 = (bf16[2,4,32,512]{3,2,1,0:T(8,128)(2,1)S(1)}, bf16[2,4,32,512]{3,2,1,0:T(8,128)(2,1)S(1)}, u32[]{:S(2)}, u32[]{:S(2)}) collective-permute-start(bf16[2,4,32,512]{3,2,1,0:T(8,128)(2,1)S(1)} %collective-permute-done.18.refs_2_), channel_id=1, source_target_pairs={{0,7},{1,0},{2,1},{3,2},{4,3},{5,4},{6,5},{7,6},{8,15},{9,8},{10,9... | collective-permute-start | bytes 786440 | tf_op jit(solution)/shard_map/ppermute | solution.py:24
  147.8 16.2 %all-to-all-start.2 = ((bf16[8,128,512]{2,1,0:T(8,128)(2,1)}), bf16[8,128,512]{2,1,0:T(8,128)(2,1)S(1)}, u32[]{:S(2)}, u32[]{:S(2)}) async-start(bf16[8,128,512]{2,1,0:T(8,128)(2,1)} %broadcast_in_dim.8), calls=%async_computation.2 | async-start | bytes 2097152 | tf_op jit(solution)/shard_map/all_to_all | solution.py:234
  154.0 7.6 %collective-permute-start.24 = (bf16[2,4,32,512]{3,2,1,0:T(8,128)(2,1)S(1)}, bf16[2,4,32,512]{3,2,1,0:T(8,128)(2,1)S(1)}, u32[]{:S(2)}, u32[]{:S(2)}) collective-permute-start(bf16[2,4,32,512]{3,2,1,0:T(8,128)(2,1)S(1)} %collective-permute-done.19.refs_3_), channel_id=1, source_target_pairs={{0,1},{1,2},{2,3},{3,4},{4,5},{5,6},{6,7},{7,0},{8,9},{9,10},{10,1... | collective-permute-start | bytes 786440 | tf_op jit(solution)/shard_map/ppermute | solution.py:24
  154.0 7.6 %collective-permute-start.25 = (bf16[2,4,32,512]{3,2,1,0:T(8,128)(2,1)S(1)}, bf16[2,4,32,512]{3,2,1,0:T(8,128)(2,1)S(1)}, u32[]{:S(2)}, u32[]{:S(2)}) collective-permute-start(bf16[2,4,32,512]{3,2,1,0:T(8,128)(2,1)S(1)} %collective-permute-done.20.refs_4_), channel_id=1, source_target_pairs={{0,7},{1,0},{2,1},{3,2},{4,3},{5,4},{6,5},{7,6},{8,15},{9,8},{10,9... | collective-permute-start | bytes 786440 | tf_op jit(solution)/shard_map/ppermute | solution.py:24
  164.0 10.4 %collective-permute-start.28 = (bf16[2,4,128,512]{3,2,1,0:T(8,128)(2,1)S(1)}, bf16[2,4,128,512]{3,2,1,0:T(8,128)(2,1)S(1)}, u32[]{:S(2)}, u32[]{:S(2)}) collective-permute-start(bf16[2,4,128,512]{3,2,1,0:T(8,128)(2,1)S(1)} %bitcast.25), channel_id=1, source_target_pairs={{0,64},{64,0},{1,65},{65,1},{2,66},{66,2},{3,67},{67,3},{4,68},{68... | collective-permute-start | bytes 3145736 | tf_op jit(solution)/shard_map/ppermute | solution.py:24
  164.1 7.0 %collective-permute-start.27 = (bf16[1,4,32,512]{3,2,1,0:T(8,128)(2,1)S(1)}, bf16[1,4,32,512]{3,2,1,0:T(8,128)(2,1)S(1)}, u32[]{:S(2)}, u32[]{:S(2)}) collective-permute-start(bf16[1,4,32,512]{3,2,1,0:T(8,128)(2,1)S(1)} %slice.55), channel_id=1, source_target_pairs={{0,7},{1,0},{2,1},{3,2},{4,3},{5,4},{6,5},{7,6},{8,15},{9,8},{10,9... | collective-permute-start | bytes 393224 | tf_op jit(solution)/shard_map/ppermute | solution.py:24
  167.6 6.8 %collective-permute-start.26 = (bf16[1,4,32,512]{3,2,1,0:T(8,128)(2,1)S(1)}, bf16[1,4,32,512]{3,2,1,0:T(8,128)(2,1)S(1)}, u32[]{:S(2)}, u32[]{:S(2)}) collective-permute-start(bf16[1,4,32,512]{3,2,1,0:T(8,128)(2,1)S(1)} %slice.54), channel_id=1, source_target_pairs={{0,1},{1,2},{2,3},{3,4},{4,5},{5,6},{6,7},{7,0},{8,9},{9,10},{10,1... | collective-permute-start | bytes 393224 | tf_op jit(solution)/shard_map/ppermute | solution.py:24

commit v4 on v2

--- a/solution.py
+++ b/solution.py
@@ -74,22 +74,24 @@
     out_ref[0] = (both[:, :COLS] + both[:, COLS:]).T
 
 
-def rotate(at, blocks, places, own, other):
+def rotate(at, entries, own, other):
     slab = pl.BlockSpec((1, 1024, 256), lambda g: (g, 0, 0))
-    return pl.pallas_call(
-        functools.partial(rotate_kernel, places),
+    blocks = [
+        pl.BlockSpec((len(parts), *array.shape[1:]), lambda g, index=index: (index, 0, 0))
+        for array, index, parts in entries
+    ]
+    return pl.pallas_call(
+        functools.partial(rotate_kernel, [parts for _, _, parts in entries]),
         grid=(4,),
         out_shape=jax.ShapeDtypeStruct((4, COLS, TOK), F32),
-        in_specs=[pl.BlockSpec(memory_space=pltpu.SMEM)]
-        + [whole(b.shape) for b in blocks]
-        + [slab, slab],
+        in_specs=[pl.BlockSpec(memory_space=pltpu.SMEM)] + blocks + [slab, slab],
         out_specs=pl.BlockSpec((1, COLS, TOK), lambda g: (g, 0, 0)),
         scratch_shapes=[pltpu.VMEM((TOK, 2048), BF16)],
         compiler_params=PARAMS,
         cost_estimate=pl.CostEstimate(
             flops=4 * TOK * 2048 * 512, bytes_accessed=7 << 20, transcendentals=0
         ),
-    )(at, *blocks, own, other)
+    )(at, *[array for array, _, _ in entries], own, other)
 
 
 def product_kernel(scale, places, at_ref, *refs):
@@ -158,64 +160,37 @@
     return shift(up, "z", 1), shift(down, "z", -1)
 
 
-PAIR = ((0, 0), (0, 1))
-
-
-def both_sides(offset):
-    return ((offset, 0), (offset, 1))
-
-
 def body(activations, gradients, basis_in, basis_out):
     z, xh, y, xl, c = (lax.axis_index(a) for a in ("z", "xh", "y", "xl", "c"))
     at = jnp.stack([z, xh, y, xl, c]).astype(jnp.int32)
     core = c.astype(jnp.int32).reshape(1)
 
-    own_in = lax.all_to_all(split_basis(core, basis_in), "y", 0, 0)
-    acts_other = shift(activations, "xh", 1)
-    g_up1, g_down1 = ring_step(gradients, gradients)
-    acts_other, g_up1, g_down1, basis_out = sync(acts_other, g_up1, g_down1, basis_out)
-
-    a0 = jnp.concatenate([activations, acts_other])
-    g_near = jnp.concatenate([gradients, g_up1, g_down1])
-    a_up1, a_down1 = ring_step(a0, a0)
-    g_near_other = shift(g_near, "xh", 1)
-    g_up2, g_down2 = ring_step(g_up1, g_down1)
-    mine_out = split_basis(core, basis_out)
-    a_up1, a_down1, g_near_other, g_up2, g_down2, mine_out = sync(
-        a_up1, a_down1, g_near_other, g_up2, g_down2, mine_out
+    acts_other, mine_in, basis_out = sync(
+        shift(activations, "xh", 1), split_basis(core, basis_in), basis_out
     )
-
-    a_up2, a_down2 = ring_step(a_up1, a_down1)
-    g_two = jnp.concatenate([g_up2, g_down2])
-    g_two_other = shift(g_two, "xh", 1)
-    g_up3, g_down3 = ring_step(g_up2, g_down2)
-    a_up2, a_down2, g_two_other, g_up3, g_down3, mine_out, own_in = sync(
-        a_up2, a_down2, g_two_other, g_up3, g_down3, mine_out, own_in
+    own_in = lax.all_to_all(mine_in, "y", 0, 0)
+    base = jnp.concatenate([activations, acts_other, gradients])
+    up1, down1, mine_out = sync(*ring_step(base, base), split_basis(core, basis_out))
+    up2, down2, mine_out, own_in = sync(*ring_step(up1, down1), mine_out, own_in)
+    own_out = lax.all_to_all(mine_out, "y", 0, 0)
+    near = jnp.concatenate([a[2:] for a in (base, up1, down1, up2, down2)])
+    up3, down3, other_in, near_other = sync(
+        *ring_step(up2, down2), shift(own_in, "c", 1), shift(near, "xh", 1)
     )
-
-    own_out = lax.all_to_all(mine_out, "y", 0, 0)
-    a_up3, a_down3 = ring_step(a_up2, a_down2)
-    g_three = jnp.concatenate([g_up3, g_down3])
-    g_three_other = shift(g_three, "xh", 1)
-    g_up4 = shift(g_up3, "z", 1)
-    other_in = shift(own_in, "c", 1)
-    a_up3, a_down3, g_three_other, g_up4, other_in = sync(
-        a_up3, a_down3, g_three_other, g_up4, other_in
-    )
-
-    a_up4, a_down4 = ring_step(a_up3[:1], a_down3[1:])
-    g_four_other = shift(g_up4, "xh", 1)
-    act_blocks = [a0, a_up1, a_down1, a_up2, a_down2, a_up3, a_down3, a_up4, a_down4]
-    act_places = [both_sides(o) for o in (0, -1, 1, -2, 2, -3, 3)] + [((-4, 0),), ((4, 1),)]
-    acts_part = rotate(at, act_blocks, act_places, own_in, other_in)
+    three = jnp.concatenate([up3[2:], down3[2:]])
+    up4, three_other = sync(shift(up3, "z", 1), shift(three, "xh", 1))
+    ring = [(base, 0), (up1, -1), (down1, 1), (up2, -2), (down2, 2), (up3, -3), (down3, 3), (up4, -4)]
+
+    acts_entries = [(a, 0, ((o, 0), (o, 1))) for a, o in ring]
+    acts_part = rotate(at, acts_entries, own_in, other_in)
     acts_in = lax.all_to_all(acts_part.reshape(16, 32, TOK), ("xl", "c", "y"), 0, 0)
 
-    grad_blocks = [g_near, g_near_other, g_two, g_two_other, g_three, g_three_other, g_up4, g_four_other]
-    grad_places = []
-    for offsets in ((0, -1, 1), (-2, 2), (-3, 3), (-4,)):
-        grad_places += [tuple((o, 0) for o in offsets), tuple((o, 1) for o in offsets)]
+    four_other = shift(up4[2:], "xh", 1)
     other_out = shift(after(own_out, acts_part), "c", 1)
-    grads_part = rotate(at, grad_blocks, grad_places, own_out, other_out)
+    grads_entries = [(a, 2, ((o, 0),)) for a, o in ring]
+    grads_entries += [(near_other, 0, tuple((o, 1) for o in (0, -1, 1, -2, 2)))]
+    grads_entries += [(three_other, 0, ((-3, 1), (3, 1))), (four_other, 0, ((4, 1),))]
+    grads_part = rotate(at, grads_entries, own_out, other_out)
     grads_in = lax.all_to_all(grads_part, "y", 0, 0)
 
     acts = jnp.sum(acts_in.reshape(4, 4, 32, TOK), axis=1).astype(BF16)[None]
@@ -226,12 +201,13 @@
     copies = jnp.broadcast_to(grads, (8, COLS, TOK))
     rot_own = lax.all_to_all(copies, ("xl", "y"), 0, 0).reshape(2, 4, COLS, TOK)
     r_up3, r_down3, rot_own = sync(*ring_step(r_up2, r_down2), rot_own)
-    r_up4, r_down4 = ring_step(r_up3[:1], r_down3[1:])
+    r_up4 = shift(r_up3, "z", 1)
     rot_grads = [rot_own, shift(rot_own, "c", 1)]
-    rot_acts = [r0, r_up1, r_down1, r_up2, r_down2, r_up3, r_down3, r_up4, r_down4]
+    rot_acts = [r0, r_up1, r_down1, r_up2, r_down2, r_up3, r_down3, r_up4]
+    rot_places = [((o, 0), (o, 1)) for _, o in ring]
 
     scale = 1.0 / (TOK * 4)
-    part = products(at, rot_acts, act_places, rot_grads, scale)
+    part = products(at, rot_acts, rot_places, rot_grads, scale)
     return weave(lax.all_to_all(part, "y", 0, 0))
 
 

time: 195 us -> 198 us (1.015)
  waiting for transfers between devices: 68.3 us -> 86.4 us
  starting transfers between devices: 72.4 us -> 57.1 us
    ppermute x32 -> x22, waiting for transfers between devices: 65.7 us -> 83.9 us  [shift(): return lax.ppermute(x, axis, [(i, (i + by) % n) for i in range(n)])]
    ppermute x32 -> x22, starting transfers between devices: 47 us -> 32.1 us  [shift(): return lax.ppermute(x, axis, [(i, (i + by) % n) for i in range(n)])]
    unnamed x39 -> x14, local copies, waits for them, and re-layouts: 5.78 us -> 4.71 us
  transfers between devices with their start and end apart: 37 -> 27, of which waited for: 15 -> 16; matrix products, arithmetic and copies ran while one was open for 2% -> 3% of each run, Pallas kernels for 8% -> 10%
where the time goes in v4:
time: 198 us; the launch traced here: 197 us
  waiting for transfers between devices  86.4 us (44%)
  starting transfers between devices  57.1 us (29%)
  Pallas kernels  26.4 us (13%)
  blocking collectives  17.9 us (9%)
  local copies, waits for them, and re-layouts  6.55 us (3%)
  other arithmetic  2.18 us (1%)
    ppermute x22, waiting for transfers between devices, shift(): return lax.ppermute(x, axis, [(i, (i + by) % n) for i in range(n)])  83.9 us
    ppermute x22, starting transfers between devices, shift(): return lax.ppermute(x, axis, [(i, (i + by) % n) for i in range(n)])  32.1 us
    all_to_all x1, blocking collectives, body(): return weave(lax.all_to_all(part, 'y', 0, 0))  17.9 us
    pallas_call x2, Pallas kernels, rotate(): pl.pallas_call(functools.partial(rotate_kernel, [parts for _, _, parts in...  12.6 us
    pallas_call x2, Pallas kernels, split_basis(): pl.pallas_call(split_kernel, grid_spec=pltpu.PrefetchScalarGridSpec(num_s...  7.9 us
    all_to_all x1, starting transfers between devices, body(): rot_own = lax.all_to_all(copies, ('xl', 'y'), 0, 0).reshape(2, 4, COLS, TOK)  6.2 us
    all_to_all x1, starting transfers between devices, body(): lax.all_to_all(acts_part.reshape(16, 32, TOK), ('xl', 'c', 'y'), 0, 0)  5.74 us
    unnamed x14, local copies, waits for them, and re-layouts  4.71 us
  transfers between devices with their start and end apart: 27, of which 16 were waited for; matrix products, arithmetic and copies ran while one was open for 3% of the time, Pallas kernels for 10%

profile of v4, /device:TPU:2, one launch (start us, length us, event | category | flops | bytes accessed | tf_op | source)
XLA Modules:
  0.0 196.6 jit_solution(5410454329464814863)
XLA Ops:
  0.0 2.1 %collective-permute-start = (bf16[1,512,128]{2,1,0:T(8,128)(2,1)}, bf16[1,512,128]{2,1,0:T(8,128)(2,1)S(1)}, u32[]{:S(2)}, u32[]{:S(2)}) collective-permute-start(bf16[1,512,128]{2,1,0:T(8,128)(2,1)} %param.4), channel_id=1, source_target_pairs={{0,8},{8,0},{1,9},{9,1},{2,10},{10,2},{3,11},{11,3},{4,12},{12,4},... | collective-permute-start | bytes 393224 | tf_op jit(solution)/shard_map/ppermute | solution.py:24
  2.1 4.0 %shard_map.46 = bf16[4,1024,256]{2,1,0:T(8,128)(2,1)} custom-call(s32[1]{0:T(128)} %bitcast.4.core_ref, f32[8192,128]{1,0:T(8,128)} %in_ref.1), custom_call_target="tpu_custom_call" | custom-call | flops 1048576 | bytes 4194304 | tf_op jit(solution)/shard_map/pallas_call | solution.py:43
  6.1 0.9 collective-permute-done
  7.0 4.5 %all-to-all-start = ((bf16[4,1024,256]{2,1,0:T(8,128)(2,1)}), bf16[4,1024,256]{2,1,0:T(8,128)(2,1)}, u32[]{:S(2)}, u32[]{:S(2)}) async-start(bf16[4,1024,256]{2,1,0:T(8,128)(2,1)} %shard_map.46), calls=%async_computation | async-start | bytes 4194304 | tf_op jit(solution)/shard_map/all_to_all | solution.py:171
  11.5 0.7 constant_dynamic-update-slice_fusion.3
  12.2 5.9 %collective-permute-start.2 = (bf16[3,512,128]{2,1,0:T(8,128)(2,1)S(1)}, bf16[3,512,128]{2,1,0:T(8,128)(2,1)S(1)}, u32[]{:S(2)}, u32[]{:S(2)}) collective-permute-start(bf16[3,512,128]{2,1,0:T(8,128)(2,1)S(1)} %get-tuple-element.56.refs_0_), channel_id=1, source_target_pairs={{0,7},{1,0},{2,1},{3,2},{4,3},{5,4},{6,5},{7,6},{8,15},{9,8},{10,9... | collective-permute-start | bytes 1179656 | tf_op jit(solution)/shard_map/ppermute | solution.py:24
  18.0 3.9 %shard_map.47 = bf16[4,1024,256]{2,1,0:T(8,128)(2,1)} custom-call(s32[1]{0:T(128)} %bitcast.4.core_ref, f32[8192,128]{1,0:T(8,128)} %in_ref.2), custom_call_target="tpu_custom_call" | custom-call | flops 1048576 | bytes 4194304 | tf_op jit(solution)/shard_map/pallas_call | solution.py:43
  22.0 3.5 %collective-permute-done.2.refs_2_ = bf16[3,512,128]{2,1,0:T(8,128)(2,1)S(1)} collective-permute-done((bf16[3,512,128]{2,1,0:T(8,128)(2,1)S(1)}, bf16[3,512,128]{2,1,0:T(8,128)(2,1)S(1)}, u32[]{:S(2)}, u32[]{:S(2)}) %collective-permute-start.2) | collective-permute-done | bytes 393248 | tf_op jit(solution)/shard_map/ppermute | solution.py:24
  25.5 3.4 %collective-permute-done.1.refs_1_ = bf16[3,512,128]{2,1,0:T(8,128)(2,1)S(1)} collective-permute-done((bf16[3,512,128]{2,1,0:T(8,128)(2,1)S(1)}, bf16[3,512,128]{2,1,0:T(8,128)(2,1)S(1)}, u32[]{:S(2)}, u32[]{:S(2)}) %collective-permute-start.1) | collective-permute-done | bytes 393248 | tf_op jit(solution)/shard_map/ppermute | solution.py:24
  28.9 0.0 collective-permute-start.3
  28.9 3.2 %collective-permute-start.4 = (bf16[3,512,128]{2,1,0:T(8,128)(2,1)S(1)}, bf16[3,512,128]{2,1,0:T(8,128)(2,1)S(1)}, u32[]{:S(2)}, u32[]{:S(2)}) collective-permute-start(bf16[3,512,128]{2,1,0:T(8,128)(2,1)S(1)} %collective-permute-done.2.refs_2_), channel_id=1, source_target_pairs={{0,7},{1,0},{2,1},{3,2},{4,3},{5,4},{6,5},{7,6},{8,15},{9,8},{10,9... | collective-permute-start | bytes 1179656 | tf_op jit(solution)/shard_map/ppermute | solution.py:24
  32.2 6.9 %collective-permute-done.3.refs_3_ = bf16[3,512,128]{2,1,0:T(8,128)(2,1)S(1)} collective-permute-done((bf16[3,512,128]{2,1,0:T(8,128)(2,1)S(1)}, bf16[3,512,128]{2,1,0:T(8,128)(2,1)S(1)}, u32[]{:S(2)}, u32[]{:S(2)}) %collective-permute-start.3) | collective-permute-done | bytes 393248 | tf_op jit(solution)/shard_map/ppermute | solution.py:24
  39.0 0.0 collective-permute-done.4.refs_4_
  39.0 0.0 all-to-all-done.refs_8_
  39.1 0.7 slice_dynamic-update-slice_fusion.3
  39.7 0.7 slice_dynamic-update-slice_fusion.2
  40.4 4.5 %all-to-all-start.2 = ((bf16[4,1024,256]{2,1,0:T(8,128)(2,1)}), bf16[4,1024,256]{2,1,0:T(8,128)(2,1)}, u32[]{:S(2)}, u32[]{:S(2)}) async-start(bf16[4,1024,256]{2,1,0:T(8,128)(2,1)} %shard_map.47), calls=%async_computation.2 | async-start | bytes 4194304 | tf_op jit(solution)/shard_map/all_to_all | solution.py:175
  44.9 0.7 slice_dynamic-update-slice_fusion.1
  45.5 0.7 slice_dynamic-update-slice_fusion
  46.2 2.1 %collective-permute-start.8 = (bf16[5,512,128]{2,1,0:T(8,128)(2,1)}, bf16[5,512,128]{2,1,0:T(8,128)(2,1)S(1)}, u32[]{:S(2)}, u32[]{:S(2)}) collective-permute-start(bf16[5,512,128]{2,1,0:T(8,128)(2,1)} %slice_dynamic-update-slice_fusion), channel_id=1, source_target_pairs={{0,8},{8,0},{1,9},{9,1},{2,10},{10,2},{3,11},{11,3},{4,12},{12,4},... | collective-permute-start | bytes 1966088 | tf_op jit(solution)/shard_map/ppermute | solution.py:24
  48.3 0.1 collective-permute-start.5
  48.4 3.9 %collective-permute-start.6 = (bf16[3,512,128]{2,1,0:T(8,128)(2,1)S(1)}, bf16[3,512,128]{2,1,0:T(8,128)(2,1)S(1)}, u32[]{:S(2)}, u32[]{:S(2)}) collective-permute-start(bf16[3,512,128]{2,1,0:T(8,128)(2,1)S(1)} %collective-permute-done.4.refs_4_), channel_id=1, source_target_pairs={{0,7},{1,0},{2,1},{3,2},{4,3},{5,4},{6,5},{7,6},{8,15},{9,8},{10,9... | collective-permute-start | bytes 1179656 | tf_op jit(solution)/shard_map/ppermute | solution.py:24
  52.3 9.5 %collective-permute-done.5.refs_5_ = bf16[3,512,128]{2,1,0:T(8,128)(2,1)S(1)} collective-permute-done((bf16[3,512,128]{2,1,0:T(8,128)(2,1)S(1)}, bf16[3,512,128]{2,1,0:T(8,128)(2,1)S(1)}, u32[]{:S(2)}, u32[]{:S(2)}) %collective-permute-start.5) | collective-permute-done | bytes 393248 | tf_op jit(solution)/shard_map/ppermute | solution.py:24
  61.8 0.0 collective-permute-done.6.refs_6_
  61.8 3.2 %collective-permute-done.8.refs_8_ = bf16[5,512,128]{2,1,0:T(8,128)(2,1)S(1)} collective-permute-done((bf16[5,512,128]{2,1,0:T(8,128)(2,1)}, bf16[5,512,128]{2,1,0:T(8,128)(2,1)S(1)}, u32[]{:S(2)}, u32[]{:S(2)}) %collective-permute-start.8) | collective-permute-done | bytes 655392 | tf_op jit(solution)/shard_map/ppermute | solution.py:24
  65.0 0.9 copy-done
  66.0 0.0 collective-permute-done.7.refs_9_
  66.0 0.1 collective-permute-start.9
  66.1 0.7 pad_maximum_fusion
  66.8 2.1 %collective-permute-start.10 = (bf16[2,512,128]{2,1,0:T(8,128)(2,1)}, bf16[2,512,128]{2,1,0:T(8,128)(2,1)S(1)}, u32[]{:S(2)}, u32[]{:S(2)}) collective-permute-start(bf16[2,512,128]{2,1,0:T(8,128)(2,1)} %pad_maximum_fusion), channel_id=1, source_target_pairs={{0,8},{8,0},{1,9},{9,1},{2,10},{10,2},{3,11},{11,3},{4,12},{12,4},... | collective-permute-start | bytes 786440 | tf_op jit(solution)/shard_map/ppermute | solution.py:24
  68.9 0.1 stack.23.at_ref
  69.0 7.4 %collective-permute-done.10.refs_9_ = bf16[2,512,128]{2,1,0:T(8,128)(2,1)S(1)} collective-permute-done((bf16[2,512,128]{2,1,0:T(8,128)(2,1)}, bf16[2,512,128]{2,1,0:T(8,128)(2,1)S(1)}, u32[]{:S(2)}, u32[]{:S(2)}) %collective-permute-start.10) | collective-permute-done | bytes 262176 | tf_op jit(solution)/shard_map/ppermute | solution.py:24
  76.5 2.6 %collective-permute-done.9.refs_7_ = bf16[3,512,128]{2,1,0:T(8,128)(2,1)S(1)} collective-permute-done((bf16[3,512,128]{2,1,0:T(8,128)(2,1)S(1)}, bf16[3,512,128]{2,1,0:T(8,128)(2,1)S(1)}, u32[]{:S(2)}, u32[]{:S(2)}) %collective-permute-start.9) | collective-permute-done | bytes 393248 | tf_op jit(solution)/shard_map/ppermute | solution.py:24
  79.1 6.3 %shard_map.48 = f32[4,128,512]{2,1,0:T(8,128)} custom-call(s32[5]{0:T(128)S(1)} %stack.23.at_ref, bf16[3,512,128]{2,1,0:T(8,128)(2,1)S(1)} %get-tuple-element.56.refs_0_, bf16[3,512,128]{2,1,0:T(8,128)(2,1)S(1)} %collective-permute-done.1.refs_1_, bf16[3,512,128]{2,1,0:T(8,128)(2,1)S(1)} %collective-permute-done.2.refs_2_, ...), custom_call_target="tpu_custom_call" | custom-call | flops 2147483648 | bytes 7340032 | tf_op jit(solution)/shard_map/pallas_call | solution.py:83
  85.4 5.7 %all-to-all-start.1 = ((f32[16,32,512]{2,1,0:T(8,128)}), f32[16,32,512]{2,1,0:T(8,128)}, u32[]{:S(2)}, u32[]{:S(2)}) async-start(f32[16,32,512]{2,1,0:T(8,128)} %bitcast.5), calls=%async_computation.1 | async-start | bytes 2097152 | tf_op jit(solution)/shard_map/all_to_all | solution.py:186
  91.2 2.1 %collective-permute-start.16 = (bf16[1,512,128]{2,1,0:T(8,128)(2,1)S(1)}, bf16[1,512,128]{2,1,0:T(8,128)(2,1)S(1)}, u32[]{:S(2)}, u32[]{:S(2)}) collective-permute-start(bf16[1,512,128]{2,1,0:T(8,128)(2,1)S(1)} %slice.27), channel_id=1, source_target_pairs={{0,8},{8,0},{1,9},{9,1},{2,10},{10,2},{3,11},{11,3},{4,12},{12,4},... | collective-permute-start | bytes 393224 | tf_op jit(solution)/shard_map/ppermute | solution.py:24
  93.3 15.2 %collective-permute-done.16.refs_10_ = bf16[1,512,128]{2,1,0:T(8,128)(2,1)S(1)} collective-permute-done((bf16[1,512,128]{2,1,0:T(8,128)(2,1)S(1)}, bf16[1,512,128]{2,1,0:T(8,128)(2,1)S(1)}, u32[]{:S(2)}, u32[]{:S(2)}) %collective-permute-start.16) | collective-permute-done | bytes 131104 | tf_op jit(solution)/shard_map/ppermute | solution.py:24
  108.5 0.0 collective-permute-done.17.refs_12_
  108.5 1.1 copy-done.1
  109.6 6.3 %shard_map.49 = f32[4,128,512]{2,1,0:T(8,128)} custom-call(s32[5]{0:T(128)S(1)} %stack.23.at_ref, bf16[3,512,128]{2,1,0:T(8,128)(2,1)S(1)} %get-tuple-element.56.refs_0_, bf16[3,512,128]{2,1,0:T(8,128)(2,1)S(1)} %collective-permute-done.1.refs_1_, bf16[3,512,128]{2,1,0:T(8,128)(2,1)S(1)} %collective-permute-done.2.refs_2_, ...), custom_call_target="tpu_custom_call" | custom-call | flops 2147483648 | bytes 7340032 | tf_op jit(solution)/shard_map/pallas_call | solution.py:83
  115.9 0.0 all-to-all-done.1
  115.9 4.2 %all-to-all-start.3 = ((f32[4,128,512]{2,1,0:T(8,128)}), f32[4,128,512]{2,1,0:T(8,128)S(1)}, u32[]{:S(2)}, u32[]{:S(2)}) async-start(f32[4,128,512]{2,1,0:T(8,128)} %shard_map.49), calls=%async_computation.3 | async-start | bytes 2097152 | tf_op jit(solution)/shard_map/all_to_all | solution.py:194
  120.1 1.3 bitcast_reduce_fusion
  121.4 1.8 collective-permute-start.11
  123.2 5.0 %collective-permute-done.11 = bf16[1,4,32,512]{3,2,1,0:T(8,128)(2,1)S(1)} collective-permute-done((bf16[1,4,32,512]{3,2,1,0:T(8,128)(2,1)S(1)}, bf16[1,4,32,512]{3,2,1,0:T(8,128)(2,1)S(1)}, u32[]{:S(2)}, u32[]{:S(2)}) %collective-permute-start.11) | collective-permute-done | bytes 131104 | tf_op jit(solution)/shard_map/ppermute | solution.py:24
  128.2 1.8 collective-permute-start.13
  130.0 0.3 collective-permute-start.12
  130.3 4.7 %collective-permute-done.13.refs_2_ = bf16[2,4,32,512]{3,2,1,0:T(8,128)(2,1)S(1)} collective-permute-done((bf16[2,4,32,512]{3,2,1,0:T(8,128)(2,1)S(1)}, bf16[2,4,32,512]{3,2,1,0:T(8,128)(2,1)S(1)}, u32[]{:S(2)}, u32[]{:S(2)}) %collective-permute-start.13) | collective-permute-done | bytes 262176 | tf_op jit(solution)/shard_map/ppermute | solution.py:24
  135.0 2.7 %collective-permute-done.12.refs_1_ = bf16[2,4,32,512]{3,2,1,0:T(8,128)(2,1)S(1)} collective-permute-done((bf16[2,4,32,512]{3,2,1,0:T(8,128)(2,1)S(1)}, bf16[2,4,32,512]{3,2,1,0:T(8,128)(2,1)S(1)}, u32[]{:S(2)}, u32[]{:S(2)}) %collective-permute-start.12) | collective-permute-done | bytes 262176 | tf_op jit(solution)/shard_map/ppermute | solution.py:24
  137.7 0.0 collective-permute-start.14
  137.7 3.2 %collective-permute-start.15 = (bf16[2,4,32,512]{3,2,1,0:T(8,128)(2,1)S(1)}, bf16[2,4,32,512]{3,2,1,0:T(8,128)(2,1)S(1)}, u32[]{:S(2)}, u32[]{:S(2)}) collective-permute-start(bf16[2,4,32,512]{3,2,1,0:T(8,128)(2,1)S(1)} %collective-permute-done.13.refs_2_), channel_id=1, source_target_pairs={{0,7},{1,0},{2,1},{3,2},{4,3},{5,4},{6,5},{7,6},{8,15},{9,8},{10,9... | collective-permute-start | bytes 786440 | tf_op jit(solution)/shard_map/ppermute | solution.py:24
  140.9 4.3 %collective-permute-done.14.refs_3_ = bf16[2,4,32,512]{3,2,1,0:T(8,128)(2,1)S(1)} collective-permute-done((bf16[2,4,32,512]{3,2,1,0:T(8,128)(2,1)S(1)}, bf16[2,4,32,512]{3,2,1,0:T(8,128)(2,1)S(1)}, u32[]{:S(2)}, u32[]{:S(2)}) %collective-permute-start.14) | collective-permute-done | bytes 262176 | tf_op jit(solution)/shard_map/ppermute | solution.py:24
  145.2 0.0 collective-permute-done.15.refs_4_
  145.2 0.0 all-to-all-done.3
  145.3 0.1 reduce_sum.19
  145.3 1.1 broadcast_in_dim.4
  146.4 6.2 %all-to-all-start.4 = ((bf16[8,128,512]{2,1,0:T(8,128)(2,1)}), bf16[8,128,512]{2,1,0:T(8,128)(2,1)S(1)}, u32[]{:S(2)}, u32[]{:S(2)}) async-start(bf16[8,128,512]{2,1,0:T(8,128)(2,1)} %broadcast_in_dim.4), calls=%async_computation.4 | async-start | bytes 2097152 | tf_op jit(solution)/shard_map/all_to_all | solution.py:202
  152.6 3.2 %collective-permute-start.19 = (bf16[2,4,32,512]{3,2,1,0:T(8,128)(2,1)S(1)}, bf16[2,4,32,512]{3,2,1,0:T(8,128)(2,1)S(1)}, u32[]{:S(2)}, u32[]{:S(2)}) collective-permute-start(bf16[2,4,32,512]{3,2,1,0:T(8,128)(2,1)S(1)} %collective-permute-done.15.refs_4_), channel_id=1, source_target_pairs={{0,7},{1,0},{2,1},{3,2},{4,3},{5,4},{6,5},{7,6},{8,15},{9,8},{10,9... | collective-permute-start | bytes 786440 | tf_op jit(solution)/shard_map/ppermute | solution.py:24
  155.8 4.3 %collective-permute-done.18.refs_5_ = bf16[2,4,32,512]{3,2,1,0:T(8,128)(2,1)S(1)} collective-permute-done((bf16[2,4,32,512]{3,2,1,0:T(8,128)(2,1)S(1)}, bf16[2,4,32,512]{3,2,1,0:T(8,128)(2,1)S(1)}, u32[]{:S(2)}, u32[]{:S(2)}) %collective-permute-start.18) | collective-permute-done | bytes 262176 | tf_op jit(solution)/shard_map/ppermute | solution.py:24
  160.2 2.5 %all-to-all-done.4 = bf16[8,128,512]{2,1,0:T(8,128)(2,1)S(1)} async-done(((bf16[8,128,512]{2,1,0:T(8,128)(2,1)}), bf16[8,128,512]{2,1,0:T(8,128)(2,1)S(1)}, u32[]{:S(2)}, u32[]{:S(2)}) %all-to-all-start.4) | async-done | bytes 1048608 | tf_op jit(solution)/shard_map/all_to_all | solution.py:202
  162.7 10.2 %collective-permute-done.20.refs_7_ = bf16[2,4,32,512]{3,2,1,0:T(8,128)(2,1)S(1)} collective-permute-done((bf16[2,4,32,512]{3,2,1,0:T(8,128)(2,1)S(1)}, bf16[2,4,32,512]{3,2,1,0:T(8,128)(2,1)S(1)}, u32[]{:S(2)}, u32[]{:S(2)}) %collective-permute-start.20) | collective-permute-done | bytes 262176 | tf_op jit(solution)/shard_map/ppermute | solution.py:24
  172.9 3.5 %shard_map.50 = f32[4,128,512]{2,1,0:T(8,128)S(1)} custom-call(s32[5]{0:T(128)S(1)} %stack.23.at_ref, bf16[2,4,32,512]{3,2,1,0:T(8,128)(2,1)S(1)} %pad_maximum_fusion.1.refs_0_, bf16[2,4,32,512]{3,2,1,0:T(8,128)(2,1)S(1)} %collective-permute-done.12.refs_1_, bf16[2,4,32,512]{3,2,1,0:T(8,128)(2,1)S(1)} %collective-permute-done.13.refs_2_, ...), custom_call_target="tpu_custom_call" | custom-call | flops 1073741824 | bytes 5242880 | tf_op jit(solution)/shard_map/pallas_call | solution.py:122
  176.4 17.9 %all_to_all.30.in_ref = f32[4,128,512]{2,1,0:T(8,128)S(1)} all-to-all(f32[4,128,512]{2,1,0:T(8,128)S(1)} %shard_map.50), channel_id=1, replica_groups=mesh['xl'=2,'c'=2,'y'=4,'xh'=2,'z'=8] {'y'}, dimensions={0} | all-to-all | bytes 2097152 | tf_op jit(solution)/shard_map/all_to_all | solution.py:211
  194.3 2.4 %shard_map.51 = f32[128,2048]{1,0:T(8,128)} custom-call(f32[4,128,512]{2,1,0:T(8,128)S(1)} %all_to_all.30.in_ref), custom_call_target="tpu_custom_call" | custom-call | tf_op jit(solution)/shard_map/pallas_call | solution.py:145
  (21 shorter events, 0.1 us)
Async XLA Ops:
  0.0 7.0 %collective-permute-start = (bf16[1,512,128]{2,1,0:T(8,128)(2,1)}, bf16[1,512,128]{2,1,0:T(8,128)(2,1)S(1)}, u32[]{:S(2)}, u32[]{:S(2)}) collective-permute-start(bf16[1,512,128]{2,1,0:T(8,128)(2,1)} %param.4), channel_id=1, source_target_pairs={{0,8},{8,0},{1,9},{9,1},{2,10},{10,2},{3,11},{11,3},{4,12},{12,4},... | collective-permute-start | bytes 393224 | tf_op jit(solution)/shard_map/ppermute | solution.py:24
  6.1 5.4 %copy-start.3 = (bf16[1,512,128]{2,1,0:T(8,128)(2,1)S(1)}, bf16[1,512,128]{2,1,0:T(8,128)(2,1)}, u32[]{:S(2)}) copy-start(bf16[1,512,128]{2,1,0:T(8,128)(2,1)} %param.4) | copy-start | bytes 393220
  6.1 5.4 %copy-start.2 = (bf16[1,512,128]{2,1,0:T(8,128)(2,1)S(1)}, bf16[1,512,128]{2,1,0:T(8,128)(2,1)}, u32[]{:S(2)}) copy-start(bf16[1,512,128]{2,1,0:T(8,128)(2,1)} %param.5) | copy-start | bytes 393220
  7.0 32.1 %all-to-all-start = ((bf16[4,1024,256]{2,1,0:T(8,128)(2,1)}), bf16[4,1024,256]{2,1,0:T(8,128)(2,1)}, u32[]{:S(2)}, u32[]{:S(2)}) async-start(bf16[4,1024,256]{2,1,0:T(8,128)(2,1)} %shard_map.46), calls=%async_computation | async-start | bytes 4194304 | tf_op jit(solution)/shard_map/all_to_all | solution.py:171
  12.2 13.4 %collective-permute-start.2 = (bf16[3,512,128]{2,1,0:T(8,128)(2,1)S(1)}, bf16[3,512,128]{2,1,0:T(8,128)(2,1)S(1)}, u32[]{:S(2)}, u32[]{:S(2)}) collective-permute-start(bf16[3,512,128]{2,1,0:T(8,128)(2,1)S(1)} %get-tuple-element.56.refs_0_), channel_id=1, source_target_pairs={{0,7},{1,0},{2,1},{3,2},{4,3},{5,4},{6,5},{7,6},{8,15},{9,8},{10,9... | collective-permute-start | bytes 1179656 | tf_op jit(solution)/shard_map/ppermute | solution.py:24
  18.0 10.9 %collective-permute-start.1 = (bf16[3,512,128]{2,1,0:T(8,128)(2,1)S(1)}, bf16[3,512,128]{2,1,0:T(8,128)(2,1)S(1)}, u32[]{:S(2)}, u32[]{:S(2)}) collective-permute-start(bf16[3,512,128]{2,1,0:T(8,128)(2,1)S(1)} %get-tuple-element.56.refs_0_), channel_id=1, source_target_pairs={{0,1},{1,2},{2,3},{3,4},{4,5},{5,6},{6,7},{7,0},{8,9},{9,10},{10,1... | collective-permute-start | bytes 1179656 | tf_op jit(solution)/shard_map/ppermute | solution.py:24
  28.9 10.1 %collective-permute-start.3 = (bf16[3,512,128]{2,1,0:T(8,128)(2,1)S(1)}, bf16[3,512,128]{2,1,0:T(8,128)(2,1)S(1)}, u32[]{:S(2)}, u32[]{:S(2)}) collective-permute-start(bf16[3,512,128]{2,1,0:T(8,128)(2,1)S(1)} %collective-permute-done.1.refs_1_), channel_id=1, source_target_pairs={{0,1},{1,2},{2,3},{3,4},{4,5},{5,6},{6,7},{7,0},{8,9},{9,10},{10,1... | collective-permute-start | bytes 1179656 | tf_op jit(solution)/shard_map/ppermute | solution.py:24
  28.9 10.1 %collective-permute-start.4 = (bf16[3,512,128]{2,1,0:T(8,128)(2,1)S(1)}, bf16[3,512,128]{2,1,0:T(8,128)(2,1)S(1)}, u32[]{:S(2)}, u32[]{:S(2)}) collective-permute-start(bf16[3,512,128]{2,1,0:T(8,128)(2,1)S(1)} %collective-permute-done.2.refs_2_), channel_id=1, source_target_pairs={{0,7},{1,0},{2,1},{3,2},{4,3},{5,4},{6,5},{7,6},{8,15},{9,8},{10,9... | collective-permute-start | bytes 1179656 | tf_op jit(solution)/shard_map/ppermute | solution.py:24
  39.1 26.9 %collective-permute-start.7 = (bf16[4,1024,256]{2,1,0:T(8,128)(2,1)}, bf16[4,1024,256]{2,1,0:T(8,128)(2,1)}, u32[]{:S(2)}, u32[]{:S(2)}) collective-permute-start(bf16[4,1024,256]{2,1,0:T(8,128)(2,1)} %all-to-all-done.refs_8_), channel_id=1, source_target_pairs={{0,64},{64,0},{1,65},{65,1},{2,66},{66,2},{3,67},{67,3},{4,68},{68... | collective-permute-start | bytes 6291464 | tf_op jit(solution)/shard_map/ppermute | solution.py:24
  40.4 45.0 %all-to-all-start.2 = ((bf16[4,1024,256]{2,1,0:T(8,128)(2,1)}), bf16[4,1024,256]{2,1,0:T(8,128)(2,1)}, u32[]{:S(2)}, u32[]{:S(2)}) async-start(bf16[4,1024,256]{2,1,0:T(8,128)(2,1)} %shard_map.47), calls=%async_computation.2 | async-start | bytes 4194304 | tf_op jit(solution)/shard_map/all_to_all | solution.py:175
  46.2 18.9 %collective-permute-start.8 = (bf16[5,512,128]{2,1,0:T(8,128)(2,1)}, bf16[5,512,128]{2,1,0:T(8,128)(2,1)S(1)}, u32[]{:S(2)}, u32[]{:S(2)}) collective-permute-start(bf16[5,512,128]{2,1,0:T(8,128)(2,1)} %slice_dynamic-update-slice_fusion), channel_id=1, source_target_pairs={{0,8},{8,0},{1,9},{9,1},{2,10},{10,2},{3,11},{11,3},{4,12},{12,4},... | collective-permute-start | bytes 1966088 | tf_op jit(solution)/shard_map/ppermute | solution.py:24
  48.3 13.5 %collective-permute-start.5 = (bf16[3,512,128]{2,1,0:T(8,128)(2,1)S(1)}, bf16[3,512,128]{2,1,0:T(8,128)(2,1)S(1)}, u32[]{:S(2)}, u32[]{:S(2)}) collective-permute-start(bf16[3,512,128]{2,1,0:T(8,128)(2,1)S(1)} %collective-permute-done.3.refs_3_), channel_id=1, source_target_pairs={{0,1},{1,2},{2,3},{3,4},{4,5},{5,6},{6,7},{7,0},{8,9},{9,10},{10,1... | collective-permute-start | bytes 1179656 | tf_op jit(solution)/shard_map/ppermute | solution.py:24
  48.4 13.4 %collective-permute-start.6 = (bf16[3,512,128]{2,1,0:T(8,128)(2,1)S(1)}, bf16[3,512,128]{2,1,0:T(8,128)(2,1)S(1)}, u32[]{:S(2)}, u32[]{:S(2)}) collective-permute-start(bf16[3,512,128]{2,1,0:T(8,128)(2,1)S(1)} %collective-permute-done.4.refs_4_), channel_id=1, source_target_pairs={{0,7},{1,0},{2,1},{3,2},{4,3},{5,4},{6,5},{7,6},{8,15},{9,8},{10,9... | collective-permute-start | bytes 1179656 | tf_op jit(solution)/shard_map/ppermute | solution.py:24
  65.0 0.9 copy-start
  66.0 13.1 %collective-permute-start.9 = (bf16[3,512,128]{2,1,0:T(8,128)(2,1)S(1)}, bf16[3,512,128]{2,1,0:T(8,128)(2,1)S(1)}, u32[]{:S(2)}, u32[]{:S(2)}) collective-permute-start(bf16[3,512,128]{2,1,0:T(8,128)(2,1)S(1)} %collective-permute-done.5.refs_5_), channel_id=1, source_target_pairs={{0,1},{1,2},{2,3},{3,4},{4,5},{5,6},{6,7},{7,0},{8,9},{9,10},{10,1... | collective-permute-start | bytes 1179656 | tf_op jit(solution)/shard_map/ppermute | solution.py:24
  66.8 9.7 %collective-permute-start.10 = (bf16[2,512,128]{2,1,0:T(8,128)(2,1)}, bf16[2,512,128]{2,1,0:T(8,128)(2,1)S(1)}, u32[]{:S(2)}, u32[]{:S(2)}) collective-permute-start(bf16[2,512,128]{2,1,0:T(8,128)(2,1)} %pad_maximum_fusion), channel_id=1, source_target_pairs={{0,8},{8,0},{1,9},{9,1},{2,10},{10,2},{3,11},{11,3},{4,12},{12,4},... | collective-permute-start | bytes 786440 | tf_op jit(solution)/shard_map/ppermute | solution.py:24
  85.4 23.1 %collective-permute-start.17 = (bf16[4,1024,256]{2,1,0:T(8,128)(2,1)}, bf16[4,1024,256]{2,1,0:T(8,128)(2,1)}, u32[]{:S(2)}, u32[]{:S(2)}) collective-permute-start(bf16[4,1024,256]{2,1,0:T(8,128)(2,1)} %all-to-all-done.2.refs_11_), channel_id=1, source_target_pairs={{0,64},{64,0},{1,65},{65,1},{2,66},{66,2},{3,67},{67,3},{4,68},{68... | collective-permute-start | bytes 6291464 | tf_op jit(solution)/shard_map/ppermute | solution.py:24
  85.4 30.4 %all-to-all-start.1 = ((f32[16,32,512]{2,1,0:T(8,128)}), f32[16,32,512]{2,1,0:T(8,128)}, u32[]{:S(2)}, u32[]{:S(2)}) async-start(f32[16,32,512]{2,1,0:T(8,128)} %bitcast.5), calls=%async_computation.1 | async-start | bytes 2097152 | tf_op jit(solution)/shard_map/all_to_all | solution.py:186
  91.2 17.3 %collective-permute-start.16 = (bf16[1,512,128]{2,1,0:T(8,128)(2,1)S(1)}, bf16[1,512,128]{2,1,0:T(8,128)(2,1)S(1)}, u32[]{:S(2)}, u32[]{:S(2)}) collective-permute-start(bf16[1,512,128]{2,1,0:T(8,128)(2,1)S(1)} %slice.27), channel_id=1, source_target_pairs={{0,8},{8,0},{1,9},{9,1},{2,10},{10,2},{3,11},{11,3},{4,12},{12,4},... | collective-permute-start | bytes 393224 | tf_op jit(solution)/shard_map/ppermute | solution.py:24
  108.5 1.1 copy-start.1
  115.9 29.4 %all-to-all-start.3 = ((f32[4,128,512]{2,1,0:T(8,128)}), f32[4,128,512]{2,1,0:T(8,128)S(1)}, u32[]{:S(2)}, u32[]{:S(2)}) async-start(f32[4,128,512]{2,1,0:T(8,128)} %shard_map.49), calls=%async_computation.3 | async-start | bytes 2097152 | tf_op jit(solution)/shard_map/all_to_all | solution.py:194
  121.4 6.7 %collective-permute-start.11 = (bf16[1,4,32,512]{3,2,1,0:T(8,128)(2,1)S(1)}, bf16[1,4,32,512]{3,2,1,0:T(8,128)(2,1)S(1)}, u32[]{:S(2)}, u32[]{:S(2)}) collective-permute-start(bf16[1,4,32,512]{3,2,1,0:T(8,128)(2,1)S(1)} %bitcast.14), channel_id=1, source_target_pairs={{0,8},{8,0},{1,9},{9,1},{2,10},{10,2},{3,11},{11,3},{4,12},{12,4},... | collective-permute-start | bytes 393224 | tf_op jit(solution)/shard_map/ppermute | solution.py:24
  128.2 6.8 %collective-permute-start.13 = (bf16[2,4,32,512]{3,2,1,0:T(8,128)(2,1)S(1)}, bf16[2,4,32,512]{3,2,1,0:T(8,128)(2,1)S(1)}, u32[]{:S(2)}, u32[]{:S(2)}) collective-permute-start(bf16[2,4,32,512]{3,2,1,0:T(8,128)(2,1)S(1)} %pad_maximum_fusion.1.refs_0_), channel_id=1, source_target_pairs={{0,7},{1,0},{2,1},{3,2},{4,3},{5,4},{6,5},{7,6},{8,15},{9,8},{10,9... | collective-permute-start | bytes 786440 | tf_op jit(solution)/shard_map/ppermute | solution.py:24
  130.0 7.6 %collective-permute-start.12 = (bf16[2,4,32,512]{3,2,1,0:T(8,128)(2,1)S(1)}, bf16[2,4,32,512]{3,2,1,0:T(8,128)(2,1)S(1)}, u32[]{:S(2)}, u32[]{:S(2)}) collective-permute-start(bf16[2,4,32,512]{3,2,1,0:T(8,128)(2,1)S(1)} %pad_maximum_fusion.1.refs_0_), channel_id=1, source_target_pairs={{0,1},{1,2},{2,3},{3,4},{4,5},{5,6},{6,7},{7,0},{8,9},{9,10},{10,1... | collective-permute-start | bytes 786440 | tf_op jit(solution)/shard_map/ppermute | solution.py:24
  137.7 7.6 %collective-permute-start.14 = (bf16[2,4,32,512]{3,2,1,0:T(8,128)(2,1)S(1)}, bf16[2,4,32,512]{3,2,1,0:T(8,128)(2,1)S(1)}, u32[]{:S(2)}, u32[]{:S(2)}) collective-permute-start(bf16[2,4,32,512]{3,2,1,0:T(8,128)(2,1)S(1)} %collective-permute-done.12.refs_1_), channel_id=1, source_target_pairs={{0,1},{1,2},{2,3},{3,4},{4,5},{5,6},{6,7},{7,0},{8,9},{9,10},{10,1... | collective-permute-start | bytes 786440 | tf_op jit(solution)/shard_map/ppermute | solution.py:24
  137.7 7.6 %collective-permute-start.15 = (bf16[2,4,32,512]{3,2,1,0:T(8,128)(2,1)S(1)}, bf16[2,4,32,512]{3,2,1,0:T(8,128)(2,1)S(1)}, u32[]{:S(2)}, u32[]{:S(2)}) collective-permute-start(bf16[2,4,32,512]{3,2,1,0:T(8,128)(2,1)S(1)} %collective-permute-done.13.refs_2_), channel_id=1, source_target_pairs={{0,7},{1,0},{2,1},{3,2},{4,3},{5,4},{6,5},{7,6},{8,15},{9,8},{10,9... | collective-permute-start | bytes 786440 | tf_op jit(solution)/shard_map/ppermute | solution.py:24
  146.4 16.2 %all-to-all-start.4 = ((bf16[8,128,512]{2,1,0:T(8,128)(2,1)}), bf16[8,128,512]{2,1,0:T(8,128)(2,1)S(1)}, u32[]{:S(2)}, u32[]{:S(2)}) async-start(bf16[8,128,512]{2,1,0:T(8,128)(2,1)} %broadcast_in_dim.4), calls=%async_computation.4 | async-start | bytes 2097152 | tf_op jit(solution)/shard_map/all_to_all | solution.py:202
  152.6 7.6 %collective-permute-start.18 = (bf16[2,4,32,512]{3,2,1,0:T(8,128)(2,1)S(1)}, bf16[2,4,32,512]{3,2,1,0:T(8,128)(2,1)S(1)}, u32[]{:S(2)}, u32[]{:S(2)}) collective-permute-start(bf16[2,4,32,512]{3,2,1,0:T(8,128)(2,1)S(1)} %collective-permute-done.14.refs_3_), channel_id=1, source_target_pairs={{0,1},{1,2},{2,3},{3,4},{4,5},{5,6},{6,7},{7,0},{8,9},{9,10},{10,1... | collective-permute-start | bytes 786440 | tf_op jit(solution)/shard_map/ppermute | solution.py:24
  152.6 7.6 %collective-permute-start.19 = (bf16[2,4,32,512]{3,2,1,0:T(8,128)(2,1)S(1)}, bf16[2,4,32,512]{3,2,1,0:T(8,128)(2,1)S(1)}, u32[]{:S(2)}, u32[]{:S(2)}) collective-permute-start(bf16[2,4,32,512]{3,2,1,0:T(8,128)(2,1)S(1)} %collective-permute-done.15.refs_4_), channel_id=1, source_target_pairs={{0,7},{1,0},{2,1},{3,2},{4,3},{5,4},{6,5},{7,6},{8,15},{9,8},{10,9... | collective-permute-start | bytes 786440 | tf_op jit(solution)/shard_map/ppermute | solution.py:24
  162.7 10.2 %collective-permute-start.21 = (bf16[2,4,128,512]{3,2,1,0:T(8,128)(2,1)S(1)}, bf16[2,4,128,512]{3,2,1,0:T(8,128)(2,1)S(1)}, u32[]{:S(2)}, u32[]{:S(2)}) collective-permute-start(bf16[2,4,128,512]{3,2,1,0:T(8,128)(2,1)S(1)} %bitcast.12), channel_id=1, source_target_pairs={{0,64},{64,0},{1,65},{65,1},{2,66},{66,2},{3,67},{67,3},{4,68},{68... | collective-permute-start | bytes 3145736 | tf_op jit(solution)/shard_map/ppermute | solution.py:24
  162.7 10.2 %collective-permute-start.20 = (bf16[2,4,32,512]{3,2,1,0:T(8,128)(2,1)S(1)}, bf16[2,4,32,512]{3,2,1,0:T(8,128)(2,1)S(1)}, u32[]{:S(2)}, u32[]{:S(2)}) collective-permute-start(bf16[2,4,32,512]{3,2,1,0:T(8,128)(2,1)S(1)} %collective-permute-done.18.refs_5_), channel_id=1, source_target_pairs={{0,1},{1,2},{2,3},{3,4},{4,5},{5,6},{6,7},{7,0},{8,9},{9,10},{10,1... | collective-permute-start | bytes 786440 | tf_op jit(solution)/shard_map/ppermute | solution.py:24

commit v5 on v3

v5 whole, which is shorter than its diff:
```python
import functools

import jax
import jax.numpy as jnp
from jax import lax
from jax.experimental import pallas as pl
from jax.experimental.pallas import tpu as pltpu
from jax.sharding import Mesh, PartitionSpec as P

AXES = ("xl", "c", "y", "xh", "z")
SIZES = (2, 2, 4, 2, 8)
DP = ("xl", "c")
TILE = ("y", "xh", "z")
TOK = 512
COLS = 128
F32 = jnp.float32
BF16 = jnp.bfloat16
VMEM_LIMIT = 48 * 1024 * 1024
PARAMS = pltpu.CompilerParams(vmem_limit_bytes=VMEM_LIMIT)


def shift(x, axis, by):
    n = lax.axis_size(axis)
    return lax.ppermute(x, axis, [(i, (i + by) % n) for i in range(n)])


def after(x, *others):
    return lax.optimization_barrier((x, *others))[0]


def whole(shape):
    return pl.BlockSpec(shape, lambda *_: (0,) * len(shape))


def split_kernel(core_ref, in_ref, out_ref):
    exact = in_ref[...]
    high = exact.astype(BF16)
    out_ref[0, :, :COLS] = high
    out_ref[0, :, COLS:] = (exact - high.astype(F32)).astype(BF16)


def split_basis(core, basis):
    return pl.pallas_call(
        split_kernel,
        grid_spec=pltpu.PrefetchScalarGridSpec(
            num_scalar_prefetch=1,
            grid=(4,),
            in_specs=[pl.BlockSpec((1024, COLS), lambda g, core: (g * 2 + core[0], 0))],
            out_specs=pl.BlockSpec((1, 1024, 256), lambda g, core: (g, 0, 0)),
        ),
        out_shape=jax.ShapeDtypeStruct((4, 1024, 256), BF16),
        compiler_params=PARAMS,
        cost_estimate=pl.CostEstimate(
            flops=1 << 20, bytes_accessed=4 << 20, transcendentals=0
        ),
    )(core, basis)


def rotate_kernel(at_ref, block_ref, own_ref, other_ref, out_ref, lhs):
    @pl.when(pl.program_id(0) == 0)
    def _():
        turned = lax.rem(at_ref[1] + at_ref[4], 2)
        for z in range(8):
            for side in range(2):
                half = turned if side == 0 else 1 - turned
                at = pl.multiple_of((half * 8 + z) * COLS, COLS)
                lhs[:, pl.ds(at, COLS)] = block_ref[z, side]

    both = jnp.dot(lhs[:, :1024], own_ref[0], preferred_element_type=F32)
    both += jnp.dot(lhs[:, 1024:], other_ref[0], preferred_element_type=F32)
    out_ref[0] = (both[:, :COLS] + both[:, COLS:]).T


def rotate(at, blocks, own, other):
    slab = pl.BlockSpec((1, 1024, 256), lambda g: (g, 0, 0))
    return pl.pallas_call(
        rotate_kernel,
        grid=(4,),
        out_shape=jax.ShapeDtypeStruct((4, COLS, TOK), F32),
        in_specs=[pl.BlockSpec(memory_space=pltpu.SMEM), whole(blocks.shape), slab, slab],
        out_specs=pl.BlockSpec((1, COLS, TOK), lambda g: (g, 0, 0)),
        scratch_shapes=[pltpu.VMEM((TOK, 2048), BF16)],
        compiler_params=PARAMS,
        cost_estimate=pl.CostEstimate(
            flops=4 * TOK * 2048 * 512, bytes_accessed=7 << 20, transcendentals=0
        ),
    )(at, blocks, own, other)


def reach_kernel(rows_ref, in_ref, own_ref, near_ref, far_ref):
    def put(out_ref):
        exact = in_ref[...]
        high = exact.astype(BF16)
        out_ref[:, :COLS] = high
        out_ref[:, COLS:] = (exact - high.astype(F32)).astype(BF16)

    step = pl.program_id(0)
    pl.when(step < 2)(lambda: put(own_ref))
    pl.when((step >= 2) & (step < 4))(lambda: put(near_ref))
    pl.when(step == 4)(lambda: put(far_ref))


def reach_basis(rows, basis):
    return pl.pallas_call(
        reach_kernel,
        grid_spec=pltpu.PrefetchScalarGridSpec(
            num_scalar_prefetch=1,
            grid=(5,),
            in_specs=[pl.BlockSpec((1024, COLS), lambda g, rows: (rows[g], 0))],
            out_specs=[
                pl.BlockSpec((1024, 256), lambda g, rows: (jnp.minimum(g, 1), 0)),
                pl.BlockSpec((1024, 256), lambda g, rows: (jnp.clip(g - 2, 0, 1), 0)),
                pl.BlockSpec((1024, 256), lambda g, rows: (0, 0)),
            ],
        ),
        out_shape=[jax.ShapeDtypeStruct((n, 256), BF16) for n in (2048, 2048, 1024)],
        compiler_params=PARAMS,
        cost_estimate=pl.CostEstimate(
            flops=1 << 20, bytes_accessed=5 << 20, transcendentals=0
        ),
    )(rows, basis)


def rotate_ring_kernel(places, at_ref, *refs):
    blocks, refs = refs[: len(places)], refs[len(places) :]
    own_ref, near_ref, near_swapped, far_ref, far_swapped, out_ref, lhs = refs
    z, xh, y, c = at_ref[0], at_ref[1], at_ref[2], at_ref[4]
    for block, parts in zip(blocks, places):
        for i, (offset, side) in enumerate(parts):
            half = xh if side == 0 else 1 - xh
            at = (half * 8 + lax.rem(z + 8 + offset, 8)) * COLS
            lhs[:, pl.ds(pl.multiple_of(at, COLS), COLS)] = block[i]

    def put(place, both):
        out_ref[lax.rem(place, 4)] = (both[:, :COLS] + both[:, COLS:]).T

    for offset, ref in ((4, own_ref), (3 + 2 * c, near_ref), (5 - 2 * c, near_swapped)):
        put(y + offset, jnp.dot(lhs[...], ref[...], preferred_element_type=F32))
    mine = lhs[:, pl.ds(pl.multiple_of(c * 1024, 1024), 1024)]
    rest = lhs[:, pl.ds(pl.multiple_of((1 - c) * 1024, 1024), 1024)]
    both = jnp.dot(mine, far_ref[...], preferred_element_type=F32)
    put(y + 2, both + jnp.dot(rest, far_swapped[...], preferred_element_type=F32))


def rotate_ring(at, entries, slabs):
    blocks = [
        pl.BlockSpec((len(parts), *array.shape[1:]), lambda g, index=index: (index, 0, 0))
        for array, index, parts in entries
    ]
    return pl.pallas_call(
        functools.partial(rotate_ring_kernel, [parts for _, _, parts in entries]),
        grid=(1,),
        out_shape=jax.ShapeDtypeStruct((4, COLS, TOK), F32),
        in_specs=[pl.BlockSpec(memory_space=pltpu.SMEM)]
        + blocks
        + [whole(slab.shape) for slab in slabs],
        out_specs=whole((4, COLS, TOK)),
        scratch_shapes=[pltpu.VMEM((TOK, 2048), BF16)],
        compiler_params=PARAMS,
        cost_estimate=pl.CostEstimate(
            flops=4 * TOK * 2048 * 512, bytes_accessed=7 << 20, transcendentals=0
        ),
    )(at, *[array for array, _, _ in entries], *slabs)


def product_kernel(scale, at_ref, acts_ref, own_ref, other_ref, out_ref, right):
    xh, c = at_ref[1], at_ref[4]
    for z in range(8):
        for side in range(2):
            place = (xh if side == 0 else 1 - xh) * 8 + z
            for s in range(4):
                right[s, pl.ds(pl.multiple_of(place * 32, 32), 32), :] = acts_ref[z, side, s]
    for row in range(4):
        total = None
        for grads_ref, core in ((own_ref, c), (other_ref, 1 - c)):
            for side in range(2):
                part = lax.dot_general(
                    grads_ref[side, row],
                    right[side * 2 + core],
                    (((1,), (1,)), ((), ())),
                    preferred_element_type=F32,
                )
                total = part * part if total is None else total + part * part
        out_ref[row] = total * scale


def products(at, acts, own, other, scale):
    return pl.pallas_call(
        functools.partial(product_kernel, scale),
        out_shape=jax.ShapeDtypeStruct((4, COLS, 512), F32),
        in_specs=[pl.BlockSpec(memory_space=pltpu.SMEM)]
        + [pl.BlockSpec(memory_space=pltpu.VMEM)] * 3,
        out_specs=pl.BlockSpec(memory_space=pltpu.VMEM),
        scratch_shapes=[pltpu.VMEM((4, 512, TOK), BF16)],
        compiler_params=PARAMS,
        cost_estimate=pl.CostEstimate(
            flops=2 * 4 * 512 * 512 * TOK, bytes_accessed=5 << 20, transcendentals=0
        ),
    )(at, acts, own, other)


def weave_kernel(in_ref, out_ref):
    for tile in range(4):
        lanes = slice(tile * 32, tile * 32 + 32)
        out_ref[:, tile * COLS : (tile + 1) * COLS] = jnp.concatenate(
            [in_ref[q, :, lanes] for q in range(4)], axis=1
        )


def weave(parts):
    return pl.pallas_call(
        weave_kernel,
        grid=(4,),
        out_shape=jax.ShapeDtypeStruct((COLS, 2048), F32),
        in_specs=[pl.BlockSpec((4, COLS, 128), lambda g: (0, 0, g))],
        out_specs=pl.BlockSpec((COLS, 512), lambda g: (0, g)),
        compiler_params=PARAMS,
    )(parts)


def sync(*arrays):
    return lax.optimization_barrier(arrays)


def pair(x):
    return jnp.concatenate([x, shift(x, "xh", 1)])


def ring_step(up, down):
    return shift(up, "z", 1), shift(down, "z", -1)


def shift_near(x):
    pairs = [(i, (i + 1) % 4) for i in range(4)] + [(4 + i, 4 + (i + 3) % 4) for i in range(4)]
    return lax.ppermute(x, ("c", "y"), pairs)


def body(activations, gradients, basis_in, basis_out):
    z, xh, y, xl, c = (lax.axis_index(a) for a in ("z", "xh", "y", "xl", "c"))
    at = jnp.stack([z, xh, y, xl, c]).astype(jnp.int32)
    core = c.astype(jnp.int32).reshape(1)
    near_y, far_y = (y + 1 + 2 * c) % 4, (y + 2) % 4
    rows = jnp.stack(
        [y * 2, y * 2 + 1, near_y * 2, near_y * 2 + 1, far_y * 2 + c]
    ).astype(jnp.int32)

    acts_pair, g0, mine_in, basis_out = sync(
        pair(activations), pair(gradients), split_basis(core, basis_in), basis_out
    )
    own_in = lax.all_to_all(mine_in, "y", 0, 0)
    act_blocks = lax.all_gather(acts_pair, "z")
    own_out, near_out, far_out = reach_basis(rows, basis_out)
    up1, down1, near_out, far_out = sync(*ring_step(g0, g0), near_out, far_out)
    up2, down2, own_in, near_out, far_out = sync(*ring_step(up1, down1), own_in, near_out, far_out)
    up3, down3, other_in, near_out, far_out = sync(
        *ring_step(up2, down2), shift(own_in, "c", 1), shift_near(near_out), far_out
    )
    up4 = shift(up3, "z", 1)
    far_out = shift(far_out, "y", 2)
    near_out2 = shift(near_out, "c", 1)
    acts_part = rotate(at, act_blocks, own_in, other_in)
    acts_part, up4, far_out, near_out2 = sync(acts_part, up4, far_out, near_out2)
    acts_in = lax.all_to_all(acts_part.reshape(16, 32, TOK), ("xl", "c", "y"), 0, 0)

    ring = [(g0, 0), (up1, -1), (down1, 1), (up2, -2), (down2, 2), (up3, -3), (down3, 3), (up4, -4)]
    far_out2 = shift(far_out, "c", 1)
    grads_part = rotate_ring(
        at,
        [(a, 0, ((o, 0), (o, 1))) for a, o in ring],
        (own_out, near_out, near_out2, far_out, far_out2),
    )
    acts_in, grads_part = sync(acts_in, grads_part)
    grads_in = lax.all_to_all(grads_part, "y", 0, 0)

    acts = jnp.sum(acts_in.reshape(4, 4, 32, TOK), axis=1).astype(BF16)[None]
    rot_acts = lax.all_gather(pair(acts), "z")

    grads = jnp.sum(grads_in, axis=0).astype(BF16)
    copies = jnp.broadcast_to(grads, (8, COLS, TOK))
    rot_own = lax.all_to_all(copies, ("xl", "y"), 0, 0).reshape(2, 4, COLS, TOK)
    rot_other = shift(rot_own, "c", 1)

    part = products(at, rot_acts, rot_own, rot_other, 1.0 / (TOK * 4))
    return weave(lax.all_to_all(part, "y", 0, 0))


def solution(mesh):
    fine = Mesh(mesh.devices.reshape(SIZES), AXES)
    return jax.shard_map(
        body,
        mesh=fine,
        in_specs=(P(DP, None, TILE), P(DP, None, TILE), P(None, TILE), P(None, TILE)),
        out_specs=P(TILE, DP),
        check_vma=False,
    )
```

time: 198 us -> 184 us (0.929)
  waiting for transfers between devices: 87.9 us -> 50.4 us
  blocking collectives: 17.4 us -> 49 us
  starting transfers between devices: 56.1 us -> 32.2 us
  between operations: 0.21 us -> 13.5 us
  local copies, waits for them, and re-layouts: 6.52 us -> 9.83 us
    ppermute x27 -> x15, waiting for transfers between devices: 85.4 us -> 37.9 us  [shift(): return lax.ppermute(x, axis, [(i, (i + by) % n) for i in range(n)])]
    all_to_all x0 -> x2, blocking collectives: none -> 33.8 us  [the longest x1 17.4 us: body(): grads_in = lax.all_to_all(grads_part, 'y', 0, 0)]
    ppermute x27 -> x15, starting transfers between devices: 38.4 us -> 20.6 us  [shift(): return lax.ppermute(x, axis, [(i, (i + by) % n) for i in range(n)])]
    all_gather x0 -> x2, waiting for transfers between devices: none -> 5.99 us  [the longest x1 3.9 us: body(): rot_acts = lax.all_gather(pair(acts), 'z')]
    all_to_all x2 -> x1, starting transfers between devices: 10.4 us -> 4.48 us  [body(): own_in = lax.all_to_all(mine_in, 'y', 0, 0)]
    all_to_all x1, waiting for transfers between devices: 0.01 us -> 5.76 us  [body(): lax.all_to_all(acts_part.reshape(16, 32, TOK), ('xl', 'c', 'y'), 0, 0)]
    pallas_call x2 -> x1, Pallas kernels: 8.95 us -> 3.98 us  [split_basis(): pl.pallas_call(split_kernel, grid_spec=pltpu.PrefetchScalarGridSpec(num_s...]
    unnamed x30 -> x22, local copies, waits for them, and re-layouts: 5.2 us -> 9.58 us
  transfers between devices with their start and end apart: 32 -> 20, of which waited for: 17 -> 13; matrix products, arithmetic and copies ran while one was open for 2% -> 1% of each run, Pallas kernels for 11% -> 10%
where the time goes in v5:
time: 184 us; the launch traced here: 183 us
  waiting for transfers between devices  50.4 us (27%)
  blocking collectives  49 us (27%)
  starting transfers between devices  32.2 us (18%)
  Pallas kernels  24.9 us (14%)
  between operations  13.5 us (7%)
  local copies, waits for them, and re-layouts  9.83 us (5%)
  other arithmetic  2.94 us (2%)
    ppermute x15, waiting for transfers between devices, shift(): return lax.ppermute(x, axis, [(i, (i + by) % n) for i in range(n)])  37.9 us
    ppermute x15, starting transfers between devices, shift(): return lax.ppermute(x, axis, [(i, (i + by) % n) for i in range(n)])  20.6 us
    all_to_all x1, blocking collectives, body(): grads_in = lax.all_to_all(grads_part, 'y', 0, 0)  17.4 us
    all_to_all x1, blocking collectives, body(): rot_own = lax.all_to_all(copies, ('xl', 'y'), 0, 0).reshape(2, 4, COLS, TOK)  16.4 us
    all_to_all x1, blocking collectives, body(): return weave(lax.all_to_all(part, 'y', 0, 0))  15.2 us
    unnamed x22, local copies, waits for them, and re-layouts  9.58 us
    pallas_call x1, Pallas kernels, rotate(): pl.pallas_call(rotate_kernel, grid=(4,), out_shape=jax.ShapeDtypeStruct((...  5.87 us
    all_to_all x1, waiting for transfers between devices, body(): lax.all_to_all(acts_part.reshape(16, 32, TOK), ('xl', 'c', 'y'), 0, 0)  5.76 us
  transfers between devices with their start and end apart: 20, of which 13 were waited for; matrix products, arithmetic and copies ran while one was open for 1% of the time, Pallas kernels for 10%

profile of v5, /device:TPU:2, one launch (start us, length us, event | category | flops | bytes accessed | tf_op | source)
XLA Modules:
  0.0 182.8 jit_solution(17032069535729388550)
XLA Ops:
  6.5 2.1 %collective-permute-start = (bf16[1,512,128]{2,1,0:T(8,128)(2,1)}, bf16[1,512,128]{2,1,0:T(8,128)(2,1)S(1)}, u32[]{:S(2)}, u32[]{:S(2)}) collective-permute-start(bf16[1,512,128]{2,1,0:T(8,128)(2,1)} %param.4), channel_id=1, source_target_pairs={{0,8},{8,0},{1,9},{9,1},{2,10},{10,2},{3,11},{11,3},{4,12},{12,4},... | collective-permute-start | bytes 393224 | tf_op jit(solution)/shard_map/ppermute | solution.py:24
  8.7 1.4 collective-permute-start.1
  10.1 4.0 %shard_map.46 = bf16[4,1024,256]{2,1,0:T(8,128)(2,1)} custom-call(s32[1]{0:T(128)} %bitcast.4.core_ref, f32[8192,128]{1,0:T(8,128)} %in_ref.1), custom_call_target="tpu_custom_call" | custom-call | flops 1048576 | bytes 4194304 | tf_op jit(solution)/shard_map/pallas_call | solution.py:43
  14.1 0.4 collective-permute-done
  14.5 0.8 pad_maximum_fusion
  15.3 1.0 collective-permute-done.1
  16.3 4.5 %all-to-all-start = ((bf16[4,1024,256]{2,1,0:T(8,128)(2,1)}), bf16[4,1024,256]{2,1,0:T(8,128)(2,1)S(1)}, u32[]{:S(2)}, u32[]{:S(2)}) async-start(bf16[4,1024,256]{2,1,0:T(8,128)(2,1)} %shard_map.46), calls=%async_computation | async-start | bytes 4194304 | tf_op jit(solution)/shard_map/all_to_all | solution.py:250
  20.8 0.7 all-gather.5.cloned.1.call-update
  21.5 5.9 %collective-permute-start.3 = (bf16[2,512,128]{2,1,0:T(8,128)(2,1)S(1)}, bf16[2,512,128]{2,1,0:T(8,128)(2,1)}, u32[]{:S(2)}, u32[]{:S(2)}) collective-permute-start(bf16[2,512,128]{2,1,0:T(8,128)(2,1)S(1)} %pad_maximum_fusion.1.refs_0_), channel_id=1, source_target_pairs={{0,7},{1,0},{2,1},{3,2},{4,3},{5,4},{6,5},{7,6},{8,15},{9,8},{10,9... | collective-permute-start | bytes 786440 | tf_op jit(solution)/shard_map/ppermute | solution.py:24
  27.5 0.0 collective-permute-start.2
  27.5 0.1 stack.47.rows_ref
  27.5 4.1 %shard_map.47 = (bf16[2048,256]{1,0:T(8,128)(2,1)S(1)}, bf16[2048,256]{1,0:T(8,128)(2,1)S(1)}, bf16[1024,256]{1,0:T(8,128)(2,1)S(1)}) custom-call(s32[5]{0:T(128)S(1)} %stack.47.rows_ref, f32[8192,128]{1,0:T(8,128)} %in_ref.2), custom_call_target="tpu_custom_call" | custom-call | flops 1048576 | bytes 5242880 | tf_op jit(solution)/shard_map/pallas_call | solution.py:104
  31.6 0.0 copy-start.2
  31.7 1.0 copy-done.2
  32.6 0.8 copy-done.3
  33.4 0.0 collective-permute-done.3.refs_2_
  33.4 2.1 %collective-permute-done.2.refs_1_ = bf16[2,512,128]{2,1,0:T(8,128)(2,1)} collective-permute-done((bf16[2,512,128]{2,1,0:T(8,128)(2,1)S(1)}, bf16[2,512,128]{2,1,0:T(8,128)(2,1)}, u32[]{:S(2)}, u32[]{:S(2)}) %collective-permute-start.2) | collective-permute-done | bytes 262176 | tf_op jit(solution)/shard_map/ppermute | solution.py:24
  35.5 0.0 collective-permute-start.4
  35.5 3.2 %collective-permute-start.5 = (bf16[2,512,128]{2,1,0:T(8,128)(2,1)}, bf16[2,512,128]{2,1,0:T(8,128)(2,1)}, u32[]{:S(2)}, u32[]{:S(2)}) collective-permute-start(bf16[2,512,128]{2,1,0:T(8,128)(2,1)} %collective-permute-done.3.refs_2_), channel_id=1, source_target_pairs={{0,7},{1,0},{2,1},{3,2},{4,3},{5,4},{6,5},{7,6},{8,15},{9,8},{10,9... | collective-permute-start | bytes 786440 | tf_op jit(solution)/shard_map/ppermute | solution.py:24
  38.8 8.0 %collective-permute-done.4.refs_3_ = bf16[2,512,128]{2,1,0:T(8,128)(2,1)S(1)} collective-permute-done((bf16[2,512,128]{2,1,0:T(8,128)(2,1)}, bf16[2,512,128]{2,1,0:T(8,128)(2,1)S(1)}, u32[]{:S(2)}, u32[]{:S(2)}) %collective-permute-start.4) | collective-permute-done | bytes 262176 | tf_op jit(solution)/shard_map/ppermute | solution.py:24
  46.8 0.7 copy-done.4
  47.5 0.0 collective-permute-done.5.refs_4_
  47.5 0.0 all-to-all-done.own_ref
  47.5 0.0 collective-permute-start.8
  47.5 2.3 %collective-permute-start.9 = (bf16[2048,256]{1,0:T(8,128)(2,1)}, bf16[2048,256]{1,0:T(8,128)(2,1)}, u32[]{:S(2)}, u32[]{:S(2)}) collective-permute-start(bf16[2048,256]{1,0:T(8,128)(2,1)} %copy-done.2), channel_id=1, source_target_pairs={{0,16},{16,32},{32,48},{48,0},{64,112},{80,64},{96,80},{112,96},{1... | collective-permute-start | bytes 3145736 | tf_op jit(solution)/shard_map/ppermute | solution.py:235
  49.8 0.0 collective-permute-start.6
  49.8 3.2 %collective-permute-start.7 = (bf16[2,512,128]{2,1,0:T(8,128)(2,1)}, bf16[2,512,128]{2,1,0:T(8,128)(2,1)S(1)}, u32[]{:S(2)}, u32[]{:S(2)}) collective-permute-start(bf16[2,512,128]{2,1,0:T(8,128)(2,1)} %collective-permute-done.5.refs_4_), channel_id=1, source_target_pairs={{0,7},{1,0},{2,1},{3,2},{4,3},{5,4},{6,5},{7,6},{8,15},{9,8},{10,9... | collective-permute-start | bytes 786440 | tf_op jit(solution)/shard_map/ppermute | solution.py:24
  53.1 12.9 %collective-permute-done.6.refs_5_ = bf16[2,512,128]{2,1,0:T(8,128)(2,1)} collective-permute-done((bf16[2,512,128]{2,1,0:T(8,128)(2,1)}, bf16[2,512,128]{2,1,0:T(8,128)(2,1)}, u32[]{:S(2)}, u32[]{:S(2)}) %collective-permute-start.6) | collective-permute-done | bytes 262176 | tf_op jit(solution)/shard_map/ppermute | solution.py:24
  65.9 0.0 collective-permute-done.7.refs_6_
  65.9 0.7 copy-done.6
  66.6 0.0 collective-permute-done.9.refs_9_
  66.6 0.0 collective-permute-done.8.other_ref
  66.6 1.3 copy-done.10
  68.0 0.1 collective-permute-start.12
  68.1 1.9 %collective-permute-start.11 = (bf16[1024,256]{1,0:T(8,128)(2,1)}, bf16[1024,256]{1,0:T(8,128)(2,1)}, u32[]{:S(2)}, u32[]{:S(2)}) collective-permute-start(bf16[1024,256]{1,0:T(8,128)(2,1)} %copy-done.3), channel_id=1, source_target_pairs={{0,32},{16,48},{32,0},{48,16},{1,33},{17,49},{33,1},{49,17},{2,34}... | collective-permute-start | bytes 1572872 | tf_op jit(solution)/shard_map/ppermute | solution.py:24
  70.0 0.1 stack.41.at_ref
  70.1 2.1 %all-gather.5.cloned.1.call-done = bf16[16,512,128]{2,1,0:T(8,128)(2,1)} async-done(((bf16[2,512,128]{2,1,0:T(8,128)(2,1)}), bf16[16,512,128]{2,1,0:T(8,128)(2,1)}) %all-gather.5.cloned.1.call-update) | async-done | bytes 2097168 | tf_op jit(solution)/shard_map/all_gather | solution.py:251
  72.2 1.6 copy-done.1
  73.8 5.9 %shard_map.48 = f32[4,128,512]{2,1,0:T(8,128)} custom-call(s32[5]{0:T(128)S(1)} %stack.41.at_ref, bf16[8,2,512,128]{3,2,1,0:T(8,128)(2,1)S(1)} %bitcast.22, bf16[4,1024,256]{2,1,0:T(8,128)(2,1)S(1)} %all-to-all-done.own_ref, bf16[4,1024,256]{2,1,0:T(8,128)(2,1)} %copy-done.10), custom_call_target="tpu_custom_call" | custom-call | flops 2147483648 | bytes 7340032 | tf_op jit(solution)/shard_map/pallas_call | solution.py:76
  79.7 0.4 collective-permute-done.10.refs_7_
  80.1 4.1 %collective-permute-done.11.refs_11_ = bf16[1024,256]{1,0:T(8,128)(2,1)} collective-permute-done((bf16[1024,256]{1,0:T(8,128)(2,1)}, bf16[1024,256]{1,0:T(8,128)(2,1)}, u32[]{:S(2)}, u32[]{:S(2)}) %collective-permute-start.11) | collective-permute-done | bytes 524320 | tf_op jit(solution)/shard_map/ppermute | solution.py:24
  84.1 4.8 %all-to-all-start.1 = ((f32[16,32,512]{2,1,0:T(8,128)}), f32[16,32,512]{2,1,0:T(8,128)}, u32[]{:S(2)}, u32[]{:S(2)}) async-start(f32[16,32,512]{2,1,0:T(8,128)} %bitcast.11), calls=%async_computation.1 | async-start | bytes 2097152 | tf_op jit(solution)/shard_map/all_to_all | solution.py:263
  88.9 0.0 all-gather.7.cloned.1.call-start
  89.0 0.4 collective-permute-start.13
  89.4 2.0 %collective-permute-done.13.refs_12_ = bf16[1024,256]{1,0:T(8,128)(2,1)S(1)} collective-permute-done((bf16[1024,256]{1,0:T(8,128)(2,1)}, bf16[1024,256]{1,0:T(8,128)(2,1)S(1)}, u32[]{:S(2)}, u32[]{:S(2)}) %collective-permute-start.13) | collective-permute-done | bytes 524320 | tf_op jit(solution)/shard_map/ppermute | solution.py:24
  91.3 0.9 copy-done.5
  92.3 0.9 copy-done.7
  93.2 5.1 %shard_map.49 = f32[4,128,512]{2,1,0:T(8,128)S(1)} custom-call(s32[5]{0:T(128)S(1)} %stack.41.at_ref, bf16[2,512,128]{2,1,0:T(8,128)(2,1)S(1)} %pad_maximum_fusion.1.refs_0_, bf16[2,512,128]{2,1,0:T(8,128)(2,1)} %collective-permute-done.2.refs_1_, bf16[2,512,128]{2,1,0:T(8,128)(2,1)} %collective-permute-done.3.refs_2_, bf16[2,512,128]{2,1,0:T(8,128)(2,1)S(1)} %copy-done.5, ...), custom_call_target="tpu_custom_call" | custom-call | flops 2147483648 | bytes 7340032 | tf_op jit(solution)/shard_map/pallas_call | solution.py:150
  98.4 5.8 %all-to-all-done.1 = f32[16,32,512]{2,1,0:T(8,128)} async-done(((f32[16,32,512]{2,1,0:T(8,128)}), f32[16,32,512]{2,1,0:T(8,128)}, u32[]{:S(2)}, u32[]{:S(2)}) %all-to-all-start.1) | async-done | bytes 1048608 | tf_op jit(solution)/shard_map/all_to_all | solution.py:263
  104.1 1.3 bitcast_reduce_fusion
  105.5 2.2 %collective-permute-start.14 = (bf16[1,4,32,512]{3,2,1,0:T(8,128)(2,1)S(1)}, bf16[1,4,32,512]{3,2,1,0:T(8,128)(2,1)S(1)}, u32[]{:S(2)}, u32[]{:S(2)}) collective-permute-start(bf16[1,4,32,512]{3,2,1,0:T(8,128)(2,1)S(1)} %bitcast.23), channel_id=1, source_target_pairs={{0,8},{8,0},{1,9},{9,1},{2,10},{10,2},{3,11},{11,3},{4,12},{12,4},... | collective-permute-start | bytes 393224 | tf_op jit(solution)/shard_map/ppermute | solution.py:24
  107.7 4.4 %collective-permute-done.14 = bf16[1,4,32,512]{3,2,1,0:T(8,128)(2,1)S(1)} collective-permute-done((bf16[1,4,32,512]{3,2,1,0:T(8,128)(2,1)S(1)}, bf16[1,4,32,512]{3,2,1,0:T(8,128)(2,1)S(1)}, u32[]{:S(2)}, u32[]{:S(2)}) %collective-permute-start.14) | collective-permute-done | bytes 131104 | tf_op jit(solution)/shard_map/ppermute | solution.py:24
  112.0 0.7 pad_maximum_fusion.2
  112.8 0.0 all-gather.7.cloned.1.call-update
  112.8 17.4 %all_to_all.25 = f32[4,128,512]{2,1,0:T(8,128)S(1)} all-to-all(f32[4,128,512]{2,1,0:T(8,128)S(1)} %shard_map.49), channel_id=1, replica_groups=mesh['xl'=2,'c'=2,'y'=4,'xh'=2,'z'=8] {'y'}, dimensions={0} | all-to-all | bytes 2097152 | tf_op jit(solution)/shard_map/all_to_all | solution.py:273
  130.2 0.1 reduce_sum.19
  130.3 0.1 broadcast_in_dim.4
  130.4 16.4 %all_to_all.26 = bf16[8,128,512]{2,1,0:T(8,128)(2,1)S(1)} all-to-all(bf16[8,128,512]{2,1,0:T(8,128)(2,1)S(1)} %broadcast_in_dim.4), channel_id=1, replica_groups=mesh['xl'=2,'c'=2,'y'=4,'xh'=2,'z'=8] {'xl','y'}, dimensions={0} | all-to-all | bytes 2097152 | tf_op jit(solution)/shard_map/all_to_all | solution.py:280
  146.7 2.7 %collective-permute-done.15.other_ref = bf16[2,4,128,512]{3,2,1,0:T(8,128)(2,1)S(1)} collective-permute-done((bf16[2,4,128,512]{3,2,1,0:T(8,128)(2,1)S(1)}, bf16[2,4,128,512]{3,2,1,0:T(8,128)(2,1)S(1)}, u32[]{:S(2)}, u32[]{:S(2)}) %collective-permute-start.15) | collective-permute-done | bytes 1048608 | tf_op jit(solution)/shard_map/ppermute | solution.py:24
  149.4 3.9 %all-gather.7.cloned.1.call-done = bf16[16,4,32,512]{3,2,1,0:T(8,128)(2,1)} async-done(((bf16[2,4,32,512]{3,2,1,0:T(8,128)(2,1)}), bf16[16,4,32,512]{3,2,1,0:T(8,128)(2,1)}) %all-gather.7.cloned.1.call-update) | async-done | bytes 2097168 | tf_op jit(solution)/shard_map/all_gather | solution.py:276
  153.3 1.6 copy-done
  154.9 3.5 %shard_map.50 = f32[4,128,512]{2,1,0:T(8,128)S(1)} custom-call(s32[5]{0:T(128)S(1)} %stack.41.at_ref, bf16[8,2,4,32,512]{4,3,2,1,0:T(8,128)(2,1)S(1)} %bitcast.21, bf16[2,4,128,512]{3,2,1,0:T(8,128)(2,1)S(1)} %bitcast.20, bf16[2,4,128,512]{3,2,1,0:T(8,128)(2,1)S(1)} %collective-permute-done.15.other_ref), custom_call_target="tpu_custom_call" | custom-call | flops 1073741824 | bytes 5242880 | tf_op jit(solution)/shard_map/pallas_call | solution.py:188
  158.4 15.2 %all_to_all.27.in_ref = f32[4,128,512]{2,1,0:T(8,128)S(1)} all-to-all(f32[4,128,512]{2,1,0:T(8,128)S(1)} %shard_map.50), channel_id=1, replica_groups=mesh['xl'=2,'c'=2,'y'=4,'xh'=2,'z'=8] {'y'}, dimensions={0} | all-to-all | bytes 2097152 | tf_op jit(solution)/shard_map/all_to_all | solution.py:284
  173.6 2.4 %shard_map.51 = f32[128,2048]{1,0:T(8,128)} custom-call(f32[4,128,512]{2,1,0:T(8,128)S(1)} %all_to_all.27.in_ref), custom_call_target="tpu_custom_call" | custom-call | tf_op jit(solution)/shard_map/pallas_call | solution.py:211
  (17 shorter events, 0.1 us)
Async XLA Ops:
  6.5 8.0 %collective-permute-start = (bf16[1,512,128]{2,1,0:T(8,128)(2,1)}, bf16[1,512,128]{2,1,0:T(8,128)(2,1)S(1)}, u32[]{:S(2)}, u32[]{:S(2)}) collective-permute-start(bf16[1,512,128]{2,1,0:T(8,128)(2,1)} %param.4), channel_id=1, source_target_pairs={{0,8},{8,0},{1,9},{9,1},{2,10},{10,2},{3,11},{11,3},{4,12},{12,4},... | collective-permute-start | bytes 393224 | tf_op jit(solution)/shard_map/ppermute | solution.py:24
  8.7 7.6 %collective-permute-start.1 = (bf16[1,512,128]{2,1,0:T(8,128)(2,1)}, bf16[1,512,128]{2,1,0:T(8,128)(2,1)S(1)}, u32[]{:S(2)}, u32[]{:S(2)}) collective-permute-start(bf16[1,512,128]{2,1,0:T(8,128)(2,1)} %param.5), channel_id=1, source_target_pairs={{0,8},{8,0},{1,9},{9,1},{2,10},{10,2},{3,11},{11,3},{4,12},{12,4},... | collective-permute-start | bytes 393224 | tf_op jit(solution)/shard_map/ppermute | solution.py:24
  10.1 4.4 %copy-start.8 = (bf16[1,512,128]{2,1,0:T(8,128)(2,1)S(1)}, bf16[1,512,128]{2,1,0:T(8,128)(2,1)}, u32[]{:S(2)}) copy-start(bf16[1,512,128]{2,1,0:T(8,128)(2,1)} %param.4) | copy-start | bytes 393220
  10.1 6.2 %copy-start.9 = (bf16[1,512,128]{2,1,0:T(8,128)(2,1)S(1)}, bf16[1,512,128]{2,1,0:T(8,128)(2,1)}, u32[]{:S(2)}) copy-start(bf16[1,512,128]{2,1,0:T(8,128)(2,1)} %param.5) | copy-start | bytes 393220
  16.3 31.1 %all-to-all-start = ((bf16[4,1024,256]{2,1,0:T(8,128)(2,1)}), bf16[4,1024,256]{2,1,0:T(8,128)(2,1)S(1)}, u32[]{:S(2)}, u32[]{:S(2)}) async-start(bf16[4,1024,256]{2,1,0:T(8,128)(2,1)} %shard_map.46), calls=%async_computation | async-start | bytes 4194304 | tf_op jit(solution)/shard_map/all_to_all | solution.py:250
  20.8 51.4 %all-gather.5.cloned.1.call-start = ((), (), s32[]{:S(2)}) async-start(), calls=%async_computation.5 | async-start | bytes 2359296 | tf_op jit(solution)/shard_map/all_gather | solution.py:251
  21.5 11.9 %collective-permute-start.3 = (bf16[2,512,128]{2,1,0:T(8,128)(2,1)S(1)}, bf16[2,512,128]{2,1,0:T(8,128)(2,1)}, u32[]{:S(2)}, u32[]{:S(2)}) collective-permute-start(bf16[2,512,128]{2,1,0:T(8,128)(2,1)S(1)} %pad_maximum_fusion.1.refs_0_), channel_id=1, source_target_pairs={{0,7},{1,0},{2,1},{3,2},{4,3},{5,4},{6,5},{7,6},{8,15},{9,8},{10,9... | collective-permute-start | bytes 786440 | tf_op jit(solution)/shard_map/ppermute | solution.py:24
  27.5 8.1 %collective-permute-start.2 = (bf16[2,512,128]{2,1,0:T(8,128)(2,1)S(1)}, bf16[2,512,128]{2,1,0:T(8,128)(2,1)}, u32[]{:S(2)}, u32[]{:S(2)}) collective-permute-start(bf16[2,512,128]{2,1,0:T(8,128)(2,1)S(1)} %pad_maximum_fusion.1.refs_0_), channel_id=1, source_target_pairs={{0,1},{1,2},{2,3},{3,4},{4,5},{5,6},{6,7},{7,0},{8,9},{9,10},{10,1... | collective-permute-start | bytes 786440 | tf_op jit(solution)/shard_map/ppermute | solution.py:24
  31.6 1.0 copy-start.2
  32.6 0.8 copy-start.3
  35.5 11.2 %collective-permute-start.4 = (bf16[2,512,128]{2,1,0:T(8,128)(2,1)}, bf16[2,512,128]{2,1,0:T(8,128)(2,1)S(1)}, u32[]{:S(2)}, u32[]{:S(2)}) collective-permute-start(bf16[2,512,128]{2,1,0:T(8,128)(2,1)} %collective-permute-done.2.refs_1_), channel_id=1, source_target_pairs={{0,1},{1,2},{2,3},{3,4},{4,5},{5,6},{6,7},{7,0},{8,9},{9,10},{10,1... | collective-permute-start | bytes 786440 | tf_op jit(solution)/shard_map/ppermute | solution.py:24
  35.5 11.9 %collective-permute-start.5 = (bf16[2,512,128]{2,1,0:T(8,128)(2,1)}, bf16[2,512,128]{2,1,0:T(8,128)(2,1)}, u32[]{:S(2)}, u32[]{:S(2)}) collective-permute-start(bf16[2,512,128]{2,1,0:T(8,128)(2,1)} %collective-permute-done.3.refs_2_), channel_id=1, source_target_pairs={{0,7},{1,0},{2,1},{3,2},{4,3},{5,4},{6,5},{7,6},{8,15},{9,8},{10,9... | collective-permute-start | bytes 786440 | tf_op jit(solution)/shard_map/ppermute | solution.py:24
  46.7 0.7 copy-start.4
  47.5 19.2 %collective-permute-start.8 = (bf16[4,1024,256]{2,1,0:T(8,128)(2,1)S(1)}, bf16[4,1024,256]{2,1,0:T(8,128)(2,1)S(1)}, u32[]{:S(2)}, u32[]{:S(2)}) collective-permute-start(bf16[4,1024,256]{2,1,0:T(8,128)(2,1)S(1)} %all-to-all-done.own_ref), channel_id=1, source_target_pairs={{0,64},{64,0},{1,65},{65,1},{2,66},{66,2},{3,67},{67,3},{4,68},{68... | collective-permute-start | bytes 6291464 | tf_op jit(solution)/shard_map/ppermute | solution.py:24
  47.5 19.2 %collective-permute-start.9 = (bf16[2048,256]{1,0:T(8,128)(2,1)}, bf16[2048,256]{1,0:T(8,128)(2,1)}, u32[]{:S(2)}, u32[]{:S(2)}) collective-permute-start(bf16[2048,256]{1,0:T(8,128)(2,1)} %copy-done.2), channel_id=1, source_target_pairs={{0,16},{16,32},{32,48},{48,0},{64,112},{80,64},{96,80},{112,96},{1... | collective-permute-start | bytes 3145736 | tf_op jit(solution)/shard_map/ppermute | solution.py:235
  49.8 16.1 %collective-permute-start.6 = (bf16[2,512,128]{2,1,0:T(8,128)(2,1)}, bf16[2,512,128]{2,1,0:T(8,128)(2,1)}, u32[]{:S(2)}, u32[]{:S(2)}) collective-permute-start(bf16[2,512,128]{2,1,0:T(8,128)(2,1)} %copy-done.4), channel_id=1, source_target_pairs={{0,1},{1,2},{2,3},{3,4},{4,5},{5,6},{6,7},{7,0},{8,9},{9,10},{10,1... | collective-permute-start | bytes 786440 | tf_op jit(solution)/shard_map/ppermute | solution.py:24
  49.8 16.1 %collective-permute-start.7 = (bf16[2,512,128]{2,1,0:T(8,128)(2,1)}, bf16[2,512,128]{2,1,0:T(8,128)(2,1)S(1)}, u32[]{:S(2)}, u32[]{:S(2)}) collective-permute-start(bf16[2,512,128]{2,1,0:T(8,128)(2,1)} %collective-permute-done.5.refs_4_), channel_id=1, source_target_pairs={{0,7},{1,0},{2,1},{3,2},{4,3},{5,4},{6,5},{7,6},{8,15},{9,8},{10,9... | collective-permute-start | bytes 786440 | tf_op jit(solution)/shard_map/ppermute | solution.py:24
  65.9 0.7 copy-start.6
  66.6 1.3 copy-start.10
  68.0 16.2 %collective-permute-start.12 = (bf16[2048,256]{1,0:T(8,128)(2,1)}, bf16[2048,256]{1,0:T(8,128)(2,1)}, u32[]{:S(2)}, u32[]{:S(2)}) collective-permute-start(bf16[2048,256]{1,0:T(8,128)(2,1)} %collective-permute-done.9.refs_9_), channel_id=1, source_target_pairs={{0,64},{64,0},{1,65},{65,1},{2,66},{66,2},{3,67},{67,3},{4,68},{68... | collective-permute-start | bytes 3145736 | tf_op jit(solution)/shard_map/ppermute | solution.py:24
  68.1 16.0 %collective-permute-start.11 = (bf16[1024,256]{1,0:T(8,128)(2,1)}, bf16[1024,256]{1,0:T(8,128)(2,1)}, u32[]{:S(2)}, u32[]{:S(2)}) collective-permute-start(bf16[1024,256]{1,0:T(8,128)(2,1)} %copy-done.3), channel_id=1, source_target_pairs={{0,32},{16,48},{32,0},{48,16},{1,33},{17,49},{33,1},{49,17},{2,34}... | collective-permute-start | bytes 1572872 | tf_op jit(solution)/shard_map/ppermute | solution.py:24
  70.0 10.1 %collective-permute-start.10 = (bf16[2,512,128]{2,1,0:T(8,128)(2,1)}, bf16[2,512,128]{2,1,0:T(8,128)(2,1)}, u32[]{:S(2)}, u32[]{:S(2)}) collective-permute-start(bf16[2,512,128]{2,1,0:T(8,128)(2,1)} %collective-permute-done.6.refs_5_), channel_id=1, source_target_pairs={{0,1},{1,2},{2,3},{3,4},{4,5},{5,6},{6,7},{7,0},{8,9},{9,10},{10,1... | collective-permute-start | bytes 786440 | tf_op jit(solution)/shard_map/ppermute | solution.py:24
  72.2 1.6 copy-start.1
  84.1 20.0 %all-to-all-start.1 = ((f32[16,32,512]{2,1,0:T(8,128)}), f32[16,32,512]{2,1,0:T(8,128)}, u32[]{:S(2)}, u32[]{:S(2)}) async-start(f32[16,32,512]{2,1,0:T(8,128)} %bitcast.11), calls=%async_computation.1 | async-start | bytes 2097152 | tf_op jit(solution)/shard_map/all_to_all | solution.py:263
  88.9 64.4 %all-gather.7.cloned.1.call-start = ((), (), s32[]{:S(2)}) async-start(), calls=%async_computation.6 | async-start | bytes 2359296 | tf_op jit(solution)/shard_map/all_gather | solution.py:276
  89.0 2.4 %collective-permute-start.13 = (bf16[1024,256]{1,0:T(8,128)(2,1)}, bf16[1024,256]{1,0:T(8,128)(2,1)S(1)}, u32[]{:S(2)}, u32[]{:S(2)}) collective-permute-start(bf16[1024,256]{1,0:T(8,128)(2,1)} %collective-permute-done.11.refs_11_), channel_id=1, source_target_pairs={{0,64},{64,0},{1,65},{65,1},{2,66},{66,2},{3,67},{67,3},{4,68},{68... | collective-permute-start | bytes 1572872 | tf_op jit(solution)/shard_map/ppermute | solution.py:24
  91.3 1.0 copy-start.5
  92.3 0.9 copy-start.7
  105.5 6.6 %collective-permute-start.14 = (bf16[1,4,32,512]{3,2,1,0:T(8,128)(2,1)S(1)}, bf16[1,4,32,512]{3,2,1,0:T(8,128)(2,1)S(1)}, u32[]{:S(2)}, u32[]{:S(2)}) collective-permute-start(bf16[1,4,32,512]{3,2,1,0:T(8,128)(2,1)S(1)} %bitcast.23), channel_id=1, source_target_pairs={{0,8},{8,0},{1,9},{9,1},{2,10},{10,2},{3,11},{11,3},{4,12},{12,4},... | collective-permute-start | bytes 393224 | tf_op jit(solution)/shard_map/ppermute | solution.py:24
  146.7 2.7 %collective-permute-start.15 = (bf16[2,4,128,512]{3,2,1,0:T(8,128)(2,1)S(1)}, bf16[2,4,128,512]{3,2,1,0:T(8,128)(2,1)S(1)}, u32[]{:S(2)}, u32[]{:S(2)}) collective-permute-start(bf16[2,4,128,512]{3,2,1,0:T(8,128)(2,1)S(1)} %bitcast.19), channel_id=1, source_target_pairs={{0,64},{64,0},{1,65},{65,1},{2,66},{66,2},{3,67},{67,3},{4,68},{68... | collective-permute-start | bytes 3145736 | tf_op jit(solution)/shard_map/ppermute | solution.py:24
  153.3 1.6 copy-start
Sparse Core Ops, SparseCore 0:
  23.4 48.7 all-gather.4
  112.9 40.3 all-gather.6

commit v6 on v4

--- a/solution.py
+++ b/solution.py
@@ -32,28 +32,34 @@
     return pl.BlockSpec(shape, lambda *_: (0,) * len(shape))
 
 
-def split_kernel(core_ref, in_ref, out_ref):
-    exact = in_ref[...]
-    high = exact.astype(BF16)
-    out_ref[0, :, :COLS] = high
-    out_ref[0, :, COLS:] = (exact - high.astype(F32)).astype(BF16)
-
-
-def split_basis(core, basis):
+def split_kernel(core_ref, in_ref, out_ref, split_ref):
+    def put(ref):
+        exact = ref[...]
+        high = exact.astype(BF16)
+        split_ref[0, :, :COLS] = high
+        split_ref[0, :, COLS:] = (exact - high.astype(F32)).astype(BF16)
+
+    of_out = lax.rem(pl.program_id(0), 2)
+    pl.when(of_out == 0)(lambda: put(in_ref))
+    pl.when(of_out == 1)(lambda: put(out_ref))
+
+
+def split_bases(core, basis_in, basis_out):
+    rows = pl.BlockSpec((1024, COLS), lambda g, core: (g // 2 * 2 + core[0], 0))
     return pl.pallas_call(
         split_kernel,
         grid_spec=pltpu.PrefetchScalarGridSpec(
             num_scalar_prefetch=1,
-            grid=(4,),
-            in_specs=[pl.BlockSpec((1024, COLS), lambda g, core: (g * 2 + core[0], 0))],
-            out_specs=pl.BlockSpec((1, 1024, 256), lambda g, core: (g, 0, 0)),
-        ),
-        out_shape=jax.ShapeDtypeStruct((4, 1024, 256), BF16),
+            grid=(8,),
+            in_specs=[rows, rows],
+            out_specs=pl.BlockSpec((1, 1024, 256), lambda g, core: (g // 2, g % 2, 0)),
+        ),
+        out_shape=jax.ShapeDtypeStruct((4, 2048, 256), BF16),
         compiler_params=PARAMS,
         cost_estimate=pl.CostEstimate(
-            flops=1 << 20, bytes_accessed=4 << 20, transcendentals=0
-        ),
-    )(core, basis)
+            flops=1 << 20, bytes_accessed=8 << 20, transcendentals=0
+        ),
+    )(core, basis_in, basis_out)
 
 
 def rotate_kernel(places, at_ref, *refs):
@@ -74,8 +80,8 @@
     out_ref[0] = (both[:, :COLS] + both[:, COLS:]).T
 
 
-def rotate(at, entries, own, other):
-    slab = pl.BlockSpec((1, 1024, 256), lambda g: (g, 0, 0))
+def rotate(at, entries, own, other, which):
+    slab = pl.BlockSpec((1, 1024, 256), lambda g: (g, which, 0))
     blocks = [
         pl.BlockSpec((len(parts), *array.shape[1:]), lambda g, index=index: (index, 0, 0))
         for array, index, parts in entries
@@ -160,41 +166,38 @@
     return shift(up, "z", 1), shift(down, "z", -1)
 
 
+def pair(x):
+    return jnp.concatenate([x, shift(x, "xh", 1)])
+
+
 def body(activations, gradients, basis_in, basis_out):
     z, xh, y, xl, c = (lax.axis_index(a) for a in ("z", "xh", "y", "xl", "c"))
     at = jnp.stack([z, xh, y, xl, c]).astype(jnp.int32)
     core = c.astype(jnp.int32).reshape(1)
 
-    acts_other, mine_in, basis_out = sync(
-        shift(activations, "xh", 1), split_basis(core, basis_in), basis_out
+    acts_other, grads_other, mine = sync(
+        shift(activations, "xh", 1),
+        shift(gradients, "xh", 1),
+        split_bases(core, basis_in, basis_out),
     )
-    own_in = lax.all_to_all(mine_in, "y", 0, 0)
-    base = jnp.concatenate([activations, acts_other, gradients])
-    up1, down1, mine_out = sync(*ring_step(base, base), split_basis(core, basis_out))
-    up2, down2, mine_out, own_in = sync(*ring_step(up1, down1), mine_out, own_in)
-    own_out = lax.all_to_all(mine_out, "y", 0, 0)
-    near = jnp.concatenate([a[2:] for a in (base, up1, down1, up2, down2)])
-    up3, down3, other_in, near_other = sync(
-        *ring_step(up2, down2), shift(own_in, "c", 1), shift(near, "xh", 1)
-    )
-    three = jnp.concatenate([up3[2:], down3[2:]])
-    up4, three_other = sync(shift(up3, "z", 1), shift(three, "xh", 1))
-    ring = [(base, 0), (up1, -1), (down1, 1), (up2, -2), (down2, 2), (up3, -3), (down3, 3), (up4, -4)]
-
-    acts_entries = [(a, 0, ((o, 0), (o, 1))) for a, o in ring]
-    acts_part = rotate(at, acts_entries, own_in, other_in)
+    own = lax.all_to_all(mine, "y", 0, 0)
+    base = jnp.concatenate([activations, acts_other, gradients, grads_other])
+    up1, down1 = sync(*ring_step(base, base))
+    up2, down2 = sync(*ring_step(up1, down1))
+    up3, down3, own = sync(*ring_step(up2, down2), own)
+    acts4, grads4, other = sync(shift(up3[:2], "z", 1), shift(down3[2:], "z", -1), shift(own, "c", 1))
+    ring = [(base, 0), (up1, -1), (down1, 1), (up2, -2), (down2, 2), (up3, -3), (down3, 3)]
+
+    acts_entries = [(a, 0, ((o, 0), (o, 1))) for a, o in ring + [(acts4, -4)]]
+    acts_part = rotate(at, acts_entries, own, other, 0)
     acts_in = lax.all_to_all(acts_part.reshape(16, 32, TOK), ("xl", "c", "y"), 0, 0)
-
-    four_other = shift(up4[2:], "xh", 1)
-    other_out = shift(after(own_out, acts_part), "c", 1)
-    grads_entries = [(a, 2, ((o, 0),)) for a, o in ring]
-    grads_entries += [(near_other, 0, tuple((o, 1) for o in (0, -1, 1, -2, 2)))]
-    grads_entries += [(three_other, 0, ((-3, 1), (3, 1))), (four_other, 0, ((4, 1),))]
-    grads_part = rotate(at, grads_entries, own_out, other_out)
+    grads_entries = [(a, 1, ((o, 0), (o, 1))) for a, o in ring] + [(grads4, 0, ((4, 0), (4, 1)))]
+    grads_part = rotate(after(at, acts_part), grads_entries, own, other, 1)
+    acts_in, grads_part = sync(acts_in, grads_part)
     grads_in = lax.all_to_all(grads_part, "y", 0, 0)
 
     acts = jnp.sum(acts_in.reshape(4, 4, 32, TOK), axis=1).astype(BF16)[None]
-    r0 = jnp.concatenate([acts, shift(acts, "xh", 1)])
+    r0 = pair(acts)
     r_up1, r_down1 = sync(*ring_step(r0, r0))
     r_up2, r_down2, grads_in = sync(*ring_step(r_up1, r_down1), grads_in)
     grads = jnp.sum(grads_in, axis=0).astype(BF16)
@@ -204,10 +207,9 @@
     r_up4 = shift(r_up3, "z", 1)
     rot_grads = [rot_own, shift(rot_own, "c", 1)]
     rot_acts = [r0, r_up1, r_down1, r_up2, r_down2, r_up3, r_down3, r_up4]
-    rot_places = [((o, 0), (o, 1)) for _, o in ring]
-
-    scale = 1.0 / (TOK * 4)
-    part = products(at, rot_acts, rot_places, rot_grads, scale)
+    rot_places = [((o, 0), (o, 1)) for _, o in ring] + [((-4, 0), (-4, 1))]
+
+    part = products(at, rot_acts, rot_places, rot_grads, 1.0 / (TOK * 4))
     return weave(lax.all_to_all(part, "y", 0, 0))
 
 

time: 198 us -> 191 us (0.965)
  starting transfers between devices: 57.1 us -> 51.6 us
  Pallas kernels: 26.4 us -> 24 us
    ppermute x22 -> x20, waiting for transfers between devices: 83.9 us -> 72.7 us  [shift(): return lax.ppermute(x, axis, [(i, (i + by) % n) for i in range(n)])]
    all_to_all x1, waiting for transfers between devices: 0.01 us -> 7.8 us  [body(): lax.all_to_all(acts_part.reshape(16, 32, TOK), ('xl', 'c', 'y'), 0, 0)]
    all_to_all x2 -> x1, starting transfers between devices: 8.93 us -> 5.02 us  [body(): own = lax.all_to_all(mine, 'y', 0, 0)]
    all_to_all x2 -> x1, waiting for transfers between devices: 0.01 us -> 2.87 us  [body(): own = lax.all_to_all(mine, 'y', 0, 0)]
    pallas_call x2 -> x1, Pallas kernels: 7.9 us -> 5.51 us  [split_bases(): pl.pallas_call(split_kernel, grid_spec=pltpu.PrefetchScalarGridSpec(num_s...]
    ppermute x22 -> x20, starting transfers between devices: 32.1 us -> 33.1 us  [shift(): return lax.ppermute(x, axis, [(i, (i + by) % n) for i in range(n)])]
    unnamed x14 -> x15, local copies, waits for them, and re-layouts: 4.71 us -> 4.96 us
  transfers between devices with their start and end apart: 27 -> 24, of which waited for: 16 -> 15; matrix products, arithmetic and copies ran while one was open for 3% -> 2% of each run, Pallas kernels for 10% -> 6%
where the time goes in v6:
time: 191 us; the launch traced here: 190 us
  waiting for transfers between devices  87.2 us (46%)
  starting transfers between devices  51.6 us (27%)
  Pallas kernels  24 us (13%)
  blocking collectives  17.7 us (9%)
  local copies, waits for them, and re-layouts  7.56 us (4%)
    ppermute x20, waiting for transfers between devices, shift(): return lax.ppermute(x, axis, [(i, (i + by) % n) for i in range(n)])  72.7 us
    ppermute x20, starting transfers between devices, shift(): return lax.ppermute(x, axis, [(i, (i + by) % n) for i in range(n)])  33.1 us
    all_to_all x1, blocking collectives, body(): return weave(lax.all_to_all(part, 'y', 0, 0))  17.7 us
    pallas_call x2, Pallas kernels, rotate(): pl.pallas_call(functools.partial(rotate_kernel, [parts for _, _, parts in...  12.7 us
    all_to_all x1, waiting for transfers between devices, body(): lax.all_to_all(acts_part.reshape(16, 32, TOK), ('xl', 'c', 'y'), 0, 0)  7.8 us
    pallas_call x1, Pallas kernels, split_bases(): pl.pallas_call(split_kernel, grid_spec=pltpu.PrefetchScalarGridSpec(num_s...  5.51 us
    all_to_all x1, starting transfers between devices, body(): rot_own = lax.all_to_all(copies, ('xl', 'y'), 0, 0).reshape(2, 4, COLS, TOK)  5.38 us
    all_to_all x1, starting transfers between devices, body(): own = lax.all_to_all(mine, 'y', 0, 0)  5.02 us
  transfers between devices with their start and end apart: 24, of which 15 were waited for; matrix products, arithmetic and copies ran while one was open for 2% of the time, Pallas kernels for 6%

profile of v6, /device:TPU:2, one launch (start us, length us, event | category | flops | bytes accessed | tf_op | source)
XLA Modules:
  0.0 189.7 jit_solution(1730324912471566366)
XLA Ops:
  0.0 2.1 %collective-permute-start = (bf16[1,512,128]{2,1,0:T(8,128)(2,1)}, bf16[1,512,128]{2,1,0:T(8,128)(2,1)S(1)}, u32[]{:S(2)}, u32[]{:S(2)}) collective-permute-start(bf16[1,512,128]{2,1,0:T(8,128)(2,1)} %param.4), channel_id=1, source_target_pairs={{0,8},{8,0},{1,9},{9,1},{2,10},{10,2},{3,11},{11,3},{4,12},{12,4},... | collective-permute-start | bytes 393224 | tf_op jit(solution)/shard_map/ppermute | solution.py:24
  2.1 1.4 collective-permute-start.1
  3.5 5.5 %shard_map.46 = bf16[4,2048,256]{2,1,0:T(8,128)(2,1)S(1)} custom-call(s32[1]{0:T(128)} %bitcast.4.core_ref, f32[8192,128]{1,0:T(8,128)} %in_ref.1, f32[8192,128]{1,0:T(8,128)} %out_ref.1), custom_call_target="tpu_custom_call" | custom-call | flops 1048576 | bytes 8388608 | tf_op jit(solution)/shard_map/pallas_call | solution.py:49
  9.1 2.0 %copy-done = bf16[4,2048,256]{2,1,0:T(8,128)(2,1)} copy-done((bf16[4,2048,256]{2,1,0:T(8,128)(2,1)}, bf16[4,2048,256]{2,1,0:T(8,128)(2,1)S(1)}, u32[]{:S(2)}) %copy-start) | copy-done | bytes 4194328
  11.1 0.0 collective-permute-done
  11.1 0.0 collective-permute-done.1
  11.1 5.0 %all-to-all-start = ((bf16[4,2048,256]{2,1,0:T(8,128)(2,1)}), bf16[4,2048,256]{2,1,0:T(8,128)(2,1)}, u32[]{:S(2)}, u32[]{:S(2)}) async-start(bf16[4,2048,256]{2,1,0:T(8,128)(2,1)} %copy-done), calls=%async_computation | async-start | bytes 8388608 | tf_op jit(solution)/shard_map/all_to_all | solution.py:183
  16.2 5.9 %collective-permute-start.3 = (bf16[4,512,128]{2,1,0:T(8,128)(2,1)S(1)}, bf16[4,512,128]{2,1,0:T(8,128)(2,1)S(1)}, u32[]{:S(2)}, u32[]{:S(2)}) collective-permute-start(bf16[4,512,128]{2,1,0:T(8,128)(2,1)S(1)} %constant_dynamic-update-slice_fusion.refs_0_), channel_id=1, source_target_pairs={{0,7},{1,0},{2,1},{3,2},{4,3},{5,4},{6,5},{7,6},{8,15},{9,8},{10,9... | collective-permute-start | bytes 1572872 | tf_op jit(solution)/shard_map/ppermute | solution.py:24
  22.2 0.0 collective-permute-start.2
  22.2 10.6 %collective-permute-done.3.refs_2_ = bf16[4,512,128]{2,1,0:T(8,128)(2,1)S(1)} collective-permute-done((bf16[4,512,128]{2,1,0:T(8,128)(2,1)S(1)}, bf16[4,512,128]{2,1,0:T(8,128)(2,1)S(1)}, u32[]{:S(2)}, u32[]{:S(2)}) %collective-permute-start.3) | collective-permute-done | bytes 524320 | tf_op jit(solution)/shard_map/ppermute | solution.py:24
  32.8 3.4 %collective-permute-done.2.refs_1_ = bf16[4,512,128]{2,1,0:T(8,128)(2,1)S(1)} collective-permute-done((bf16[4,512,128]{2,1,0:T(8,128)(2,1)S(1)}, bf16[4,512,128]{2,1,0:T(8,128)(2,1)S(1)}, u32[]{:S(2)}, u32[]{:S(2)}) %collective-permute-start.2) | collective-permute-done | bytes 524320 | tf_op jit(solution)/shard_map/ppermute | solution.py:24
  36.2 0.0 collective-permute-start.4
  36.2 3.2 %collective-permute-start.5 = (bf16[4,512,128]{2,1,0:T(8,128)(2,1)S(1)}, bf16[4,512,128]{2,1,0:T(8,128)(2,1)S(1)}, u32[]{:S(2)}, u32[]{:S(2)}) collective-permute-start(bf16[4,512,128]{2,1,0:T(8,128)(2,1)S(1)} %collective-permute-done.3.refs_2_), channel_id=1, source_target_pairs={{0,7},{1,0},{2,1},{3,2},{4,3},{5,4},{6,5},{7,6},{8,15},{9,8},{10,9... | collective-permute-start | bytes 1572872 | tf_op jit(solution)/shard_map/ppermute | solution.py:24
  39.4 10.0 %collective-permute-done.4.refs_3_ = bf16[4,512,128]{2,1,0:T(8,128)(2,1)S(1)} collective-permute-done((bf16[4,512,128]{2,1,0:T(8,128)(2,1)S(1)}, bf16[4,512,128]{2,1,0:T(8,128)(2,1)S(1)}, u32[]{:S(2)}, u32[]{:S(2)}) %collective-permute-start.4) | collective-permute-done | bytes 524320 | tf_op jit(solution)/shard_map/ppermute | solution.py:24
  49.4 0.0 collective-permute-done.5.refs_4_
  49.4 0.0 collective-permute-start.6
  49.4 3.2 %collective-permute-start.7 = (bf16[4,512,128]{2,1,0:T(8,128)(2,1)S(1)}, bf16[4,512,128]{2,1,0:T(8,128)(2,1)S(1)}, u32[]{:S(2)}, u32[]{:S(2)}) collective-permute-start(bf16[4,512,128]{2,1,0:T(8,128)(2,1)S(1)} %collective-permute-done.5.refs_4_), channel_id=1, source_target_pairs={{0,7},{1,0},{2,1},{3,2},{4,3},{5,4},{6,5},{7,6},{8,15},{9,8},{10,9... | collective-permute-start | bytes 1572872 | tf_op jit(solution)/shard_map/ppermute | solution.py:24
  52.7 0.8 copy-done.1
  53.5 8.4 %collective-permute-done.6.refs_5_ = bf16[4,512,128]{2,1,0:T(8,128)(2,1)S(1)} collective-permute-done((bf16[4,512,128]{2,1,0:T(8,128)(2,1)S(1)}, bf16[4,512,128]{2,1,0:T(8,128)(2,1)S(1)}, u32[]{:S(2)}, u32[]{:S(2)}) %collective-permute-start.6) | collective-permute-done | bytes 524320 | tf_op jit(solution)/shard_map/ppermute | solution.py:24
  61.8 0.0 collective-permute-done.7.refs_6_
  61.8 2.9 %all-to-all-done.refs_8_ = bf16[4,2048,256]{2,1,0:T(8,128)(2,1)} async-done(((bf16[4,2048,256]{2,1,0:T(8,128)(2,1)}), bf16[4,2048,256]{2,1,0:T(8,128)(2,1)}, u32[]{:S(2)}, u32[]{:S(2)}) %all-to-all-start) | async-done | bytes 4194336 | tf_op jit(solution)/shard_map/all_to_all | solution.py:183
  64.7 0.0 collective-permute-start.10
  64.7 0.7 slice.6
  65.4 0.7 slice.7
  66.2 5.9 %collective-permute-start.9 = (bf16[2,512,128]{2,1,0:T(8,128)(2,1)}, bf16[2,512,128]{2,1,0:T(8,128)(2,1)S(1)}, u32[]{:S(2)}, u32[]{:S(2)}) collective-permute-start(bf16[2,512,128]{2,1,0:T(8,128)(2,1)} %slice.7), channel_id=1, source_target_pairs={{0,7},{1,0},{2,1},{3,2},{4,3},{5,4},{6,5},{7,6},{8,15},{9,8},{10,9... | collective-permute-start | bytes 786440 | tf_op jit(solution)/shard_map/ppermute | solution.py:24
  72.0 0.0 collective-permute-start.8
  72.0 0.1 stack.23.at_ref
  72.1 6.5 %collective-permute-done.9.refs_7_ = bf16[2,512,128]{2,1,0:T(8,128)(2,1)S(1)} collective-permute-done((bf16[2,512,128]{2,1,0:T(8,128)(2,1)}, bf16[2,512,128]{2,1,0:T(8,128)(2,1)S(1)}, u32[]{:S(2)}, u32[]{:S(2)}) %collective-permute-start.9) | collective-permute-done | bytes 262176 | tf_op jit(solution)/shard_map/ppermute | solution.py:24
  78.6 3.4 %collective-permute-done.8.refs_7_ = bf16[2,512,128]{2,1,0:T(8,128)(2,1)} collective-permute-done((bf16[2,512,128]{2,1,0:T(8,128)(2,1)}, bf16[2,512,128]{2,1,0:T(8,128)(2,1)}, u32[]{:S(2)}, u32[]{:S(2)}) %collective-permute-start.8) | collective-permute-done | bytes 262176 | tf_op jit(solution)/shard_map/ppermute | solution.py:24
  82.0 0.0 collective-permute-done.10.refs_9_
  82.0 1.0 copy-done.2
  83.0 6.4 %shard_map.47 = f32[4,128,512]{2,1,0:T(8,128)} custom-call(s32[5]{0:T(128)S(1)} %stack.23.at_ref, bf16[4,512,128]{2,1,0:T(8,128)(2,1)S(1)} %constant_dynamic-update-slice_fusion.refs_0_, bf16[4,512,128]{2,1,0:T(8,128)(2,1)S(1)} %collective-permute-done.2.refs_1_, bf16[4,512,128]{2,1,0:T(8,128)(2,1)S(1)} %collective-permute-done.3.refs_2_, ...), custom_call_target="tpu_custom_call" | custom-call | flops 2147483648 | bytes 7340032 | tf_op jit(solution)/shard_map/pallas_call | solution.py:89
  89.4 4.7 %all-to-all-start.1 = ((f32[16,32,512]{2,1,0:T(8,128)}), f32[16,32,512]{2,1,0:T(8,128)}, u32[]{:S(2)}, u32[]{:S(2)}) async-start(f32[16,32,512]{2,1,0:T(8,128)} %bitcast.5), calls=%async_computation.1 | async-start | bytes 2097152 | tf_op jit(solution)/shard_map/all_to_all | solution.py:193
  94.1 1.0 copy-done.3
  95.1 6.3 %shard_map.48 = f32[4,128,512]{2,1,0:T(8,128)} custom-call(s32[5]{0:T(128)S(1)} %stack.23.at_ref, bf16[4,512,128]{2,1,0:T(8,128)(2,1)S(1)} %constant_dynamic-update-slice_fusion.refs_0_, bf16[4,512,128]{2,1,0:T(8,128)(2,1)S(1)} %collective-permute-done.2.refs_1_, bf16[4,512,128]{2,1,0:T(8,128)(2,1)S(1)} %collective-permute-done.3.refs_2_, ...), custom_call_target="tpu_custom_call" | custom-call | flops 2147483648 | bytes 7340032 | tf_op jit(solution)/shard_map/pallas_call | solution.py:89
  101.4 7.8 %all-to-all-done.1 = f32[16,32,512]{2,1,0:T(8,128)} async-done(((f32[16,32,512]{2,1,0:T(8,128)}), f32[16,32,512]{2,1,0:T(8,128)}, u32[]{:S(2)}, u32[]{:S(2)}) %all-to-all-start.1) | async-done | bytes 1048608 | tf_op jit(solution)/shard_map/all_to_all | solution.py:193
  109.2 3.5 %all-to-all-start.2 = ((f32[4,128,512]{2,1,0:T(8,128)}), f32[4,128,512]{2,1,0:T(8,128)S(1)}, u32[]{:S(2)}, u32[]{:S(2)}) async-start(f32[4,128,512]{2,1,0:T(8,128)} %shard_map.48), calls=%async_computation.2 | async-start | bytes 2097152 | tf_op jit(solution)/shard_map/all_to_all | solution.py:197
  112.7 1.3 bitcast_reduce_fusion
  114.1 2.5 %collective-permute-start.11 = (bf16[1,4,32,512]{3,2,1,0:T(8,128)(2,1)S(1)}, bf16[1,4,32,512]{3,2,1,0:T(8,128)(2,1)S(1)}, u32[]{:S(2)}, u32[]{:S(2)}) collective-permute-start(bf16[1,4,32,512]{3,2,1,0:T(8,128)(2,1)S(1)} %bitcast.14), channel_id=1, source_target_pairs={{0,8},{8,0},{1,9},{9,1},{2,10},{10,2},{3,11},{11,3},{4,12},{12,4},... | collective-permute-start | bytes 393224 | tf_op jit(solution)/shard_map/ppermute | solution.py:24
  116.6 4.7 %collective-permute-done.11 = bf16[1,4,32,512]{3,2,1,0:T(8,128)(2,1)S(1)} collective-permute-done((bf16[1,4,32,512]{3,2,1,0:T(8,128)(2,1)S(1)}, bf16[1,4,32,512]{3,2,1,0:T(8,128)(2,1)S(1)}, u32[]{:S(2)}, u32[]{:S(2)}) %collective-permute-start.11) | collective-permute-done | bytes 131104 | tf_op jit(solution)/shard_map/ppermute | solution.py:24
  121.3 0.4 collective-permute-start.13
  121.8 1.8 collective-permute-start.12
  123.6 5.6 %collective-permute-done.13.refs_2_ = bf16[2,4,32,512]{3,2,1,0:T(8,128)(2,1)S(1)} collective-permute-done((bf16[2,4,32,512]{3,2,1,0:T(8,128)(2,1)S(1)}, bf16[2,4,32,512]{3,2,1,0:T(8,128)(2,1)S(1)}, u32[]{:S(2)}, u32[]{:S(2)}) %collective-permute-start.13) | collective-permute-done | bytes 262176 | tf_op jit(solution)/shard_map/ppermute | solution.py:24
  129.2 1.3 collective-permute-done.12.refs_1_
  130.5 0.4 collective-permute-start.14
  131.0 2.8 %collective-permute-start.15 = (bf16[2,4,32,512]{3,2,1,0:T(8,128)(2,1)S(1)}, bf16[2,4,32,512]{3,2,1,0:T(8,128)(2,1)S(1)}, u32[]{:S(2)}, u32[]{:S(2)}) collective-permute-start(bf16[2,4,32,512]{3,2,1,0:T(8,128)(2,1)S(1)} %collective-permute-done.13.refs_2_), channel_id=1, source_target_pairs={{0,7},{1,0},{2,1},{3,2},{4,3},{5,4},{6,5},{7,6},{8,15},{9,8},{10,9... | collective-permute-start | bytes 786440 | tf_op jit(solution)/shard_map/ppermute | solution.py:24
  133.8 4.6 %collective-permute-done.14.refs_3_ = bf16[2,4,32,512]{3,2,1,0:T(8,128)(2,1)S(1)} collective-permute-done((bf16[2,4,32,512]{3,2,1,0:T(8,128)(2,1)S(1)}, bf16[2,4,32,512]{3,2,1,0:T(8,128)(2,1)S(1)}, u32[]{:S(2)}, u32[]{:S(2)}) %collective-permute-start.14) | collective-permute-done | bytes 262176 | tf_op jit(solution)/shard_map/ppermute | solution.py:24
  138.3 0.0 collective-permute-done.15.refs_4_
  138.4 0.0 all-to-all-done.2
  138.4 0.1 reduce_sum.19
  138.5 1.1 broadcast_in_dim.4
  139.5 5.4 %all-to-all-start.3 = ((bf16[8,128,512]{2,1,0:T(8,128)(2,1)}), bf16[8,128,512]{2,1,0:T(8,128)(2,1)S(1)}, u32[]{:S(2)}, u32[]{:S(2)}) async-start(bf16[8,128,512]{2,1,0:T(8,128)(2,1)} %broadcast_in_dim.4), calls=%async_computation.3 | async-start | bytes 2097152 | tf_op jit(solution)/shard_map/all_to_all | solution.py:205
  144.9 0.0 collective-permute-start.16
  144.9 3.2 %collective-permute-start.17 = (bf16[2,4,32,512]{3,2,1,0:T(8,128)(2,1)S(1)}, bf16[2,4,32,512]{3,2,1,0:T(8,128)(2,1)S(1)}, u32[]{:S(2)}, u32[]{:S(2)}) collective-permute-start(bf16[2,4,32,512]{3,2,1,0:T(8,128)(2,1)S(1)} %collective-permute-done.15.refs_4_), channel_id=1, source_target_pairs={{0,7},{1,0},{2,1},{3,2},{4,3},{5,4},{6,5},{7,6},{8,15},{9,8},{10,9... | collective-permute-start | bytes 786440 | tf_op jit(solution)/shard_map/ppermute | solution.py:24
  148.1 4.3 %collective-permute-done.16.refs_5_ = bf16[2,4,32,512]{3,2,1,0:T(8,128)(2,1)S(1)} collective-permute-done((bf16[2,4,32,512]{3,2,1,0:T(8,128)(2,1)S(1)}, bf16[2,4,32,512]{3,2,1,0:T(8,128)(2,1)S(1)}, u32[]{:S(2)}, u32[]{:S(2)}) %collective-permute-start.16) | collective-permute-done | bytes 262176 | tf_op jit(solution)/shard_map/ppermute | solution.py:24
  152.5 0.0 collective-permute-done.17.refs_6_
  152.5 3.8 %all-to-all-done.3 = bf16[8,128,512]{2,1,0:T(8,128)(2,1)S(1)} async-done(((bf16[8,128,512]{2,1,0:T(8,128)(2,1)}), bf16[8,128,512]{2,1,0:T(8,128)(2,1)S(1)}, u32[]{:S(2)}, u32[]{:S(2)}) %all-to-all-start.3) | async-done | bytes 1048608 | tf_op jit(solution)/shard_map/all_to_all | solution.py:205
  156.2 0.0 collective-permute-start.19
  156.2 0.0 collective-permute-start.18
  156.2 9.9 %collective-permute-done.18.refs_7_ = bf16[2,4,32,512]{3,2,1,0:T(8,128)(2,1)S(1)} collective-permute-done((bf16[2,4,32,512]{3,2,1,0:T(8,128)(2,1)S(1)}, bf16[2,4,32,512]{3,2,1,0:T(8,128)(2,1)S(1)}, u32[]{:S(2)}, u32[]{:S(2)}) %collective-permute-start.18) | collective-permute-done | bytes 262176 | tf_op jit(solution)/shard_map/ppermute | solution.py:24
  166.2 0.0 collective-permute-done.19.refs_9_
  166.2 3.5 %shard_map.49 = f32[4,128,512]{2,1,0:T(8,128)S(1)} custom-call(s32[5]{0:T(128)S(1)} %stack.23.at_ref, bf16[2,4,32,512]{3,2,1,0:T(8,128)(2,1)S(1)} %pad_maximum_fusion.refs_0_, bf16[2,4,32,512]{3,2,1,0:T(8,128)(2,1)S(1)} %collective-permute-done.12.refs_1_, bf16[2,4,32,512]{3,2,1,0:T(8,128)(2,1)S(1)} %collective-permute-done.13.refs_2_, ...), custom_call_target="tpu_custom_call" | custom-call | flops 1073741824 | bytes 5242880 | tf_op jit(solution)/shard_map/pallas_call | solution.py:128
  169.7 17.7 %all_to_all.25.in_ref = f32[4,128,512]{2,1,0:T(8,128)S(1)} all-to-all(f32[4,128,512]{2,1,0:T(8,128)S(1)} %shard_map.49), channel_id=1, replica_groups=mesh['xl'=2,'c'=2,'y'=4,'xh'=2,'z'=8] {'y'}, dimensions={0} | all-to-all | bytes 2097152 | tf_op jit(solution)/shard_map/all_to_all | solution.py:213
  187.3 2.4 %shard_map.50 = f32[128,2048]{1,0:T(8,128)} custom-call(f32[4,128,512]{2,1,0:T(8,128)S(1)} %all_to_all.25.in_ref), custom_call_target="tpu_custom_call" | custom-call | tf_op jit(solution)/shard_map/pallas_call | solution.py:151
  (13 shorter events, 0.1 us)
Async XLA Ops:
  0.0 11.1 %collective-permute-start = (bf16[1,512,128]{2,1,0:T(8,128)(2,1)}, bf16[1,512,128]{2,1,0:T(8,128)(2,1)S(1)}, u32[]{:S(2)}, u32[]{:S(2)}) collective-permute-start(bf16[1,512,128]{2,1,0:T(8,128)(2,1)} %param.4), channel_id=1, source_target_pairs={{0,8},{8,0},{1,9},{9,1},{2,10},{10,2},{3,11},{11,3},{4,12},{12,4},... | collective-permute-start | bytes 393224 | tf_op jit(solution)/shard_map/ppermute | solution.py:24
  2.1 9.0 %collective-permute-start.1 = (bf16[1,512,128]{2,1,0:T(8,128)(2,1)}, bf16[1,512,128]{2,1,0:T(8,128)(2,1)S(1)}, u32[]{:S(2)}, u32[]{:S(2)}) collective-permute-start(bf16[1,512,128]{2,1,0:T(8,128)(2,1)} %param.5), channel_id=1, source_target_pairs={{0,8},{8,0},{1,9},{9,1},{2,10},{10,2},{3,11},{11,3},{4,12},{12,4},... | collective-permute-start | bytes 393224 | tf_op jit(solution)/shard_map/ppermute | solution.py:24
  9.0 2.0 %copy-start = (bf16[4,2048,256]{2,1,0:T(8,128)(2,1)}, bf16[4,2048,256]{2,1,0:T(8,128)(2,1)S(1)}, u32[]{:S(2)}) copy-start(bf16[4,2048,256]{2,1,0:T(8,128)(2,1)S(1)} %shard_map.46) | copy-start | bytes 12582916
  11.1 5.0 %copy-start.4 = (bf16[1,512,128]{2,1,0:T(8,128)(2,1)S(1)}, bf16[1,512,128]{2,1,0:T(8,128)(2,1)}, u32[]{:S(2)}) copy-start(bf16[1,512,128]{2,1,0:T(8,128)(2,1)} %param.4) | copy-start | bytes 393220
  11.1 5.1 %copy-start.5 = (bf16[1,512,128]{2,1,0:T(8,128)(2,1)S(1)}, bf16[1,512,128]{2,1,0:T(8,128)(2,1)}, u32[]{:S(2)}) copy-start(bf16[1,512,128]{2,1,0:T(8,128)(2,1)} %param.5) | copy-start | bytes 393220
  11.1 53.6 %all-to-all-start = ((bf16[4,2048,256]{2,1,0:T(8,128)(2,1)}), bf16[4,2048,256]{2,1,0:T(8,128)(2,1)}, u32[]{:S(2)}, u32[]{:S(2)}) async-start(bf16[4,2048,256]{2,1,0:T(8,128)(2,1)} %copy-done), calls=%async_computation | async-start | bytes 8388608 | tf_op jit(solution)/shard_map/all_to_all | solution.py:183
  16.2 16.6 %collective-permute-start.3 = (bf16[4,512,128]{2,1,0:T(8,128)(2,1)S(1)}, bf16[4,512,128]{2,1,0:T(8,128)(2,1)S(1)}, u32[]{:S(2)}, u32[]{:S(2)}) collective-permute-start(bf16[4,512,128]{2,1,0:T(8,128)(2,1)S(1)} %constant_dynamic-update-slice_fusion.refs_0_), channel_id=1, source_target_pairs={{0,7},{1,0},{2,1},{3,2},{4,3},{5,4},{6,5},{7,6},{8,15},{9,8},{10,9... | collective-permute-start | bytes 1572872 | tf_op jit(solution)/shard_map/ppermute | solution.py:24
  22.2 14.0 %collective-permute-start.2 = (bf16[4,512,128]{2,1,0:T(8,128)(2,1)S(1)}, bf16[4,512,128]{2,1,0:T(8,128)(2,1)S(1)}, u32[]{:S(2)}, u32[]{:S(2)}) collective-permute-start(bf16[4,512,128]{2,1,0:T(8,128)(2,1)S(1)} %constant_dynamic-update-slice_fusion.refs_0_), channel_id=1, source_target_pairs={{0,1},{1,2},{2,3},{3,4},{4,5},{5,6},{6,7},{7,0},{8,9},{9,10},{10,1... | collective-permute-start | bytes 1572872 | tf_op jit(solution)/shard_map/ppermute | solution.py:24
  36.2 13.2 %collective-permute-start.4 = (bf16[4,512,128]{2,1,0:T(8,128)(2,1)S(1)}, bf16[4,512,128]{2,1,0:T(8,128)(2,1)S(1)}, u32[]{:S(2)}, u32[]{:S(2)}) collective-permute-start(bf16[4,512,128]{2,1,0:T(8,128)(2,1)S(1)} %collective-permute-done.2.refs_1_), channel_id=1, source_target_pairs={{0,1},{1,2},{2,3},{3,4},{4,5},{5,6},{6,7},{7,0},{8,9},{9,10},{10,1... | collective-permute-start | bytes 1572872 | tf_op jit(solution)/shard_map/ppermute | solution.py:24
  36.2 13.2 %collective-permute-start.5 = (bf16[4,512,128]{2,1,0:T(8,128)(2,1)S(1)}, bf16[4,512,128]{2,1,0:T(8,128)(2,1)S(1)}, u32[]{:S(2)}, u32[]{:S(2)}) collective-permute-start(bf16[4,512,128]{2,1,0:T(8,128)(2,1)S(1)} %collective-permute-done.3.refs_2_), channel_id=1, source_target_pairs={{0,7},{1,0},{2,1},{3,2},{4,3},{5,4},{6,5},{7,6},{8,15},{9,8},{10,9... | collective-permute-start | bytes 1572872 | tf_op jit(solution)/shard_map/ppermute | solution.py:24
  49.4 12.4 %collective-permute-start.6 = (bf16[4,512,128]{2,1,0:T(8,128)(2,1)S(1)}, bf16[4,512,128]{2,1,0:T(8,128)(2,1)S(1)}, u32[]{:S(2)}, u32[]{:S(2)}) collective-permute-start(bf16[4,512,128]{2,1,0:T(8,128)(2,1)S(1)} %collective-permute-done.4.refs_3_), channel_id=1, source_target_pairs={{0,1},{1,2},{2,3},{3,4},{4,5},{5,6},{6,7},{7,0},{8,9},{9,10},{10,1... | collective-permute-start | bytes 1572872 | tf_op jit(solution)/shard_map/ppermute | solution.py:24
  49.4 12.4 %collective-permute-start.7 = (bf16[4,512,128]{2,1,0:T(8,128)(2,1)S(1)}, bf16[4,512,128]{2,1,0:T(8,128)(2,1)S(1)}, u32[]{:S(2)}, u32[]{:S(2)}) collective-permute-start(bf16[4,512,128]{2,1,0:T(8,128)(2,1)S(1)} %collective-permute-done.5.refs_4_), channel_id=1, source_target_pairs={{0,7},{1,0},{2,1},{3,2},{4,3},{5,4},{6,5},{7,6},{8,15},{9,8},{10,9... | collective-permute-start | bytes 1572872 | tf_op jit(solution)/shard_map/ppermute | solution.py:24
  52.7 0.8 copy-start.1
  64.7 17.3 %collective-permute-start.10 = (bf16[4,2048,256]{2,1,0:T(8,128)(2,1)}, bf16[4,2048,256]{2,1,0:T(8,128)(2,1)}, u32[]{:S(2)}, u32[]{:S(2)}) collective-permute-start(bf16[4,2048,256]{2,1,0:T(8,128)(2,1)} %all-to-all-done.refs_8_), channel_id=1, source_target_pairs={{0,64},{64,0},{1,65},{65,1},{2,66},{66,2},{3,67},{67,3},{4,68},{68... | collective-permute-start | bytes 12582920 | tf_op jit(solution)/shard_map/ppermute | solution.py:24
  66.2 12.4 %collective-permute-start.9 = (bf16[2,512,128]{2,1,0:T(8,128)(2,1)}, bf16[2,512,128]{2,1,0:T(8,128)(2,1)S(1)}, u32[]{:S(2)}, u32[]{:S(2)}) collective-permute-start(bf16[2,512,128]{2,1,0:T(8,128)(2,1)} %slice.7), channel_id=1, source_target_pairs={{0,7},{1,0},{2,1},{3,2},{4,3},{5,4},{6,5},{7,6},{8,15},{9,8},{10,9... | collective-permute-start | bytes 786440 | tf_op jit(solution)/shard_map/ppermute | solution.py:24
  72.0 10.0 %collective-permute-start.8 = (bf16[2,512,128]{2,1,0:T(8,128)(2,1)}, bf16[2,512,128]{2,1,0:T(8,128)(2,1)}, u32[]{:S(2)}, u32[]{:S(2)}) collective-permute-start(bf16[2,512,128]{2,1,0:T(8,128)(2,1)} %slice.6), channel_id=1, source_target_pairs={{0,1},{1,2},{2,3},{3,4},{4,5},{5,6},{6,7},{7,0},{8,9},{9,10},{10,1... | collective-permute-start | bytes 786440 | tf_op jit(solution)/shard_map/ppermute | solution.py:24
  82.0 1.0 copy-start.2
  89.4 19.8 %all-to-all-start.1 = ((f32[16,32,512]{2,1,0:T(8,128)}), f32[16,32,512]{2,1,0:T(8,128)}, u32[]{:S(2)}, u32[]{:S(2)}) async-start(f32[16,32,512]{2,1,0:T(8,128)} %bitcast.5), calls=%async_computation.1 | async-start | bytes 2097152 | tf_op jit(solution)/shard_map/all_to_all | solution.py:193
  94.1 1.0 copy-start.3
  109.2 29.1 %all-to-all-start.2 = ((f32[4,128,512]{2,1,0:T(8,128)}), f32[4,128,512]{2,1,0:T(8,128)S(1)}, u32[]{:S(2)}, u32[]{:S(2)}) async-start(f32[4,128,512]{2,1,0:T(8,128)} %shard_map.48), calls=%async_computation.2 | async-start | bytes 2097152 | tf_op jit(solution)/shard_map/all_to_all | solution.py:197
  114.1 7.2 %collective-permute-start.11 = (bf16[1,4,32,512]{3,2,1,0:T(8,128)(2,1)S(1)}, bf16[1,4,32,512]{3,2,1,0:T(8,128)(2,1)S(1)}, u32[]{:S(2)}, u32[]{:S(2)}) collective-permute-start(bf16[1,4,32,512]{3,2,1,0:T(8,128)(2,1)S(1)} %bitcast.14), channel_id=1, source_target_pairs={{0,8},{8,0},{1,9},{9,1},{2,10},{10,2},{3,11},{11,3},{4,12},{12,4},... | collective-permute-start | bytes 393224 | tf_op jit(solution)/shard_map/ppermute | solution.py:24
  121.3 7.9 %collective-permute-start.13 = (bf16[2,4,32,512]{3,2,1,0:T(8,128)(2,1)S(1)}, bf16[2,4,32,512]{3,2,1,0:T(8,128)(2,1)S(1)}, u32[]{:S(2)}, u32[]{:S(2)}) collective-permute-start(bf16[2,4,32,512]{3,2,1,0:T(8,128)(2,1)S(1)} %pad_maximum_fusion.refs_0_), channel_id=1, source_target_pairs={{0,7},{1,0},{2,1},{3,2},{4,3},{5,4},{6,5},{7,6},{8,15},{9,8},{10,9... | collective-permute-start | bytes 786440 | tf_op jit(solution)/shard_map/ppermute | solution.py:24
  121.8 8.7 %collective-permute-start.12 = (bf16[2,4,32,512]{3,2,1,0:T(8,128)(2,1)S(1)}, bf16[2,4,32,512]{3,2,1,0:T(8,128)(2,1)S(1)}, u32[]{:S(2)}, u32[]{:S(2)}) collective-permute-start(bf16[2,4,32,512]{3,2,1,0:T(8,128)(2,1)S(1)} %pad_maximum_fusion.refs_0_), channel_id=1, source_target_pairs={{0,1},{1,2},{2,3},{3,4},{4,5},{5,6},{6,7},{7,0},{8,9},{9,10},{10,1... | collective-permute-start | bytes 786440 | tf_op jit(solution)/shard_map/ppermute | solution.py:24
  130.5 7.8 %collective-permute-start.14 = (bf16[2,4,32,512]{3,2,1,0:T(8,128)(2,1)S(1)}, bf16[2,4,32,512]{3,2,1,0:T(8,128)(2,1)S(1)}, u32[]{:S(2)}, u32[]{:S(2)}) collective-permute-start(bf16[2,4,32,512]{3,2,1,0:T(8,128)(2,1)S(1)} %collective-permute-done.12.refs_1_), channel_id=1, source_target_pairs={{0,1},{1,2},{2,3},{3,4},{4,5},{5,6},{6,7},{7,0},{8,9},{9,10},{10,1... | collective-permute-start | bytes 786440 | tf_op jit(solution)/shard_map/ppermute | solution.py:24
  131.0 7.4 %collective-permute-start.15 = (bf16[2,4,32,512]{3,2,1,0:T(8,128)(2,1)S(1)}, bf16[2,4,32,512]{3,2,1,0:T(8,128)(2,1)S(1)}, u32[]{:S(2)}, u32[]{:S(2)}) collective-permute-start(bf16[2,4,32,512]{3,2,1,0:T(8,128)(2,1)S(1)} %collective-permute-done.13.refs_2_), channel_id=1, source_target_pairs={{0,7},{1,0},{2,1},{3,2},{4,3},{5,4},{6,5},{7,6},{8,15},{9,8},{10,9... | collective-permute-start | bytes 786440 | tf_op jit(solution)/shard_map/ppermute | solution.py:24
  139.5 16.7 %all-to-all-start.3 = ((bf16[8,128,512]{2,1,0:T(8,128)(2,1)}), bf16[8,128,512]{2,1,0:T(8,128)(2,1)S(1)}, u32[]{:S(2)}, u32[]{:S(2)}) async-start(bf16[8,128,512]{2,1,0:T(8,128)(2,1)} %broadcast_in_dim.4), calls=%async_computation.3 | async-start | bytes 2097152 | tf_op jit(solution)/shard_map/all_to_all | solution.py:205
  144.9 7.6 %collective-permute-start.16 = (bf16[2,4,32,512]{3,2,1,0:T(8,128)(2,1)S(1)}, bf16[2,4,32,512]{3,2,1,0:T(8,128)(2,1)S(1)}, u32[]{:S(2)}, u32[]{:S(2)}) collective-permute-start(bf16[2,4,32,512]{3,2,1,0:T(8,128)(2,1)S(1)} %collective-permute-done.14.refs_3_), channel_id=1, source_target_pairs={{0,1},{1,2},{2,3},{3,4},{4,5},{5,6},{6,7},{7,0},{8,9},{9,10},{10,1... | collective-permute-start | bytes 786440 | tf_op jit(solution)/shard_map/ppermute | solution.py:24
  144.9 7.6 %collective-permute-start.17 = (bf16[2,4,32,512]{3,2,1,0:T(8,128)(2,1)S(1)}, bf16[2,4,32,512]{3,2,1,0:T(8,128)(2,1)S(1)}, u32[]{:S(2)}, u32[]{:S(2)}) collective-permute-start(bf16[2,4,32,512]{3,2,1,0:T(8,128)(2,1)S(1)} %collective-permute-done.15.refs_4_), channel_id=1, source_target_pairs={{0,7},{1,0},{2,1},{3,2},{4,3},{5,4},{6,5},{7,6},{8,15},{9,8},{10,9... | collective-permute-start | bytes 786440 | tf_op jit(solution)/shard_map/ppermute | solution.py:24
  156.2 9.9 %collective-permute-start.19 = (bf16[2,4,128,512]{3,2,1,0:T(8,128)(2,1)S(1)}, bf16[2,4,128,512]{3,2,1,0:T(8,128)(2,1)S(1)}, u32[]{:S(2)}, u32[]{:S(2)}) collective-permute-start(bf16[2,4,128,512]{3,2,1,0:T(8,128)(2,1)S(1)} %bitcast.12), channel_id=1, source_target_pairs={{0,64},{64,0},{1,65},{65,1},{2,66},{66,2},{3,67},{67,3},{4,68},{68... | collective-permute-start | bytes 3145736 | tf_op jit(solution)/shard_map/ppermute | solution.py:24
  156.2 9.9 %collective-permute-start.18 = (bf16[2,4,32,512]{3,2,1,0:T(8,128)(2,1)S(1)}, bf16[2,4,32,512]{3,2,1,0:T(8,128)(2,1)S(1)}, u32[]{:S(2)}, u32[]{:S(2)}) collective-permute-start(bf16[2,4,32,512]{3,2,1,0:T(8,128)(2,1)S(1)} %collective-permute-done.16.refs_5_), channel_id=1, source_target_pairs={{0,1},{1,2},{2,3},{3,4},{4,5},{5,6},{6,7},{7,0},{8,9},{9,10},{10,1... | collective-permute-start | bytes 786440 | tf_op jit(solution)/shard_map/ppermute | solution.py:24

commit v7 on v5

--- a/solution.py
+++ b/solution.py
@@ -87,80 +87,74 @@
     )(at, blocks, own, other)
 
 
-def reach_kernel(rows_ref, in_ref, own_ref, near_ref, far_ref):
-    def put(out_ref):
-        exact = in_ref[...]
-        high = exact.astype(BF16)
-        out_ref[:, :COLS] = high
-        out_ref[:, COLS:] = (exact - high.astype(F32)).astype(BF16)
-
-    step = pl.program_id(0)
-    pl.when(step < 2)(lambda: put(own_ref))
-    pl.when((step >= 2) & (step < 4))(lambda: put(near_ref))
-    pl.when(step == 4)(lambda: put(far_ref))
-
-
-def reach_basis(rows, basis):
-    return pl.pallas_call(
-        reach_kernel,
+def rotate_head_kernel(offsets, at_ref, *refs):
+    blocks, (own_ref, other_ref, out_ref, lhs) = refs[: len(offsets)], refs[len(offsets) :]
+
+    @pl.when(pl.program_id(0) == 0)
+    def _():
+        turned = lax.rem(at_ref[1] + at_ref[4], 2)
+        for side in range(2):
+            half = turned if side == 0 else 1 - turned
+            for block, offset in zip(blocks, offsets):
+                at = (half * 8 + lax.rem(at_ref[0] + 8 + offset, 8)) * COLS
+                lhs[:, pl.ds(pl.multiple_of(at, COLS), COLS)] = block[side]
+            at = (half * 8 + lax.rem(at_ref[0] + 4, 8)) * COLS
+            lhs[:, pl.ds(pl.multiple_of(at, COLS), COLS)] = jnp.zeros((TOK, COLS), BF16)
+
+    both = jnp.dot(lhs[:, :1024], own_ref[0], preferred_element_type=F32)
+    both += jnp.dot(lhs[:, 1024:], other_ref[0], preferred_element_type=F32)
+    out_ref[0] = (both[:, :COLS] + both[:, COLS:]).T
+
+
+def rotate_head(at, ring, own, other):
+    slab = pl.BlockSpec((1, 1024, 256), lambda g: (g, 0, 0))
+    return pl.pallas_call(
+        functools.partial(rotate_head_kernel, [offset for _, offset in ring]),
+        grid=(4,),
+        out_shape=jax.ShapeDtypeStruct((4, COLS, TOK), F32),
+        in_specs=[pl.BlockSpec(memory_space=pltpu.SMEM)]
+        + [whole((2, TOK, COLS))] * len(ring)
+        + [slab, slab],
+        out_specs=pl.BlockSpec((1, COLS, TOK), lambda g: (g, 0, 0)),
+        scratch_shapes=[pltpu.VMEM((TOK, 2048), BF16)],
+        compiler_params=PARAMS,
+        cost_estimate=pl.CostEstimate(
+            flops=4 * TOK * 2048 * 512, bytes_accessed=7 << 20, transcendentals=0
+        ),
+    )(at, *[block for block, _ in ring], own, other)
+
+
+def rotate_tail_kernel(at_ref, head_ref, block_ref, own_ref, other_ref, out_ref, lhs):
+    @pl.when(pl.program_id(0) == 0)
+    def _():
+        turned = lax.rem(at_ref[1] + at_ref[4], 2)
+        for side in range(2):
+            half = turned if side == 0 else 1 - turned
+            lhs[:, pl.ds(pl.multiple_of(half * COLS, COLS), COLS)] = block_ref[side]
+
+    both = jnp.dot(lhs[:, :COLS], own_ref[0], preferred_element_type=F32)
+    both += jnp.dot(lhs[:, COLS:], other_ref[0], preferred_element_type=F32)
+    out_ref[0] = head_ref[0] + (both[:, :COLS] + both[:, COLS:]).T
+
+
+def rotate_tail(at, head, block, own, other):
+    slab = pl.BlockSpec((1, COLS, 256), lambda g, at: (g, (at[0] + 4) % 8, 0))
+    part = pl.BlockSpec((1, COLS, TOK), lambda g, at: (g, 0, 0))
+    return pl.pallas_call(
+        rotate_tail_kernel,
         grid_spec=pltpu.PrefetchScalarGridSpec(
             num_scalar_prefetch=1,
-            grid=(5,),
-            in_specs=[pl.BlockSpec((1024, COLS), lambda g, rows: (rows[g], 0))],
-            out_specs=[
-                pl.BlockSpec((1024, 256), lambda g, rows: (jnp.minimum(g, 1), 0)),
-                pl.BlockSpec((1024, 256), lambda g, rows: (jnp.clip(g - 2, 0, 1), 0)),
-                pl.BlockSpec((1024, 256), lambda g, rows: (0, 0)),
-            ],
-        ),
-        out_shape=[jax.ShapeDtypeStruct((n, 256), BF16) for n in (2048, 2048, 1024)],
-        compiler_params=PARAMS,
-        cost_estimate=pl.CostEstimate(
-            flops=1 << 20, bytes_accessed=5 << 20, transcendentals=0
-        ),
-    )(rows, basis)
-
-
-def rotate_ring_kernel(places, at_ref, *refs):
-    blocks, refs = refs[: len(places)], refs[len(places) :]
-    own_ref, near_ref, near_swapped, far_ref, far_swapped, out_ref, lhs = refs
-    z, xh, y, c = at_ref[0], at_ref[1], at_ref[2], at_ref[4]
-    for block, parts in zip(blocks, places):
-        for i, (offset, side) in enumerate(parts):
-            half = xh if side == 0 else 1 - xh
-            at = (half * 8 + lax.rem(z + 8 + offset, 8)) * COLS
-            lhs[:, pl.ds(pl.multiple_of(at, COLS), COLS)] = block[i]
-
-    def put(place, both):
-        out_ref[lax.rem(place, 4)] = (both[:, :COLS] + both[:, COLS:]).T
-
-    for offset, ref in ((4, own_ref), (3 + 2 * c, near_ref), (5 - 2 * c, near_swapped)):
-        put(y + offset, jnp.dot(lhs[...], ref[...], preferred_element_type=F32))
-    mine = lhs[:, pl.ds(pl.multiple_of(c * 1024, 1024), 1024)]
-    rest = lhs[:, pl.ds(pl.multiple_of((1 - c) * 1024, 1024), 1024)]
-    both = jnp.dot(mine, far_ref[...], preferred_element_type=F32)
-    put(y + 2, both + jnp.dot(rest, far_swapped[...], preferred_element_type=F32))
-
-
-def rotate_ring(at, entries, slabs):
-    blocks = [
-        pl.BlockSpec((len(parts), *array.shape[1:]), lambda g, index=index: (index, 0, 0))
-        for array, index, parts in entries
-    ]
-    return pl.pallas_call(
-        functools.partial(rotate_ring_kernel, [parts for _, _, parts in entries]),
-        grid=(1,),
+            grid=(4,),
+            in_specs=[part, whole((2, TOK, COLS)), slab, slab],
+            out_specs=part,
+            scratch_shapes=[pltpu.VMEM((TOK, 256), BF16)],
+        ),
         out_shape=jax.ShapeDtypeStruct((4, COLS, TOK), F32),
-        in_specs=[pl.BlockSpec(memory_space=pltpu.SMEM)]
-        + blocks
-        + [whole(slab.shape) for slab in slabs],
-        out_specs=whole((4, COLS, TOK)),
-        scratch_shapes=[pltpu.VMEM((TOK, 2048), BF16)],
-        compiler_params=PARAMS,
-        cost_estimate=pl.CostEstimate(
-            flops=4 * TOK * 2048 * 512, bytes_accessed=7 << 20, transcendentals=0
-        ),
-    )(at, *[array for array, _, _ in entries], *slabs)
+        compiler_params=PARAMS,
+        cost_estimate=pl.CostEstimate(
+            flops=4 * TOK * 256 * 512, bytes_accessed=3 << 20, transcendentals=0
+        ),
+    )(at, head, block, own, other)
 
 
 def product_kernel(scale, at_ref, acts_ref, own_ref, other_ref, out_ref, right):
@@ -230,45 +224,29 @@
     return shift(up, "z", 1), shift(down, "z", -1)
 
 
-def shift_near(x):
-    pairs = [(i, (i + 1) % 4) for i in range(4)] + [(4 + i, 4 + (i + 3) % 4) for i in range(4)]
-    return lax.ppermute(x, ("c", "y"), pairs)
-
-
 def body(activations, gradients, basis_in, basis_out):
     z, xh, y, xl, c = (lax.axis_index(a) for a in ("z", "xh", "y", "xl", "c"))
     at = jnp.stack([z, xh, y, xl, c]).astype(jnp.int32)
     core = c.astype(jnp.int32).reshape(1)
-    near_y, far_y = (y + 1 + 2 * c) % 4, (y + 2) % 4
-    rows = jnp.stack(
-        [y * 2, y * 2 + 1, near_y * 2, near_y * 2 + 1, far_y * 2 + c]
-    ).astype(jnp.int32)
-
-    acts_pair, g0, mine_in, basis_out = sync(
+
+    a0, grads_pair, mine_in, basis_out = sync(
         pair(activations), pair(gradients), split_basis(core, basis_in), basis_out
     )
     own_in = lax.all_to_all(mine_in, "y", 0, 0)
-    act_blocks = lax.all_gather(acts_pair, "z")
-    own_out, near_out, far_out = reach_basis(rows, basis_out)
-    up1, down1, near_out, far_out = sync(*ring_step(g0, g0), near_out, far_out)
-    up2, down2, own_in, near_out, far_out = sync(*ring_step(up1, down1), own_in, near_out, far_out)
-    up3, down3, other_in, near_out, far_out = sync(
-        *ring_step(up2, down2), shift(own_in, "c", 1), shift_near(near_out), far_out
+    grad_blocks = lax.all_gather(grads_pair, "z")
+    up1, down1, mine_out = sync(*ring_step(a0, a0), split_basis(core, basis_out))
+    up2, down2, own_in, mine_out = sync(*ring_step(up1, down1), own_in, mine_out)
+    own_out = lax.all_to_all(mine_out, "y", 0, 0)
+    up3, down3, other_in = sync(*ring_step(up2, down2), shift(own_in, "c", 1))
+    ring = [(a0, 0), (up1, -1), (down1, 1), (up2, -2), (down2, 2), (up3, -3), (down3, 3)]
+    up4, head, grad_blocks = sync(
+        shift(up3, "z", 1), rotate_head(at, ring, own_in, other_in), grad_blocks
     )
-    up4 = shift(up3, "z", 1)
-    far_out = shift(far_out, "y", 2)
-    near_out2 = shift(near_out, "c", 1)
-    acts_part = rotate(at, act_blocks, own_in, other_in)
-    acts_part, up4, far_out, near_out2 = sync(acts_part, up4, far_out, near_out2)
+    acts_part = rotate_tail(at, head, up4, own_in, other_in)
     acts_in = lax.all_to_all(acts_part.reshape(16, 32, TOK), ("xl", "c", "y"), 0, 0)
 
-    ring = [(g0, 0), (up1, -1), (down1, 1), (up2, -2), (down2, 2), (up3, -3), (down3, 3), (up4, -4)]
-    far_out2 = shift(far_out, "c", 1)
-    grads_part = rotate_ring(
-        at,
-        [(a, 0, ((o, 0), (o, 1))) for a, o in ring],
-        (own_out, near_out, near_out2, far_out, far_out2),
-    )
+    other_out = shift(after(own_out, acts_part), "c", 1)
+    grads_part = rotate(at, grad_blocks, own_out, other_out)
     acts_in, grads_part = sync(acts_in, grads_part)
     grads_in = lax.all_to_all(grads_part, "y", 0, 0)
 

time: 184 us -> 187 us (1.016)
  Pallas kernels: 24.9 us -> 29 us
  starting transfers between devices: 32.2 us -> 36.1 us
  waiting for transfers between devices: 50.4 us -> 47.2 us
  local copies, waits for them, and re-layouts: 9.83 us -> 7.26 us
    ppermute x15 -> x13, waiting for transfers between devices: 37.9 us -> 29.5 us  [shift(): return lax.ppermute(x, axis, [(i, (i + by) % n) for i in range(n)])]
    all_to_all x0 -> x1, starting transfers between devices: none -> 4.47 us  [body(): own_out = lax.all_to_all(mine_out, 'y', 0, 0)]
    pallas_call x1 -> x2, Pallas kernels: 3.98 us -> 7.93 us  [split_basis(): pl.pallas_call(split_kernel, grid_spec=pltpu.PrefetchScalarGridSpec(num_s...]
    all_to_all x1, waiting for transfers between devices: 5.76 us -> 9.7 us  [body(): lax.all_to_all(acts_part.reshape(16, 32, TOK), ('xl', 'c', 'y'), 0, 0)]
    all_to_all x1, waiting for transfers between devices: 0.01 us -> 3.63 us  [body(): own_in = lax.all_to_all(mine_in, 'y', 0, 0)]
    unnamed x22 -> x28, local copies, waits for them, and re-layouts: 9.58 us -> 7.09 us
    ppermute x1 -> x0, starting transfers between devices: 2.34 us -> none  [shift_near(): return lax.ppermute(x, ('c', 'y'), pairs)]
    all_gather x1, waiting for transfers between devices: 2.1 us -> 0.02 us  [body(): grad_blocks = lax.all_gather(grads_pair, 'z')]
  transfers between devices with their start and end apart: 20 -> 18, of which waited for: 13 -> 11; matrix products, arithmetic and copies ran while one was open for 1% -> 0% of each run, Pallas kernels for 10% -> 13%
where the time goes in v7:
time: 187 us; the launch traced here: 185 us
  blocking collectives  49.2 us (26%)
  waiting for transfers between devices  47.2 us (25%)
  starting transfers between devices  36.1 us (19%)
  Pallas kernels  29 us (16%)
  between operations  13.5 us (7%)
  local copies, waits for them, and re-layouts  7.26 us (4%)
  other arithmetic  2.93 us (2%)
    ppermute x13, waiting for transfers between devices, shift(): return lax.ppermute(x, axis, [(i, (i + by) % n) for i in range(n)])  29.5 us
    ppermute x13, starting transfers between devices, shift(): return lax.ppermute(x, axis, [(i, (i + by) % n) for i in range(n)])  21 us
    all_to_all x1, blocking collectives, body(): grads_in = lax.all_to_all(grads_part, 'y', 0, 0)  17.6 us
    all_to_all x1, blocking collectives, body(): rot_own = lax.all_to_all(copies, ('xl', 'y'), 0, 0).reshape(2, 4, COLS, TOK)  16.4 us
    all_to_all x1, blocking collectives, body(): return weave(lax.all_to_all(part, 'y', 0, 0))  15.3 us
    all_to_all x1, waiting for transfers between devices, body(): lax.all_to_all(acts_part.reshape(16, 32, TOK), ('xl', 'c', 'y'), 0, 0)  9.7 us
    pallas_call x2, Pallas kernels, split_basis(): pl.pallas_call(split_kernel, grid_spec=pltpu.PrefetchScalarGridSpec(num_s...  7.93 us
    unnamed x28, local copies, waits for them, and re-layouts  7.09 us
  transfers between devices with their start and end apart: 18, of which 11 were waited for; matrix products, arithmetic and copies ran while one was open for 0% of the time, Pallas kernels for 13%

profile of v7, /device:TPU:2, one launch (start us, length us, event | category | flops | bytes accessed | tf_op | source)
XLA Modules:
  0.0 185.2 jit_solution(11378049375464922007)
XLA Ops:
  6.5 2.1 %collective-permute-start = (bf16[1,512,128]{2,1,0:T(8,128)(2,1)}, bf16[1,512,128]{2,1,0:T(8,128)(2,1)S(1)}, u32[]{:S(2)}, u32[]{:S(2)}) collective-permute-start(bf16[1,512,128]{2,1,0:T(8,128)(2,1)} %param.4), channel_id=1, source_target_pairs={{0,8},{8,0},{1,9},{9,1},{2,10},{10,2},{3,11},{11,3},{4,12},{12,4},... | collective-permute-start | bytes 393224 | tf_op jit(solution)/shard_map/ppermute | solution.py:24
  8.7 1.4 collective-permute-start.1
  10.1 4.0 %shard_map.46 = bf16[4,1024,256]{2,1,0:T(8,128)(2,1)} custom-call(s32[1]{0:T(128)} %bitcast.4.core_ref, f32[8192,128]{1,0:T(8,128)} %in_ref.1), custom_call_target="tpu_custom_call" | custom-call | flops 1048576 | bytes 4194304 | tf_op jit(solution)/shard_map/pallas_call | solution.py:43
  14.1 0.4 collective-permute-done
  14.5 0.0 copy-done.12
  14.5 1.8 collective-permute-done.1
  16.3 0.0 copy-done.13
  16.3 0.7 pad_maximum_fusion.1
  17.0 4.5 %all-to-all-start = ((bf16[4,1024,256]{2,1,0:T(8,128)(2,1)}), bf16[4,1024,256]{2,1,0:T(8,128)(2,1)S(1)}, u32[]{:S(2)}, u32[]{:S(2)}) async-start(bf16[4,1024,256]{2,1,0:T(8,128)(2,1)} %shard_map.46), calls=%async_computation | async-start | bytes 4194304 | tf_op jit(solution)/shard_map/all_to_all | solution.py:235
  21.5 0.0 all-gather.5.cloned.1.call-start
  21.5 0.7 all-gather.5.cloned.1.call-update
  22.2 2.0 %collective-permute-start.2 = (bf16[2,512,128]{2,1,0:T(8,128)(2,1)S(1)}, bf16[2,512,128]{2,1,0:T(8,128)(2,1)S(1)}, u32[]{:S(2)}, u32[]{:S(2)}) collective-permute-start(bf16[2,512,128]{2,1,0:T(8,128)(2,1)S(1)} %pad_maximum_fusion.refs_0_), channel_id=1, source_target_pairs={{0,1},{1,2},{2,3},{3,4},{4,5},{5,6},{6,7},{7,0},{8,9},{9,10},{10,1... | collective-permute-start | bytes 786440 | tf_op jit(solution)/shard_map/ppermute | solution.py:24
  24.2 4.0 %collective-permute-start.3 = (bf16[2,512,128]{2,1,0:T(8,128)(2,1)S(1)}, bf16[2,512,128]{2,1,0:T(8,128)(2,1)S(1)}, u32[]{:S(2)}, u32[]{:S(2)}) collective-permute-start(bf16[2,512,128]{2,1,0:T(8,128)(2,1)S(1)} %pad_maximum_fusion.refs_0_), channel_id=1, source_target_pairs={{0,7},{1,0},{2,1},{3,2},{4,3},{5,4},{6,5},{7,6},{8,15},{9,8},{10,9... | collective-permute-start | bytes 786440 | tf_op jit(solution)/shard_map/ppermute | solution.py:24
  28.3 3.9 %shard_map.47 = bf16[4,1024,256]{2,1,0:T(8,128)(2,1)} custom-call(s32[1]{0:T(128)} %bitcast.4.core_ref, f32[8192,128]{1,0:T(8,128)} %in_ref.2), custom_call_target="tpu_custom_call" | custom-call | flops 1048576 | bytes 4194304 | tf_op jit(solution)/shard_map/pallas_call | solution.py:43
  32.2 1.3 collective-permute-done.2.refs_1_
  33.5 0.0 collective-permute-done.3.refs_2_
  33.5 0.1 collective-permute-start.4
  33.6 3.2 %collective-permute-start.5 = (bf16[2,512,128]{2,1,0:T(8,128)(2,1)S(1)}, bf16[2,512,128]{2,1,0:T(8,128)(2,1)S(1)}, u32[]{:S(2)}, u32[]{:S(2)}) collective-permute-start(bf16[2,512,128]{2,1,0:T(8,128)(2,1)S(1)} %collective-permute-done.3.refs_2_), channel_id=1, source_target_pairs={{0,7},{1,0},{2,1},{3,2},{4,3},{5,4},{6,5},{7,6},{8,15},{9,8},{10,9... | collective-permute-start | bytes 786440 | tf_op jit(solution)/shard_map/ppermute | solution.py:24
  36.8 4.4 %collective-permute-done.4.refs_3_ = bf16[2,512,128]{2,1,0:T(8,128)(2,1)S(1)} collective-permute-done((bf16[2,512,128]{2,1,0:T(8,128)(2,1)S(1)}, bf16[2,512,128]{2,1,0:T(8,128)(2,1)S(1)}, u32[]{:S(2)}, u32[]{:S(2)}) %collective-permute-start.4) | collective-permute-done | bytes 262176 | tf_op jit(solution)/shard_map/ppermute | solution.py:24
  41.1 2.3 %collective-permute-done.5.refs_4_ = bf16[2,512,128]{2,1,0:T(8,128)(2,1)S(1)} collective-permute-done((bf16[2,512,128]{2,1,0:T(8,128)(2,1)S(1)}, bf16[2,512,128]{2,1,0:T(8,128)(2,1)S(1)}, u32[]{:S(2)}, u32[]{:S(2)}) %collective-permute-start.5) | collective-permute-done | bytes 262176 | tf_op jit(solution)/shard_map/ppermute | solution.py:24
  43.5 3.6 %all-to-all-done.refs_7_.own_ref = bf16[4,1024,256]{2,1,0:T(8,128)(2,1)S(1)} async-done(((bf16[4,1024,256]{2,1,0:T(8,128)(2,1)}), bf16[4,1024,256]{2,1,0:T(8,128)(2,1)S(1)}, u32[]{:S(2)}, u32[]{:S(2)}) %all-to-all-start) | async-done | bytes 2097184 | tf_op jit(solution)/shard_map/all_to_all | solution.py:235
  47.1 0.0 collective-permute-start.8
  47.1 4.5 %all-to-all-start.2 = ((bf16[4,1024,256]{2,1,0:T(8,128)(2,1)}), bf16[4,1024,256]{2,1,0:T(8,128)(2,1)}, u32[]{:S(2)}, u32[]{:S(2)}) async-start(bf16[4,1024,256]{2,1,0:T(8,128)(2,1)} %shard_map.47), calls=%async_computation.2 | async-start | bytes 4194304 | tf_op jit(solution)/shard_map/all_to_all | solution.py:239
  51.6 2.0 %collective-permute-start.6 = (bf16[2,512,128]{2,1,0:T(8,128)(2,1)S(1)}, bf16[2,512,128]{2,1,0:T(8,128)(2,1)}, u32[]{:S(2)}, u32[]{:S(2)}) collective-permute-start(bf16[2,512,128]{2,1,0:T(8,128)(2,1)S(1)} %collective-permute-done.4.refs_3_), channel_id=1, source_target_pairs={{0,1},{1,2},{2,3},{3,4},{4,5},{5,6},{6,7},{7,0},{8,9},{9,10},{10,1... | collective-permute-start | bytes 786440 | tf_op jit(solution)/shard_map/ppermute | solution.py:24
  53.6 4.0 %collective-permute-start.7 = (bf16[2,512,128]{2,1,0:T(8,128)(2,1)S(1)}, bf16[2,512,128]{2,1,0:T(8,128)(2,1)S(1)}, u32[]{:S(2)}, u32[]{:S(2)}) collective-permute-start(bf16[2,512,128]{2,1,0:T(8,128)(2,1)S(1)} %collective-permute-done.5.refs_4_), channel_id=1, source_target_pairs={{0,7},{1,0},{2,1},{3,2},{4,3},{5,4},{6,5},{7,6},{8,15},{9,8},{10,9... | collective-permute-start | bytes 786440 | tf_op jit(solution)/shard_map/ppermute | solution.py:24
  57.6 12.1 %collective-permute-done.6.refs_5_ = bf16[2,512,128]{2,1,0:T(8,128)(2,1)} collective-permute-done((bf16[2,512,128]{2,1,0:T(8,128)(2,1)S(1)}, bf16[2,512,128]{2,1,0:T(8,128)(2,1)}, u32[]{:S(2)}, u32[]{:S(2)}) %collective-permute-start.6) | collective-permute-done | bytes 262176 | tf_op jit(solution)/shard_map/ppermute | solution.py:24
  69.7 0.0 collective-permute-done.7.refs_6_
  69.7 0.7 copy-done.10
  70.4 0.0 collective-permute-done.8.refs_8_.other_ref
  70.4 0.0 collective-permute-start.9
  70.4 0.0 copy-done.2
  70.5 0.1 stack.23.at_ref
  70.6 0.9 copy-done.3
  71.5 0.9 copy-done.5
  72.5 0.9 copy-done.7
  73.4 0.9 copy-done.9
  74.4 0.9 copy-done.11
  75.3 5.2 %shard_map.48.head_ref = f32[4,128,512]{2,1,0:T(8,128)S(1)} custom-call(s32[5]{0:T(128)S(1)} %stack.23.at_ref, bf16[2,512,128]{2,1,0:T(8,128)(2,1)S(1)} %pad_maximum_fusion.refs_0_, bf16[2,512,128]{2,1,0:T(8,128)(2,1)S(1)} %copy-done.3, bf16[2,512,128]{2,1,0:T(8,128)(2,1)S(1)} %copy-done.5, bf16[2,512,128]{2,1,0:T(8,128)(2,1)S(1)} %copy-done.7, ...), custom_call_target="tpu_custom_call" | custom-call | flops 2147483648 | bytes 7340032 | tf_op jit(solution)/shard_map/pallas_call | solution.py:111
  80.5 0.0 all-gather.5.cloned.1.call-done
  80.6 0.0 collective-permute-done.9.block_ref
  80.6 4.6 %shard_map.49 = f32[4,128,512]{2,1,0:T(8,128)} custom-call(s32[5]{0:T(128)S(1)} %stack.23.at_ref, f32[4,128,512]{2,1,0:T(8,128)S(1)} %shard_map.48.head_ref, bf16[2,512,128]{2,1,0:T(8,128)(2,1)} %collective-permute-done.9.block_ref, bf16[4,1024,256]{2,1,0:T(8,128)(2,1)S(1)} %all-to-all-done.refs_7_.own_ref, ...), custom_call_target="tpu_custom_call" | custom-call | flops 268435456 | bytes 3145728 | tf_op jit(solution)/shard_map/pallas_call | solution.py:143
  85.2 0.0 all-to-all-done.2.own_ref
  85.2 0.1 collective-permute-start.10
  85.2 6.2 %all-to-all-start.1 = ((f32[16,32,512]{2,1,0:T(8,128)}), f32[16,32,512]{2,1,0:T(8,128)}, u32[]{:S(2)}, u32[]{:S(2)}) async-start(f32[16,32,512]{2,1,0:T(8,128)} %bitcast.6), calls=%async_computation.1 | async-start | bytes 2097152 | tf_op jit(solution)/shard_map/all_to_all | solution.py:246
  91.4 0.0 all-gather.7.cloned.1.call-start
  91.5 0.0 collective-permute-done.10.other_ref
  91.5 5.4 %shard_map.50 = f32[4,128,512]{2,1,0:T(8,128)S(1)} custom-call(s32[5]{0:T(128)S(1)} %stack.23.at_ref, bf16[8,2,512,128]{3,2,1,0:T(8,128)(2,1)S(1)} %bitcast.17, bf16[4,1024,256]{2,1,0:T(8,128)(2,1)} %all-to-all-done.2.own_ref, bf16[4,1024,256]{2,1,0:T(8,128)(2,1)} %collective-permute-done.10.other_ref), custom_call_target="tpu_custom_call" | custom-call | flops 2147483648 | bytes 7340032 | tf_op jit(solution)/shard_map/pallas_call | solution.py:76
  96.9 9.7 %all-to-all-done.1 = f32[16,32,512]{2,1,0:T(8,128)} async-done(((f32[16,32,512]{2,1,0:T(8,128)}), f32[16,32,512]{2,1,0:T(8,128)}, u32[]{:S(2)}, u32[]{:S(2)}) %all-to-all-start.1) | async-done | bytes 1048608 | tf_op jit(solution)/shard_map/all_to_all | solution.py:246
  106.6 1.3 bitcast_reduce_fusion
  108.0 2.0 %collective-permute-start.11 = (bf16[1,4,32,512]{3,2,1,0:T(8,128)(2,1)S(1)}, bf16[1,4,32,512]{3,2,1,0:T(8,128)(2,1)S(1)}, u32[]{:S(2)}, u32[]{:S(2)}) collective-permute-start(bf16[1,4,32,512]{3,2,1,0:T(8,128)(2,1)S(1)} %bitcast.18), channel_id=1, source_target_pairs={{0,8},{8,0},{1,9},{9,1},{2,10},{10,2},{3,11},{11,3},{4,12},{12,4},... | collective-permute-start | bytes 393224 | tf_op jit(solution)/shard_map/ppermute | solution.py:24
  110.0 4.5 %collective-permute-done.11 = bf16[1,4,32,512]{3,2,1,0:T(8,128)(2,1)S(1)} collective-permute-done((bf16[1,4,32,512]{3,2,1,0:T(8,128)(2,1)S(1)}, bf16[1,4,32,512]{3,2,1,0:T(8,128)(2,1)S(1)}, u32[]{:S(2)}, u32[]{:S(2)}) %collective-permute-start.11) | collective-permute-done | bytes 131104 | tf_op jit(solution)/shard_map/ppermute | solution.py:24
  114.5 0.7 pad_maximum_fusion.2
  115.3 0.0 all-gather.7.cloned.1.call-update
  115.3 17.6 %all_to_all.30 = f32[4,128,512]{2,1,0:T(8,128)S(1)} all-to-all(f32[4,128,512]{2,1,0:T(8,128)S(1)} %shard_map.50), channel_id=1, replica_groups=mesh['xl'=2,'c'=2,'y'=4,'xh'=2,'z'=8] {'y'}, dimensions={0} | all-to-all | bytes 2097152 | tf_op jit(solution)/shard_map/all_to_all | solution.py:251
  132.8 0.1 reduce_sum.19
  132.9 0.1 broadcast_in_dim.4
  133.0 16.4 %all_to_all.31 = bf16[8,128,512]{2,1,0:T(8,128)(2,1)S(1)} all-to-all(bf16[8,128,512]{2,1,0:T(8,128)(2,1)S(1)} %broadcast_in_dim.4), channel_id=1, replica_groups=mesh['xl'=2,'c'=2,'y'=4,'xh'=2,'z'=8] {'xl','y'}, dimensions={0} | all-to-all | bytes 2097152 | tf_op jit(solution)/shard_map/all_to_all | solution.py:258
  149.4 0.0 collective-permute-start.12
  149.4 2.7 %collective-permute-done.12.other_ref = bf16[2,4,128,512]{3,2,1,0:T(8,128)(2,1)S(1)} collective-permute-done((bf16[2,4,128,512]{3,2,1,0:T(8,128)(2,1)S(1)}, bf16[2,4,128,512]{3,2,1,0:T(8,128)(2,1)S(1)}, u32[]{:S(2)}, u32[]{:S(2)}) %collective-permute-start.12) | collective-permute-done | bytes 1048608 | tf_op jit(solution)/shard_map/ppermute | solution.py:24
  152.1 3.6 %all-gather.7.cloned.1.call-done = bf16[16,4,32,512]{3,2,1,0:T(8,128)(2,1)} async-done(((bf16[2,4,32,512]{3,2,1,0:T(8,128)(2,1)}), bf16[16,4,32,512]{3,2,1,0:T(8,128)(2,1)}) %all-gather.7.cloned.1.call-update) | async-done | bytes 2097168 | tf_op jit(solution)/shard_map/all_gather | solution.py:254
  155.7 1.6 copy-done
  157.3 3.5 %shard_map.51 = f32[4,128,512]{2,1,0:T(8,128)S(1)} custom-call(s32[5]{0:T(128)S(1)} %stack.23.at_ref, bf16[8,2,4,32,512]{4,3,2,1,0:T(8,128)(2,1)S(1)} %bitcast.16, bf16[2,4,128,512]{3,2,1,0:T(8,128)(2,1)S(1)} %bitcast.15, bf16[2,4,128,512]{3,2,1,0:T(8,128)(2,1)S(1)} %collective-permute-done.12.other_ref), custom_call_target="tpu_custom_call" | custom-call | flops 1073741824 | bytes 5242880 | tf_op jit(solution)/shard_map/pallas_call | solution.py:182
  160.7 15.3 %all_to_all.32.in_ref = f32[4,128,512]{2,1,0:T(8,128)S(1)} all-to-all(f32[4,128,512]{2,1,0:T(8,128)S(1)} %shard_map.51), channel_id=1, replica_groups=mesh['xl'=2,'c'=2,'y'=4,'xh'=2,'z'=8] {'y'}, dimensions={0} | all-to-all | bytes 2097152 | tf_op jit(solution)/shard_map/all_to_all | solution.py:262
  176.0 2.4 %shard_map.52 = f32[128,2048]{1,0:T(8,128)} custom-call(f32[4,128,512]{2,1,0:T(8,128)S(1)} %all_to_all.32.in_ref), custom_call_target="tpu_custom_call" | custom-call | tf_op jit(solution)/shard_map/pallas_call | solution.py:205
  (19 shorter events, 0.1 us)
Async XLA Ops:
  6.5 8.0 %collective-permute-start = (bf16[1,512,128]{2,1,0:T(8,128)(2,1)}, bf16[1,512,128]{2,1,0:T(8,128)(2,1)S(1)}, u32[]{:S(2)}, u32[]{:S(2)}) collective-permute-start(bf16[1,512,128]{2,1,0:T(8,128)(2,1)} %param.4), channel_id=1, source_target_pairs={{0,8},{8,0},{1,9},{9,1},{2,10},{10,2},{3,11},{11,3},{4,12},{12,4},... | collective-permute-start | bytes 393224 | tf_op jit(solution)/shard_map/ppermute | solution.py:24
  8.7 7.6 %collective-permute-start.1 = (bf16[1,512,128]{2,1,0:T(8,128)(2,1)}, bf16[1,512,128]{2,1,0:T(8,128)(2,1)S(1)}, u32[]{:S(2)}, u32[]{:S(2)}) collective-permute-start(bf16[1,512,128]{2,1,0:T(8,128)(2,1)} %param.5), channel_id=1, source_target_pairs={{0,8},{8,0},{1,9},{9,1},{2,10},{10,2},{3,11},{11,3},{4,12},{12,4},... | collective-permute-start | bytes 393224 | tf_op jit(solution)/shard_map/ppermute | solution.py:24
  10.1 4.4 %copy-start.12 = (bf16[1,512,128]{2,1,0:T(8,128)(2,1)S(1)}, bf16[1,512,128]{2,1,0:T(8,128)(2,1)}, u32[]{:S(2)}) copy-start(bf16[1,512,128]{2,1,0:T(8,128)(2,1)} %param.4) | copy-start | bytes 393220
  10.1 6.2 %copy-start.13 = (bf16[1,512,128]{2,1,0:T(8,128)(2,1)S(1)}, bf16[1,512,128]{2,1,0:T(8,128)(2,1)}, u32[]{:S(2)}) copy-start(bf16[1,512,128]{2,1,0:T(8,128)(2,1)} %param.5) | copy-start | bytes 393220
  17.0 30.1 %all-to-all-start = ((bf16[4,1024,256]{2,1,0:T(8,128)(2,1)}), bf16[4,1024,256]{2,1,0:T(8,128)(2,1)S(1)}, u32[]{:S(2)}, u32[]{:S(2)}) async-start(bf16[4,1024,256]{2,1,0:T(8,128)(2,1)} %shard_map.46), calls=%async_computation | async-start | bytes 4194304 | tf_op jit(solution)/shard_map/all_to_all | solution.py:235
  21.5 59.0 %all-gather.5.cloned.1.call-start = ((), (), s32[]{:S(2)}) async-start(), calls=%async_computation.6 | async-start | bytes 2359296 | tf_op jit(solution)/shard_map/all_gather | solution.py:236
  22.2 11.2 %collective-permute-start.2 = (bf16[2,512,128]{2,1,0:T(8,128)(2,1)S(1)}, bf16[2,512,128]{2,1,0:T(8,128)(2,1)S(1)}, u32[]{:S(2)}, u32[]{:S(2)}) collective-permute-start(bf16[2,512,128]{2,1,0:T(8,128)(2,1)S(1)} %pad_maximum_fusion.refs_0_), channel_id=1, source_target_pairs={{0,1},{1,2},{2,3},{3,4},{4,5},{5,6},{6,7},{7,0},{8,9},{9,10},{10,1... | collective-permute-start | bytes 786440 | tf_op jit(solution)/shard_map/ppermute | solution.py:24
  24.2 9.2 %collective-permute-start.3 = (bf16[2,512,128]{2,1,0:T(8,128)(2,1)S(1)}, bf16[2,512,128]{2,1,0:T(8,128)(2,1)S(1)}, u32[]{:S(2)}, u32[]{:S(2)}) collective-permute-start(bf16[2,512,128]{2,1,0:T(8,128)(2,1)S(1)} %pad_maximum_fusion.refs_0_), channel_id=1, source_target_pairs={{0,7},{1,0},{2,1},{3,2},{4,3},{5,4},{6,5},{7,6},{8,15},{9,8},{10,9... | collective-permute-start | bytes 786440 | tf_op jit(solution)/shard_map/ppermute | solution.py:24
  33.5 37.0 %copy-start.2 = (bf16[2,512,128]{2,1,0:T(8,128)(2,1)}, bf16[2,512,128]{2,1,0:T(8,128)(2,1)S(1)}, u32[]{:S(2)}) copy-start(bf16[2,512,128]{2,1,0:T(8,128)(2,1)S(1)} %collective-permute-done.2.refs_1_) | copy-start | bytes 786436
  33.5 37.0 %copy-start.4 = (bf16[2,512,128]{2,1,0:T(8,128)(2,1)}, bf16[2,512,128]{2,1,0:T(8,128)(2,1)S(1)}, u32[]{:S(2)}) copy-start(bf16[2,512,128]{2,1,0:T(8,128)(2,1)S(1)} %collective-permute-done.3.refs_2_) | copy-start | bytes 786436
  33.5 7.7 %collective-permute-start.4 = (bf16[2,512,128]{2,1,0:T(8,128)(2,1)S(1)}, bf16[2,512,128]{2,1,0:T(8,128)(2,1)S(1)}, u32[]{:S(2)}, u32[]{:S(2)}) collective-permute-start(bf16[2,512,128]{2,1,0:T(8,128)(2,1)S(1)} %collective-permute-done.2.refs_1_), channel_id=1, source_target_pairs={{0,1},{1,2},{2,3},{3,4},{4,5},{5,6},{6,7},{7,0},{8,9},{9,10},{10,1... | collective-permute-start | bytes 786440 | tf_op jit(solution)/shard_map/ppermute | solution.py:24
  33.6 9.9 %collective-permute-start.5 = (bf16[2,512,128]{2,1,0:T(8,128)(2,1)S(1)}, bf16[2,512,128]{2,1,0:T(8,128)(2,1)S(1)}, u32[]{:S(2)}, u32[]{:S(2)}) collective-permute-start(bf16[2,512,128]{2,1,0:T(8,128)(2,1)S(1)} %collective-permute-done.3.refs_2_), channel_id=1, source_target_pairs={{0,7},{1,0},{2,1},{3,2},{4,3},{5,4},{6,5},{7,6},{8,15},{9,8},{10,9... | collective-permute-start | bytes 786440 | tf_op jit(solution)/shard_map/ppermute | solution.py:24
  41.1 29.3 %copy-start.6 = (bf16[2,512,128]{2,1,0:T(8,128)(2,1)}, bf16[2,512,128]{2,1,0:T(8,128)(2,1)S(1)}, u32[]{:S(2)}) copy-start(bf16[2,512,128]{2,1,0:T(8,128)(2,1)S(1)} %collective-permute-done.4.refs_3_) | copy-start | bytes 786436
  43.5 27.0 %copy-start.8 = (bf16[2,512,128]{2,1,0:T(8,128)(2,1)}, bf16[2,512,128]{2,1,0:T(8,128)(2,1)S(1)}, u32[]{:S(2)}) copy-start(bf16[2,512,128]{2,1,0:T(8,128)(2,1)S(1)} %collective-permute-done.5.refs_4_) | copy-start | bytes 786436
  47.1 23.3 %collective-permute-start.8 = (bf16[4,1024,256]{2,1,0:T(8,128)(2,1)S(1)}, bf16[4,1024,256]{2,1,0:T(8,128)(2,1)}, u32[]{:S(2)}, u32[]{:S(2)}) collective-permute-start(bf16[4,1024,256]{2,1,0:T(8,128)(2,1)S(1)} %all-to-all-done.refs_7_.own_ref), channel_id=1, source_target_pairs={{0,64},{64,0},{1,65},{65,1},{2,66},{66,2},{3,67},{67,3},{4,68},{68... | collective-permute-start | bytes 6291464 | tf_op jit(solution)/shard_map/ppermute | solution.py:24
  47.1 38.0 %all-to-all-start.2 = ((bf16[4,1024,256]{2,1,0:T(8,128)(2,1)}), bf16[4,1024,256]{2,1,0:T(8,128)(2,1)}, u32[]{:S(2)}, u32[]{:S(2)}) async-start(bf16[4,1024,256]{2,1,0:T(8,128)(2,1)} %shard_map.47), calls=%async_computation.2 | async-start | bytes 4194304 | tf_op jit(solution)/shard_map/all_to_all | solution.py:239
  51.6 18.1 %collective-permute-start.6 = (bf16[2,512,128]{2,1,0:T(8,128)(2,1)S(1)}, bf16[2,512,128]{2,1,0:T(8,128)(2,1)}, u32[]{:S(2)}, u32[]{:S(2)}) collective-permute-start(bf16[2,512,128]{2,1,0:T(8,128)(2,1)S(1)} %collective-permute-done.4.refs_3_), channel_id=1, source_target_pairs={{0,1},{1,2},{2,3},{3,4},{4,5},{5,6},{6,7},{7,0},{8,9},{9,10},{10,1... | collective-permute-start | bytes 786440 | tf_op jit(solution)/shard_map/ppermute | solution.py:24
  53.6 16.1 %collective-permute-start.7 = (bf16[2,512,128]{2,1,0:T(8,128)(2,1)S(1)}, bf16[2,512,128]{2,1,0:T(8,128)(2,1)S(1)}, u32[]{:S(2)}, u32[]{:S(2)}) collective-permute-start(bf16[2,512,128]{2,1,0:T(8,128)(2,1)S(1)} %collective-permute-done.5.refs_4_), channel_id=1, source_target_pairs={{0,7},{1,0},{2,1},{3,2},{4,3},{5,4},{6,5},{7,6},{8,15},{9,8},{10,9... | collective-permute-start | bytes 786440 | tf_op jit(solution)/shard_map/ppermute | solution.py:24
  69.7 0.7 copy-start.10
  70.4 10.1 %collective-permute-start.9 = (bf16[2,512,128]{2,1,0:T(8,128)(2,1)}, bf16[2,512,128]{2,1,0:T(8,128)(2,1)}, u32[]{:S(2)}, u32[]{:S(2)}) collective-permute-start(bf16[2,512,128]{2,1,0:T(8,128)(2,1)} %collective-permute-done.6.refs_5_), channel_id=1, source_target_pairs={{0,1},{1,2},{2,3},{3,4},{4,5},{5,6},{6,7},{7,0},{8,9},{9,10},{10,1... | collective-permute-start | bytes 786440 | tf_op jit(solution)/shard_map/ppermute | solution.py:24
  70.6 1.0 copy-start.3
  71.5 0.9 copy-start.5
  72.5 0.9 copy-start.7
  73.4 0.9 copy-start.9
  74.4 0.9 copy-start.11
  85.2 6.3 %copy-start.1 = (bf16[16,512,128]{2,1,0:T(8,128)(2,1)S(1)}, bf16[16,512,128]{2,1,0:T(8,128)(2,1)}, u32[]{:S(2)}) copy-start(bf16[16,512,128]{2,1,0:T(8,128)(2,1)} %all-gather.5.cloned.1.call-done) | copy-start | bytes 6291460
  85.2 6.3 %collective-permute-start.10 = (bf16[4,1024,256]{2,1,0:T(8,128)(2,1)}, bf16[4,1024,256]{2,1,0:T(8,128)(2,1)}, u32[]{:S(2)}, u32[]{:S(2)}) collective-permute-start(bf16[4,1024,256]{2,1,0:T(8,128)(2,1)} %all-to-all-done.2.own_ref), channel_id=1, source_target_pairs={{0,64},{64,0},{1,65},{65,1},{2,66},{66,2},{3,67},{67,3},{4,68},{68... | collective-permute-start | bytes 6291464 | tf_op jit(solution)/shard_map/ppermute | solution.py:24
  85.2 21.4 %all-to-all-start.1 = ((f32[16,32,512]{2,1,0:T(8,128)}), f32[16,32,512]{2,1,0:T(8,128)}, u32[]{:S(2)}, u32[]{:S(2)}) async-start(f32[16,32,512]{2,1,0:T(8,128)} %bitcast.6), calls=%async_computation.1 | async-start | bytes 2097152 | tf_op jit(solution)/shard_map/all_to_all | solution.py:246
  91.4 64.3 %all-gather.7.cloned.1.call-start = ((), (), s32[]{:S(2)}) async-start(), calls=%async_computation.7 | async-start | bytes 2359296 | tf_op jit(solution)/shard_map/all_gather | solution.py:254
  108.0 6.6 %collective-permute-start.11 = (bf16[1,4,32,512]{3,2,1,0:T(8,128)(2,1)S(1)}, bf16[1,4,32,512]{3,2,1,0:T(8,128)(2,1)S(1)}, u32[]{:S(2)}, u32[]{:S(2)}) collective-permute-start(bf16[1,4,32,512]{3,2,1,0:T(8,128)(2,1)S(1)} %bitcast.18), channel_id=1, source_target_pairs={{0,8},{8,0},{1,9},{9,1},{2,10},{10,2},{3,11},{11,3},{4,12},{12,4},... | collective-permute-start | bytes 393224 | tf_op jit(solution)/shard_map/ppermute | solution.py:24
  149.4 2.7 %collective-permute-start.12 = (bf16[2,4,128,512]{3,2,1,0:T(8,128)(2,1)S(1)}, bf16[2,4,128,512]{3,2,1,0:T(8,128)(2,1)S(1)}, u32[]{:S(2)}, u32[]{:S(2)}) collective-permute-start(bf16[2,4,128,512]{3,2,1,0:T(8,128)(2,1)S(1)} %bitcast.14), channel_id=1, source_target_pairs={{0,64},{64,0},{1,65},{65,1},{2,66},{66,2},{3,67},{67,3},{4,68},{68... | collective-permute-start | bytes 3145736 | tf_op jit(solution)/shard_map/ppermute | solution.py:24
  155.7 1.6 copy-start
Sparse Core Ops, SparseCore 0:
  24.1 48.3 all-gather.4
  115.4 40.2 all-gather.6

commit v8 on v7

v8 whole, which is shorter than its diff:
```python
import functools

import jax
import jax.numpy as jnp
from jax import lax
from jax.experimental import pallas as pl
from jax.experimental.pallas import tpu as pltpu
from jax.sharding import Mesh, PartitionSpec as P

AXES = ("xl", "c", "y", "xh", "z")
SIZES = (2, 2, 4, 2, 8)
DP = ("xl", "c")
TILE = ("y", "xh", "z")
TOK = 512
COLS = 128
F32 = jnp.float32
BF16 = jnp.bfloat16
VMEM_LIMIT = 58 * 1024 * 1024
PARAMS = pltpu.CompilerParams(vmem_limit_bytes=VMEM_LIMIT)


def shift(x, axis, by):
    n = lax.axis_size(axis)
    return lax.ppermute(x, axis, [(i, (i + by) % n) for i in range(n)])


def after(x, *others):
    return lax.optimization_barrier((x, *others))[0]


def whole(shape):
    return pl.BlockSpec(shape, lambda *_: (0,) * len(shape))


def split_kernel(core_ref, in_ref, out_ref):
    exact = in_ref[...]
    high = exact.astype(BF16)
    out_ref[0, :, :COLS] = high
    out_ref[0, :, COLS:] = (exact - high.astype(F32)).astype(BF16)


def split_basis(share, count, basis):
    rows = 2048 // count
    return pl.pallas_call(
        split_kernel,
        grid_spec=pltpu.PrefetchScalarGridSpec(
            num_scalar_prefetch=1,
            grid=(4,),
            in_specs=[pl.BlockSpec((rows, COLS), lambda g, share: (g * count + share[0], 0))],
            out_specs=pl.BlockSpec((1, rows, 256), lambda g, share: (g, 0, 0)),
        ),
        out_shape=jax.ShapeDtypeStruct((4, rows, 256), BF16),
        compiler_params=PARAMS,
        cost_estimate=pl.CostEstimate(
            flops=1 << 20, bytes_accessed=4 << 20, transcendentals=0
        ),
    )(share, basis)


def rotate_ring_kernel(offsets, at_ref, *refs):
    blocks, (own_ref, other_ref, out_ref, lhs, sems) = refs[: len(offsets)], refs[len(offsets) :]

    @pl.when(pl.program_id(0) == 0)
    def _():
        turned = lax.rem(at_ref[1] + at_ref[4], 2)
        copies = []
        for i, (block, offset) in enumerate(zip(blocks, offsets)):
            for side in range(2):
                half = turned if side == 0 else 1 - turned
                at = (half * 8 + lax.rem(at_ref[0] + 8 + offset, 8)) * COLS
                lanes = pl.ds(pl.multiple_of(at, COLS), COLS)
                copies.append(
                    pltpu.make_async_copy(block.at[side], lhs.at[:, lanes], sems.at[i * 2 + side])
                )
        for copy in copies:
            copy.start()
        for copy in copies:
            copy.wait()

    both = jnp.dot(lhs[:, :1024], own_ref[0], preferred_element_type=F32)
    both += jnp.dot(lhs[:, 1024:], other_ref[0], preferred_element_type=F32)
    out_ref[0] = (both[:, :COLS] + both[:, COLS:]).T


def rotate_ring(at, ring, own, other):
    slab = pl.BlockSpec((1, 1024, 256), lambda g: (g, 0, 0))
    return pl.pallas_call(
        functools.partial(rotate_ring_kernel, [offset for _, offset in ring]),
        grid=(4,),
        out_shape=jax.ShapeDtypeStruct((4, COLS, TOK), F32),
        in_specs=[pl.BlockSpec(memory_space=pltpu.SMEM)]
        + [pl.BlockSpec(memory_space=pltpu.HBM)] * len(ring)
        + [slab, slab],
        out_specs=pl.BlockSpec((1, COLS, TOK), lambda g: (g, 0, 0)),
        scratch_shapes=[pltpu.VMEM((TOK, 2048), BF16), pltpu.SemaphoreType.DMA((16,))],
        compiler_params=PARAMS,
        cost_estimate=pl.CostEstimate(
            flops=4 * TOK * 2048 * 512, bytes_accessed=7 << 20, transcendentals=0
        ),
    )(at, *[block for block, _ in ring], own, other)


def rotate_kernel(at_ref, block_ref, *refs):
    slabs, (out_ref, lhs, sems) = refs[:4], refs[4:]
    xh, xl, c = at_ref[1], at_ref[3], at_ref[4]

    @pl.when(pl.program_id(0) == 0)
    def _():
        copies = []
        for z in range(8):
            for side in range(2):
                at = ((xh if side == 0 else 1 - xh) * 8 + z) * COLS
                lanes = pl.ds(pl.multiple_of(at, COLS), COLS)
                copies.append(
                    pltpu.make_async_copy(block_ref.at[z, side], lhs.at[:, lanes], sems.at[z * 2 + side])
                )
        for copy in copies:
            copy.start()
        for copy in copies:
            copy.wait()

    both = None
    for i, slab_ref in enumerate(slabs):
        quarter = (c if i < 2 else 1 - c) * 2 + (xl if i % 2 == 0 else 1 - xl)
        lanes = pl.ds(pl.multiple_of(quarter * 512, 512), 512)
        part = jnp.dot(lhs[:, lanes], slab_ref[0], preferred_element_type=F32)
        both = part if both is None else both + part
    out_ref[0] = (both[:, :COLS] + both[:, COLS:]).T


def rotate(at, blocks, slabs):
    slab = pl.BlockSpec((1, 512, 256), lambda g: (g, 0, 0))
    return pl.pallas_call(
        rotate_kernel,
        grid=(4,),
        out_shape=jax.ShapeDtypeStruct((4, COLS, TOK), F32),
        in_specs=[pl.BlockSpec(memory_space=pltpu.SMEM), pl.BlockSpec(memory_space=pltpu.HBM)]
        + [slab] * 4,
        out_specs=pl.BlockSpec((1, COLS, TOK), lambda g: (g, 0, 0)),
        scratch_shapes=[pltpu.VMEM((TOK, 2048), BF16), pltpu.SemaphoreType.DMA((16,))],
        compiler_params=PARAMS,
        cost_estimate=pl.CostEstimate(
            flops=4 * TOK * 2048 * 512, bytes_accessed=7 << 20, transcendentals=0
        ),
    )(at, blocks, *slabs)


def product_kernel(scale, at_ref, acts_ref, own_ref, other_ref, out_ref, right, sems):
    xh, c = at_ref[1], at_ref[4]
    copies = []
    for z in range(8):
        for side in range(2):
            place = (xh if side == 0 else 1 - xh) * 8 + z
            rows = pl.ds(pl.multiple_of(place * 32, 32), 32)
            copies.append(
                pltpu.make_async_copy(acts_ref.at[z, side], right.at[:, rows], sems.at[z * 2 + side])
            )
    for copy in copies:
        copy.start()
    for copy in copies:
        copy.wait()
    for row in range(4):
        total = None
        for grads_ref, core in ((own_ref, c), (other_ref, 1 - c)):
            for side in range(2):
                part = lax.dot_general(
                    grads_ref[side, row],
                    right[side * 2 + core],
                    (((1,), (1,)), ((), ())),
                    preferred_element_type=F32,
                )
                total = part * part if total is None else total + part * part
        out_ref[row] = total * scale


def products(at, acts, own, other, scale):
    return pl.pallas_call(
        functools.partial(product_kernel, scale),
        out_shape=jax.ShapeDtypeStruct((4, COLS, 512), F32),
        in_specs=[pl.BlockSpec(memory_space=pltpu.SMEM), pl.BlockSpec(memory_space=pltpu.HBM)]
        + [pl.BlockSpec(memory_space=pltpu.VMEM)] * 2,
        out_specs=pl.BlockSpec(memory_space=pltpu.VMEM),
        scratch_shapes=[pltpu.VMEM((4, 512, TOK), BF16), pltpu.SemaphoreType.DMA((16,))],
        compiler_params=PARAMS,
        cost_estimate=pl.CostEstimate(
            flops=2 * 4 * 512 * 512 * TOK, bytes_accessed=5 << 20, transcendentals=0
        ),
    )(at, acts, own, other)


def weave_kernel(in_ref, out_ref):
    for tile in range(4):
        lanes = slice(tile * 32, tile * 32 + 32)
        out_ref[:, tile * COLS : (tile + 1) * COLS] = jnp.concatenate(
            [in_ref[q, :, lanes] for q in range(4)], axis=1
        )


def weave(parts):
    return pl.pallas_call(
        weave_kernel,
        grid=(4,),
        out_shape=jax.ShapeDtypeStruct((COLS, 2048), F32),
        in_specs=[pl.BlockSpec((4, COLS, 128), lambda g: (0, 0, g))],
        out_specs=pl.BlockSpec((COLS, 512), lambda g: (0, g)),
        compiler_params=PARAMS,
    )(parts)


def sync(*arrays):
    return lax.optimization_barrier(arrays)


def pair(x):
    return jnp.concatenate([x, shift(x, "xh", 1)])


def ring_step(up, down):
    return shift(up, "z", 1), shift(down, "z", -1)


def body(activations, gradients, basis_in, basis_out):
    z, xh, y, xl, c = (lax.axis_index(a) for a in ("z", "xh", "y", "xl", "c"))
    at = jnp.stack([z, xh, y, xl, c]).astype(jnp.int32)
    half = c.astype(jnp.int32).reshape(1)
    quarter = (c * 2 + xl).astype(jnp.int32).reshape(1)

    a0, grads_pair, mine_in, basis_out = sync(
        pair(activations), pair(gradients), split_basis(half, 2, basis_in), basis_out
    )
    own_in = lax.all_to_all(mine_in, "y", 0, 0)
    up1, down1, mine_out = sync(*ring_step(a0, a0), split_basis(quarter, 4, basis_out))
    up2, down2, mine_out = sync(*ring_step(up1, down1), mine_out)
    up3, down3, own_in, mine_out = sync(*ring_step(up2, down2), own_in, mine_out)
    own_out = lax.all_to_all(mine_out, "y", 0, 0)
    grad_blocks = lax.all_gather(after(grads_pair, up2), "z")
    up4, other_in = sync(shift(up3, "z", 1), shift(own_in, "c", 1))
    ring = [(a0, 0), (up1, -1), (down1, 1), (up2, -2), (down2, 2), (up3, -3), (down3, 3), (up4, -4)]
    acts_part = rotate_ring(at, ring, own_in, other_in)
    acts_in = lax.all_to_all(acts_part.reshape(16, 32, TOK), ("xl", "c", "y"), 0, 0)

    own_out = after(own_out, acts_part)
    beside_out = shift(own_out, "xl", 1)
    others = shift(own_out, "c", 1), shift(beside_out, "c", 1)
    grads_part = rotate(at, grad_blocks, (own_out, beside_out, *others))
    acts_in, grads_part = sync(acts_in, grads_part)
    grads_in = lax.all_to_all(grads_part, "y", 0, 0)

    acts = jnp.sum(acts_in.reshape(4, 4, 32, TOK), axis=1).astype(BF16)[None]
    rot_acts = lax.all_gather(pair(acts), "z")

    grads = jnp.sum(grads_in, axis=0).astype(BF16)
    copies = jnp.broadcast_to(grads, (8, COLS, TOK))
    rot_own = lax.all_to_all(copies, ("xl", "y"), 0, 0).reshape(2, 4, COLS, TOK)
    rot_other = shift(rot_own, "c", 1)

    part = products(at, rot_acts, rot_own, rot_other, 1.0 / (TOK * 4))
    return weave(lax.all_to_all(part, "y", 0, 0))


def solution(mesh):
    fine = Mesh(mesh.devices.reshape(SIZES), AXES)
    return jax.shard_map(
        body,
        mesh=fine,
        in_specs=(P(DP, None, TILE), P(DP, None, TILE), P(None, TILE), P(None, TILE)),
        out_specs=P(TILE, DP),
        check_vma=False,
    )
```

time: 187 us -> 202 us (1.080)
  waiting for transfers between devices: 47.2 us -> 63.3 us
  local copies, waits for them, and re-layouts: 7.26 us -> 0.73 us
  Pallas kernels: 29 us -> 33.2 us
    ppermute x13 -> x15, waiting for transfers between devices: 29.5 us -> 51.6 us  [shift(): return lax.ppermute(x, axis, [(i, (i + by) % n) for i in range(n)])]
    unnamed x28, local copies, waits for them, and re-layouts: 7.09 us -> 0.05 us
    all_to_all x1, waiting for transfers between devices: 3.63 us -> 0.01 us  [body(): own_in = lax.all_to_all(mine_in, 'y', 0, 0)]
    pallas_call x1, Pallas kernels: 3.46 us -> 7.08 us  [products(): pl.pallas_call(functools.partial(product_kernel, scale), out_shape=jax.Sh...]
    pallas_call x2 -> x1, Pallas kernels: 9.79 us -> 7.45 us  [rotate_ring(): pl.pallas_call(functools.partial(rotate_ring_kernel, [offset for _, offse...]
    all_to_all x1, waiting for transfers between devices: 9.7 us -> 7.57 us  [body(): lax.all_to_all(acts_part.reshape(16, 32, TOK), ('xl', 'c', 'y'), 0, 0)]
    ppermute x13 -> x15, starting transfers between devices: 21 us -> 21.9 us  [shift(): return lax.ppermute(x, axis, [(i, (i + by) % n) for i in range(n)])]
  transfers between devices with their start and end apart: 18 -> 20, of which waited for: 11 -> 12; matrix products, arithmetic and copies ran while one was open for 0% -> 0% of each run, Pallas kernels for 13% -> 11%
where the time goes in v8:
time: 202 us; the launch traced here: 200 us
  waiting for transfers between devices  63.3 us (31%)
  blocking collectives  50.7 us (25%)
  starting transfers between devices  36.5 us (18%)
  Pallas kernels  33.2 us (16%)
  between operations  13.6 us (7%)
    ppermute x15, waiting for transfers between devices, shift(): return lax.ppermute(x, axis, [(i, (i + by) % n) for i in range(n)])  51.6 us
    ppermute x15, starting transfers between devices, shift(): return lax.ppermute(x, axis, [(i, (i + by) % n) for i in range(n)])  21.9 us
    all_to_all x1, blocking collectives, body(): grads_in = lax.all_to_all(grads_part, 'y', 0, 0)  17.4 us
    all_to_all x1, blocking collectives, body(): return weave(lax.all_to_all(part, 'y', 0, 0))  16.9 us
    all_to_all x1, blocking collectives, body(): rot_own = lax.all_to_all(copies, ('xl', 'y'), 0, 0).reshape(2, 4, COLS, TOK)  16.4 us
    all_to_all x1, waiting for transfers between devices, body(): lax.all_to_all(acts_part.reshape(16, 32, TOK), ('xl', 'c', 'y'), 0, 0)  7.57 us
    pallas_call x1, Pallas kernels, rotate_ring(): pl.pallas_call(functools.partial(rotate_ring_kernel, [offset for _, offse...  7.45 us
    pallas_call x1, Pallas kernels, rotate(): pl.pallas_call(rotate_kernel, grid=(4,), out_shape=jax.ShapeDtypeStruct((...  7.41 us
  transfers between devices with their start and end apart: 20, of which 12 were waited for; matrix products, arithmetic and copies ran while one was open for 0% of the time, Pallas kernels for 11%

profile of v8, /device:TPU:2, one launch (start us, length us, event | category | flops | bytes accessed | tf_op | source)
XLA Modules:
  0.0 199.6 jit_solution(10788395125510397921)
XLA Ops:
  6.5 2.1 %collective-permute-start = (bf16[1,512,128]{2,1,0:T(8,128)(2,1)}, bf16[1,512,128]{2,1,0:T(8,128)(2,1)S(1)}, u32[]{:S(2)}, u32[]{:S(2)}) collective-permute-start(bf16[1,512,128]{2,1,0:T(8,128)(2,1)} %param.4), channel_id=1, source_target_pairs={{0,8},{8,0},{1,9},{9,1},{2,10},{10,2},{3,11},{11,3},{4,12},{12,4},... | collective-permute-start | bytes 393224 | tf_op jit(solution)/shard_map/ppermute | solution.py:24
  8.7 1.4 collective-permute-start.1
  10.1 4.0 %shard_map.46 = bf16[4,1024,256]{2,1,0:T(8,128)(2,1)} custom-call(s32[1]{0:T(128)} %bitcast.4.core_ref, f32[8192,128]{1,0:T(8,128)} %in_ref.1), custom_call_target="tpu_custom_call" | custom-call | flops 1048576 | bytes 4194304 | tf_op jit(solution)/shard_map/pallas_call | solution.py:44
  14.0 0.5 collective-permute-done
  14.5 0.0 copy-done.6
  14.5 0.0 copy-start.5
  14.5 1.8 collective-permute-done.1
  16.3 0.0 copy-done.7
  16.3 0.7 pad_maximum_fusion.1
  17.0 4.5 %all-to-all-start = ((bf16[4,1024,256]{2,1,0:T(8,128)(2,1)}), bf16[4,1024,256]{2,1,0:T(8,128)(2,1)S(1)}, u32[]{:S(2)}, u32[]{:S(2)}) async-start(bf16[4,1024,256]{2,1,0:T(8,128)(2,1)} %shard_map.46), calls=%async_computation | async-start | bytes 4194304 | tf_op jit(solution)/shard_map/all_to_all | solution.py:231
  21.5 0.0 all-gather.5.cloned.1.call-start
  21.5 1.9 collective-permute-start.2
  23.4 0.0 copy-done.5
  23.4 4.0 %collective-permute-start.3 = (bf16[2,512,128]{2,1,0:T(8,128)(2,1)S(1)}, bf16[2,512,128]{2,1,0:T(8,128)(2,1)S(1)}, u32[]{:S(2)}, u32[]{:S(2)}) collective-permute-start(bf16[2,512,128]{2,1,0:T(8,128)(2,1)S(1)} %pad_maximum_fusion.refs_0_), channel_id=1, source_target_pairs={{0,7},{1,0},{2,1},{3,2},{4,3},{5,4},{6,5},{7,6},{8,15},{9,8},{10,9... | collective-permute-start | bytes 786440 | tf_op jit(solution)/shard_map/ppermute | solution.py:24
  27.4 3.4 %shard_map.47 = bf16[4,512,256]{2,1,0:T(8,128)(2,1)} custom-call(s32[1]{0:T(128)} %bitcast.5.core_ref, f32[8192,128]{1,0:T(8,128)} %in_ref.2), custom_call_target="tpu_custom_call" | custom-call | flops 1048576 | bytes 4194304 | tf_op jit(solution)/shard_map/pallas_call | solution.py:44
  30.9 1.8 collective-permute-done.2.refs_1_
  32.6 0.0 collective-permute-done.3.refs_2_
  32.7 0.1 collective-permute-start.4
  32.7 3.2 %collective-permute-start.5 = (bf16[2,512,128]{2,1,0:T(8,128)(2,1)S(1)}, bf16[2,512,128]{2,1,0:T(8,128)(2,1)S(1)}, u32[]{:S(2)}, u32[]{:S(2)}) collective-permute-start(bf16[2,512,128]{2,1,0:T(8,128)(2,1)S(1)} %collective-permute-done.3.refs_2_), channel_id=1, source_target_pairs={{0,7},{1,0},{2,1},{3,2},{4,3},{5,4},{6,5},{7,6},{8,15},{9,8},{10,9... | collective-permute-start | bytes 786440 | tf_op jit(solution)/shard_map/ppermute | solution.py:24
  36.0 4.4 %collective-permute-done.4.refs_3_ = bf16[2,512,128]{2,1,0:T(8,128)(2,1)S(1)} collective-permute-done((bf16[2,512,128]{2,1,0:T(8,128)(2,1)S(1)}, bf16[2,512,128]{2,1,0:T(8,128)(2,1)S(1)}, u32[]{:S(2)}, u32[]{:S(2)}) %collective-permute-start.4) | collective-permute-done | bytes 262176 | tf_op jit(solution)/shard_map/ppermute | solution.py:24
  40.3 0.0 collective-permute-done.5.refs_4_
  40.3 2.4 %collective-permute-start.6 = (bf16[2,512,128]{2,1,0:T(8,128)(2,1)S(1)}, bf16[2,512,128]{2,1,0:T(8,128)(2,1)S(1)}, u32[]{:S(2)}, u32[]{:S(2)}) collective-permute-start(bf16[2,512,128]{2,1,0:T(8,128)(2,1)S(1)} %collective-permute-done.4.refs_3_), channel_id=1, source_target_pairs={{0,1},{1,2},{2,3},{3,4},{4,5},{5,6},{6,7},{7,0},{8,9},{9,10},{10,1... | collective-permute-start | bytes 786440 | tf_op jit(solution)/shard_map/ppermute | solution.py:24
  42.7 0.9 collective-permute-start.7
  43.7 4.3 %collective-permute-done.6.refs_5_ = bf16[2,512,128]{2,1,0:T(8,128)(2,1)S(1)} collective-permute-done((bf16[2,512,128]{2,1,0:T(8,128)(2,1)S(1)}, bf16[2,512,128]{2,1,0:T(8,128)(2,1)S(1)}, u32[]{:S(2)}, u32[]{:S(2)}) %collective-permute-start.6) | collective-permute-done | bytes 262176 | tf_op jit(solution)/shard_map/ppermute | solution.py:24
  48.0 1.2 collective-permute-done.7.refs_6_
  49.2 0.0 all-to-all-done.refs_8_
  49.2 0.0 collective-permute-start.9
  49.2 0.0 all-gather.5.cloned.1.call-update
  49.3 4.5 %all-to-all-start.2 = ((bf16[4,512,256]{2,1,0:T(8,128)(2,1)}), bf16[4,512,256]{2,1,0:T(8,128)(2,1)S(1)}, u32[]{:S(2)}, u32[]{:S(2)}) async-start(bf16[4,512,256]{2,1,0:T(8,128)(2,1)} %shard_map.47), calls=%async_computation.2 | async-start | bytes 2097152 | tf_op jit(solution)/shard_map/all_to_all | solution.py:235
  53.8 2.0 %collective-permute-start.8 = (bf16[2,512,128]{2,1,0:T(8,128)(2,1)}, bf16[2,512,128]{2,1,0:T(8,128)(2,1)}, u32[]{:S(2)}, u32[]{:S(2)}) collective-permute-start(bf16[2,512,128]{2,1,0:T(8,128)(2,1)} %copy-done.13), channel_id=1, source_target_pairs={{0,1},{1,2},{2,3},{3,4},{4,5},{5,6},{6,7},{7,0},{8,9},{9,10},{10,1... | collective-permute-start | bytes 786440 | tf_op jit(solution)/shard_map/ppermute | solution.py:24
  55.8 0.6 stack.23.at_ref
  56.4 8.2 %collective-permute-done.8.refs_7_ = bf16[2,512,128]{2,1,0:T(8,128)(2,1)} collective-permute-done((bf16[2,512,128]{2,1,0:T(8,128)(2,1)}, bf16[2,512,128]{2,1,0:T(8,128)(2,1)}, u32[]{:S(2)}, u32[]{:S(2)}) %collective-permute-start.8) | collective-permute-done | bytes 262176 | tf_op jit(solution)/shard_map/ppermute | solution.py:24
  64.6 0.0 collective-permute-done.9.refs_9_
  64.6 0.0 copy-done.1
  64.6 7.4 %shard_map.48 = f32[4,128,512]{2,1,0:T(8,128)} custom-call(s32[5]{0:T(128)} %stack.23.at_ref, bf16[2,512,128]{2,1,0:T(8,128)(2,1)} %copy-done.5, bf16[2,512,128]{2,1,0:T(8,128)(2,1)} %copy-done.9, bf16[2,512,128]{2,1,0:T(8,128)(2,1)} %copy-done.10, bf16[2,512,128]{2,1,0:T(8,128)(2,1)} %copy-done.11, bf16[2,512,128]{2,1,0:T(8,128)(2,1)} %copy-done.12, ...), custom_call_target="tpu_custom_call" | custom-call | flops 2147483648 | bytes 7340032 | tf_op jit(solution)/shard_map/pallas_call | solution.py:87
  72.1 0.0 all-to-all-done.2.refs_0_
  72.1 1.7 collective-permute-start.10
  73.8 0.0 collective-permute-start.11
  73.8 22.4 %collective-permute-done.10.refs_1_ = bf16[4,512,256]{2,1,0:T(8,128)(2,1)S(1)} collective-permute-done((bf16[4,512,256]{2,1,0:T(8,128)(2,1)S(1)}, bf16[4,512,256]{2,1,0:T(8,128)(2,1)S(1)}, u32[]{:S(2)}, u32[]{:S(2)}) %collective-permute-start.10) | collective-permute-done | bytes 1048608 | tf_op jit(solution)/shard_map/ppermute | solution.py:24
  96.2 0.0 collective-permute-start.12
  96.2 5.5 %all-to-all-start.1 = ((f32[16,32,512]{2,1,0:T(8,128)}), f32[16,32,512]{2,1,0:T(8,128)S(1)}, u32[]{:S(2)}, u32[]{:S(2)}) async-start(f32[16,32,512]{2,1,0:T(8,128)} %bitcast.18), calls=%async_computation.1 | async-start | bytes 2097152 | tf_op jit(solution)/shard_map/all_to_all | solution.py:240
  101.7 0.0 all-gather.7.cloned.1.call-start
  101.7 0.0 all-gather.5.cloned.1.call-done
  101.8 0.0 collective-permute-done.11.refs_2_
  101.8 0.0 collective-permute-done.12.refs_3_
  101.8 7.4 %shard_map.49 = f32[4,128,512]{2,1,0:T(8,128)} custom-call(s32[5]{0:T(128)} %stack.23.at_ref, bf16[8,2,512,128]{3,2,1,0:T(8,128)(2,1)} %bitcast.21, bf16[4,512,256]{2,1,0:T(8,128)(2,1)} %copy-done.2, bf16[4,512,256]{2,1,0:T(8,128)(2,1)} %copy-done.8, bf16[4,512,256]{2,1,0:T(8,128)(2,1)} %collective-permute-done.11.refs_2_, ...), custom_call_target="tpu_custom_call" | custom-call | flops 2147483648 | bytes 7340032 | tf_op jit(solution)/shard_map/pallas_call | solution.py:133
  109.2 7.6 %all-to-all-done.1 = f32[16,32,512]{2,1,0:T(8,128)S(1)} async-done(((f32[16,32,512]{2,1,0:T(8,128)}), f32[16,32,512]{2,1,0:T(8,128)S(1)}, u32[]{:S(2)}, u32[]{:S(2)}) %all-to-all-start.1) | async-done | bytes 1048608 | tf_op jit(solution)/shard_map/all_to_all | solution.py:240
  116.8 0.1 bitcast_reduce_fusion
  116.9 2.0 %collective-permute-start.13 = (bf16[1,4,32,512]{3,2,1,0:T(8,128)(2,1)S(1)}, bf16[1,4,32,512]{3,2,1,0:T(8,128)(2,1)S(1)}, u32[]{:S(2)}, u32[]{:S(2)}) collective-permute-start(bf16[1,4,32,512]{3,2,1,0:T(8,128)(2,1)S(1)} %bitcast.19), channel_id=1, source_target_pairs={{0,8},{8,0},{1,9},{9,1},{2,10},{10,2},{3,11},{11,3},{4,12},{12,4},... | collective-permute-start | bytes 393224 | tf_op jit(solution)/shard_map/ppermute | solution.py:24
  118.9 4.5 %collective-permute-done.13 = bf16[1,4,32,512]{3,2,1,0:T(8,128)(2,1)S(1)} collective-permute-done((bf16[1,4,32,512]{3,2,1,0:T(8,128)(2,1)S(1)}, bf16[1,4,32,512]{3,2,1,0:T(8,128)(2,1)S(1)}, u32[]{:S(2)}, u32[]{:S(2)}) %collective-permute-start.13) | collective-permute-done | bytes 131104 | tf_op jit(solution)/shard_map/ppermute | solution.py:24
  123.5 0.7 pad_maximum_fusion.2
  124.2 0.0 all-gather.7.cloned.1.call-update
  124.2 0.0 copy-done.3
  124.2 17.4 %all_to_all.30 = f32[4,128,512]{2,1,0:T(8,128)S(1)} all-to-all(f32[4,128,512]{2,1,0:T(8,128)S(1)} %copy-done.3), channel_id=1, replica_groups=mesh['xl'=2,'c'=2,'y'=4,'xh'=2,'z'=8] {'y'}, dimensions={0} | all-to-all | bytes 2097152 | tf_op jit(solution)/shard_map/all_to_all | solution.py:247
  141.6 0.1 reduce_sum.19
  141.7 0.1 broadcast_in_dim.4
  141.8 16.4 %all_to_all.31 = bf16[8,128,512]{2,1,0:T(8,128)(2,1)S(1)} all-to-all(bf16[8,128,512]{2,1,0:T(8,128)(2,1)S(1)} %broadcast_in_dim.4), channel_id=1, replica_groups=mesh['xl'=2,'c'=2,'y'=4,'xh'=2,'z'=8] {'xl','y'}, dimensions={0} | all-to-all | bytes 2097152 | tf_op jit(solution)/shard_map/all_to_all | solution.py:254
  158.1 0.0 collective-permute-start.14
  158.1 2.7 %collective-permute-done.14.other_ref = bf16[2,4,128,512]{3,2,1,0:T(8,128)(2,1)S(1)} collective-permute-done((bf16[2,4,128,512]{3,2,1,0:T(8,128)(2,1)S(1)}, bf16[2,4,128,512]{3,2,1,0:T(8,128)(2,1)S(1)}, u32[]{:S(2)}, u32[]{:S(2)}) %collective-permute-start.14) | collective-permute-done | bytes 1048608 | tf_op jit(solution)/shard_map/ppermute | solution.py:24
  160.8 4.1 %all-gather.7.cloned.1.call-done = bf16[16,4,32,512]{3,2,1,0:T(8,128)(2,1)} async-done(((bf16[2,4,32,512]{3,2,1,0:T(8,128)(2,1)}), bf16[16,4,32,512]{3,2,1,0:T(8,128)(2,1)}) %all-gather.7.cloned.1.call-update) | async-done | bytes 2097168 | tf_op jit(solution)/shard_map/all_gather | solution.py:250
  164.9 0.0 copy-done.4
  164.9 7.1 %shard_map.50 = f32[4,128,512]{2,1,0:T(8,128)} custom-call(s32[5]{0:T(128)} %stack.23.at_ref, bf16[8,2,4,32,512]{4,3,2,1,0:T(8,128)(2,1)} %bitcast.17, bf16[2,4,128,512]{3,2,1,0:T(8,128)(2,1)} %bitcast.16, bf16[2,4,128,512]{3,2,1,0:T(8,128)(2,1)} %copy-done.4), custom_call_target="tpu_custom_call" | custom-call | flops 1073741824 | bytes 5242880 | tf_op jit(solution)/shard_map/pallas_call | solution.py:177
  172.0 16.9 %all_to_all.32.in_ref = f32[4,128,512]{2,1,0:T(8,128)} all-to-all(f32[4,128,512]{2,1,0:T(8,128)} %shard_map.50), channel_id=1, replica_groups=mesh['xl'=2,'c'=2,'y'=4,'xh'=2,'z'=8] {'y'}, dimensions={0} | all-to-all | bytes 2097152 | tf_op jit(solution)/shard_map/all_to_all | solution.py:258
  188.9 3.9 %shard_map.51 = f32[128,2048]{1,0:T(8,128)} custom-call(f32[4,128,512]{2,1,0:T(8,128)} %all_to_all.32.in_ref), custom_call_target="tpu_custom_call" | custom-call | tf_op jit(solution)/shard_map/pallas_call | solution.py:200
  (22 shorter events, 0.1 us)
Async XLA Ops:
  6.5 8.0 %collective-permute-start = (bf16[1,512,128]{2,1,0:T(8,128)(2,1)}, bf16[1,512,128]{2,1,0:T(8,128)(2,1)S(1)}, u32[]{:S(2)}, u32[]{:S(2)}) collective-permute-start(bf16[1,512,128]{2,1,0:T(8,128)(2,1)} %param.4), channel_id=1, source_target_pairs={{0,8},{8,0},{1,9},{9,1},{2,10},{10,2},{3,11},{11,3},{4,12},{12,4},... | collective-permute-start | bytes 393224 | tf_op jit(solution)/shard_map/ppermute | solution.py:24
  8.7 7.6 %collective-permute-start.1 = (bf16[1,512,128]{2,1,0:T(8,128)(2,1)}, bf16[1,512,128]{2,1,0:T(8,128)(2,1)S(1)}, u32[]{:S(2)}, u32[]{:S(2)}) collective-permute-start(bf16[1,512,128]{2,1,0:T(8,128)(2,1)} %param.5), channel_id=1, source_target_pairs={{0,8},{8,0},{1,9},{9,1},{2,10},{10,2},{3,11},{11,3},{4,12},{12,4},... | collective-permute-start | bytes 393224 | tf_op jit(solution)/shard_map/ppermute | solution.py:24
  10.1 4.4 %copy-start.6 = (bf16[1,512,128]{2,1,0:T(8,128)(2,1)S(1)}, bf16[1,512,128]{2,1,0:T(8,128)(2,1)}, u32[]{:S(2)}) copy-start(bf16[1,512,128]{2,1,0:T(8,128)(2,1)} %param.4) | copy-start | bytes 393220
  10.1 6.2 %copy-start.7 = (bf16[1,512,128]{2,1,0:T(8,128)(2,1)S(1)}, bf16[1,512,128]{2,1,0:T(8,128)(2,1)}, u32[]{:S(2)}) copy-start(bf16[1,512,128]{2,1,0:T(8,128)(2,1)} %param.5) | copy-start | bytes 393220
  14.5 8.9 %copy-start.5 = (bf16[2,512,128]{2,1,0:T(8,128)(2,1)}, bf16[2,512,128]{2,1,0:T(8,128)(2,1)S(1)}, u32[]{:S(2)}) copy-start(bf16[2,512,128]{2,1,0:T(8,128)(2,1)S(1)} %pad_maximum_fusion.refs_0_) | copy-start | bytes 786436
  17.0 32.2 %all-to-all-start = ((bf16[4,1024,256]{2,1,0:T(8,128)(2,1)}), bf16[4,1024,256]{2,1,0:T(8,128)(2,1)S(1)}, u32[]{:S(2)}, u32[]{:S(2)}) async-start(bf16[4,1024,256]{2,1,0:T(8,128)(2,1)} %shard_map.46), calls=%async_computation | async-start | bytes 4194304 | tf_op jit(solution)/shard_map/all_to_all | solution.py:231
  21.5 80.3 %all-gather.5.cloned.1.call-start = ((), (), s32[]{:S(2)}) async-start(), calls=%async_computation.6 | async-start | bytes 2359296 | tf_op jit(solution)/shard_map/all_gather | solution.py:236
  21.5 11.2 %collective-permute-start.2 = (bf16[2,512,128]{2,1,0:T(8,128)(2,1)S(1)}, bf16[2,512,128]{2,1,0:T(8,128)(2,1)S(1)}, u32[]{:S(2)}, u32[]{:S(2)}) collective-permute-start(bf16[2,512,128]{2,1,0:T(8,128)(2,1)S(1)} %pad_maximum_fusion.refs_0_), channel_id=1, source_target_pairs={{0,1},{1,2},{2,3},{3,4},{4,5},{5,6},{6,7},{7,0},{8,9},{9,10},{10,1... | collective-permute-start | bytes 786440 | tf_op jit(solution)/shard_map/ppermute | solution.py:24
  23.4 9.2 %collective-permute-start.3 = (bf16[2,512,128]{2,1,0:T(8,128)(2,1)S(1)}, bf16[2,512,128]{2,1,0:T(8,128)(2,1)S(1)}, u32[]{:S(2)}, u32[]{:S(2)}) collective-permute-start(bf16[2,512,128]{2,1,0:T(8,128)(2,1)S(1)} %pad_maximum_fusion.refs_0_), channel_id=1, source_target_pairs={{0,7},{1,0},{2,1},{3,2},{4,3},{5,4},{6,5},{7,6},{8,15},{9,8},{10,9... | collective-permute-start | bytes 786440 | tf_op jit(solution)/shard_map/ppermute | solution.py:24
  32.6 16.6 %copy-start.9 = (bf16[2,512,128]{2,1,0:T(8,128)(2,1)}, bf16[2,512,128]{2,1,0:T(8,128)(2,1)S(1)}, u32[]{:S(2)}) copy-start(bf16[2,512,128]{2,1,0:T(8,128)(2,1)S(1)} %collective-permute-done.2.refs_1_) | copy-start | bytes 786436
  32.7 16.6 %copy-start.10 = (bf16[2,512,128]{2,1,0:T(8,128)(2,1)}, bf16[2,512,128]{2,1,0:T(8,128)(2,1)S(1)}, u32[]{:S(2)}) copy-start(bf16[2,512,128]{2,1,0:T(8,128)(2,1)S(1)} %collective-permute-done.3.refs_2_) | copy-start | bytes 786436
  32.7 7.7 %collective-permute-start.4 = (bf16[2,512,128]{2,1,0:T(8,128)(2,1)S(1)}, bf16[2,512,128]{2,1,0:T(8,128)(2,1)S(1)}, u32[]{:S(2)}, u32[]{:S(2)}) collective-permute-start(bf16[2,512,128]{2,1,0:T(8,128)(2,1)S(1)} %collective-permute-done.2.refs_1_), channel_id=1, source_target_pairs={{0,1},{1,2},{2,3},{3,4},{4,5},{5,6},{6,7},{7,0},{8,9},{9,10},{10,1... | collective-permute-start | bytes 786440 | tf_op jit(solution)/shard_map/ppermute | solution.py:24
  32.7 7.6 %collective-permute-start.5 = (bf16[2,512,128]{2,1,0:T(8,128)(2,1)S(1)}, bf16[2,512,128]{2,1,0:T(8,128)(2,1)S(1)}, u32[]{:S(2)}, u32[]{:S(2)}) collective-permute-start(bf16[2,512,128]{2,1,0:T(8,128)(2,1)S(1)} %collective-permute-done.3.refs_2_), channel_id=1, source_target_pairs={{0,7},{1,0},{2,1},{3,2},{4,3},{5,4},{6,5},{7,6},{8,15},{9,8},{10,9... | collective-permute-start | bytes 786440 | tf_op jit(solution)/shard_map/ppermute | solution.py:24
  40.3 24.3 %copy-start.11 = (bf16[2,512,128]{2,1,0:T(8,128)(2,1)}, bf16[2,512,128]{2,1,0:T(8,128)(2,1)S(1)}, u32[]{:S(2)}) copy-start(bf16[2,512,128]{2,1,0:T(8,128)(2,1)S(1)} %collective-permute-done.4.refs_3_) | copy-start | bytes 786436
  40.3 8.9 %copy-start.12 = (bf16[2,512,128]{2,1,0:T(8,128)(2,1)}, bf16[2,512,128]{2,1,0:T(8,128)(2,1)S(1)}, u32[]{:S(2)}) copy-start(bf16[2,512,128]{2,1,0:T(8,128)(2,1)S(1)} %collective-permute-done.5.refs_4_) | copy-start | bytes 786436
  40.3 7.7 %collective-permute-start.6 = (bf16[2,512,128]{2,1,0:T(8,128)(2,1)S(1)}, bf16[2,512,128]{2,1,0:T(8,128)(2,1)S(1)}, u32[]{:S(2)}, u32[]{:S(2)}) collective-permute-start(bf16[2,512,128]{2,1,0:T(8,128)(2,1)S(1)} %collective-permute-done.4.refs_3_), channel_id=1, source_target_pairs={{0,1},{1,2},{2,3},{3,4},{4,5},{5,6},{6,7},{7,0},{8,9},{9,10},{10,1... | collective-permute-start | bytes 786440 | tf_op jit(solution)/shard_map/ppermute | solution.py:24
  42.7 6.5 %collective-permute-start.7 = (bf16[2,512,128]{2,1,0:T(8,128)(2,1)S(1)}, bf16[2,512,128]{2,1,0:T(8,128)(2,1)}, u32[]{:S(2)}, u32[]{:S(2)}) collective-permute-start(bf16[2,512,128]{2,1,0:T(8,128)(2,1)S(1)} %collective-permute-done.5.refs_4_), channel_id=1, source_target_pairs={{0,7},{1,0},{2,1},{3,2},{4,3},{5,4},{6,5},{7,6},{8,15},{9,8},{10,9... | collective-permute-start | bytes 786440 | tf_op jit(solution)/shard_map/ppermute | solution.py:24
  48.0 1.3 copy-start.13
  49.2 15.4 %copy-start.1 = (bf16[4,1024,256]{2,1,0:T(8,128)(2,1)}, bf16[4,1024,256]{2,1,0:T(8,128)(2,1)S(1)}, u32[]{:S(2)}) copy-start(bf16[4,1024,256]{2,1,0:T(8,128)(2,1)S(1)} %all-to-all-done.refs_8_) | copy-start | bytes 6291460
  49.2 15.4 %collective-permute-start.9 = (bf16[4,1024,256]{2,1,0:T(8,128)(2,1)S(1)}, bf16[4,1024,256]{2,1,0:T(8,128)(2,1)}, u32[]{:S(2)}, u32[]{:S(2)}) collective-permute-start(bf16[4,1024,256]{2,1,0:T(8,128)(2,1)S(1)} %all-to-all-done.refs_8_), channel_id=1, source_target_pairs={{0,64},{64,0},{1,65},{65,1},{2,66},{66,2},{3,67},{67,3},{4,68},{68... | collective-permute-start | bytes 6291464 | tf_op jit(solution)/shard_map/ppermute | solution.py:24
  49.3 22.8 %all-to-all-start.2 = ((bf16[4,512,256]{2,1,0:T(8,128)(2,1)}), bf16[4,512,256]{2,1,0:T(8,128)(2,1)S(1)}, u32[]{:S(2)}, u32[]{:S(2)}) async-start(bf16[4,512,256]{2,1,0:T(8,128)(2,1)} %shard_map.47), calls=%async_computation.2 | async-start | bytes 2097152 | tf_op jit(solution)/shard_map/all_to_all | solution.py:235
  53.8 10.8 %collective-permute-start.8 = (bf16[2,512,128]{2,1,0:T(8,128)(2,1)}, bf16[2,512,128]{2,1,0:T(8,128)(2,1)}, u32[]{:S(2)}, u32[]{:S(2)}) collective-permute-start(bf16[2,512,128]{2,1,0:T(8,128)(2,1)} %copy-done.13), channel_id=1, source_target_pairs={{0,1},{1,2},{2,3},{3,4},{4,5},{5,6},{6,7},{7,0},{8,9},{9,10},{10,1... | collective-permute-start | bytes 786440 | tf_op jit(solution)/shard_map/ppermute | solution.py:24
  72.1 29.7 %copy-start.2 = (bf16[4,512,256]{2,1,0:T(8,128)(2,1)}, bf16[4,512,256]{2,1,0:T(8,128)(2,1)S(1)}, u32[]{:S(2)}) copy-start(bf16[4,512,256]{2,1,0:T(8,128)(2,1)S(1)} %all-to-all-done.2.refs_0_) | copy-start | bytes 3145732
  72.1 24.1 %collective-permute-start.10 = (bf16[4,512,256]{2,1,0:T(8,128)(2,1)S(1)}, bf16[4,512,256]{2,1,0:T(8,128)(2,1)S(1)}, u32[]{:S(2)}, u32[]{:S(2)}) collective-permute-start(bf16[4,512,256]{2,1,0:T(8,128)(2,1)S(1)} %all-to-all-done.2.refs_0_), channel_id=1, source_target_pairs={{0,128},{128,0},{1,129},{129,1},{2,130},{130,2},{3,131},{131,3},{4... | collective-permute-start | bytes 3145736 | tf_op jit(solution)/shard_map/ppermute | solution.py:24
  73.8 28.0 %collective-permute-start.11 = (bf16[4,512,256]{2,1,0:T(8,128)(2,1)S(1)}, bf16[4,512,256]{2,1,0:T(8,128)(2,1)}, u32[]{:S(2)}, u32[]{:S(2)}) collective-permute-start(bf16[4,512,256]{2,1,0:T(8,128)(2,1)S(1)} %all-to-all-done.2.refs_0_), channel_id=1, source_target_pairs={{0,64},{64,0},{1,65},{65,1},{2,66},{66,2},{3,67},{67,3},{4,68},{68... | collective-permute-start | bytes 3145736 | tf_op jit(solution)/shard_map/ppermute | solution.py:24
  96.2 5.6 %copy-start.8 = (bf16[4,512,256]{2,1,0:T(8,128)(2,1)}, bf16[4,512,256]{2,1,0:T(8,128)(2,1)S(1)}, u32[]{:S(2)}) copy-start(bf16[4,512,256]{2,1,0:T(8,128)(2,1)S(1)} %collective-permute-done.10.refs_1_) | copy-start | bytes 3145732
  96.2 5.6 %collective-permute-start.12 = (bf16[4,512,256]{2,1,0:T(8,128)(2,1)S(1)}, bf16[4,512,256]{2,1,0:T(8,128)(2,1)}, u32[]{:S(2)}, u32[]{:S(2)}) collective-permute-start(bf16[4,512,256]{2,1,0:T(8,128)(2,1)S(1)} %collective-permute-done.10.refs_1_), channel_id=1, source_target_pairs={{0,64},{64,0},{1,65},{65,1},{2,66},{66,2},{3,67},{67,3},{4,68},{68... | collective-permute-start | bytes 3145736 | tf_op jit(solution)/shard_map/ppermute | solution.py:24
  96.2 20.7 %all-to-all-start.1 = ((f32[16,32,512]{2,1,0:T(8,128)}), f32[16,32,512]{2,1,0:T(8,128)S(1)}, u32[]{:S(2)}, u32[]{:S(2)}) async-start(f32[16,32,512]{2,1,0:T(8,128)} %bitcast.18), calls=%async_computation.1 | async-start | bytes 2097152 | tf_op jit(solution)/shard_map/all_to_all | solution.py:240
  101.7 63.2 %all-gather.7.cloned.1.call-start = ((), (), s32[]{:S(2)}) async-start(), calls=%async_computation.7 | async-start | bytes 2359296 | tf_op jit(solution)/shard_map/all_gather | solution.py:250
  109.2 15.0 %copy-start.3 = (f32[4,128,512]{2,1,0:T(8,128)S(1)}, f32[4,128,512]{2,1,0:T(8,128)}, u32[]{:S(2)}) copy-start(f32[4,128,512]{2,1,0:T(8,128)} %shard_map.49) | copy-start | bytes 3145732
  116.9 6.6 %collective-permute-start.13 = (bf16[1,4,32,512]{3,2,1,0:T(8,128)(2,1)S(1)}, bf16[1,4,32,512]{3,2,1,0:T(8,128)(2,1)S(1)}, u32[]{:S(2)}, u32[]{:S(2)}) collective-permute-start(bf16[1,4,32,512]{3,2,1,0:T(8,128)(2,1)S(1)} %bitcast.19), channel_id=1, source_target_pairs={{0,8},{8,0},{1,9},{9,1},{2,10},{10,2},{3,11},{11,3},{4,12},{12,4},... | collective-permute-start | bytes 393224 | tf_op jit(solution)/shard_map/ppermute | solution.py:24
  158.1 6.7 %copy-start = (bf16[8,128,512]{2,1,0:T(8,128)(2,1)}, bf16[8,128,512]{2,1,0:T(8,128)(2,1)S(1)}, u32[]{:S(2)}) copy-start(bf16[8,128,512]{2,1,0:T(8,128)(2,1)S(1)} %all_to_all.31) | copy-start | bytes 3145732
  158.1 2.7 %collective-permute-start.14 = (bf16[2,4,128,512]{3,2,1,0:T(8,128)(2,1)S(1)}, bf16[2,4,128,512]{3,2,1,0:T(8,128)(2,1)S(1)}, u32[]{:S(2)}, u32[]{:S(2)}) collective-permute-start(bf16[2,4,128,512]{3,2,1,0:T(8,128)(2,1)S(1)} %bitcast.15), channel_id=1, source_target_pairs={{0,64},{64,0},{1,65},{65,1},{2,66},{66,2},{3,67},{67,3},{4,68},{68... | collective-permute-start | bytes 3145736 | tf_op jit(solution)/shard_map/ppermute | solution.py:24
  160.8 4.1 %copy-start.4 = (bf16[2,4,128,512]{3,2,1,0:T(8,128)(2,1)}, bf16[2,4,128,512]{3,2,1,0:T(8,128)(2,1)S(1)}, u32[]{:S(2)}) copy-start(bf16[2,4,128,512]{3,2,1,0:T(8,128)(2,1)S(1)} %collective-permute-done.14.other_ref) | copy-start | bytes 3145732
Sparse Core Ops, SparseCore 0:
  49.3 41.6 all-gather.4
  124.3 40.5 all-gather.6

commit v9 on v8

--- a/solution.py
+++ b/solution.py
@@ -15,8 +15,8 @@
 COLS = 128
 F32 = jnp.float32
 BF16 = jnp.bfloat16
-VMEM_LIMIT = 58 * 1024 * 1024
-PARAMS = pltpu.CompilerParams(vmem_limit_bytes=VMEM_LIMIT)
+ALL_VMEM = pltpu.CompilerParams(vmem_limit_bytes=58 * 1024 * 1024)
+PARAMS = pltpu.CompilerParams(vmem_limit_bytes=48 * 1024 * 1024)
 
 
 def shift(x, axis, by):
@@ -32,29 +32,29 @@
     return pl.BlockSpec(shape, lambda *_: (0,) * len(shape))
 
 
-def split_kernel(core_ref, in_ref, out_ref):
+def split_kernel(half_ref, in_ref, out_ref):
     exact = in_ref[...]
     high = exact.astype(BF16)
     out_ref[0, :, :COLS] = high
     out_ref[0, :, COLS:] = (exact - high.astype(F32)).astype(BF16)
 
 
-def split_basis(share, count, basis):
-    rows = 2048 // count
+def split_basis(half, basis):
+    rows = 1024
     return pl.pallas_call(
         split_kernel,
         grid_spec=pltpu.PrefetchScalarGridSpec(
             num_scalar_prefetch=1,
             grid=(4,),
-            in_specs=[pl.BlockSpec((rows, COLS), lambda g, share: (g * count + share[0], 0))],
-            out_specs=pl.BlockSpec((1, rows, 256), lambda g, share: (g, 0, 0)),
+            in_specs=[pl.BlockSpec((rows, COLS), lambda g, half: (g * 2 + half[0], 0))],
+            out_specs=pl.BlockSpec((1, rows, 256), lambda g, half: (g, 0, 0)),
         ),
         out_shape=jax.ShapeDtypeStruct((4, rows, 256), BF16),
-        compiler_params=PARAMS,
+        compiler_params=ALL_VMEM,
         cost_estimate=pl.CostEstimate(
             flops=1 << 20, bytes_accessed=4 << 20, transcendentals=0
         ),
-    )(share, basis)
+    )(half, basis)
 
 
 def rotate_ring_kernel(offsets, at_ref, *refs):
@@ -93,23 +93,22 @@
         + [slab, slab],
         out_specs=pl.BlockSpec((1, COLS, TOK), lambda g: (g, 0, 0)),
         scratch_shapes=[pltpu.VMEM((TOK, 2048), BF16), pltpu.SemaphoreType.DMA((16,))],
-        compiler_params=PARAMS,
+        compiler_params=ALL_VMEM,
         cost_estimate=pl.CostEstimate(
             flops=4 * TOK * 2048 * 512, bytes_accessed=7 << 20, transcendentals=0
         ),
     )(at, *[block for block, _ in ring], own, other)
 
 
-def rotate_kernel(at_ref, block_ref, *refs):
-    slabs, (out_ref, lhs, sems) = refs[:4], refs[4:]
-    xh, xl, c = at_ref[1], at_ref[3], at_ref[4]
+def rotate_kernel(at_ref, block_ref, own_ref, other_ref, out_ref, lhs, sems):
+    turned = lax.rem(at_ref[1] + at_ref[4], 2)
 
     @pl.when(pl.program_id(0) == 0)
     def _():
         copies = []
         for z in range(8):
             for side in range(2):
-                at = ((xh if side == 0 else 1 - xh) * 8 + z) * COLS
+                at = ((turned if side == 0 else 1 - turned) * 8 + z) * COLS
                 lanes = pl.ds(pl.multiple_of(at, COLS), COLS)
                 copies.append(
                     pltpu.make_async_copy(block_ref.at[z, side], lhs.at[:, lanes], sems.at[z * 2 + side])
@@ -119,46 +118,35 @@
         for copy in copies:
             copy.wait()
 
-    both = None
-    for i, slab_ref in enumerate(slabs):
-        quarter = (c if i < 2 else 1 - c) * 2 + (xl if i % 2 == 0 else 1 - xl)
-        lanes = pl.ds(pl.multiple_of(quarter * 512, 512), 512)
-        part = jnp.dot(lhs[:, lanes], slab_ref[0], preferred_element_type=F32)
-        both = part if both is None else both + part
+    both = jnp.dot(lhs[:, :1024], own_ref[0], preferred_element_type=F32)
+    both += jnp.dot(lhs[:, 1024:], other_ref[0], preferred_element_type=F32)
     out_ref[0] = (both[:, :COLS] + both[:, COLS:]).T
 
 
-def rotate(at, blocks, slabs):
-    slab = pl.BlockSpec((1, 512, 256), lambda g: (g, 0, 0))
+def rotate(at, blocks, own, other):
+    slab = pl.BlockSpec((1, 1024, 256), lambda g: (g, 0, 0))
     return pl.pallas_call(
         rotate_kernel,
         grid=(4,),
         out_shape=jax.ShapeDtypeStruct((4, COLS, TOK), F32),
         in_specs=[pl.BlockSpec(memory_space=pltpu.SMEM), pl.BlockSpec(memory_space=pltpu.HBM)]
-        + [slab] * 4,
+        + [slab] * 2,
         out_specs=pl.BlockSpec((1, COLS, TOK), lambda g: (g, 0, 0)),
         scratch_shapes=[pltpu.VMEM((TOK, 2048), BF16), pltpu.SemaphoreType.DMA((16,))],
-        compiler_params=PARAMS,
+        compiler_params=ALL_VMEM,
         cost_estimate=pl.CostEstimate(
             flops=4 * TOK * 2048 * 512, bytes_accessed=7 << 20, transcendentals=0
         ),
-    )(at, blocks, *slabs)
-
-
-def product_kernel(scale, at_ref, acts_ref, own_ref, other_ref, out_ref, right, sems):
+    )(at, blocks, own, other)
+
+
+def product_kernel(scale, at_ref, acts_ref, own_ref, other_ref, out_ref, right):
     xh, c = at_ref[1], at_ref[4]
-    copies = []
     for z in range(8):
         for side in range(2):
             place = (xh if side == 0 else 1 - xh) * 8 + z
-            rows = pl.ds(pl.multiple_of(place * 32, 32), 32)
-            copies.append(
-                pltpu.make_async_copy(acts_ref.at[z, side], right.at[:, rows], sems.at[z * 2 + side])
-            )
-    for copy in copies:
-        copy.start()
-    for copy in copies:
-        copy.wait()
+            for s in range(4):
+                right[s, pl.ds(pl.multiple_of(place * 32, 32), 32), :] = acts_ref[z, side, s]
     for row in range(4):
         total = None
         for grads_ref, core in ((own_ref, c), (other_ref, 1 - c)):
@@ -177,10 +165,10 @@
     return pl.pallas_call(
         functools.partial(product_kernel, scale),
         out_shape=jax.ShapeDtypeStruct((4, COLS, 512), F32),
-        in_specs=[pl.BlockSpec(memory_space=pltpu.SMEM), pl.BlockSpec(memory_space=pltpu.HBM)]
-        + [pl.BlockSpec(memory_space=pltpu.VMEM)] * 2,
+        in_specs=[pl.BlockSpec(memory_space=pltpu.SMEM)]
+        + [pl.BlockSpec(memory_space=pltpu.VMEM)] * 3,
         out_specs=pl.BlockSpec(memory_space=pltpu.VMEM),
-        scratch_shapes=[pltpu.VMEM((4, 512, TOK), BF16), pltpu.SemaphoreType.DMA((16,))],
+        scratch_shapes=[pltpu.VMEM((4, 512, TOK), BF16)],
         compiler_params=PARAMS,
         cost_estimate=pl.CostEstimate(
             flops=2 * 4 * 512 * 512 * TOK, bytes_accessed=5 << 20, transcendentals=0
@@ -223,13 +211,12 @@
     z, xh, y, xl, c = (lax.axis_index(a) for a in ("z", "xh", "y", "xl", "c"))
     at = jnp.stack([z, xh, y, xl, c]).astype(jnp.int32)
     half = c.astype(jnp.int32).reshape(1)
-    quarter = (c * 2 + xl).astype(jnp.int32).reshape(1)
 
     a0, grads_pair, mine_in, basis_out = sync(
-        pair(activations), pair(gradients), split_basis(half, 2, basis_in), basis_out
+        pair(activations), pair(gradients), split_basis(half, basis_in), basis_out
     )
     own_in = lax.all_to_all(mine_in, "y", 0, 0)
-    up1, down1, mine_out = sync(*ring_step(a0, a0), split_basis(quarter, 4, basis_out))
+    up1, down1, mine_out = sync(*ring_step(a0, a0), split_basis(half, basis_out))
     up2, down2, mine_out = sync(*ring_step(up1, down1), mine_out)
     up3, down3, own_in, mine_out = sync(*ring_step(up2, down2), own_in, mine_out)
     own_out = lax.all_to_all(mine_out, "y", 0, 0)
@@ -239,10 +226,8 @@
     acts_part = rotate_ring(at, ring, own_in, other_in)
     acts_in = lax.all_to_all(acts_part.reshape(16, 32, TOK), ("xl", "c", "y"), 0, 0)
 
-    own_out = after(own_out, acts_part)
-    beside_out = shift(own_out, "xl", 1)
-    others = shift(own_out, "c", 1), shift(beside_out, "c", 1)
-    grads_part = rotate(at, grad_blocks, (own_out, beside_out, *others))
+    other_out = shift(after(own_out, acts_part), "c", 1)
+    grads_part = rotate(at, grad_blocks, own_out, other_out)
     acts_in, grads_part = sync(acts_in, grads_part)
     grads_in = lax.all_to_all(grads_part, "y", 0, 0)
 

time: 202 us -> 185 us (0.916)
  blocking collectives: 50.7 us -> 44.5 us
  waiting for transfers between devices: 63.3 us -> 58.3 us
  Pallas kernels: 33.2 us -> 28.6 us
  local copies, waits for them, and re-layouts: 0.73 us -> 3.67 us
  starting transfers between devices: 36.5 us -> 34 us
    ppermute x15 -> x13, waiting for transfers between devices: 51.6 us -> 28.6 us  [shift(): return lax.ppermute(x, axis, [(i, (i + by) % n) for i in range(n)])]
    all_gather x1, waiting for transfers between devices: 0.02 us -> 13 us  [body(): grad_blocks = lax.all_gather(after(grads_pair, up2), 'z')]
    all_to_all x1, waiting for transfers between devices: 0.01 us -> 8.24 us  [body(): own_out = lax.all_to_all(mine_out, 'y', 0, 0)]
    all_to_all x1, waiting for transfers between devices: 7.57 us -> 0.01 us  [body(): lax.all_to_all(acts_part.reshape(16, 32, TOK), ('xl', 'c', 'y'), 0, 0)]
    all_gather x1, waiting for transfers between devices: 4.06 us -> 7.71 us  [body(): rot_acts = lax.all_gather(pair(acts), 'z')]
    pallas_call x1, Pallas kernels: 7.08 us -> 3.52 us  [products(): pl.pallas_call(functools.partial(product_kernel, scale), out_shape=jax.Sh...]
    unnamed x28 -> x26, local copies, waits for them, and re-layouts: 0.05 us -> 2.99 us
    all_to_all x1, blocking collectives: 17.4 us -> 15 us  [body(): grads_in = lax.all_to_all(grads_part, 'y', 0, 0)]
  transfers between devices with their start and end apart: 20 -> 18, of which waited for: 12 -> 12; matrix products, arithmetic and copies ran while one was open for 0% -> 0% of each run, Pallas kernels for 11% -> 12%
where the time goes in v9:
time: 185 us; the launch traced here: 184 us
  waiting for transfers between devices  58.3 us (32%)
  blocking collectives  44.5 us (24%)
  starting transfers between devices  34 us (18%)
  Pallas kernels  28.6 us (15%)
  between operations  13.6 us (7%)
  local copies, waits for them, and re-layouts  3.67 us (2%)
    ppermute x13, waiting for transfers between devices, shift(): return lax.ppermute(x, axis, [(i, (i + by) % n) for i in range(n)])  28.6 us
    ppermute x13, starting transfers between devices, shift(): return lax.ppermute(x, axis, [(i, (i + by) % n) for i in range(n)])  20.3 us
    all_to_all x1, blocking collectives, body(): return weave(lax.all_to_all(part, 'y', 0, 0))  15.5 us
    all_to_all x1, blocking collectives, body(): grads_in = lax.all_to_all(grads_part, 'y', 0, 0)  15 us
    all_to_all x1, blocking collectives, body(): rot_own = lax.all_to_all(copies, ('xl', 'y'), 0, 0).reshape(2, 4, COLS, TOK)  14 us
    all_gather x1, waiting for transfers between devices, body(): grad_blocks = lax.all_gather(after(grads_pair, up2), 'z')  13 us
    all_to_all x1, waiting for transfers between devices, body(): own_out = lax.all_to_all(mine_out, 'y', 0, 0)  8.24 us
    pallas_call x2, Pallas kernels, split_basis(): pl.pallas_call(split_kernel, grid_spec=pltpu.PrefetchScalarGridSpec(num_s...  7.93 us
  transfers between devices with their start and end apart: 18, of which 12 were waited for; matrix products, arithmetic and copies ran while one was open for 0% of the time, Pallas kernels for 12%

profile of v9, /device:TPU:2, one launch (start us, length us, event | category | flops | bytes accessed | tf_op | source)
XLA Modules:
  0.0 184.2 jit_solution(1806141979122919774)
XLA Ops:
  6.5 2.1 %collective-permute-start = (bf16[1,512,128]{2,1,0:T(8,128)(2,1)}, bf16[1,512,128]{2,1,0:T(8,128)(2,1)S(1)}, u32[]{:S(2)}, u32[]{:S(2)}) collective-permute-start(bf16[1,512,128]{2,1,0:T(8,128)(2,1)} %param.4), channel_id=1, source_target_pairs={{0,8},{8,0},{1,9},{9,1},{2,10},{10,2},{3,11},{11,3},{4,12},{12,4},... | collective-permute-start | bytes 393224 | tf_op jit(solution)/shard_map/ppermute | solution.py:24
  8.7 1.4 collective-permute-start.1
  10.1 4.0 %shard_map.46 = bf16[4,1024,256]{2,1,0:T(8,128)(2,1)} custom-call(s32[1]{0:T(128)} %bitcast.4.half_ref, f32[8192,128]{1,0:T(8,128)} %in_ref.1), custom_call_target="tpu_custom_call" | custom-call | flops 1048576 | bytes 4194304 | tf_op jit(solution)/shard_map/pallas_call | solution.py:44
  14.1 0.4 collective-permute-done
  14.5 0.0 copy-done.5
  14.5 0.0 copy-start.4
  14.5 1.8 collective-permute-done.1
  16.3 0.0 copy-done.6
  16.3 0.7 pad_maximum_fusion.1
  17.0 4.5 %all-to-all-start = ((bf16[4,1024,256]{2,1,0:T(8,128)(2,1)}), bf16[4,1024,256]{2,1,0:T(8,128)(2,1)S(1)}, u32[]{:S(2)}, u32[]{:S(2)}) async-start(bf16[4,1024,256]{2,1,0:T(8,128)(2,1)} %shard_map.46), calls=%async_computation | async-start | bytes 4194304 | tf_op jit(solution)/shard_map/all_to_all | solution.py:218
  21.5 1.9 %collective-permute-start.2 = (bf16[2,512,128]{2,1,0:T(8,128)(2,1)S(1)}, bf16[2,512,128]{2,1,0:T(8,128)(2,1)S(1)}, u32[]{:S(2)}, u32[]{:S(2)}) collective-permute-start(bf16[2,512,128]{2,1,0:T(8,128)(2,1)S(1)} %pad_maximum_fusion.refs_0_), channel_id=1, source_target_pairs={{0,1},{1,2},{2,3},{3,4},{4,5},{5,6},{6,7},{7,0},{8,9},{9,10},{10,1... | collective-permute-start | bytes 786440 | tf_op jit(solution)/shard_map/ppermute | solution.py:24
  23.4 0.0 copy-done.4
  23.4 4.0 %collective-permute-start.3 = (bf16[2,512,128]{2,1,0:T(8,128)(2,1)S(1)}, bf16[2,512,128]{2,1,0:T(8,128)(2,1)S(1)}, u32[]{:S(2)}, u32[]{:S(2)}) collective-permute-start(bf16[2,512,128]{2,1,0:T(8,128)(2,1)S(1)} %pad_maximum_fusion.refs_0_), channel_id=1, source_target_pairs={{0,7},{1,0},{2,1},{3,2},{4,3},{5,4},{6,5},{7,6},{8,15},{9,8},{10,9... | collective-permute-start | bytes 786440 | tf_op jit(solution)/shard_map/ppermute | solution.py:24
  27.4 3.9 %shard_map.47 = bf16[4,1024,256]{2,1,0:T(8,128)(2,1)} custom-call(s32[1]{0:T(128)} %bitcast.4.half_ref, f32[8192,128]{1,0:T(8,128)} %in_ref.2), custom_call_target="tpu_custom_call" | custom-call | flops 1048576 | bytes 4194304 | tf_op jit(solution)/shard_map/pallas_call | solution.py:44
  31.4 1.3 collective-permute-done.2.refs_1_
  32.7 0.0 collective-permute-done.3.refs_2_
  32.7 0.1 collective-permute-start.4
  32.7 3.2 %collective-permute-start.5 = (bf16[2,512,128]{2,1,0:T(8,128)(2,1)S(1)}, bf16[2,512,128]{2,1,0:T(8,128)(2,1)S(1)}, u32[]{:S(2)}, u32[]{:S(2)}) collective-permute-start(bf16[2,512,128]{2,1,0:T(8,128)(2,1)S(1)} %collective-permute-done.3.refs_2_), channel_id=1, source_target_pairs={{0,7},{1,0},{2,1},{3,2},{4,3},{5,4},{6,5},{7,6},{8,15},{9,8},{10,9... | collective-permute-start | bytes 786440 | tf_op jit(solution)/shard_map/ppermute | solution.py:24
  36.0 4.4 %collective-permute-done.4.refs_3_ = bf16[2,512,128]{2,1,0:T(8,128)(2,1)S(1)} collective-permute-done((bf16[2,512,128]{2,1,0:T(8,128)(2,1)S(1)}, bf16[2,512,128]{2,1,0:T(8,128)(2,1)S(1)}, u32[]{:S(2)}, u32[]{:S(2)}) %collective-permute-start.4) | collective-permute-done | bytes 262176 | tf_op jit(solution)/shard_map/ppermute | solution.py:24
  40.3 0.0 collective-permute-done.5.refs_4_
  40.3 2.4 %collective-permute-start.6 = (bf16[2,512,128]{2,1,0:T(8,128)(2,1)S(1)}, bf16[2,512,128]{2,1,0:T(8,128)(2,1)S(1)}, u32[]{:S(2)}, u32[]{:S(2)}) collective-permute-start(bf16[2,512,128]{2,1,0:T(8,128)(2,1)S(1)} %collective-permute-done.4.refs_3_), channel_id=1, source_target_pairs={{0,1},{1,2},{2,3},{3,4},{4,5},{5,6},{6,7},{7,0},{8,9},{9,10},{10,1... | collective-permute-start | bytes 786440 | tf_op jit(solution)/shard_map/ppermute | solution.py:24
  42.7 0.9 collective-permute-start.7
  43.7 4.3 %collective-permute-done.6.refs_5_ = bf16[2,512,128]{2,1,0:T(8,128)(2,1)S(1)} collective-permute-done((bf16[2,512,128]{2,1,0:T(8,128)(2,1)S(1)}, bf16[2,512,128]{2,1,0:T(8,128)(2,1)S(1)}, u32[]{:S(2)}, u32[]{:S(2)}) %collective-permute-start.6) | collective-permute-done | bytes 262176 | tf_op jit(solution)/shard_map/ppermute | solution.py:24
  48.0 1.2 collective-permute-done.7.refs_6_
  49.2 0.0 all-to-all-done.refs_8_
  49.2 0.0 collective-permute-start.9
  49.2 4.5 %all-to-all-start.2 = ((bf16[4,1024,256]{2,1,0:T(8,128)(2,1)}), bf16[4,1024,256]{2,1,0:T(8,128)(2,1)}, u32[]{:S(2)}, u32[]{:S(2)}) async-start(bf16[4,1024,256]{2,1,0:T(8,128)(2,1)} %shard_map.47), calls=%async_computation.2 | async-start | bytes 4194304 | tf_op jit(solution)/shard_map/all_to_all | solution.py:222
  53.7 0.0 all-gather.5.cloned.1.call-start
  53.7 0.7 all-gather.5.cloned.1.call-update
  54.4 0.0 copy-done.8
  54.5 0.0 copy-done.9
  54.5 0.0 copy-done.10
  54.5 0.0 copy-done.11
  54.5 2.1 %collective-permute-start.8 = (bf16[2,512,128]{2,1,0:T(8,128)(2,1)S(1)}, bf16[2,512,128]{2,1,0:T(8,128)(2,1)}, u32[]{:S(2)}, u32[]{:S(2)}) collective-permute-start(bf16[2,512,128]{2,1,0:T(8,128)(2,1)S(1)} %collective-permute-done.6.refs_5_), channel_id=1, source_target_pairs={{0,1},{1,2},{2,3},{3,4},{4,5},{5,6},{6,7},{7,0},{8,9},{9,10},{10,1... | collective-permute-start | bytes 786440 | tf_op jit(solution)/shard_map/ppermute | solution.py:24
  56.6 0.6 stack.23.at_ref
  57.2 8.2 %collective-permute-done.8.refs_7_ = bf16[2,512,128]{2,1,0:T(8,128)(2,1)} collective-permute-done((bf16[2,512,128]{2,1,0:T(8,128)(2,1)S(1)}, bf16[2,512,128]{2,1,0:T(8,128)(2,1)}, u32[]{:S(2)}, u32[]{:S(2)}) %collective-permute-start.8) | collective-permute-done | bytes 262176 | tf_op jit(solution)/shard_map/ppermute | solution.py:24
  65.4 0.0 collective-permute-done.9.refs_9_
  65.4 7.4 %shard_map.48 = f32[4,128,512]{2,1,0:T(8,128)} custom-call(s32[5]{0:T(128)} %stack.23.at_ref, bf16[2,512,128]{2,1,0:T(8,128)(2,1)} %copy-done.4, bf16[2,512,128]{2,1,0:T(8,128)(2,1)} %copy-done.8, bf16[2,512,128]{2,1,0:T(8,128)(2,1)} %copy-done.9, bf16[2,512,128]{2,1,0:T(8,128)(2,1)} %copy-done.10, bf16[2,512,128]{2,1,0:T(8,128)(2,1)} %copy-done.11, ...), custom_call_target="tpu_custom_call" | custom-call | flops 2147483648 | bytes 7340032 | tf_op jit(solution)/shard_map/pallas_call | solution.py:87
  72.8 8.2 %all-to-all-done.2.own_ref = bf16[4,1024,256]{2,1,0:T(8,128)(2,1)} async-done(((bf16[4,1024,256]{2,1,0:T(8,128)(2,1)}), bf16[4,1024,256]{2,1,0:T(8,128)(2,1)}, u32[]{:S(2)}, u32[]{:S(2)}) %all-to-all-start.2) | async-done | bytes 2097184 | tf_op jit(solution)/shard_map/all_to_all | solution.py:222
  81.0 0.0 collective-permute-start.10
  81.0 4.6 %all-to-all-start.1 = ((f32[16,32,512]{2,1,0:T(8,128)}), f32[16,32,512]{2,1,0:T(8,128)S(1)}, u32[]{:S(2)}, u32[]{:S(2)}) async-start(f32[16,32,512]{2,1,0:T(8,128)} %bitcast.17), calls=%async_computation.1 | async-start | bytes 2097152 | tf_op jit(solution)/shard_map/all_to_all | solution.py:227
  85.6 0.0 all-gather.7.cloned.1.call-start
  85.7 13.0 %all-gather.5.cloned.1.call-done = bf16[16,512,128]{2,1,0:T(8,128)(2,1)} async-done(((bf16[2,512,128]{2,1,0:T(8,128)(2,1)}), bf16[16,512,128]{2,1,0:T(8,128)(2,1)}) %all-gather.5.cloned.1.call-update) | async-done | bytes 2097168 | tf_op jit(solution)/shard_map/all_gather | solution.py:223
  98.7 0.0 collective-permute-done.10.other_ref
  98.7 1.4 copy-done.7
  100.0 7.4 %shard_map.49 = f32[4,128,512]{2,1,0:T(8,128)} custom-call(s32[5]{0:T(128)} %stack.23.at_ref, bf16[8,2,512,128]{3,2,1,0:T(8,128)(2,1)} %bitcast.20, bf16[4,1024,256]{2,1,0:T(8,128)(2,1)} %all-to-all-done.2.own_ref, bf16[4,1024,256]{2,1,0:T(8,128)(2,1)} %copy-done.7), custom_call_target="tpu_custom_call" | custom-call | flops 2147483648 | bytes 7340032 | tf_op jit(solution)/shard_map/pallas_call | solution.py:128
  107.4 0.0 all-to-all-done.1
  107.4 0.1 bitcast_reduce_fusion
  107.5 2.1 %collective-permute-start.11 = (bf16[1,4,32,512]{3,2,1,0:T(8,128)(2,1)S(1)}, bf16[1,4,32,512]{3,2,1,0:T(8,128)(2,1)S(1)}, u32[]{:S(2)}, u32[]{:S(2)}) collective-permute-start(bf16[1,4,32,512]{3,2,1,0:T(8,128)(2,1)S(1)} %bitcast.18), channel_id=1, source_target_pairs={{0,8},{8,0},{1,9},{9,1},{2,10},{10,2},{3,11},{11,3},{4,12},{12,4},... | collective-permute-start | bytes 393224 | tf_op jit(solution)/shard_map/ppermute | solution.py:24
  109.7 4.4 %collective-permute-done.11 = bf16[1,4,32,512]{3,2,1,0:T(8,128)(2,1)S(1)} collective-permute-done((bf16[1,4,32,512]{3,2,1,0:T(8,128)(2,1)S(1)}, bf16[1,4,32,512]{3,2,1,0:T(8,128)(2,1)S(1)}, u32[]{:S(2)}, u32[]{:S(2)}) %collective-permute-start.11) | collective-permute-done | bytes 131104 | tf_op jit(solution)/shard_map/ppermute | solution.py:24
  114.1 0.7 pad_maximum_fusion.2
  114.8 0.0 all-gather.7.cloned.1.call-update
  114.8 15.0 %all_to_all.30 = f32[4,128,512]{2,1,0:T(8,128)S(1)} all-to-all(f32[4,128,512]{2,1,0:T(8,128)S(1)} %copy-done.3), channel_id=1, replica_groups=mesh['xl'=2,'c'=2,'y'=4,'xh'=2,'z'=8] {'y'}, dimensions={0} | all-to-all | bytes 2097152 | tf_op jit(solution)/shard_map/all_to_all | solution.py:232
  129.8 0.1 reduce_sum.19
  129.9 0.1 broadcast_in_dim.4
  130.0 14.0 %all_to_all.31 = bf16[8,128,512]{2,1,0:T(8,128)(2,1)S(1)} all-to-all(bf16[8,128,512]{2,1,0:T(8,128)(2,1)S(1)} %broadcast_in_dim.4), channel_id=1, replica_groups=mesh['xl'=2,'c'=2,'y'=4,'xh'=2,'z'=8] {'xl','y'}, dimensions={0} | all-to-all | bytes 2097152 | tf_op jit(solution)/shard_map/all_to_all | solution.py:239
  144.0 0.0 collective-permute-start.12
  144.0 2.7 %collective-permute-done.12.other_ref = bf16[2,4,128,512]{3,2,1,0:T(8,128)(2,1)S(1)} collective-permute-done((bf16[2,4,128,512]{3,2,1,0:T(8,128)(2,1)S(1)}, bf16[2,4,128,512]{3,2,1,0:T(8,128)(2,1)S(1)}, u32[]{:S(2)}, u32[]{:S(2)}) %collective-permute-start.12) | collective-permute-done | bytes 1048608 | tf_op jit(solution)/shard_map/ppermute | solution.py:24
  146.7 7.7 %all-gather.7.cloned.1.call-done = bf16[16,4,32,512]{3,2,1,0:T(8,128)(2,1)} async-done(((bf16[2,4,32,512]{3,2,1,0:T(8,128)(2,1)}), bf16[16,4,32,512]{3,2,1,0:T(8,128)(2,1)}) %all-gather.7.cloned.1.call-update) | async-done | bytes 2097168 | tf_op jit(solution)/shard_map/all_gather | solution.py:235
  154.4 0.0 copy-done.1
  154.4 1.6 copy-done
  156.0 3.5 %shard_map.50 = f32[4,128,512]{2,1,0:T(8,128)S(1)} custom-call(s32[5]{0:T(128)S(1)} %copy-done.1, bf16[8,2,4,32,512]{4,3,2,1,0:T(8,128)(2,1)S(1)} %bitcast.16, bf16[2,4,128,512]{3,2,1,0:T(8,128)(2,1)S(1)} %bitcast.15, bf16[2,4,128,512]{3,2,1,0:T(8,128)(2,1)S(1)} %collective-permute-done.12.other_ref), custom_call_target="tpu_custom_call" | custom-call | flops 1073741824 | bytes 5242880 | tf_op jit(solution)/shard_map/pallas_call | solution.py:165
  159.5 15.5 %all_to_all.32.in_ref = f32[4,128,512]{2,1,0:T(8,128)S(1)} all-to-all(f32[4,128,512]{2,1,0:T(8,128)S(1)} %shard_map.50), channel_id=1, replica_groups=mesh['xl'=2,'c'=2,'y'=4,'xh'=2,'z'=8] {'y'}, dimensions={0} | all-to-all | bytes 2097152 | tf_op jit(solution)/shard_map/all_to_all | solution.py:243
  175.0 2.4 %shard_map.51 = f32[128,2048]{1,0:T(8,128)} custom-call(f32[4,128,512]{2,1,0:T(8,128)S(1)} %all_to_all.32.in_ref), custom_call_target="tpu_custom_call" | custom-call | tf_op jit(solution)/shard_map/pallas_call | solution.py:188
  (16 shorter events, 0.1 us)
Async XLA Ops:
  6.5 8.0 %collective-permute-start = (bf16[1,512,128]{2,1,0:T(8,128)(2,1)}, bf16[1,512,128]{2,1,0:T(8,128)(2,1)S(1)}, u32[]{:S(2)}, u32[]{:S(2)}) collective-permute-start(bf16[1,512,128]{2,1,0:T(8,128)(2,1)} %param.4), channel_id=1, source_target_pairs={{0,8},{8,0},{1,9},{9,1},{2,10},{10,2},{3,11},{11,3},{4,12},{12,4},... | collective-permute-start | bytes 393224 | tf_op jit(solution)/shard_map/ppermute | solution.py:24
  8.7 7.6 %collective-permute-start.1 = (bf16[1,512,128]{2,1,0:T(8,128)(2,1)}, bf16[1,512,128]{2,1,0:T(8,128)(2,1)S(1)}, u32[]{:S(2)}, u32[]{:S(2)}) collective-permute-start(bf16[1,512,128]{2,1,0:T(8,128)(2,1)} %param.5), channel_id=1, source_target_pairs={{0,8},{8,0},{1,9},{9,1},{2,10},{10,2},{3,11},{11,3},{4,12},{12,4},... | collective-permute-start | bytes 393224 | tf_op jit(solution)/shard_map/ppermute | solution.py:24
  10.1 4.4 %copy-start.5 = (bf16[1,512,128]{2,1,0:T(8,128)(2,1)S(1)}, bf16[1,512,128]{2,1,0:T(8,128)(2,1)}, u32[]{:S(2)}) copy-start(bf16[1,512,128]{2,1,0:T(8,128)(2,1)} %param.4) | copy-start | bytes 393220
  10.1 6.2 %copy-start.6 = (bf16[1,512,128]{2,1,0:T(8,128)(2,1)S(1)}, bf16[1,512,128]{2,1,0:T(8,128)(2,1)}, u32[]{:S(2)}) copy-start(bf16[1,512,128]{2,1,0:T(8,128)(2,1)} %param.5) | copy-start | bytes 393220
  14.5 8.9 %copy-start.4 = (bf16[2,512,128]{2,1,0:T(8,128)(2,1)}, bf16[2,512,128]{2,1,0:T(8,128)(2,1)S(1)}, u32[]{:S(2)}) copy-start(bf16[2,512,128]{2,1,0:T(8,128)(2,1)S(1)} %pad_maximum_fusion.refs_0_) | copy-start | bytes 786436
  17.0 32.1 %all-to-all-start = ((bf16[4,1024,256]{2,1,0:T(8,128)(2,1)}), bf16[4,1024,256]{2,1,0:T(8,128)(2,1)S(1)}, u32[]{:S(2)}, u32[]{:S(2)}) async-start(bf16[4,1024,256]{2,1,0:T(8,128)(2,1)} %shard_map.46), calls=%async_computation | async-start | bytes 4194304 | tf_op jit(solution)/shard_map/all_to_all | solution.py:218
  21.5 11.2 %collective-permute-start.2 = (bf16[2,512,128]{2,1,0:T(8,128)(2,1)S(1)}, bf16[2,512,128]{2,1,0:T(8,128)(2,1)S(1)}, u32[]{:S(2)}, u32[]{:S(2)}) collective-permute-start(bf16[2,512,128]{2,1,0:T(8,128)(2,1)S(1)} %pad_maximum_fusion.refs_0_), channel_id=1, source_target_pairs={{0,1},{1,2},{2,3},{3,4},{4,5},{5,6},{6,7},{7,0},{8,9},{9,10},{10,1... | collective-permute-start | bytes 786440 | tf_op jit(solution)/shard_map/ppermute | solution.py:24
  23.4 9.2 %collective-permute-start.3 = (bf16[2,512,128]{2,1,0:T(8,128)(2,1)S(1)}, bf16[2,512,128]{2,1,0:T(8,128)(2,1)S(1)}, u32[]{:S(2)}, u32[]{:S(2)}) collective-permute-start(bf16[2,512,128]{2,1,0:T(8,128)(2,1)S(1)} %pad_maximum_fusion.refs_0_), channel_id=1, source_target_pairs={{0,7},{1,0},{2,1},{3,2},{4,3},{5,4},{6,5},{7,6},{8,15},{9,8},{10,9... | collective-permute-start | bytes 786440 | tf_op jit(solution)/shard_map/ppermute | solution.py:24
  32.7 21.8 %copy-start.8 = (bf16[2,512,128]{2,1,0:T(8,128)(2,1)}, bf16[2,512,128]{2,1,0:T(8,128)(2,1)S(1)}, u32[]{:S(2)}) copy-start(bf16[2,512,128]{2,1,0:T(8,128)(2,1)S(1)} %collective-permute-done.2.refs_1_) | copy-start | bytes 786436
  32.7 21.8 %copy-start.9 = (bf16[2,512,128]{2,1,0:T(8,128)(2,1)}, bf16[2,512,128]{2,1,0:T(8,128)(2,1)S(1)}, u32[]{:S(2)}) copy-start(bf16[2,512,128]{2,1,0:T(8,128)(2,1)S(1)} %collective-permute-done.3.refs_2_) | copy-start | bytes 786436
  32.7 7.7 %collective-permute-start.4 = (bf16[2,512,128]{2,1,0:T(8,128)(2,1)S(1)}, bf16[2,512,128]{2,1,0:T(8,128)(2,1)S(1)}, u32[]{:S(2)}, u32[]{:S(2)}) collective-permute-start(bf16[2,512,128]{2,1,0:T(8,128)(2,1)S(1)} %collective-permute-done.2.refs_1_), channel_id=1, source_target_pairs={{0,1},{1,2},{2,3},{3,4},{4,5},{5,6},{6,7},{7,0},{8,9},{9,10},{10,1... | collective-permute-start | bytes 786440 | tf_op jit(solution)/shard_map/ppermute | solution.py:24
  32.7 7.6 %collective-permute-start.5 = (bf16[2,512,128]{2,1,0:T(8,128)(2,1)S(1)}, bf16[2,512,128]{2,1,0:T(8,128)(2,1)S(1)}, u32[]{:S(2)}, u32[]{:S(2)}) collective-permute-start(bf16[2,512,128]{2,1,0:T(8,128)(2,1)S(1)} %collective-permute-done.3.refs_2_), channel_id=1, source_target_pairs={{0,7},{1,0},{2,1},{3,2},{4,3},{5,4},{6,5},{7,6},{8,15},{9,8},{10,9... | collective-permute-start | bytes 786440 | tf_op jit(solution)/shard_map/ppermute | solution.py:24
  40.3 14.1 %copy-start.10 = (bf16[2,512,128]{2,1,0:T(8,128)(2,1)}, bf16[2,512,128]{2,1,0:T(8,128)(2,1)S(1)}, u32[]{:S(2)}) copy-start(bf16[2,512,128]{2,1,0:T(8,128)(2,1)S(1)} %collective-permute-done.4.refs_3_) | copy-start | bytes 786436
  40.3 14.1 %copy-start.11 = (bf16[2,512,128]{2,1,0:T(8,128)(2,1)}, bf16[2,512,128]{2,1,0:T(8,128)(2,1)S(1)}, u32[]{:S(2)}) copy-start(bf16[2,512,128]{2,1,0:T(8,128)(2,1)S(1)} %collective-permute-done.5.refs_4_) | copy-start | bytes 786436
  40.3 7.7 %collective-permute-start.6 = (bf16[2,512,128]{2,1,0:T(8,128)(2,1)S(1)}, bf16[2,512,128]{2,1,0:T(8,128)(2,1)S(1)}, u32[]{:S(2)}, u32[]{:S(2)}) collective-permute-start(bf16[2,512,128]{2,1,0:T(8,128)(2,1)S(1)} %collective-permute-done.4.refs_3_), channel_id=1, source_target_pairs={{0,1},{1,2},{2,3},{3,4},{4,5},{5,6},{6,7},{7,0},{8,9},{9,10},{10,1... | collective-permute-start | bytes 786440 | tf_op jit(solution)/shard_map/ppermute | solution.py:24
  42.7 6.5 %collective-permute-start.7 = (bf16[2,512,128]{2,1,0:T(8,128)(2,1)S(1)}, bf16[2,512,128]{2,1,0:T(8,128)(2,1)}, u32[]{:S(2)}, u32[]{:S(2)}) collective-permute-start(bf16[2,512,128]{2,1,0:T(8,128)(2,1)S(1)} %collective-permute-done.5.refs_4_), channel_id=1, source_target_pairs={{0,7},{1,0},{2,1},{3,2},{4,3},{5,4},{6,5},{7,6},{8,15},{9,8},{10,9... | collective-permute-start | bytes 786440 | tf_op jit(solution)/shard_map/ppermute | solution.py:24
  48.0 6.5 %copy-start.12 = (bf16[2,512,128]{2,1,0:T(8,128)(2,1)}, bf16[2,512,128]{2,1,0:T(8,128)(2,1)S(1)}, u32[]{:S(2)}) copy-start(bf16[2,512,128]{2,1,0:T(8,128)(2,1)S(1)} %collective-permute-done.6.refs_5_) | copy-start | bytes 786436
  49.2 5.3 %copy-start.2 = (bf16[4,1024,256]{2,1,0:T(8,128)(2,1)}, bf16[4,1024,256]{2,1,0:T(8,128)(2,1)S(1)}, u32[]{:S(2)}) copy-start(bf16[4,1024,256]{2,1,0:T(8,128)(2,1)S(1)} %all-to-all-done.refs_8_) | copy-start | bytes 6291460
  49.2 16.2 %collective-permute-start.9 = (bf16[4,1024,256]{2,1,0:T(8,128)(2,1)S(1)}, bf16[4,1024,256]{2,1,0:T(8,128)(2,1)}, u32[]{:S(2)}, u32[]{:S(2)}) collective-permute-start(bf16[4,1024,256]{2,1,0:T(8,128)(2,1)S(1)} %all-to-all-done.refs_8_), channel_id=1, source_target_pairs={{0,64},{64,0},{1,65},{65,1},{2,66},{66,2},{3,67},{67,3},{4,68},{68... | collective-permute-start | bytes 6291464 | tf_op jit(solution)/shard_map/ppermute | solution.py:24
  49.2 31.8 %all-to-all-start.2 = ((bf16[4,1024,256]{2,1,0:T(8,128)(2,1)}), bf16[4,1024,256]{2,1,0:T(8,128)(2,1)}, u32[]{:S(2)}, u32[]{:S(2)}) async-start(bf16[4,1024,256]{2,1,0:T(8,128)(2,1)} %shard_map.47), calls=%async_computation.2 | async-start | bytes 4194304 | tf_op jit(solution)/shard_map/all_to_all | solution.py:222
  53.7 44.9 %all-gather.5.cloned.1.call-start = ((), (), s32[]{:S(2)}) async-start(), calls=%async_computation.6 | async-start | bytes 2359296 | tf_op jit(solution)/shard_map/all_gather | solution.py:223
  54.5 10.9 %collective-permute-start.8 = (bf16[2,512,128]{2,1,0:T(8,128)(2,1)S(1)}, bf16[2,512,128]{2,1,0:T(8,128)(2,1)}, u32[]{:S(2)}, u32[]{:S(2)}) collective-permute-start(bf16[2,512,128]{2,1,0:T(8,128)(2,1)S(1)} %collective-permute-done.6.refs_5_), channel_id=1, source_target_pairs={{0,1},{1,2},{2,3},{3,4},{4,5},{5,6},{6,7},{7,0},{8,9},{9,10},{10,1... | collective-permute-start | bytes 786440 | tf_op jit(solution)/shard_map/ppermute | solution.py:24
  81.0 17.6 %collective-permute-start.10 = (bf16[4,1024,256]{2,1,0:T(8,128)(2,1)}, bf16[4,1024,256]{2,1,0:T(8,128)(2,1)S(1)}, u32[]{:S(2)}, u32[]{:S(2)}) collective-permute-start(bf16[4,1024,256]{2,1,0:T(8,128)(2,1)} %all-to-all-done.2.own_ref), channel_id=1, source_target_pairs={{0,64},{64,0},{1,65},{65,1},{2,66},{66,2},{3,67},{67,3},{4,68},{68... | collective-permute-start | bytes 6291464 | tf_op jit(solution)/shard_map/ppermute | solution.py:24
  81.0 26.4 %all-to-all-start.1 = ((f32[16,32,512]{2,1,0:T(8,128)}), f32[16,32,512]{2,1,0:T(8,128)S(1)}, u32[]{:S(2)}, u32[]{:S(2)}) async-start(f32[16,32,512]{2,1,0:T(8,128)} %bitcast.17), calls=%async_computation.1 | async-start | bytes 2097152 | tf_op jit(solution)/shard_map/all_to_all | solution.py:227
  85.6 68.8 %all-gather.7.cloned.1.call-start = ((), (), s32[]{:S(2)}) async-start(), calls=%async_computation.7 | async-start | bytes 2359296 | tf_op jit(solution)/shard_map/all_gather | solution.py:235
  98.7 1.4 copy-start.7
  107.4 7.4 %copy-start.3 = (f32[4,128,512]{2,1,0:T(8,128)S(1)}, f32[4,128,512]{2,1,0:T(8,128)}, u32[]{:S(2)}) copy-start(f32[4,128,512]{2,1,0:T(8,128)} %shard_map.49) | copy-start | bytes 3145732
  107.5 6.6 %collective-permute-start.11 = (bf16[1,4,32,512]{3,2,1,0:T(8,128)(2,1)S(1)}, bf16[1,4,32,512]{3,2,1,0:T(8,128)(2,1)S(1)}, u32[]{:S(2)}, u32[]{:S(2)}) collective-permute-start(bf16[1,4,32,512]{3,2,1,0:T(8,128)(2,1)S(1)} %bitcast.18), channel_id=1, source_target_pairs={{0,8},{8,0},{1,9},{9,1},{2,10},{10,2},{3,11},{11,3},{4,12},{12,4},... | collective-permute-start | bytes 393224 | tf_op jit(solution)/shard_map/ppermute | solution.py:24
  129.8 24.6 %copy-start.1 = (s32[5]{0:T(128)S(1)}, s32[5]{0:T(128)}, u32[]{:S(2)}) copy-start(s32[5]{0:T(128)} %stack.23.at_ref) | copy-start | bytes 64
  144.0 2.7 %collective-permute-start.12 = (bf16[2,4,128,512]{3,2,1,0:T(8,128)(2,1)S(1)}, bf16[2,4,128,512]{3,2,1,0:T(8,128)(2,1)S(1)}, u32[]{:S(2)}, u32[]{:S(2)}) collective-permute-start(bf16[2,4,128,512]{3,2,1,0:T(8,128)(2,1)S(1)} %bitcast.14), channel_id=1, source_target_pairs={{0,64},{64,0},{1,65},{65,1},{2,66},{66,2},{3,67},{67,3},{4,68},{68... | collective-permute-start | bytes 3145736 | tf_op jit(solution)/shard_map/ppermute | solution.py:24
  154.4 1.6 copy-start
Sparse Core Ops, SparseCore 0:
  56.3 42.2 all-gather.4
  115.0 39.4 all-gather.6

commit v10 on v9

--- a/solution.py
+++ b/solution.py
@@ -100,44 +100,80 @@
     )(at, *[block for block, _ in ring], own, other)
 
 
-def rotate_kernel(at_ref, block_ref, own_ref, other_ref, out_ref, lhs, sems):
-    turned = lax.rem(at_ref[1] + at_ref[4], 2)
-
-    @pl.when(pl.program_id(0) == 0)
-    def _():
-        copies = []
-        for z in range(8):
-            for side in range(2):
-                at = ((turned if side == 0 else 1 - turned) * 8 + z) * COLS
-                lanes = pl.ds(pl.multiple_of(at, COLS), COLS)
-                copies.append(
-                    pltpu.make_async_copy(block_ref.at[z, side], lhs.at[:, lanes], sems.at[z * 2 + side])
-                )
-        for copy in copies:
-            copy.start()
-        for copy in copies:
-            copy.wait()
-
-    both = jnp.dot(lhs[:, :1024], own_ref[0], preferred_element_type=F32)
-    both += jnp.dot(lhs[:, 1024:], other_ref[0], preferred_element_type=F32)
-    out_ref[0] = (both[:, :COLS] + both[:, COLS:]).T
-
-
-def rotate(at, blocks, own, other):
-    slab = pl.BlockSpec((1, 1024, 256), lambda g: (g, 0, 0))
+def reach_kernel(rows_ref, in_ref, own_ref, near_ref, far_ref):
+    def put(out_ref):
+        exact = in_ref[...]
+        high = exact.astype(BF16)
+        out_ref[:, :COLS] = high
+        out_ref[:, COLS:] = (exact - high.astype(F32)).astype(BF16)
+
+    step = pl.program_id(0)
+    pl.when(step < 2)(lambda: put(own_ref))
+    pl.when((step >= 2) & (step < 4))(lambda: put(near_ref))
+    pl.when(step == 4)(lambda: put(far_ref))
+
+
+def reach_basis(rows, basis):
+    return pl.pallas_call(
+        reach_kernel,
+        grid_spec=pltpu.PrefetchScalarGridSpec(
+            num_scalar_prefetch=1,
+            grid=(5,),
+            in_specs=[pl.BlockSpec((1024, COLS), lambda g, rows: (rows[g], 0))],
+            out_specs=[
+                pl.BlockSpec((1024, 256), lambda g, rows: (jnp.minimum(g, 1), 0)),
+                pl.BlockSpec((1024, 256), lambda g, rows: (jnp.clip(g - 2, 0, 1), 0)),
+                pl.BlockSpec((1024, 256), lambda g, rows: (0, 0)),
+            ],
+        ),
+        out_shape=[jax.ShapeDtypeStruct((n, 256), BF16) for n in (2048, 2048, 1024)],
+        compiler_params=ALL_VMEM,
+        cost_estimate=pl.CostEstimate(
+            flops=1 << 20, bytes_accessed=5 << 20, transcendentals=0
+        ),
+    )(rows, basis)
+
+
+def rotate_kernel(at_ref, block_ref, *refs):
+    own_ref, near_ref, near_swapped, far_ref, far_swapped, out_ref, lhs, sems = refs
+    xh, y, c = at_ref[1], at_ref[2], at_ref[4]
+    copies = []
+    for z in range(8):
+        for side in range(2):
+            at = ((xh if side == 0 else 1 - xh) * 8 + z) * COLS
+            lanes = pl.ds(pl.multiple_of(at, COLS), COLS)
+            copies.append(
+                pltpu.make_async_copy(block_ref.at[z, side], lhs.at[:, lanes], sems.at[z * 2 + side])
+            )
+    for copy in copies:
+        copy.start()
+    for copy in copies:
+        copy.wait()
+
+    def put(place, both):
+        out_ref[lax.rem(place, 4)] = (both[:, :COLS] + both[:, COLS:]).T
+
+    for offset, ref in ((4, own_ref), (3 + 2 * c, near_ref), (5 - 2 * c, near_swapped)):
+        put(y + offset, jnp.dot(lhs[...], ref[...], preferred_element_type=F32))
+    mine = lhs[:, pl.ds(pl.multiple_of(c * 1024, 1024), 1024)]
+    rest = lhs[:, pl.ds(pl.multiple_of((1 - c) * 1024, 1024), 1024)]
+    both = jnp.dot(mine, far_ref[...], preferred_element_type=F32)
+    put(y + 2, both + jnp.dot(rest, far_swapped[...], preferred_element_type=F32))
+
+
+def rotate(at, blocks, slabs):
     return pl.pallas_call(
         rotate_kernel,
-        grid=(4,),
         out_shape=jax.ShapeDtypeStruct((4, COLS, TOK), F32),
         in_specs=[pl.BlockSpec(memory_space=pltpu.SMEM), pl.BlockSpec(memory_space=pltpu.HBM)]
-        + [slab] * 2,
-        out_specs=pl.BlockSpec((1, COLS, TOK), lambda g: (g, 0, 0)),
+        + [pl.BlockSpec(memory_space=pltpu.VMEM)] * 5,
+        out_specs=pl.BlockSpec(memory_space=pltpu.VMEM),
         scratch_shapes=[pltpu.VMEM((TOK, 2048), BF16), pltpu.SemaphoreType.DMA((16,))],
-        compiler_params=ALL_VMEM,
+        compiler_params=PARAMS,
         cost_estimate=pl.CostEstimate(
             flops=4 * TOK * 2048 * 512, bytes_accessed=7 << 20, transcendentals=0
         ),
-    )(at, blocks, own, other)
+    )(at, blocks, *slabs)
 
 
 def product_kernel(scale, at_ref, acts_ref, own_ref, other_ref, out_ref, right):
@@ -207,33 +243,45 @@
     return shift(up, "z", 1), shift(down, "z", -1)
 
 
+def shift_near(x):
+    pairs = [(i, (i + 1) % 4) for i in range(4)] + [(4 + i, 4 + (i + 3) % 4) for i in range(4)]
+    return lax.ppermute(x, ("c", "y"), pairs)
+
+
 def body(activations, gradients, basis_in, basis_out):
     z, xh, y, xl, c = (lax.axis_index(a) for a in ("z", "xh", "y", "xl", "c"))
     at = jnp.stack([z, xh, y, xl, c]).astype(jnp.int32)
     half = c.astype(jnp.int32).reshape(1)
+    near_y, far_y = (y + 1 + 2 * c) % 4, (y + 2) % 4
+    rows = jnp.stack(
+        [y * 2, y * 2 + 1, near_y * 2, near_y * 2 + 1, far_y * 2 + c]
+    ).astype(jnp.int32)
 
     a0, grads_pair, mine_in, basis_out = sync(
         pair(activations), pair(gradients), split_basis(half, basis_in), basis_out
     )
     own_in = lax.all_to_all(mine_in, "y", 0, 0)
-    up1, down1, mine_out = sync(*ring_step(a0, a0), split_basis(half, basis_out))
-    up2, down2, mine_out = sync(*ring_step(up1, down1), mine_out)
-    up3, down3, own_in, mine_out = sync(*ring_step(up2, down2), own_in, mine_out)
-    own_out = lax.all_to_all(mine_out, "y", 0, 0)
+    own_out, near_out, far_out = reach_basis(rows, basis_out)
+    up1, down1, near_out, far_out = sync(*ring_step(a0, a0), near_out, far_out)
+    up2, down2, near_out, far_out = sync(*ring_step(up1, down1), near_out, far_out)
+    near_out = shift_near(near_out)
+    up3, down3, own_in, far_out = sync(*ring_step(up2, down2), own_in, far_out)
     grad_blocks = lax.all_gather(after(grads_pair, up2), "z")
+    far_out = shift(far_out, "y", 2)
     up4, other_in = sync(shift(up3, "z", 1), shift(own_in, "c", 1))
     ring = [(a0, 0), (up1, -1), (down1, 1), (up2, -2), (down2, 2), (up3, -3), (down3, 3), (up4, -4)]
     acts_part = rotate_ring(at, ring, own_in, other_in)
+    near_out, far_out, acts_part = sync(near_out, far_out, acts_part)
     acts_in = lax.all_to_all(acts_part.reshape(16, 32, TOK), ("xl", "c", "y"), 0, 0)
-
-    other_out = shift(after(own_out, acts_part), "c", 1)
-    grads_part = rotate(at, grad_blocks, own_out, other_out)
-    acts_in, grads_part = sync(acts_in, grads_part)
+    near_out2, far_out2 = shift(near_out, "c", 1), shift(far_out, "c", 1)
+
+    acts = jnp.sum(acts_in.reshape(4, 4, 32, TOK), axis=1).astype(BF16)[None]
+    rot_pair = pair(acts)
+    rot_acts = lax.all_gather(rot_pair, "z")
+
+    grad_blocks, rot_pair = sync(grad_blocks, rot_pair)
+    grads_part = rotate(at, grad_blocks, (own_out, near_out, near_out2, far_out, far_out2))
     grads_in = lax.all_to_all(grads_part, "y", 0, 0)
-
-    acts = jnp.sum(acts_in.reshape(4, 4, 32, TOK), axis=1).astype(BF16)[None]
-    rot_acts = lax.all_gather(pair(acts), "z")
-
     grads = jnp.sum(grads_in, axis=0).astype(BF16)
     copies = jnp.broadcast_to(grads, (8, COLS, TOK))
     rot_own = lax.all_to_all(copies, ("xl", "y"), 0, 0).reshape(2, 4, COLS, TOK)

time: 185 us -> 190 us (1.027); the launches traced: 184 us -> 187 us
  waiting for transfers between devices: 58.3 us -> 48.9 us
  blocking collectives: 44.5 us -> 53.5 us
    all_to_all x1, waiting for transfers between devices: 0.01 us -> 14.9 us  [body(): lax.all_to_all(acts_part.reshape(16, 32, TOK), ('xl', 'c', 'y'), 0, 0)]
    all_gather x1, waiting for transfers between devices: 13 us -> 0.02 us  [body(): grad_blocks = lax.all_gather(after(grads_pair, up2), 'z')]
    all_to_all x1 -> x0, waiting for transfers between devices: 8.24 us -> none  [body(): own_out = lax.all_to_all(mine_out, 'y', 0, 0)]
    all_gather x1, waiting for transfers between devices: 7.71 us -> 0.01 us  [body(): rot_acts = lax.all_gather(rot_pair, 'z')]
    ppermute x13 -> x15, waiting for transfers between devices: 28.6 us -> 33.5 us  [shift(): return lax.ppermute(x, axis, [(i, (i + by) % n) for i in range(n)])]
    all_to_all x1 -> x0, starting transfers between devices: 4.53 us -> none  [body(): own_out = lax.all_to_all(mine_out, 'y', 0, 0)]
    ppermute x13 -> x15, starting transfers between devices: 20.3 us -> 24.6 us  [shift(): return lax.ppermute(x, axis, [(i, (i + by) % n) for i in range(n)])]
    pallas_call x2 -> x1, Pallas kernels: 7.93 us -> 4.01 us  [split_basis(): pl.pallas_call(split_kernel, grid_spec=pltpu.PrefetchScalarGridSpec(num_s...]
  transfers between devices with their start and end apart: 18 -> 20, of which waited for: 12 -> 11; matrix products, arithmetic and copies ran while one was open for 0% -> 2% of each run, Pallas kernels for 12% -> 12%
where the time goes in v10:
time: 190 us; the launch traced here: 187 us
  blocking collectives  53.5 us (28%)
  waiting for transfers between devices  48.9 us (26%)
  starting transfers between devices  35.1 us (18%)
  Pallas kernels  28.3 us (15%)
  between operations  13.6 us (7%)
  local copies, waits for them, and re-layouts  4.66 us (2%)
  other arithmetic  2.9 us (2%)
    ppermute x15, waiting for transfers between devices, shift(): return lax.ppermute(x, axis, [(i, (i + by) % n) for i in range(n)])  33.5 us
    ppermute x15, starting transfers between devices, shift(): return lax.ppermute(x, axis, [(i, (i + by) % n) for i in range(n)])  24.6 us
    all_to_all x1, blocking collectives, body(): return weave(lax.all_to_all(part, 'y', 0, 0))  18.1 us
    all_to_all x1, blocking collectives, body(): grads_in = lax.all_to_all(grads_part, 'y', 0, 0)  18.1 us
    all_to_all x1, blocking collectives, body(): rot_own = lax.all_to_all(copies, ('xl', 'y'), 0, 0).reshape(2, 4, COLS, TOK)  17.3 us
    all_to_all x1, waiting for transfers between devices, body(): lax.all_to_all(acts_part.reshape(16, 32, TOK), ('xl', 'c', 'y'), 0, 0)  14.9 us
    pallas_call x1, Pallas kernels, rotate_ring(): pl.pallas_call(functools.partial(rotate_ring_kernel, [offset for _, offse...  7.4 us
    pallas_call x1, Pallas kernels, reach_basis(): pl.pallas_call(reach_kernel, grid_spec=pltpu.PrefetchScalarGridSpec(num_s...  5.83 us
  transfers between devices with their start and end apart: 20, of which 11 were waited for; matrix products, arithmetic and copies ran while one was open for 2% of the time, Pallas kernels for 12%

profile of v10, /device:TPU:2, one launch (start us, length us, event | category | flops | bytes accessed | tf_op | source)
XLA Modules:
  0.0 187.1 jit_solution(18245393812015961283)
XLA Ops:
  6.5 2.1 %collective-permute-start = (bf16[1,512,128]{2,1,0:T(8,128)(2,1)}, bf16[1,512,128]{2,1,0:T(8,128)(2,1)S(1)}, u32[]{:S(2)}, u32[]{:S(2)}) collective-permute-start(bf16[1,512,128]{2,1,0:T(8,128)(2,1)} %param.4), channel_id=1, source_target_pairs={{0,8},{8,0},{1,9},{9,1},{2,10},{10,2},{3,11},{11,3},{4,12},{12,4},... | collective-permute-start | bytes 393224 | tf_op jit(solution)/shard_map/ppermute | solution.py:24
  8.7 1.4 collective-permute-start.1
  10.1 4.0 %shard_map.46 = bf16[4,1024,256]{2,1,0:T(8,128)(2,1)} custom-call(s32[1]{0:T(128)} %bitcast.4.half_ref, f32[8192,128]{1,0:T(8,128)} %in_ref.1), custom_call_target="tpu_custom_call" | custom-call | flops 1048576 | bytes 4194304 | tf_op jit(solution)/shard_map/pallas_call | solution.py:44
  14.1 0.4 collective-permute-done
  14.5 0.0 copy-done.6
  14.5 1.8 collective-permute-done.1
  16.3 0.0 copy-done.7
  16.3 0.7 pad_maximum_fusion.1
  17.0 4.5 %all-to-all-start = ((bf16[4,1024,256]{2,1,0:T(8,128)(2,1)}), bf16[4,1024,256]{2,1,0:T(8,128)(2,1)}, u32[]{:S(2)}, u32[]{:S(2)}) async-start(bf16[4,1024,256]{2,1,0:T(8,128)(2,1)} %shard_map.46), calls=%async_computation | async-start | bytes 4194304 | tf_op jit(solution)/shard_map/all_to_all | solution.py:263
  21.5 0.0 all-gather.7.cloned.1.call-start
  21.5 2.0 %collective-permute-start.2 = (bf16[2,512,128]{2,1,0:T(8,128)(2,1)S(1)}, bf16[2,512,128]{2,1,0:T(8,128)(2,1)S(1)}, u32[]{:S(2)}, u32[]{:S(2)}) collective-permute-start(bf16[2,512,128]{2,1,0:T(8,128)(2,1)S(1)} %pad_maximum_fusion.refs_0_), channel_id=1, source_target_pairs={{0,1},{1,2},{2,3},{3,4},{4,5},{5,6},{6,7},{7,0},{8,9},{9,10},{10,1... | collective-permute-start | bytes 786440 | tf_op jit(solution)/shard_map/ppermute | solution.py:24
  23.5 4.0 %collective-permute-start.3 = (bf16[2,512,128]{2,1,0:T(8,128)(2,1)S(1)}, bf16[2,512,128]{2,1,0:T(8,128)(2,1)S(1)}, u32[]{:S(2)}, u32[]{:S(2)}) collective-permute-start(bf16[2,512,128]{2,1,0:T(8,128)(2,1)S(1)} %pad_maximum_fusion.refs_0_), channel_id=1, source_target_pairs={{0,7},{1,0},{2,1},{3,2},{4,3},{5,4},{6,5},{7,6},{8,15},{9,8},{10,9... | collective-permute-start | bytes 786440 | tf_op jit(solution)/shard_map/ppermute | solution.py:24
  27.6 0.7 stack.47.rows_ref
  28.2 5.8 %shard_map.47 = (bf16[2048,256]{1,0:T(8,128)(2,1)}, bf16[2048,256]{1,0:T(8,128)(2,1)}, bf16[1024,256]{1,0:T(8,128)(2,1)}) custom-call(s32[5]{0:T(128)} %stack.47.rows_ref, f32[8192,128]{1,0:T(8,128)} %in_ref.2), custom_call_target="tpu_custom_call" | custom-call | flops 1048576 | bytes 5242880 | tf_op jit(solution)/shard_map/pallas_call | solution.py:117
  34.1 0.0 collective-permute-done.2.refs_1_
  34.1 0.0 collective-permute-done.3.refs_2_
  34.1 0.1 collective-permute-start.4
  34.2 3.2 %collective-permute-start.5 = (bf16[2,512,128]{2,1,0:T(8,128)(2,1)S(1)}, bf16[2,512,128]{2,1,0:T(8,128)(2,1)S(1)}, u32[]{:S(2)}, u32[]{:S(2)}) collective-permute-start(bf16[2,512,128]{2,1,0:T(8,128)(2,1)S(1)} %collective-permute-done.3.refs_2_), channel_id=1, source_target_pairs={{0,7},{1,0},{2,1},{3,2},{4,3},{5,4},{6,5},{7,6},{8,15},{9,8},{10,9... | collective-permute-start | bytes 786440 | tf_op jit(solution)/shard_map/ppermute | solution.py:24
  37.4 5.0 %collective-permute-done.4.refs_3_ = bf16[2,512,128]{2,1,0:T(8,128)(2,1)S(1)} collective-permute-done((bf16[2,512,128]{2,1,0:T(8,128)(2,1)S(1)}, bf16[2,512,128]{2,1,0:T(8,128)(2,1)S(1)}, u32[]{:S(2)}, u32[]{:S(2)}) %collective-permute-start.4) | collective-permute-done | bytes 262176 | tf_op jit(solution)/shard_map/ppermute | solution.py:24
  42.4 0.0 collective-permute-done.5.refs_4_
  42.4 0.7 collective-permute-start.7
  43.1 2.6 %collective-permute-start.8 = (bf16[2,512,128]{2,1,0:T(8,128)(2,1)S(1)}, bf16[2,512,128]{2,1,0:T(8,128)(2,1)S(1)}, u32[]{:S(2)}, u32[]{:S(2)}) collective-permute-start(bf16[2,512,128]{2,1,0:T(8,128)(2,1)S(1)} %collective-permute-done.5.refs_4_), channel_id=1, source_target_pairs={{0,7},{1,0},{2,1},{3,2},{4,3},{5,4},{6,5},{7,6},{8,15},{9,8},{10,9... | collective-permute-start | bytes 786440 | tf_op jit(solution)/shard_map/ppermute | solution.py:24
  45.7 4.3 %collective-permute-done.7.refs_5_ = bf16[2,512,128]{2,1,0:T(8,128)(2,1)S(1)} collective-permute-done((bf16[2,512,128]{2,1,0:T(8,128)(2,1)S(1)}, bf16[2,512,128]{2,1,0:T(8,128)(2,1)S(1)}, u32[]{:S(2)}, u32[]{:S(2)}) %collective-permute-start.7) | collective-permute-done | bytes 262176 | tf_op jit(solution)/shard_map/ppermute | solution.py:24
  50.1 0.0 collective-permute-done.8.refs_6_
  50.1 0.0 all-to-all-done.refs_8_
  50.1 0.1 collective-permute-start.11
  50.2 0.0 all-gather.7.cloned.1.call-update
  50.2 1.7 collective-permute-start.6
  51.9 2.9 %collective-permute-start.9 = (bf16[1024,256]{1,0:T(8,128)(2,1)}, bf16[1024,256]{1,0:T(8,128)(2,1)S(1)}, u32[]{:S(2)}, u32[]{:S(2)}) collective-permute-start(bf16[1024,256]{1,0:T(8,128)(2,1)} %get-tuple-element.44), channel_id=1, source_target_pairs={{0,32},{16,48},{32,0},{48,16},{1,33},{17,49},{33,1},{49,17},{2,34}... | collective-permute-start | bytes 1572872 | tf_op jit(solution)/shard_map/ppermute | solution.py:24
  54.8 2.2 %collective-permute-start.10 = (bf16[2,512,128]{2,1,0:T(8,128)(2,1)S(1)}, bf16[2,512,128]{2,1,0:T(8,128)(2,1)S(1)}, u32[]{:S(2)}, u32[]{:S(2)}) collective-permute-start(bf16[2,512,128]{2,1,0:T(8,128)(2,1)S(1)} %collective-permute-done.7.refs_5_), channel_id=1, source_target_pairs={{0,1},{1,2},{2,3},{3,4},{4,5},{5,6},{6,7},{7,0},{8,9},{9,10},{10,1... | collective-permute-start | bytes 786440 | tf_op jit(solution)/shard_map/ppermute | solution.py:24
  57.0 0.6 stack.41.at_ref
  57.5 5.9 %collective-permute-done.10.refs_7_ = bf16[2,512,128]{2,1,0:T(8,128)(2,1)S(1)} collective-permute-done((bf16[2,512,128]{2,1,0:T(8,128)(2,1)S(1)}, bf16[2,512,128]{2,1,0:T(8,128)(2,1)S(1)}, u32[]{:S(2)}, u32[]{:S(2)}) %collective-permute-start.10) | collective-permute-done | bytes 262176 | tf_op jit(solution)/shard_map/ppermute | solution.py:24
  63.5 0.0 collective-permute-done.11.refs_9_
  63.5 0.6 copy-done.14
  64.2 7.4 %shard_map.48 = f32[4,128,512]{2,1,0:T(8,128)} custom-call(s32[5]{0:T(128)} %stack.41.at_ref, bf16[2,512,128]{2,1,0:T(8,128)(2,1)} %copy-done.5, bf16[2,512,128]{2,1,0:T(8,128)(2,1)} %copy-done.8, bf16[2,512,128]{2,1,0:T(8,128)(2,1)} %copy-done.9, bf16[2,512,128]{2,1,0:T(8,128)(2,1)} %copy-done.10, bf16[2,512,128]{2,1,0:T(8,128)(2,1)} %copy-done.11, ...), custom_call_target="tpu_custom_call" | custom-call | flops 2147483648 | bytes 7340032 | tf_op jit(solution)/shard_map/pallas_call | solution.py:87
  71.6 0.0 copy-start.1
  71.6 0.0 copy-start.2
  71.6 0.5 collective-permute-done.6.refs_1_
  72.1 6.8 %collective-permute-done.9.refs_3_ = bf16[1024,256]{1,0:T(8,128)(2,1)S(1)} collective-permute-done((bf16[1024,256]{1,0:T(8,128)(2,1)}, bf16[1024,256]{1,0:T(8,128)(2,1)S(1)}, u32[]{:S(2)}, u32[]{:S(2)}) %collective-permute-start.9) | collective-permute-done | bytes 524320 | tf_op jit(solution)/shard_map/ppermute | solution.py:24
  79.0 4.2 %all-to-all-start.1 = ((f32[16,32,512]{2,1,0:T(8,128)}), f32[16,32,512]{2,1,0:T(8,128)}, u32[]{:S(2)}, u32[]{:S(2)}) async-start(f32[16,32,512]{2,1,0:T(8,128)} %bitcast.22), calls=%async_computation.1 | async-start | bytes 2097152 | tf_op jit(solution)/shard_map/all_to_all | solution.py:275
  83.2 0.0 all-gather.5.cloned.1.call-start
  83.3 0.1 collective-permute-start.13
  83.4 14.9 %all-to-all-done.1 = f32[16,32,512]{2,1,0:T(8,128)} async-done(((f32[16,32,512]{2,1,0:T(8,128)}), f32[16,32,512]{2,1,0:T(8,128)}, u32[]{:S(2)}, u32[]{:S(2)}) %all-to-all-start.1) | async-done | bytes 1048608 | tf_op jit(solution)/shard_map/all_to_all | solution.py:275
  98.2 1.3 bitcast_reduce_fusion
  99.6 2.9 %collective-permute-start.12 = (bf16[1,4,32,512]{3,2,1,0:T(8,128)(2,1)S(1)}, bf16[1,4,32,512]{3,2,1,0:T(8,128)(2,1)S(1)}, u32[]{:S(2)}, u32[]{:S(2)}) collective-permute-start(bf16[1,4,32,512]{3,2,1,0:T(8,128)(2,1)S(1)} %bitcast.23), channel_id=1, source_target_pairs={{0,8},{8,0},{1,9},{9,1},{2,10},{10,2},{3,11},{11,3},{4,12},{12,4},... | collective-permute-start | bytes 393224 | tf_op jit(solution)/shard_map/ppermute | solution.py:24
  102.5 4.3 %collective-permute-done.12 = bf16[1,4,32,512]{3,2,1,0:T(8,128)(2,1)S(1)} collective-permute-done((bf16[1,4,32,512]{3,2,1,0:T(8,128)(2,1)S(1)}, bf16[1,4,32,512]{3,2,1,0:T(8,128)(2,1)S(1)}, u32[]{:S(2)}, u32[]{:S(2)}) %collective-permute-start.12) | collective-permute-done | bytes 131104 | tf_op jit(solution)/shard_map/ppermute | solution.py:24
  106.8 0.7 pad_maximum_fusion.2
  107.5 0.0 all-gather.5.cloned.1.call-update
  107.6 0.3 collective-permute-start.14
  107.8 0.0 all-gather.7.cloned.1.call-done
  107.9 2.2 %collective-permute-done.14.refs_4_ = bf16[1024,256]{1,0:T(8,128)(2,1)} collective-permute-done((bf16[1024,256]{1,0:T(8,128)(2,1)}, bf16[1024,256]{1,0:T(8,128)(2,1)}, u32[]{:S(2)}, u32[]{:S(2)}) %collective-permute-start.14) | collective-permute-done | bytes 524320 | tf_op jit(solution)/shard_map/ppermute | solution.py:24
  110.1 0.0 collective-permute-done.13.refs_2_
  110.1 1.0 copy-done.4
  111.1 5.3 %shard_map.49 = f32[4,128,512]{2,1,0:T(8,128)S(1)} custom-call(s32[5]{0:T(128)S(1)} %copy-done.1, bf16[8,2,512,128]{3,2,1,0:T(8,128)(2,1)} %bitcast.25, bf16[2048,256]{1,0:T(8,128)(2,1)S(1)} %copy-done.2, bf16[2048,256]{1,0:T(8,128)(2,1)S(1)} %collective-permute-done.6.refs_1_, bf16[2048,256]{1,0:T(8,128)(2,1)S(1)} %collective-permute-done.13.refs_2_, ...), custom_call_target="tpu_custom_call" | custom-call | flops 2147483648 | bytes 7340032 | tf_op jit(solution)/shard_map/pallas_call | solution.py:165
  116.4 18.1 %all_to_all.25 = f32[4,128,512]{2,1,0:T(8,128)S(1)} all-to-all(f32[4,128,512]{2,1,0:T(8,128)S(1)} %shard_map.49), channel_id=1, replica_groups=mesh['xl'=2,'c'=2,'y'=4,'xh'=2,'z'=8] {'y'}, dimensions={0} | all-to-all | bytes 2097152 | tf_op jit(solution)/shard_map/all_to_all | solution.py:284
  134.5 0.1 reduce_sum.19
  134.6 0.1 broadcast_in_dim.4
  134.7 17.3 %all_to_all.26 = bf16[8,128,512]{2,1,0:T(8,128)(2,1)S(1)} all-to-all(bf16[8,128,512]{2,1,0:T(8,128)(2,1)S(1)} %broadcast_in_dim.4), channel_id=1, replica_groups=mesh['xl'=2,'c'=2,'y'=4,'xh'=2,'z'=8] {'xl','y'}, dimensions={0} | all-to-all | bytes 2097152 | tf_op jit(solution)/shard_map/all_to_all | solution.py:287
  152.0 0.0 collective-permute-start.15
  152.0 2.7 %collective-permute-done.15.other_ref = bf16[2,4,128,512]{3,2,1,0:T(8,128)(2,1)S(1)} collective-permute-done((bf16[2,4,128,512]{3,2,1,0:T(8,128)(2,1)S(1)}, bf16[2,4,128,512]{3,2,1,0:T(8,128)(2,1)S(1)}, u32[]{:S(2)}, u32[]{:S(2)}) %collective-permute-start.15) | collective-permute-done | bytes 1048608 | tf_op jit(solution)/shard_map/ppermute | solution.py:24
  154.7 1.6 copy-done
  156.3 3.5 %shard_map.50 = f32[4,128,512]{2,1,0:T(8,128)S(1)} custom-call(s32[5]{0:T(128)S(1)} %copy-done.1, bf16[8,2,4,32,512]{4,3,2,1,0:T(8,128)(2,1)S(1)} %bitcast.21, bf16[2,4,128,512]{3,2,1,0:T(8,128)(2,1)S(1)} %bitcast.20, bf16[2,4,128,512]{3,2,1,0:T(8,128)(2,1)S(1)} %collective-permute-done.15.other_ref), custom_call_target="tpu_custom_call" | custom-call | flops 1073741824 | bytes 5242880 | tf_op jit(solution)/shard_map/pallas_call | solution.py:201
  159.8 18.1 %all_to_all.27.in_ref = f32[4,128,512]{2,1,0:T(8,128)S(1)} all-to-all(f32[4,128,512]{2,1,0:T(8,128)S(1)} %shard_map.50), channel_id=1, replica_groups=mesh['xl'=2,'c'=2,'y'=4,'xh'=2,'z'=8] {'y'}, dimensions={0} | all-to-all | bytes 2097152 | tf_op jit(solution)/shard_map/all_to_all | solution.py:291
  177.9 2.4 %shard_map.51 = f32[128,2048]{1,0:T(8,128)} custom-call(f32[4,128,512]{2,1,0:T(8,128)S(1)} %all_to_all.27.in_ref), custom_call_target="tpu_custom_call" | custom-call | tf_op jit(solution)/shard_map/pallas_call | solution.py:224
  (25 shorter events, 0.1 us)
Async XLA Ops:
  6.5 8.0 %collective-permute-start = (bf16[1,512,128]{2,1,0:T(8,128)(2,1)}, bf16[1,512,128]{2,1,0:T(8,128)(2,1)S(1)}, u32[]{:S(2)}, u32[]{:S(2)}) collective-permute-start(bf16[1,512,128]{2,1,0:T(8,128)(2,1)} %param.4), channel_id=1, source_target_pairs={{0,8},{8,0},{1,9},{9,1},{2,10},{10,2},{3,11},{11,3},{4,12},{12,4},... | collective-permute-start | bytes 393224 | tf_op jit(solution)/shard_map/ppermute | solution.py:24
  8.7 7.6 %collective-permute-start.1 = (bf16[1,512,128]{2,1,0:T(8,128)(2,1)}, bf16[1,512,128]{2,1,0:T(8,128)(2,1)S(1)}, u32[]{:S(2)}, u32[]{:S(2)}) collective-permute-start(bf16[1,512,128]{2,1,0:T(8,128)(2,1)} %param.5), channel_id=1, source_target_pairs={{0,8},{8,0},{1,9},{9,1},{2,10},{10,2},{3,11},{11,3},{4,12},{12,4},... | collective-permute-start | bytes 393224 | tf_op jit(solution)/shard_map/ppermute | solution.py:24
  10.1 4.4 %copy-start.6 = (bf16[1,512,128]{2,1,0:T(8,128)(2,1)S(1)}, bf16[1,512,128]{2,1,0:T(8,128)(2,1)}, u32[]{:S(2)}) copy-start(bf16[1,512,128]{2,1,0:T(8,128)(2,1)} %param.4) | copy-start | bytes 393220
  10.1 6.2 %copy-start.7 = (bf16[1,512,128]{2,1,0:T(8,128)(2,1)S(1)}, bf16[1,512,128]{2,1,0:T(8,128)(2,1)}, u32[]{:S(2)}) copy-start(bf16[1,512,128]{2,1,0:T(8,128)(2,1)} %param.5) | copy-start | bytes 393220
  14.5 9.0 %copy-start.5 = (bf16[2,512,128]{2,1,0:T(8,128)(2,1)}, bf16[2,512,128]{2,1,0:T(8,128)(2,1)S(1)}, u32[]{:S(2)}) copy-start(bf16[2,512,128]{2,1,0:T(8,128)(2,1)S(1)} %pad_maximum_fusion.refs_0_) | copy-start | bytes 786436
  17.0 33.1 %all-to-all-start = ((bf16[4,1024,256]{2,1,0:T(8,128)(2,1)}), bf16[4,1024,256]{2,1,0:T(8,128)(2,1)}, u32[]{:S(2)}, u32[]{:S(2)}) async-start(bf16[4,1024,256]{2,1,0:T(8,128)(2,1)} %shard_map.46), calls=%async_computation | async-start | bytes 4194304 | tf_op jit(solution)/shard_map/all_to_all | solution.py:263
  21.5 86.4 %all-gather.7.cloned.1.call-start = ((), (), s32[]{:S(2)}) async-start(), calls=%async_computation.6 | async-start | bytes 2359296 | tf_op jit(solution)/shard_map/all_gather | solution.py:269
  21.5 12.5 %collective-permute-start.2 = (bf16[2,512,128]{2,1,0:T(8,128)(2,1)S(1)}, bf16[2,512,128]{2,1,0:T(8,128)(2,1)S(1)}, u32[]{:S(2)}, u32[]{:S(2)}) collective-permute-start(bf16[2,512,128]{2,1,0:T(8,128)(2,1)S(1)} %pad_maximum_fusion.refs_0_), channel_id=1, source_target_pairs={{0,1},{1,2},{2,3},{3,4},{4,5},{5,6},{6,7},{7,0},{8,9},{9,10},{10,1... | collective-permute-start | bytes 786440 | tf_op jit(solution)/shard_map/ppermute | solution.py:24
  23.5 10.5 %collective-permute-start.3 = (bf16[2,512,128]{2,1,0:T(8,128)(2,1)S(1)}, bf16[2,512,128]{2,1,0:T(8,128)(2,1)S(1)}, u32[]{:S(2)}, u32[]{:S(2)}) collective-permute-start(bf16[2,512,128]{2,1,0:T(8,128)(2,1)S(1)} %pad_maximum_fusion.refs_0_), channel_id=1, source_target_pairs={{0,7},{1,0},{2,1},{3,2},{4,3},{5,4},{6,5},{7,6},{8,15},{9,8},{10,9... | collective-permute-start | bytes 786440 | tf_op jit(solution)/shard_map/ppermute | solution.py:24
  34.1 29.4 %copy-start.8 = (bf16[2,512,128]{2,1,0:T(8,128)(2,1)}, bf16[2,512,128]{2,1,0:T(8,128)(2,1)S(1)}, u32[]{:S(2)}) copy-start(bf16[2,512,128]{2,1,0:T(8,128)(2,1)S(1)} %collective-permute-done.2.refs_1_) | copy-start | bytes 786436
  34.1 29.4 %copy-start.9 = (bf16[2,512,128]{2,1,0:T(8,128)(2,1)}, bf16[2,512,128]{2,1,0:T(8,128)(2,1)S(1)}, u32[]{:S(2)}) copy-start(bf16[2,512,128]{2,1,0:T(8,128)(2,1)S(1)} %collective-permute-done.3.refs_2_) | copy-start | bytes 786436
  34.1 8.3 %collective-permute-start.4 = (bf16[2,512,128]{2,1,0:T(8,128)(2,1)S(1)}, bf16[2,512,128]{2,1,0:T(8,128)(2,1)S(1)}, u32[]{:S(2)}, u32[]{:S(2)}) collective-permute-start(bf16[2,512,128]{2,1,0:T(8,128)(2,1)S(1)} %collective-permute-done.2.refs_1_), channel_id=1, source_target_pairs={{0,1},{1,2},{2,3},{3,4},{4,5},{5,6},{6,7},{7,0},{8,9},{9,10},{10,1... | collective-permute-start | bytes 786440 | tf_op jit(solution)/shard_map/ppermute | solution.py:24
  34.2 8.2 %collective-permute-start.5 = (bf16[2,512,128]{2,1,0:T(8,128)(2,1)S(1)}, bf16[2,512,128]{2,1,0:T(8,128)(2,1)S(1)}, u32[]{:S(2)}, u32[]{:S(2)}) collective-permute-start(bf16[2,512,128]{2,1,0:T(8,128)(2,1)S(1)} %collective-permute-done.3.refs_2_), channel_id=1, source_target_pairs={{0,7},{1,0},{2,1},{3,2},{4,3},{5,4},{6,5},{7,6},{8,15},{9,8},{10,9... | collective-permute-start | bytes 786440 | tf_op jit(solution)/shard_map/ppermute | solution.py:24
  42.4 21.1 %copy-start.10 = (bf16[2,512,128]{2,1,0:T(8,128)(2,1)}, bf16[2,512,128]{2,1,0:T(8,128)(2,1)S(1)}, u32[]{:S(2)}) copy-start(bf16[2,512,128]{2,1,0:T(8,128)(2,1)S(1)} %collective-permute-done.4.refs_3_) | copy-start | bytes 786436
  42.4 21.1 %copy-start.11 = (bf16[2,512,128]{2,1,0:T(8,128)(2,1)}, bf16[2,512,128]{2,1,0:T(8,128)(2,1)S(1)}, u32[]{:S(2)}) copy-start(bf16[2,512,128]{2,1,0:T(8,128)(2,1)S(1)} %collective-permute-done.5.refs_4_) | copy-start | bytes 786436
  42.4 7.7 %collective-permute-start.7 = (bf16[2,512,128]{2,1,0:T(8,128)(2,1)S(1)}, bf16[2,512,128]{2,1,0:T(8,128)(2,1)S(1)}, u32[]{:S(2)}, u32[]{:S(2)}) collective-permute-start(bf16[2,512,128]{2,1,0:T(8,128)(2,1)S(1)} %collective-permute-done.4.refs_3_), channel_id=1, source_target_pairs={{0,1},{1,2},{2,3},{3,4},{4,5},{5,6},{6,7},{7,0},{8,9},{9,10},{10,1... | collective-permute-start | bytes 786440 | tf_op jit(solution)/shard_map/ppermute | solution.py:24
  43.1 7.0 %collective-permute-start.8 = (bf16[2,512,128]{2,1,0:T(8,128)(2,1)S(1)}, bf16[2,512,128]{2,1,0:T(8,128)(2,1)S(1)}, u32[]{:S(2)}, u32[]{:S(2)}) collective-permute-start(bf16[2,512,128]{2,1,0:T(8,128)(2,1)S(1)} %collective-permute-done.5.refs_4_), channel_id=1, source_target_pairs={{0,7},{1,0},{2,1},{3,2},{4,3},{5,4},{6,5},{7,6},{8,15},{9,8},{10,9... | collective-permute-start | bytes 786440 | tf_op jit(solution)/shard_map/ppermute | solution.py:24
  50.1 13.5 %copy-start.12 = (bf16[2,512,128]{2,1,0:T(8,128)(2,1)}, bf16[2,512,128]{2,1,0:T(8,128)(2,1)S(1)}, u32[]{:S(2)}) copy-start(bf16[2,512,128]{2,1,0:T(8,128)(2,1)S(1)} %collective-permute-done.7.refs_5_) | copy-start | bytes 786436
  50.1 13.5 %copy-start.13 = (bf16[2,512,128]{2,1,0:T(8,128)(2,1)}, bf16[2,512,128]{2,1,0:T(8,128)(2,1)S(1)}, u32[]{:S(2)}) copy-start(bf16[2,512,128]{2,1,0:T(8,128)(2,1)S(1)} %collective-permute-done.8.refs_6_) | copy-start | bytes 786436
  50.1 13.4 %collective-permute-start.11 = (bf16[4,1024,256]{2,1,0:T(8,128)(2,1)}, bf16[4,1024,256]{2,1,0:T(8,128)(2,1)}, u32[]{:S(2)}, u32[]{:S(2)}) collective-permute-start(bf16[4,1024,256]{2,1,0:T(8,128)(2,1)} %all-to-all-done.refs_8_), channel_id=1, source_target_pairs={{0,64},{64,0},{1,65},{65,1},{2,66},{66,2},{3,67},{67,3},{4,68},{68... | collective-permute-start | bytes 6291464 | tf_op jit(solution)/shard_map/ppermute | solution.py:24
  50.2 21.9 %collective-permute-start.6 = (bf16[2048,256]{1,0:T(8,128)(2,1)}, bf16[2048,256]{1,0:T(8,128)(2,1)S(1)}, u32[]{:S(2)}, u32[]{:S(2)}) collective-permute-start(bf16[2048,256]{1,0:T(8,128)(2,1)} %get-tuple-element.39), channel_id=1, source_target_pairs={{0,16},{16,32},{32,48},{48,0},{64,112},{80,64},{96,80},{112,96},{1... | collective-permute-start | bytes 3145736 | tf_op jit(solution)/shard_map/ppermute | solution.py:248
  51.9 27.1 %collective-permute-start.9 = (bf16[1024,256]{1,0:T(8,128)(2,1)}, bf16[1024,256]{1,0:T(8,128)(2,1)S(1)}, u32[]{:S(2)}, u32[]{:S(2)}) collective-permute-start(bf16[1024,256]{1,0:T(8,128)(2,1)} %get-tuple-element.44), channel_id=1, source_target_pairs={{0,32},{16,48},{32,0},{48,16},{1,33},{17,49},{33,1},{49,17},{2,34}... | collective-permute-start | bytes 1572872 | tf_op jit(solution)/shard_map/ppermute | solution.py:24
  54.8 8.7 %collective-permute-start.10 = (bf16[2,512,128]{2,1,0:T(8,128)(2,1)S(1)}, bf16[2,512,128]{2,1,0:T(8,128)(2,1)S(1)}, u32[]{:S(2)}, u32[]{:S(2)}) collective-permute-start(bf16[2,512,128]{2,1,0:T(8,128)(2,1)S(1)} %collective-permute-done.7.refs_5_), channel_id=1, source_target_pairs={{0,1},{1,2},{2,3},{3,4},{4,5},{5,6},{6,7},{7,0},{8,9},{9,10},{10,1... | collective-permute-start | bytes 786440 | tf_op jit(solution)/shard_map/ppermute | solution.py:24
  63.5 0.7 copy-start.14
  71.6 38.5 %copy-start.1 = (s32[5]{0:T(128)S(1)}, s32[5]{0:T(128)}, u32[]{:S(2)}) copy-start(s32[5]{0:T(128)} %stack.41.at_ref) | copy-start | bytes 64
  71.6 38.5 %copy-start.2 = (bf16[2048,256]{1,0:T(8,128)(2,1)S(1)}, bf16[2048,256]{1,0:T(8,128)(2,1)}, u32[]{:S(2)}) copy-start(bf16[2048,256]{1,0:T(8,128)(2,1)} %get-tuple-element.54.refs_0_) | copy-start | bytes 3145732
  79.0 4.3 %copy-start.3 = (bf16[1024,256]{1,0:T(8,128)(2,1)}, bf16[1024,256]{1,0:T(8,128)(2,1)S(1)}, u32[]{:S(2)}) copy-start(bf16[1024,256]{1,0:T(8,128)(2,1)S(1)} %collective-permute-done.9.refs_3_) | copy-start | bytes 1572868
  79.0 19.3 %all-to-all-start.1 = ((f32[16,32,512]{2,1,0:T(8,128)}), f32[16,32,512]{2,1,0:T(8,128)}, u32[]{:S(2)}, u32[]{:S(2)}) async-start(f32[16,32,512]{2,1,0:T(8,128)} %bitcast.22), calls=%async_computation.1 | async-start | bytes 2097152 | tf_op jit(solution)/shard_map/all_to_all | solution.py:275
  83.2 71.4 %all-gather.5.cloned.1.call-start = ((), (), s32[]{:S(2)}) async-start(), calls=%async_computation.5 | async-start | bytes 2359296 | tf_op jit(solution)/shard_map/all_gather | solution.py:280
  83.3 26.8 %collective-permute-start.13 = (bf16[2048,256]{1,0:T(8,128)(2,1)S(1)}, bf16[2048,256]{1,0:T(8,128)(2,1)S(1)}, u32[]{:S(2)}, u32[]{:S(2)}) collective-permute-start(bf16[2048,256]{1,0:T(8,128)(2,1)S(1)} %collective-permute-done.6.refs_1_), channel_id=1, source_target_pairs={{0,64},{64,0},{1,65},{65,1},{2,66},{66,2},{3,67},{67,3},{4,68},{68... | collective-permute-start | bytes 3145736 | tf_op jit(solution)/shard_map/ppermute | solution.py:24
  99.6 7.2 %collective-permute-start.12 = (bf16[1,4,32,512]{3,2,1,0:T(8,128)(2,1)S(1)}, bf16[1,4,32,512]{3,2,1,0:T(8,128)(2,1)S(1)}, u32[]{:S(2)}, u32[]{:S(2)}) collective-permute-start(bf16[1,4,32,512]{3,2,1,0:T(8,128)(2,1)S(1)} %bitcast.23), channel_id=1, source_target_pairs={{0,8},{8,0},{1,9},{9,1},{2,10},{10,2},{3,11},{11,3},{4,12},{12,4},... | collective-permute-start | bytes 393224 | tf_op jit(solution)/shard_map/ppermute | solution.py:24
  107.6 2.5 %collective-permute-start.14 = (bf16[1024,256]{1,0:T(8,128)(2,1)}, bf16[1024,256]{1,0:T(8,128)(2,1)}, u32[]{:S(2)}, u32[]{:S(2)}) collective-permute-start(bf16[1024,256]{1,0:T(8,128)(2,1)} %copy-done.3), channel_id=1, source_target_pairs={{0,64},{64,0},{1,65},{65,1},{2,66},{66,2},{3,67},{67,3},{4,68},{68... | collective-permute-start | bytes 1572872 | tf_op jit(solution)/shard_map/ppermute | solution.py:24
  110.1 1.0 copy-start.4
  152.0 2.7 %collective-permute-start.15 = (bf16[2,4,128,512]{3,2,1,0:T(8,128)(2,1)S(1)}, bf16[2,4,128,512]{3,2,1,0:T(8,128)(2,1)S(1)}, u32[]{:S(2)}, u32[]{:S(2)}) collective-permute-start(bf16[2,4,128,512]{3,2,1,0:T(8,128)(2,1)S(1)} %bitcast.19), channel_id=1, source_target_pairs={{0,64},{64,0},{1,65},{65,1},{2,66},{66,2},{3,67},{67,3},{4,68},{68... | collective-permute-start | bytes 3145736 | tf_op jit(solution)/shard_map/ppermute | solution.py:24
  154.7 1.6 copy-start
Sparse Core Ops, SparseCore 0:
  50.3 41.7 all-gather.6
  107.7 40.2 all-gather.4

commit v11 on v10

--- a/solution.py
+++ b/solution.py
@@ -194,13 +194,13 @@
                     preferred_element_type=F32,
                 )
                 total = part * part if total is None else total + part * part
-        out_ref[row] = total * scale
+        out_ref[row] = (total * scale).astype(BF16)
 
 
 def products(at, acts, own, other, scale):
     return pl.pallas_call(
         functools.partial(product_kernel, scale),
-        out_shape=jax.ShapeDtypeStruct((4, COLS, 512), F32),
+        out_shape=jax.ShapeDtypeStruct((4, COLS, 512), BF16),
         in_specs=[pl.BlockSpec(memory_space=pltpu.SMEM)]
         + [pl.BlockSpec(memory_space=pltpu.VMEM)] * 3,
         out_specs=pl.BlockSpec(memory_space=pltpu.VMEM),
@@ -216,7 +216,7 @@
     for tile in range(4):
         lanes = slice(tile * 32, tile * 32 + 32)
         out_ref[:, tile * COLS : (tile + 1) * COLS] = jnp.concatenate(
-            [in_ref[q, :, lanes] for q in range(4)], axis=1
+            [in_ref[q].astype(F32)[:, lanes] for q in range(4)], axis=1
         )
 
 

time: 190 us -> 184 us (0.968)
  blocking collectives: 53.5 us -> 47.9 us
    all_to_all x1, blocking collectives: 18.1 us -> 12.5 us  [body(): return weave(lax.all_to_all(part, 'y', 0, 0))]
where the time goes in v11:
time: 184 us; the launch traced here: 181 us
  waiting for transfers between devices  48.9 us (27%)
  blocking collectives  47.9 us (26%)
  starting transfers between devices  35.1 us (19%)
  Pallas kernels  28 us (15%)
  between operations  13.6 us (7%)
  local copies, waits for them, and re-layouts  4.66 us (3%)
  other arithmetic  2.9 us (2%)
    ppermute x15, waiting for transfers between devices, shift(): return lax.ppermute(x, axis, [(i, (i + by) % n) for i in range(n)])  33.5 us
    ppermute x15, starting transfers between devices, shift(): return lax.ppermute(x, axis, [(i, (i + by) % n) for i in range(n)])  24.6 us
    all_to_all x1, blocking collectives, body(): grads_in = lax.all_to_all(grads_part, 'y', 0, 0)  18.1 us
    all_to_all x1, blocking collectives, body(): rot_own = lax.all_to_all(copies, ('xl', 'y'), 0, 0).reshape(2, 4, COLS, TOK)  17.3 us
    all_to_all x1, waiting for transfers between devices, body(): lax.all_to_all(acts_part.reshape(16, 32, TOK), ('xl', 'c', 'y'), 0, 0)  14.9 us
    all_to_all x1, blocking collectives, body(): return weave(lax.all_to_all(part, 'y', 0, 0))  12.5 us
    pallas_call x1, Pallas kernels, rotate_ring(): pl.pallas_call(functools.partial(rotate_ring_kernel, [offset for _, offse...  7.4 us
    pallas_call x1, Pallas kernels, reach_basis(): pl.pallas_call(reach_kernel, grid_spec=pltpu.PrefetchScalarGridSpec(num_s...  5.83 us
  transfers between devices with their start and end apart: 20, of which 11 were waited for; matrix products, arithmetic and copies ran while one was open for 2% of the time, Pallas kernels for 12%

profile of v11, /device:TPU:2, one launch (start us, length us, event | category | flops | bytes accessed | tf_op | source)
XLA Modules:
  0.0 181.1 jit_solution(3132848567754314747)
XLA Ops:
  6.5 2.1 %collective-permute-start = (bf16[1,512,128]{2,1,0:T(8,128)(2,1)}, bf16[1,512,128]{2,1,0:T(8,128)(2,1)S(1)}, u32[]{:S(2)}, u32[]{:S(2)}) collective-permute-start(bf16[1,512,128]{2,1,0:T(8,128)(2,1)} %param.4), channel_id=1, source_target_pairs={{0,8},{8,0},{1,9},{9,1},{2,10},{10,2},{3,11},{11,3},{4,12},{12,4},... | collective-permute-start | bytes 393224 | tf_op jit(solution)/shard_map/ppermute | solution.py:24
  8.7 1.4 collective-permute-start.1
  10.1 4.0 %shard_map.46 = bf16[4,1024,256]{2,1,0:T(8,128)(2,1)} custom-call(s32[1]{0:T(128)} %bitcast.4.half_ref, f32[8192,128]{1,0:T(8,128)} %in_ref.1), custom_call_target="tpu_custom_call" | custom-call | flops 1048576 | bytes 4194304 | tf_op jit(solution)/shard_map/pallas_call | solution.py:44
  14.1 0.4 collective-permute-done
  14.5 0.0 copy-done.6
  14.5 1.8 collective-permute-done.1
  16.3 0.0 copy-done.7
  16.3 0.7 pad_maximum_fusion.1
  17.0 4.5 %all-to-all-start = ((bf16[4,1024,256]{2,1,0:T(8,128)(2,1)}), bf16[4,1024,256]{2,1,0:T(8,128)(2,1)}, u32[]{:S(2)}, u32[]{:S(2)}) async-start(bf16[4,1024,256]{2,1,0:T(8,128)(2,1)} %shard_map.46), calls=%async_computation | async-start | bytes 4194304 | tf_op jit(solution)/shard_map/all_to_all | solution.py:263
  21.5 0.0 all-gather.7.cloned.1.call-start
  21.5 2.0 %collective-permute-start.2 = (bf16[2,512,128]{2,1,0:T(8,128)(2,1)S(1)}, bf16[2,512,128]{2,1,0:T(8,128)(2,1)S(1)}, u32[]{:S(2)}, u32[]{:S(2)}) collective-permute-start(bf16[2,512,128]{2,1,0:T(8,128)(2,1)S(1)} %pad_maximum_fusion.refs_0_), channel_id=1, source_target_pairs={{0,1},{1,2},{2,3},{3,4},{4,5},{5,6},{6,7},{7,0},{8,9},{9,10},{10,1... | collective-permute-start | bytes 786440 | tf_op jit(solution)/shard_map/ppermute | solution.py:24
  23.5 4.0 %collective-permute-start.3 = (bf16[2,512,128]{2,1,0:T(8,128)(2,1)S(1)}, bf16[2,512,128]{2,1,0:T(8,128)(2,1)S(1)}, u32[]{:S(2)}, u32[]{:S(2)}) collective-permute-start(bf16[2,512,128]{2,1,0:T(8,128)(2,1)S(1)} %pad_maximum_fusion.refs_0_), channel_id=1, source_target_pairs={{0,7},{1,0},{2,1},{3,2},{4,3},{5,4},{6,5},{7,6},{8,15},{9,8},{10,9... | collective-permute-start | bytes 786440 | tf_op jit(solution)/shard_map/ppermute | solution.py:24
  27.6 0.7 stack.47.rows_ref
  28.2 5.8 %shard_map.47 = (bf16[2048,256]{1,0:T(8,128)(2,1)}, bf16[2048,256]{1,0:T(8,128)(2,1)}, bf16[1024,256]{1,0:T(8,128)(2,1)}) custom-call(s32[5]{0:T(128)} %stack.47.rows_ref, f32[8192,128]{1,0:T(8,128)} %in_ref.2), custom_call_target="tpu_custom_call" | custom-call | flops 1048576 | bytes 5242880 | tf_op jit(solution)/shard_map/pallas_call | solution.py:117
  34.1 0.0 collective-permute-done.2.refs_1_
  34.1 0.0 collective-permute-done.3.refs_2_
  34.1 0.1 collective-permute-start.4
  34.2 3.2 %collective-permute-start.5 = (bf16[2,512,128]{2,1,0:T(8,128)(2,1)S(1)}, bf16[2,512,128]{2,1,0:T(8,128)(2,1)S(1)}, u32[]{:S(2)}, u32[]{:S(2)}) collective-permute-start(bf16[2,512,128]{2,1,0:T(8,128)(2,1)S(1)} %collective-permute-done.3.refs_2_), channel_id=1, source_target_pairs={{0,7},{1,0},{2,1},{3,2},{4,3},{5,4},{6,5},{7,6},{8,15},{9,8},{10,9... | collective-permute-start | bytes 786440 | tf_op jit(solution)/shard_map/ppermute | solution.py:24
  37.4 5.0 %collective-permute-done.4.refs_3_ = bf16[2,512,128]{2,1,0:T(8,128)(2,1)S(1)} collective-permute-done((bf16[2,512,128]{2,1,0:T(8,128)(2,1)S(1)}, bf16[2,512,128]{2,1,0:T(8,128)(2,1)S(1)}, u32[]{:S(2)}, u32[]{:S(2)}) %collective-permute-start.4) | collective-permute-done | bytes 262176 | tf_op jit(solution)/shard_map/ppermute | solution.py:24
  42.4 0.0 collective-permute-done.5.refs_4_
  42.4 0.7 collective-permute-start.7
  43.1 2.6 %collective-permute-start.8 = (bf16[2,512,128]{2,1,0:T(8,128)(2,1)S(1)}, bf16[2,512,128]{2,1,0:T(8,128)(2,1)S(1)}, u32[]{:S(2)}, u32[]{:S(2)}) collective-permute-start(bf16[2,512,128]{2,1,0:T(8,128)(2,1)S(1)} %collective-permute-done.5.refs_4_), channel_id=1, source_target_pairs={{0,7},{1,0},{2,1},{3,2},{4,3},{5,4},{6,5},{7,6},{8,15},{9,8},{10,9... | collective-permute-start | bytes 786440 | tf_op jit(solution)/shard_map/ppermute | solution.py:24
  45.7 4.3 %collective-permute-done.7.refs_5_ = bf16[2,512,128]{2,1,0:T(8,128)(2,1)S(1)} collective-permute-done((bf16[2,512,128]{2,1,0:T(8,128)(2,1)S(1)}, bf16[2,512,128]{2,1,0:T(8,128)(2,1)S(1)}, u32[]{:S(2)}, u32[]{:S(2)}) %collective-permute-start.7) | collective-permute-done | bytes 262176 | tf_op jit(solution)/shard_map/ppermute | solution.py:24
  50.1 0.0 collective-permute-done.8.refs_6_
  50.1 0.0 all-to-all-done.refs_8_
  50.1 0.1 collective-permute-start.11
  50.2 0.0 all-gather.7.cloned.1.call-update
  50.2 1.7 collective-permute-start.6
  51.9 2.9 %collective-permute-start.9 = (bf16[1024,256]{1,0:T(8,128)(2,1)}, bf16[1024,256]{1,0:T(8,128)(2,1)S(1)}, u32[]{:S(2)}, u32[]{:S(2)}) collective-permute-start(bf16[1024,256]{1,0:T(8,128)(2,1)} %get-tuple-element.44), channel_id=1, source_target_pairs={{0,32},{16,48},{32,0},{48,16},{1,33},{17,49},{33,1},{49,17},{2,34}... | collective-permute-start | bytes 1572872 | tf_op jit(solution)/shard_map/ppermute | solution.py:24
  54.8 2.2 %collective-permute-start.10 = (bf16[2,512,128]{2,1,0:T(8,128)(2,1)S(1)}, bf16[2,512,128]{2,1,0:T(8,128)(2,1)S(1)}, u32[]{:S(2)}, u32[]{:S(2)}) collective-permute-start(bf16[2,512,128]{2,1,0:T(8,128)(2,1)S(1)} %collective-permute-done.7.refs_5_), channel_id=1, source_target_pairs={{0,1},{1,2},{2,3},{3,4},{4,5},{5,6},{6,7},{7,0},{8,9},{9,10},{10,1... | collective-permute-start | bytes 786440 | tf_op jit(solution)/shard_map/ppermute | solution.py:24
  57.0 0.6 stack.41.at_ref
  57.5 5.9 %collective-permute-done.10.refs_7_ = bf16[2,512,128]{2,1,0:T(8,128)(2,1)S(1)} collective-permute-done((bf16[2,512,128]{2,1,0:T(8,128)(2,1)S(1)}, bf16[2,512,128]{2,1,0:T(8,128)(2,1)S(1)}, u32[]{:S(2)}, u32[]{:S(2)}) %collective-permute-start.10) | collective-permute-done | bytes 262176 | tf_op jit(solution)/shard_map/ppermute | solution.py:24
  63.5 0.0 collective-permute-done.11.refs_9_
  63.5 0.6 copy-done.14
  64.2 7.4 %shard_map.48 = f32[4,128,512]{2,1,0:T(8,128)} custom-call(s32[5]{0:T(128)} %stack.41.at_ref, bf16[2,512,128]{2,1,0:T(8,128)(2,1)} %copy-done.5, bf16[2,512,128]{2,1,0:T(8,128)(2,1)} %copy-done.8, bf16[2,512,128]{2,1,0:T(8,128)(2,1)} %copy-done.9, bf16[2,512,128]{2,1,0:T(8,128)(2,1)} %copy-done.10, bf16[2,512,128]{2,1,0:T(8,128)(2,1)} %copy-done.11, ...), custom_call_target="tpu_custom_call" | custom-call | flops 2147483648 | bytes 7340032 | tf_op jit(solution)/shard_map/pallas_call | solution.py:87
  71.6 0.0 copy-start.1
  71.6 0.0 copy-start.2
  71.6 0.5 collective-permute-done.6.refs_1_
  72.1 6.8 %collective-permute-done.9.refs_3_ = bf16[1024,256]{1,0:T(8,128)(2,1)S(1)} collective-permute-done((bf16[1024,256]{1,0:T(8,128)(2,1)}, bf16[1024,256]{1,0:T(8,128)(2,1)S(1)}, u32[]{:S(2)}, u32[]{:S(2)}) %collective-permute-start.9) | collective-permute-done | bytes 524320 | tf_op jit(solution)/shard_map/ppermute | solution.py:24
  79.0 4.2 %all-to-all-start.1 = ((f32[16,32,512]{2,1,0:T(8,128)}), f32[16,32,512]{2,1,0:T(8,128)}, u32[]{:S(2)}, u32[]{:S(2)}) async-start(f32[16,32,512]{2,1,0:T(8,128)} %bitcast.22), calls=%async_computation.1 | async-start | bytes 2097152 | tf_op jit(solution)/shard_map/all_to_all | solution.py:275
  83.2 0.0 all-gather.5.cloned.1.call-start
  83.3 0.1 collective-permute-start.13
  83.4 14.9 %all-to-all-done.1 = f32[16,32,512]{2,1,0:T(8,128)} async-done(((f32[16,32,512]{2,1,0:T(8,128)}), f32[16,32,512]{2,1,0:T(8,128)}, u32[]{:S(2)}, u32[]{:S(2)}) %all-to-all-start.1) | async-done | bytes 1048608 | tf_op jit(solution)/shard_map/all_to_all | solution.py:275
  98.2 1.3 bitcast_reduce_fusion
  99.6 2.9 %collective-permute-start.12 = (bf16[1,4,32,512]{3,2,1,0:T(8,128)(2,1)S(1)}, bf16[1,4,32,512]{3,2,1,0:T(8,128)(2,1)S(1)}, u32[]{:S(2)}, u32[]{:S(2)}) collective-permute-start(bf16[1,4,32,512]{3,2,1,0:T(8,128)(2,1)S(1)} %bitcast.23), channel_id=1, source_target_pairs={{0,8},{8,0},{1,9},{9,1},{2,10},{10,2},{3,11},{11,3},{4,12},{12,4},... | collective-permute-start | bytes 393224 | tf_op jit(solution)/shard_map/ppermute | solution.py:24
  102.5 4.3 %collective-permute-done.12 = bf16[1,4,32,512]{3,2,1,0:T(8,128)(2,1)S(1)} collective-permute-done((bf16[1,4,32,512]{3,2,1,0:T(8,128)(2,1)S(1)}, bf16[1,4,32,512]{3,2,1,0:T(8,128)(2,1)S(1)}, u32[]{:S(2)}, u32[]{:S(2)}) %collective-permute-start.12) | collective-permute-done | bytes 131104 | tf_op jit(solution)/shard_map/ppermute | solution.py:24
  106.8 0.7 pad_maximum_fusion.2
  107.5 0.0 all-gather.5.cloned.1.call-update
  107.6 0.3 collective-permute-start.14
  107.8 0.0 all-gather.7.cloned.1.call-done
  107.9 2.2 %collective-permute-done.14.refs_4_ = bf16[1024,256]{1,0:T(8,128)(2,1)} collective-permute-done((bf16[1024,256]{1,0:T(8,128)(2,1)}, bf16[1024,256]{1,0:T(8,128)(2,1)}, u32[]{:S(2)}, u32[]{:S(2)}) %collective-permute-start.14) | collective-permute-done | bytes 524320 | tf_op jit(solution)/shard_map/ppermute | solution.py:24
  110.1 0.0 collective-permute-done.13.refs_2_
  110.1 1.0 copy-done.4
  111.1 5.3 %shard_map.49 = f32[4,128,512]{2,1,0:T(8,128)S(1)} custom-call(s32[5]{0:T(128)S(1)} %copy-done.1, bf16[8,2,512,128]{3,2,1,0:T(8,128)(2,1)} %bitcast.25, bf16[2048,256]{1,0:T(8,128)(2,1)S(1)} %copy-done.2, bf16[2048,256]{1,0:T(8,128)(2,1)S(1)} %collective-permute-done.6.refs_1_, bf16[2048,256]{1,0:T(8,128)(2,1)S(1)} %collective-permute-done.13.refs_2_, ...), custom_call_target="tpu_custom_call" | custom-call | flops 2147483648 | bytes 7340032 | tf_op jit(solution)/shard_map/pallas_call | solution.py:165
  116.4 18.1 %all_to_all.25 = f32[4,128,512]{2,1,0:T(8,128)S(1)} all-to-all(f32[4,128,512]{2,1,0:T(8,128)S(1)} %shard_map.49), channel_id=1, replica_groups=mesh['xl'=2,'c'=2,'y'=4,'xh'=2,'z'=8] {'y'}, dimensions={0} | all-to-all | bytes 2097152 | tf_op jit(solution)/shard_map/all_to_all | solution.py:284
  134.5 0.1 reduce_sum.19
  134.6 0.1 broadcast_in_dim.4
  134.7 17.3 %all_to_all.26 = bf16[8,128,512]{2,1,0:T(8,128)(2,1)S(1)} all-to-all(bf16[8,128,512]{2,1,0:T(8,128)(2,1)S(1)} %broadcast_in_dim.4), channel_id=1, replica_groups=mesh['xl'=2,'c'=2,'y'=4,'xh'=2,'z'=8] {'xl','y'}, dimensions={0} | all-to-all | bytes 2097152 | tf_op jit(solution)/shard_map/all_to_all | solution.py:287
  152.0 0.0 collective-permute-start.15
  152.0 2.7 %collective-permute-done.15.other_ref = bf16[2,4,128,512]{3,2,1,0:T(8,128)(2,1)S(1)} collective-permute-done((bf16[2,4,128,512]{3,2,1,0:T(8,128)(2,1)S(1)}, bf16[2,4,128,512]{3,2,1,0:T(8,128)(2,1)S(1)}, u32[]{:S(2)}, u32[]{:S(2)}) %collective-permute-start.15) | collective-permute-done | bytes 1048608 | tf_op jit(solution)/shard_map/ppermute | solution.py:24
  154.7 1.6 copy-done
  156.3 3.5 %shard_map.50 = bf16[4,128,512]{2,1,0:T(8,128)(2,1)S(1)} custom-call(s32[5]{0:T(128)S(1)} %copy-done.1, bf16[8,2,4,32,512]{4,3,2,1,0:T(8,128)(2,1)S(1)} %bitcast.21, bf16[2,4,128,512]{3,2,1,0:T(8,128)(2,1)S(1)} %bitcast.20, bf16[2,4,128,512]{3,2,1,0:T(8,128)(2,1)S(1)} %collective-permute-done.15.other_ref), custom_call_target="tpu_custom_call" | custom-call | flops 1073741824 | bytes 5242880 | tf_op jit(solution)/shard_map/pallas_call | solution.py:201
  159.8 12.5 %all_to_all.27.in_ref = bf16[4,128,512]{2,1,0:T(8,128)(2,1)S(1)} all-to-all(bf16[4,128,512]{2,1,0:T(8,128)(2,1)S(1)} %shard_map.50), channel_id=1, replica_groups=mesh['xl'=2,'c'=2,'y'=4,'xh'=2,'z'=8] {'y'}, dimensions={0} | all-to-all | bytes 1048576 | tf_op jit(solution)/shard_map/all_to_all | solution.py:291
  172.2 2.0 %shard_map.51 = f32[128,2048]{1,0:T(8,128)} custom-call(bf16[4,128,512]{2,1,0:T(8,128)(2,1)S(1)} %all_to_all.27.in_ref), custom_call_target="tpu_custom_call" | custom-call | tf_op jit(solution)/shard_map/pallas_call | solution.py:224
  (25 shorter events, 0.1 us)
Async XLA Ops:
  6.5 8.0 %collective-permute-start = (bf16[1,512,128]{2,1,0:T(8,128)(2,1)}, bf16[1,512,128]{2,1,0:T(8,128)(2,1)S(1)}, u32[]{:S(2)}, u32[]{:S(2)}) collective-permute-start(bf16[1,512,128]{2,1,0:T(8,128)(2,1)} %param.4), channel_id=1, source_target_pairs={{0,8},{8,0},{1,9},{9,1},{2,10},{10,2},{3,11},{11,3},{4,12},{12,4},... | collective-permute-start | bytes 393224 | tf_op jit(solution)/shard_map/ppermute | solution.py:24
  8.7 7.6 %collective-permute-start.1 = (bf16[1,512,128]{2,1,0:T(8,128)(2,1)}, bf16[1,512,128]{2,1,0:T(8,128)(2,1)S(1)}, u32[]{:S(2)}, u32[]{:S(2)}) collective-permute-start(bf16[1,512,128]{2,1,0:T(8,128)(2,1)} %param.5), channel_id=1, source_target_pairs={{0,8},{8,0},{1,9},{9,1},{2,10},{10,2},{3,11},{11,3},{4,12},{12,4},... | collective-permute-start | bytes 393224 | tf_op jit(solution)/shard_map/ppermute | solution.py:24
  10.1 4.4 %copy-start.6 = (bf16[1,512,128]{2,1,0:T(8,128)(2,1)S(1)}, bf16[1,512,128]{2,1,0:T(8,128)(2,1)}, u32[]{:S(2)}) copy-start(bf16[1,512,128]{2,1,0:T(8,128)(2,1)} %param.4) | copy-start | bytes 393220
  10.1 6.2 %copy-start.7 = (bf16[1,512,128]{2,1,0:T(8,128)(2,1)S(1)}, bf16[1,512,128]{2,1,0:T(8,128)(2,1)}, u32[]{:S(2)}) copy-start(bf16[1,512,128]{2,1,0:T(8,128)(2,1)} %param.5) | copy-start | bytes 393220
  14.5 9.0 %copy-start.5 = (bf16[2,512,128]{2,1,0:T(8,128)(2,1)}, bf16[2,512,128]{2,1,0:T(8,128)(2,1)S(1)}, u32[]{:S(2)}) copy-start(bf16[2,512,128]{2,1,0:T(8,128)(2,1)S(1)} %pad_maximum_fusion.refs_0_) | copy-start | bytes 786436
  17.0 33.1 %all-to-all-start = ((bf16[4,1024,256]{2,1,0:T(8,128)(2,1)}), bf16[4,1024,256]{2,1,0:T(8,128)(2,1)}, u32[]{:S(2)}, u32[]{:S(2)}) async-start(bf16[4,1024,256]{2,1,0:T(8,128)(2,1)} %shard_map.46), calls=%async_computation | async-start | bytes 4194304 | tf_op jit(solution)/shard_map/all_to_all | solution.py:263
  21.5 86.4 %all-gather.7.cloned.1.call-start = ((), (), s32[]{:S(2)}) async-start(), calls=%async_computation.6 | async-start | bytes 2359296 | tf_op jit(solution)/shard_map/all_gather | solution.py:269
  21.5 12.5 %collective-permute-start.2 = (bf16[2,512,128]{2,1,0:T(8,128)(2,1)S(1)}, bf16[2,512,128]{2,1,0:T(8,128)(2,1)S(1)}, u32[]{:S(2)}, u32[]{:S(2)}) collective-permute-start(bf16[2,512,128]{2,1,0:T(8,128)(2,1)S(1)} %pad_maximum_fusion.refs_0_), channel_id=1, source_target_pairs={{0,1},{1,2},{2,3},{3,4},{4,5},{5,6},{6,7},{7,0},{8,9},{9,10},{10,1... | collective-permute-start | bytes 786440 | tf_op jit(solution)/shard_map/ppermute | solution.py:24
  23.5 10.5 %collective-permute-start.3 = (bf16[2,512,128]{2,1,0:T(8,128)(2,1)S(1)}, bf16[2,512,128]{2,1,0:T(8,128)(2,1)S(1)}, u32[]{:S(2)}, u32[]{:S(2)}) collective-permute-start(bf16[2,512,128]{2,1,0:T(8,128)(2,1)S(1)} %pad_maximum_fusion.refs_0_), channel_id=1, source_target_pairs={{0,7},{1,0},{2,1},{3,2},{4,3},{5,4},{6,5},{7,6},{8,15},{9,8},{10,9... | collective-permute-start | bytes 786440 | tf_op jit(solution)/shard_map/ppermute | solution.py:24
  34.1 29.4 %copy-start.8 = (bf16[2,512,128]{2,1,0:T(8,128)(2,1)}, bf16[2,512,128]{2,1,0:T(8,128)(2,1)S(1)}, u32[]{:S(2)}) copy-start(bf16[2,512,128]{2,1,0:T(8,128)(2,1)S(1)} %collective-permute-done.2.refs_1_) | copy-start | bytes 786436
  34.1 29.4 %copy-start.9 = (bf16[2,512,128]{2,1,0:T(8,128)(2,1)}, bf16[2,512,128]{2,1,0:T(8,128)(2,1)S(1)}, u32[]{:S(2)}) copy-start(bf16[2,512,128]{2,1,0:T(8,128)(2,1)S(1)} %collective-permute-done.3.refs_2_) | copy-start | bytes 786436
  34.1 8.3 %collective-permute-start.4 = (bf16[2,512,128]{2,1,0:T(8,128)(2,1)S(1)}, bf16[2,512,128]{2,1,0:T(8,128)(2,1)S(1)}, u32[]{:S(2)}, u32[]{:S(2)}) collective-permute-start(bf16[2,512,128]{2,1,0:T(8,128)(2,1)S(1)} %collective-permute-done.2.refs_1_), channel_id=1, source_target_pairs={{0,1},{1,2},{2,3},{3,4},{4,5},{5,6},{6,7},{7,0},{8,9},{9,10},{10,1... | collective-permute-start | bytes 786440 | tf_op jit(solution)/shard_map/ppermute | solution.py:24
  34.2 8.2 %collective-permute-start.5 = (bf16[2,512,128]{2,1,0:T(8,128)(2,1)S(1)}, bf16[2,512,128]{2,1,0:T(8,128)(2,1)S(1)}, u32[]{:S(2)}, u32[]{:S(2)}) collective-permute-start(bf16[2,512,128]{2,1,0:T(8,128)(2,1)S(1)} %collective-permute-done.3.refs_2_), channel_id=1, source_target_pairs={{0,7},{1,0},{2,1},{3,2},{4,3},{5,4},{6,5},{7,6},{8,15},{9,8},{10,9... | collective-permute-start | bytes 786440 | tf_op jit(solution)/shard_map/ppermute | solution.py:24
  42.4 21.1 %copy-start.10 = (bf16[2,512,128]{2,1,0:T(8,128)(2,1)}, bf16[2,512,128]{2,1,0:T(8,128)(2,1)S(1)}, u32[]{:S(2)}) copy-start(bf16[2,512,128]{2,1,0:T(8,128)(2,1)S(1)} %collective-permute-done.4.refs_3_) | copy-start | bytes 786436
  42.4 21.1 %copy-start.11 = (bf16[2,512,128]{2,1,0:T(8,128)(2,1)}, bf16[2,512,128]{2,1,0:T(8,128)(2,1)S(1)}, u32[]{:S(2)}) copy-start(bf16[2,512,128]{2,1,0:T(8,128)(2,1)S(1)} %collective-permute-done.5.refs_4_) | copy-start | bytes 786436
  42.4 7.7 %collective-permute-start.7 = (bf16[2,512,128]{2,1,0:T(8,128)(2,1)S(1)}, bf16[2,512,128]{2,1,0:T(8,128)(2,1)S(1)}, u32[]{:S(2)}, u32[]{:S(2)}) collective-permute-start(bf16[2,512,128]{2,1,0:T(8,128)(2,1)S(1)} %collective-permute-done.4.refs_3_), channel_id=1, source_target_pairs={{0,1},{1,2},{2,3},{3,4},{4,5},{5,6},{6,7},{7,0},{8,9},{9,10},{10,1... | collective-permute-start | bytes 786440 | tf_op jit(solution)/shard_map/ppermute | solution.py:24
  43.1 7.0 %collective-permute-start.8 = (bf16[2,512,128]{2,1,0:T(8,128)(2,1)S(1)}, bf16[2,512,128]{2,1,0:T(8,128)(2,1)S(1)}, u32[]{:S(2)}, u32[]{:S(2)}) collective-permute-start(bf16[2,512,128]{2,1,0:T(8,128)(2,1)S(1)} %collective-permute-done.5.refs_4_), channel_id=1, source_target_pairs={{0,7},{1,0},{2,1},{3,2},{4,3},{5,4},{6,5},{7,6},{8,15},{9,8},{10,9... | collective-permute-start | bytes 786440 | tf_op jit(solution)/shard_map/ppermute | solution.py:24
  50.1 13.5 %copy-start.12 = (bf16[2,512,128]{2,1,0:T(8,128)(2,1)}, bf16[2,512,128]{2,1,0:T(8,128)(2,1)S(1)}, u32[]{:S(2)}) copy-start(bf16[2,512,128]{2,1,0:T(8,128)(2,1)S(1)} %collective-permute-done.7.refs_5_) | copy-start | bytes 786436
  50.1 13.5 %copy-start.13 = (bf16[2,512,128]{2,1,0:T(8,128)(2,1)}, bf16[2,512,128]{2,1,0:T(8,128)(2,1)S(1)}, u32[]{:S(2)}) copy-start(bf16[2,512,128]{2,1,0:T(8,128)(2,1)S(1)} %collective-permute-done.8.refs_6_) | copy-start | bytes 786436
  50.1 13.4 %collective-permute-start.11 = (bf16[4,1024,256]{2,1,0:T(8,128)(2,1)}, bf16[4,1024,256]{2,1,0:T(8,128)(2,1)}, u32[]{:S(2)}, u32[]{:S(2)}) collective-permute-start(bf16[4,1024,256]{2,1,0:T(8,128)(2,1)} %all-to-all-done.refs_8_), channel_id=1, source_target_pairs={{0,64},{64,0},{1,65},{65,1},{2,66},{66,2},{3,67},{67,3},{4,68},{68... | collective-permute-start | bytes 6291464 | tf_op jit(solution)/shard_map/ppermute | solution.py:24
  50.2 21.9 %collective-permute-start.6 = (bf16[2048,256]{1,0:T(8,128)(2,1)}, bf16[2048,256]{1,0:T(8,128)(2,1)S(1)}, u32[]{:S(2)}, u32[]{:S(2)}) collective-permute-start(bf16[2048,256]{1,0:T(8,128)(2,1)} %get-tuple-element.39), channel_id=1, source_target_pairs={{0,16},{16,32},{32,48},{48,0},{64,112},{80,64},{96,80},{112,96},{1... | collective-permute-start | bytes 3145736 | tf_op jit(solution)/shard_map/ppermute | solution.py:248
  51.9 27.1 %collective-permute-start.9 = (bf16[1024,256]{1,0:T(8,128)(2,1)}, bf16[1024,256]{1,0:T(8,128)(2,1)S(1)}, u32[]{:S(2)}, u32[]{:S(2)}) collective-permute-start(bf16[1024,256]{1,0:T(8,128)(2,1)} %get-tuple-element.44), channel_id=1, source_target_pairs={{0,32},{16,48},{32,0},{48,16},{1,33},{17,49},{33,1},{49,17},{2,34}... | collective-permute-start | bytes 1572872 | tf_op jit(solution)/shard_map/ppermute | solution.py:24
  54.8 8.7 %collective-permute-start.10 = (bf16[2,512,128]{2,1,0:T(8,128)(2,1)S(1)}, bf16[2,512,128]{2,1,0:T(8,128)(2,1)S(1)}, u32[]{:S(2)}, u32[]{:S(2)}) collective-permute-start(bf16[2,512,128]{2,1,0:T(8,128)(2,1)S(1)} %collective-permute-done.7.refs_5_), channel_id=1, source_target_pairs={{0,1},{1,2},{2,3},{3,4},{4,5},{5,6},{6,7},{7,0},{8,9},{9,10},{10,1... | collective-permute-start | bytes 786440 | tf_op jit(solution)/shard_map/ppermute | solution.py:24
  63.5 0.7 copy-start.14
  71.6 38.5 %copy-start.1 = (s32[5]{0:T(128)S(1)}, s32[5]{0:T(128)}, u32[]{:S(2)}) copy-start(s32[5]{0:T(128)} %stack.41.at_ref) | copy-start | bytes 64
  71.6 38.5 %copy-start.2 = (bf16[2048,256]{1,0:T(8,128)(2,1)S(1)}, bf16[2048,256]{1,0:T(8,128)(2,1)}, u32[]{:S(2)}) copy-start(bf16[2048,256]{1,0:T(8,128)(2,1)} %get-tuple-element.54.refs_0_) | copy-start | bytes 3145732
  79.0 4.3 %copy-start.3 = (bf16[1024,256]{1,0:T(8,128)(2,1)}, bf16[1024,256]{1,0:T(8,128)(2,1)S(1)}, u32[]{:S(2)}) copy-start(bf16[1024,256]{1,0:T(8,128)(2,1)S(1)} %collective-permute-done.9.refs_3_) | copy-start | bytes 1572868
  79.0 19.3 %all-to-all-start.1 = ((f32[16,32,512]{2,1,0:T(8,128)}), f32[16,32,512]{2,1,0:T(8,128)}, u32[]{:S(2)}, u32[]{:S(2)}) async-start(f32[16,32,512]{2,1,0:T(8,128)} %bitcast.22), calls=%async_computation.1 | async-start | bytes 2097152 | tf_op jit(solution)/shard_map/all_to_all | solution.py:275
  83.2 71.4 %all-gather.5.cloned.1.call-start = ((), (), s32[]{:S(2)}) async-start(), calls=%async_computation.5 | async-start | bytes 2359296 | tf_op jit(solution)/shard_map/all_gather | solution.py:280
  83.3 26.8 %collective-permute-start.13 = (bf16[2048,256]{1,0:T(8,128)(2,1)S(1)}, bf16[2048,256]{1,0:T(8,128)(2,1)S(1)}, u32[]{:S(2)}, u32[]{:S(2)}) collective-permute-start(bf16[2048,256]{1,0:T(8,128)(2,1)S(1)} %collective-permute-done.6.refs_1_), channel_id=1, source_target_pairs={{0,64},{64,0},{1,65},{65,1},{2,66},{66,2},{3,67},{67,3},{4,68},{68... | collective-permute-start | bytes 3145736 | tf_op jit(solution)/shard_map/ppermute | solution.py:24
  99.6 7.2 %collective-permute-start.12 = (bf16[1,4,32,512]{3,2,1,0:T(8,128)(2,1)S(1)}, bf16[1,4,32,512]{3,2,1,0:T(8,128)(2,1)S(1)}, u32[]{:S(2)}, u32[]{:S(2)}) collective-permute-start(bf16[1,4,32,512]{3,2,1,0:T(8,128)(2,1)S(1)} %bitcast.23), channel_id=1, source_target_pairs={{0,8},{8,0},{1,9},{9,1},{2,10},{10,2},{3,11},{11,3},{4,12},{12,4},... | collective-permute-start | bytes 393224 | tf_op jit(solution)/shard_map/ppermute | solution.py:24
  107.6 2.5 %collective-permute-start.14 = (bf16[1024,256]{1,0:T(8,128)(2,1)}, bf16[1024,256]{1,0:T(8,128)(2,1)}, u32[]{:S(2)}, u32[]{:S(2)}) collective-permute-start(bf16[1024,256]{1,0:T(8,128)(2,1)} %copy-done.3), channel_id=1, source_target_pairs={{0,64},{64,0},{1,65},{65,1},{2,66},{66,2},{3,67},{67,3},{4,68},{68... | collective-permute-start | bytes 1572872 | tf_op jit(solution)/shard_map/ppermute | solution.py:24
  110.1 1.0 copy-start.4
  152.0 2.7 %collective-permute-start.15 = (bf16[2,4,128,512]{3,2,1,0:T(8,128)(2,1)S(1)}, bf16[2,4,128,512]{3,2,1,0:T(8,128)(2,1)S(1)}, u32[]{:S(2)}, u32[]{:S(2)}) collective-permute-start(bf16[2,4,128,512]{3,2,1,0:T(8,128)(2,1)S(1)} %bitcast.19), channel_id=1, source_target_pairs={{0,64},{64,0},{1,65},{65,1},{2,66},{66,2},{3,67},{67,3},{4,68},{68... | collective-permute-start | bytes 3145736 | tf_op jit(solution)/shard_map/ppermute | solution.py:24
  154.7 1.6 copy-start
Sparse Core Ops, SparseCore 0:
  50.3 41.7 all-gather.6
  107.7 40.2 all-gather.4

commit v12 on v11

--- a/solution.py
+++ b/solution.py
@@ -274,13 +274,12 @@
     near_out, far_out, acts_part = sync(near_out, far_out, acts_part)
     acts_in = lax.all_to_all(acts_part.reshape(16, 32, TOK), ("xl", "c", "y"), 0, 0)
     near_out2, far_out2 = shift(near_out, "c", 1), shift(far_out, "c", 1)
+    grads_part = rotate(at, grad_blocks, (own_out, near_out, near_out2, far_out, far_out2))
+    acts_in, grads_part = sync(acts_in, grads_part)
 
     acts = jnp.sum(acts_in.reshape(4, 4, 32, TOK), axis=1).astype(BF16)[None]
-    rot_pair = pair(acts)
-    rot_acts = lax.all_gather(rot_pair, "z")
-
-    grad_blocks, rot_pair = sync(grad_blocks, rot_pair)
-    grads_part = rotate(at, grad_blocks, (own_out, near_out, near_out2, far_out, far_out2))
+    rot_acts = lax.all_gather(pair(acts), "z")
+
     grads_in = lax.all_to_all(grads_part, "y", 0, 0)
     grads = jnp.sum(grads_in, axis=0).astype(BF16)
     copies = jnp.broadcast_to(grads, (8, COLS, TOK))

time: 184 us -> 175 us (0.951); the launches traced: 181 us -> 174 us
  waiting for transfers between devices: 48.9 us -> 43 us
  blocking collectives: 47.9 us -> 45.9 us
    all_to_all x1, waiting for transfers between devices: 14.9 us -> 3.46 us  [body(): lax.all_to_all(acts_part.reshape(16, 32, TOK), ('xl', 'c', 'y'), 0, 0)]
    all_gather x1, waiting for transfers between devices: 0.01 us -> 3.53 us  [body(): rot_acts = lax.all_gather(pair(acts), 'z')]
    all_gather x1, waiting for transfers between devices: 0.02 us -> 3.54 us  [body(): grad_blocks = lax.all_gather(after(grads_pair, up2), 'z')]
    unnamed x30 -> x28, local copies, waits for them, and re-layouts: 3.32 us -> 4.48 us
  transfers between devices with their start and end apart: 20 -> 20, of which waited for: 11 -> 11; matrix products, arithmetic and copies ran while one was open for 2% -> 1% of each run, Pallas kernels for 12% -> 13%
where the time goes in v12:
time: 175 us; the launch traced here: 174 us
  blocking collectives  45.9 us (26%)
  waiting for transfers between devices  43 us (25%)
  starting transfers between devices  35 us (20%)
  Pallas kernels  28.2 us (16%)
  between operations  13.6 us (8%)
  local copies, waits for them, and re-layouts  5.82 us (3%)
  other arithmetic  2.92 us (2%)
    ppermute x15, waiting for transfers between devices, shift(): return lax.ppermute(x, axis, [(i, (i + by) % n) for i in range(n)])  32.4 us
    ppermute x15, starting transfers between devices, shift(): return lax.ppermute(x, axis, [(i, (i + by) % n) for i in range(n)])  24.2 us
    all_to_all x1, blocking collectives, body(): grads_in = lax.all_to_all(grads_part, 'y', 0, 0)  17.4 us
    all_to_all x1, blocking collectives, body(): rot_own = lax.all_to_all(copies, ('xl', 'y'), 0, 0).reshape(2, 4, COLS, TOK)  16.6 us
    all_to_all x1, blocking collectives, body(): return weave(lax.all_to_all(part, 'y', 0, 0))  12 us
    pallas_call x1, Pallas kernels, rotate_ring(): pl.pallas_call(functools.partial(rotate_ring_kernel, [offset for _, offse...  7.45 us
    pallas_call x1, Pallas kernels, reach_basis(): pl.pallas_call(reach_kernel, grid_spec=pltpu.PrefetchScalarGridSpec(num_s...  5.83 us
    pallas_call x1, Pallas kernels, rotate(): pl.pallas_call(rotate_kernel, out_shape=jax.ShapeDtypeStruct((4, COLS, TO...  5.41 us
  transfers between devices with their start and end apart: 20, of which 11 were waited for; matrix products, arithmetic and copies ran while one was open for 1% of the time, Pallas kernels for 13%

profile of v12, /device:TPU:2, one launch (start us, length us, event | category | flops | bytes accessed | tf_op | source)
XLA Modules:
  0.0 174.4 jit_solution(14994576490994526128)
XLA Ops:
  6.5 2.1 %collective-permute-start = (bf16[1,512,128]{2,1,0:T(8,128)(2,1)}, bf16[1,512,128]{2,1,0:T(8,128)(2,1)S(1)}, u32[]{:S(2)}, u32[]{:S(2)}) collective-permute-start(bf16[1,512,128]{2,1,0:T(8,128)(2,1)} %param.4), channel_id=1, source_target_pairs={{0,8},{8,0},{1,9},{9,1},{2,10},{10,2},{3,11},{11,3},{4,12},{12,4},... | collective-permute-start | bytes 393224 | tf_op jit(solution)/shard_map/ppermute | solution.py:24
  8.7 1.4 collective-permute-start.1
  10.1 4.0 %shard_map.46 = bf16[4,1024,256]{2,1,0:T(8,128)(2,1)} custom-call(s32[1]{0:T(128)} %bitcast.4.half_ref, f32[8192,128]{1,0:T(8,128)} %in_ref.1), custom_call_target="tpu_custom_call" | custom-call | flops 1048576 | bytes 4194304 | tf_op jit(solution)/shard_map/pallas_call | solution.py:44
  14.1 0.4 collective-permute-done
  14.5 1.8 %collective-permute-done.1 = bf16[1,512,128]{2,1,0:T(8,128)(2,1)S(1)} collective-permute-done((bf16[1,512,128]{2,1,0:T(8,128)(2,1)}, bf16[1,512,128]{2,1,0:T(8,128)(2,1)S(1)}, u32[]{:S(2)}, u32[]{:S(2)}) %collective-permute-start.1) | collective-permute-done | bytes 131104 | tf_op jit(solution)/shard_map/ppermute | solution.py:24
  16.3 0.0 copy-done.8
  16.3 0.7 pad_maximum_fusion.1
  17.0 4.5 %all-to-all-start = ((bf16[4,1024,256]{2,1,0:T(8,128)(2,1)}), bf16[4,1024,256]{2,1,0:T(8,128)(2,1)S(1)}, u32[]{:S(2)}, u32[]{:S(2)}) async-start(bf16[4,1024,256]{2,1,0:T(8,128)(2,1)} %shard_map.46), calls=%async_computation | async-start | bytes 4194304 | tf_op jit(solution)/shard_map/all_to_all | solution.py:263
  21.5 1.9 %collective-permute-start.2 = (bf16[2,512,128]{2,1,0:T(8,128)(2,1)S(1)}, bf16[2,512,128]{2,1,0:T(8,128)(2,1)S(1)}, u32[]{:S(2)}, u32[]{:S(2)}) collective-permute-start(bf16[2,512,128]{2,1,0:T(8,128)(2,1)S(1)} %pad_maximum_fusion.refs_0_), channel_id=1, source_target_pairs={{0,1},{1,2},{2,3},{3,4},{4,5},{5,6},{6,7},{7,0},{8,9},{9,10},{10,1... | collective-permute-start | bytes 786440 | tf_op jit(solution)/shard_map/ppermute | solution.py:24
  23.4 4.0 %collective-permute-start.3 = (bf16[2,512,128]{2,1,0:T(8,128)(2,1)S(1)}, bf16[2,512,128]{2,1,0:T(8,128)(2,1)S(1)}, u32[]{:S(2)}, u32[]{:S(2)}) collective-permute-start(bf16[2,512,128]{2,1,0:T(8,128)(2,1)S(1)} %pad_maximum_fusion.refs_0_), channel_id=1, source_target_pairs={{0,7},{1,0},{2,1},{3,2},{4,3},{5,4},{6,5},{7,6},{8,15},{9,8},{10,9... | collective-permute-start | bytes 786440 | tf_op jit(solution)/shard_map/ppermute | solution.py:24
  27.4 0.7 stack.47.rows_ref
  28.1 5.8 %shard_map.47 = (bf16[2048,256]{1,0:T(8,128)(2,1)}, bf16[2048,256]{1,0:T(8,128)(2,1)}, bf16[1024,256]{1,0:T(8,128)(2,1)}) custom-call(s32[5]{0:T(128)} %stack.47.rows_ref, f32[8192,128]{1,0:T(8,128)} %in_ref.2), custom_call_target="tpu_custom_call" | custom-call | flops 1048576 | bytes 5242880 | tf_op jit(solution)/shard_map/pallas_call | solution.py:117
  33.9 0.0 collective-permute-done.2.refs_1_
  33.9 0.0 copy-start.9
  33.9 0.0 collective-permute-done.3.refs_2_
  34.0 0.1 collective-permute-start.4
  34.1 3.2 %collective-permute-start.5 = (bf16[2,512,128]{2,1,0:T(8,128)(2,1)S(1)}, bf16[2,512,128]{2,1,0:T(8,128)(2,1)S(1)}, u32[]{:S(2)}, u32[]{:S(2)}) collective-permute-start(bf16[2,512,128]{2,1,0:T(8,128)(2,1)S(1)} %collective-permute-done.3.refs_2_), channel_id=1, source_target_pairs={{0,7},{1,0},{2,1},{3,2},{4,3},{5,4},{6,5},{7,6},{8,15},{9,8},{10,9... | collective-permute-start | bytes 786440 | tf_op jit(solution)/shard_map/ppermute | solution.py:24
  37.3 4.7 %collective-permute-done.4.refs_3_ = bf16[2,512,128]{2,1,0:T(8,128)(2,1)S(1)} collective-permute-done((bf16[2,512,128]{2,1,0:T(8,128)(2,1)S(1)}, bf16[2,512,128]{2,1,0:T(8,128)(2,1)S(1)}, u32[]{:S(2)}, u32[]{:S(2)}) %collective-permute-start.4) | collective-permute-done | bytes 262176 | tf_op jit(solution)/shard_map/ppermute | solution.py:24
  42.0 0.0 collective-permute-done.5.refs_4_
  42.0 0.0 all-gather.5.cloned.1.call-update
  42.0 0.8 collective-permute-start.7
  42.8 2.6 %collective-permute-start.8 = (bf16[2,512,128]{2,1,0:T(8,128)(2,1)S(1)}, bf16[2,512,128]{2,1,0:T(8,128)(2,1)}, u32[]{:S(2)}, u32[]{:S(2)}) collective-permute-start(bf16[2,512,128]{2,1,0:T(8,128)(2,1)S(1)} %collective-permute-done.5.refs_4_), channel_id=1, source_target_pairs={{0,7},{1,0},{2,1},{3,2},{4,3},{5,4},{6,5},{7,6},{8,15},{9,8},{10,9... | collective-permute-start | bytes 786440 | tf_op jit(solution)/shard_map/ppermute | solution.py:24
  45.4 4.3 %collective-permute-done.7.refs_5_ = bf16[2,512,128]{2,1,0:T(8,128)(2,1)S(1)} collective-permute-done((bf16[2,512,128]{2,1,0:T(8,128)(2,1)S(1)}, bf16[2,512,128]{2,1,0:T(8,128)(2,1)S(1)}, u32[]{:S(2)}, u32[]{:S(2)}) %collective-permute-start.7) | collective-permute-done | bytes 262176 | tf_op jit(solution)/shard_map/ppermute | solution.py:24
  49.7 0.0 collective-permute-done.8.refs_6_
  49.7 0.0 all-to-all-done.refs_8_
  49.7 0.0 copy-done.9
  49.7 0.6 copy-done.13
  50.4 0.0 collective-permute-start.11
  50.4 1.7 collective-permute-start.6
  52.1 2.7 %collective-permute-start.9 = (bf16[1024,256]{1,0:T(8,128)(2,1)}, bf16[1024,256]{1,0:T(8,128)(2,1)}, u32[]{:S(2)}, u32[]{:S(2)}) collective-permute-start(bf16[1024,256]{1,0:T(8,128)(2,1)} %get-tuple-element.45), channel_id=1, source_target_pairs={{0,32},{16,48},{32,0},{48,16},{1,33},{17,49},{33,1},{49,17},{2,34}... | collective-permute-start | bytes 1572872 | tf_op jit(solution)/shard_map/ppermute | solution.py:24
  54.8 2.5 %collective-permute-start.10 = (bf16[2,512,128]{2,1,0:T(8,128)(2,1)}, bf16[2,512,128]{2,1,0:T(8,128)(2,1)}, u32[]{:S(2)}, u32[]{:S(2)}) collective-permute-start(bf16[2,512,128]{2,1,0:T(8,128)(2,1)} %copy-done.13), channel_id=1, source_target_pairs={{0,1},{1,2},{2,3},{3,4},{4,5},{5,6},{6,7},{7,0},{8,9},{9,10},{10,1... | collective-permute-start | bytes 786440 | tf_op jit(solution)/shard_map/ppermute | solution.py:24
  57.3 0.6 stack.41.at_ref
  57.9 12.6 %collective-permute-done.10.refs_7_ = bf16[2,512,128]{2,1,0:T(8,128)(2,1)} collective-permute-done((bf16[2,512,128]{2,1,0:T(8,128)(2,1)}, bf16[2,512,128]{2,1,0:T(8,128)(2,1)}, u32[]{:S(2)}, u32[]{:S(2)}) %collective-permute-start.10) | collective-permute-done | bytes 262176 | tf_op jit(solution)/shard_map/ppermute | solution.py:24
  70.5 0.0 collective-permute-done.11.refs_9_
  70.5 7.5 %shard_map.48 = f32[4,128,512]{2,1,0:T(8,128)} custom-call(s32[5]{0:T(128)} %stack.41.at_ref, bf16[2,512,128]{2,1,0:T(8,128)(2,1)} %copy-done.6, bf16[2,512,128]{2,1,0:T(8,128)(2,1)} %copy-done.9, bf16[2,512,128]{2,1,0:T(8,128)(2,1)} %copy-done.10, bf16[2,512,128]{2,1,0:T(8,128)(2,1)} %copy-done.11, bf16[2,512,128]{2,1,0:T(8,128)(2,1)} %copy-done.12, ...), custom_call_target="tpu_custom_call" | custom-call | flops 2147483648 | bytes 7340032 | tf_op jit(solution)/shard_map/pallas_call | solution.py:87
  78.0 0.0 collective-permute-done.6.refs_1_
  78.0 1.1 collective-permute-done.9.refs_3_
  79.1 0.0 collective-permute-start.12
  79.1 4.5 %all-to-all-start.1 = ((f32[16,32,512]{2,1,0:T(8,128)}), f32[16,32,512]{2,1,0:T(8,128)}, u32[]{:S(2)}, u32[]{:S(2)}) async-start(f32[16,32,512]{2,1,0:T(8,128)} %bitcast.22), calls=%async_computation.1 | async-start | bytes 2097152 | tf_op jit(solution)/shard_map/all_to_all | solution.py:275
  83.7 0.0 all-gather.7.cloned.1.call-start
  83.7 0.5 collective-permute-start.13
  84.2 3.5 %all-gather.5.cloned.1.call-done = bf16[16,512,128]{2,1,0:T(8,128)(2,1)} async-done(((bf16[2,512,128]{2,1,0:T(8,128)(2,1)}), bf16[16,512,128]{2,1,0:T(8,128)(2,1)}) %all-gather.5.cloned.1.call-update) | async-done | bytes 2097168 | tf_op jit(solution)/shard_map/all_gather | solution.py:269
  87.8 0.0 collective-permute-done.13.refs_4_
  87.8 0.0 collective-permute-done.12.refs_2_
  87.8 1.0 copy-done.3
  88.7 1.2 copy-done.4
  90.0 5.4 %shard_map.49 = f32[4,128,512]{2,1,0:T(8,128)S(1)} custom-call(s32[5]{0:T(128)S(1)} %copy-done.1, bf16[8,2,512,128]{3,2,1,0:T(8,128)(2,1)} %bitcast.25, bf16[2048,256]{1,0:T(8,128)(2,1)S(1)} %copy-done.2, bf16[2048,256]{1,0:T(8,128)(2,1)S(1)} %collective-permute-done.6.refs_1_, bf16[2048,256]{1,0:T(8,128)(2,1)S(1)} %copy-done.4, ...), custom_call_target="tpu_custom_call" | custom-call | flops 2147483648 | bytes 7340032 | tf_op jit(solution)/shard_map/pallas_call | solution.py:165
  95.4 3.5 %all-to-all-done.1 = f32[16,32,512]{2,1,0:T(8,128)} async-done(((f32[16,32,512]{2,1,0:T(8,128)}), f32[16,32,512]{2,1,0:T(8,128)}, u32[]{:S(2)}, u32[]{:S(2)}) %all-to-all-start.1) | async-done | bytes 1048608 | tf_op jit(solution)/shard_map/all_to_all | solution.py:275
  98.8 1.3 bitcast_reduce_fusion
  100.2 2.5 %collective-permute-start.14 = (bf16[1,4,32,512]{3,2,1,0:T(8,128)(2,1)S(1)}, bf16[1,4,32,512]{3,2,1,0:T(8,128)(2,1)S(1)}, u32[]{:S(2)}, u32[]{:S(2)}) collective-permute-start(bf16[1,4,32,512]{3,2,1,0:T(8,128)(2,1)S(1)} %bitcast.23), channel_id=1, source_target_pairs={{0,8},{8,0},{1,9},{9,1},{2,10},{10,2},{3,11},{11,3},{4,12},{12,4},... | collective-permute-start | bytes 393224 | tf_op jit(solution)/shard_map/ppermute | solution.py:24
  102.7 4.7 %collective-permute-done.14 = bf16[1,4,32,512]{3,2,1,0:T(8,128)(2,1)S(1)} collective-permute-done((bf16[1,4,32,512]{3,2,1,0:T(8,128)(2,1)S(1)}, bf16[1,4,32,512]{3,2,1,0:T(8,128)(2,1)S(1)}, u32[]{:S(2)}, u32[]{:S(2)}) %collective-permute-start.14) | collective-permute-done | bytes 131104 | tf_op jit(solution)/shard_map/ppermute | solution.py:24
  107.4 0.7 pad_maximum_fusion.2
  108.1 0.0 all-gather.7.cloned.1.call-update
  108.2 17.4 %all_to_all.25 = f32[4,128,512]{2,1,0:T(8,128)S(1)} all-to-all(f32[4,128,512]{2,1,0:T(8,128)S(1)} %shard_map.49), channel_id=1, replica_groups=mesh['xl'=2,'c'=2,'y'=4,'xh'=2,'z'=8] {'y'}, dimensions={0} | all-to-all | bytes 2097152 | tf_op jit(solution)/shard_map/all_to_all | solution.py:283
  125.5 0.1 reduce_sum.19
  125.6 0.1 broadcast_in_dim.4
  125.7 16.6 %all_to_all.26 = bf16[8,128,512]{2,1,0:T(8,128)(2,1)S(1)} all-to-all(bf16[8,128,512]{2,1,0:T(8,128)(2,1)S(1)} %broadcast_in_dim.4), channel_id=1, replica_groups=mesh['xl'=2,'c'=2,'y'=4,'xh'=2,'z'=8] {'xl','y'}, dimensions={0} | all-to-all | bytes 2097152 | tf_op jit(solution)/shard_map/all_to_all | solution.py:286
  142.3 0.0 collective-permute-start.15
  142.3 2.7 %collective-permute-done.15.other_ref = bf16[2,4,128,512]{3,2,1,0:T(8,128)(2,1)S(1)} collective-permute-done((bf16[2,4,128,512]{3,2,1,0:T(8,128)(2,1)S(1)}, bf16[2,4,128,512]{3,2,1,0:T(8,128)(2,1)S(1)}, u32[]{:S(2)}, u32[]{:S(2)}) %collective-permute-start.15) | collective-permute-done | bytes 1048608 | tf_op jit(solution)/shard_map/ppermute | solution.py:24
  145.0 3.5 %all-gather.7.cloned.1.call-done = bf16[16,4,32,512]{3,2,1,0:T(8,128)(2,1)} async-done(((bf16[2,4,32,512]{3,2,1,0:T(8,128)(2,1)}), bf16[16,4,32,512]{3,2,1,0:T(8,128)(2,1)}) %all-gather.7.cloned.1.call-update) | async-done | bytes 2097168 | tf_op jit(solution)/shard_map/all_gather | solution.py:281
  148.5 1.6 copy-done
  150.1 3.5 %shard_map.50 = bf16[4,128,512]{2,1,0:T(8,128)(2,1)S(1)} custom-call(s32[5]{0:T(128)S(1)} %copy-done.1, bf16[8,2,4,32,512]{4,3,2,1,0:T(8,128)(2,1)S(1)} %bitcast.21, bf16[2,4,128,512]{3,2,1,0:T(8,128)(2,1)S(1)} %bitcast.20, bf16[2,4,128,512]{3,2,1,0:T(8,128)(2,1)S(1)} %collective-permute-done.15.other_ref), custom_call_target="tpu_custom_call" | custom-call | flops 1073741824 | bytes 5242880 | tf_op jit(solution)/shard_map/pallas_call | solution.py:201
  153.6 12.0 %all_to_all.27.in_ref = bf16[4,128,512]{2,1,0:T(8,128)(2,1)S(1)} all-to-all(bf16[4,128,512]{2,1,0:T(8,128)(2,1)S(1)} %shard_map.50), channel_id=1, replica_groups=mesh['xl'=2,'c'=2,'y'=4,'xh'=2,'z'=8] {'y'}, dimensions={0} | all-to-all | bytes 1048576 | tf_op jit(solution)/shard_map/all_to_all | solution.py:290
  165.6 2.0 %shard_map.51 = f32[128,2048]{1,0:T(8,128)} custom-call(bf16[4,128,512]{2,1,0:T(8,128)(2,1)S(1)} %all_to_all.27.in_ref), custom_call_target="tpu_custom_call" | custom-call | tf_op jit(solution)/shard_map/pallas_call | solution.py:224
  (23 shorter events, 0.1 us)
Async XLA Ops:
  6.5 8.0 %collective-permute-start = (bf16[1,512,128]{2,1,0:T(8,128)(2,1)}, bf16[1,512,128]{2,1,0:T(8,128)(2,1)S(1)}, u32[]{:S(2)}, u32[]{:S(2)}) collective-permute-start(bf16[1,512,128]{2,1,0:T(8,128)(2,1)} %param.4), channel_id=1, source_target_pairs={{0,8},{8,0},{1,9},{9,1},{2,10},{10,2},{3,11},{11,3},{4,12},{12,4},... | collective-permute-start | bytes 393224 | tf_op jit(solution)/shard_map/ppermute | solution.py:24
  8.7 7.6 %collective-permute-start.1 = (bf16[1,512,128]{2,1,0:T(8,128)(2,1)}, bf16[1,512,128]{2,1,0:T(8,128)(2,1)S(1)}, u32[]{:S(2)}, u32[]{:S(2)}) collective-permute-start(bf16[1,512,128]{2,1,0:T(8,128)(2,1)} %param.5), channel_id=1, source_target_pairs={{0,8},{8,0},{1,9},{9,1},{2,10},{10,2},{3,11},{11,3},{4,12},{12,4},... | collective-permute-start | bytes 393224 | tf_op jit(solution)/shard_map/ppermute | solution.py:24
  10.1 4.4 %copy-start.7 = (bf16[1,512,128]{2,1,0:T(8,128)(2,1)S(1)}, bf16[1,512,128]{2,1,0:T(8,128)(2,1)}, u32[]{:S(2)}) copy-start(bf16[1,512,128]{2,1,0:T(8,128)(2,1)} %param.4) | copy-start | bytes 393220
  10.1 6.2 %copy-start.8 = (bf16[1,512,128]{2,1,0:T(8,128)(2,1)S(1)}, bf16[1,512,128]{2,1,0:T(8,128)(2,1)}, u32[]{:S(2)}) copy-start(bf16[1,512,128]{2,1,0:T(8,128)(2,1)} %param.5) | copy-start | bytes 393220
  14.5 8.9 %copy-start.6 = (bf16[2,512,128]{2,1,0:T(8,128)(2,1)}, bf16[2,512,128]{2,1,0:T(8,128)(2,1)S(1)}, u32[]{:S(2)}) copy-start(bf16[2,512,128]{2,1,0:T(8,128)(2,1)S(1)} %pad_maximum_fusion.refs_0_) | copy-start | bytes 786436
  17.0 32.7 %all-to-all-start = ((bf16[4,1024,256]{2,1,0:T(8,128)(2,1)}), bf16[4,1024,256]{2,1,0:T(8,128)(2,1)S(1)}, u32[]{:S(2)}, u32[]{:S(2)}) async-start(bf16[4,1024,256]{2,1,0:T(8,128)(2,1)} %shard_map.46), calls=%async_computation | async-start | bytes 4194304 | tf_op jit(solution)/shard_map/all_to_all | solution.py:263
  21.5 66.3 %all-gather.5.cloned.1.call-start = ((), (), s32[]{:S(2)}) async-start(), calls=%async_computation.5 | async-start | bytes 2359296 | tf_op jit(solution)/shard_map/all_gather | solution.py:269
  21.5 12.4 %collective-permute-start.2 = (bf16[2,512,128]{2,1,0:T(8,128)(2,1)S(1)}, bf16[2,512,128]{2,1,0:T(8,128)(2,1)S(1)}, u32[]{:S(2)}, u32[]{:S(2)}) collective-permute-start(bf16[2,512,128]{2,1,0:T(8,128)(2,1)S(1)} %pad_maximum_fusion.refs_0_), channel_id=1, source_target_pairs={{0,1},{1,2},{2,3},{3,4},{4,5},{5,6},{6,7},{7,0},{8,9},{9,10},{10,1... | collective-permute-start | bytes 786440 | tf_op jit(solution)/shard_map/ppermute | solution.py:24
  23.4 10.5 %collective-permute-start.3 = (bf16[2,512,128]{2,1,0:T(8,128)(2,1)S(1)}, bf16[2,512,128]{2,1,0:T(8,128)(2,1)S(1)}, u32[]{:S(2)}, u32[]{:S(2)}) collective-permute-start(bf16[2,512,128]{2,1,0:T(8,128)(2,1)S(1)} %pad_maximum_fusion.refs_0_), channel_id=1, source_target_pairs={{0,7},{1,0},{2,1},{3,2},{4,3},{5,4},{6,5},{7,6},{8,15},{9,8},{10,9... | collective-permute-start | bytes 786440 | tf_op jit(solution)/shard_map/ppermute | solution.py:24
  33.9 15.8 %copy-start.9 = (bf16[2,512,128]{2,1,0:T(8,128)(2,1)}, bf16[2,512,128]{2,1,0:T(8,128)(2,1)S(1)}, u32[]{:S(2)}) copy-start(bf16[2,512,128]{2,1,0:T(8,128)(2,1)S(1)} %collective-permute-done.2.refs_1_) | copy-start | bytes 786436
  34.0 15.8 %copy-start.10 = (bf16[2,512,128]{2,1,0:T(8,128)(2,1)}, bf16[2,512,128]{2,1,0:T(8,128)(2,1)S(1)}, u32[]{:S(2)}) copy-start(bf16[2,512,128]{2,1,0:T(8,128)(2,1)S(1)} %collective-permute-done.3.refs_2_) | copy-start | bytes 786436
  34.0 8.0 %collective-permute-start.4 = (bf16[2,512,128]{2,1,0:T(8,128)(2,1)S(1)}, bf16[2,512,128]{2,1,0:T(8,128)(2,1)S(1)}, u32[]{:S(2)}, u32[]{:S(2)}) collective-permute-start(bf16[2,512,128]{2,1,0:T(8,128)(2,1)S(1)} %collective-permute-done.2.refs_1_), channel_id=1, source_target_pairs={{0,1},{1,2},{2,3},{3,4},{4,5},{5,6},{6,7},{7,0},{8,9},{9,10},{10,1... | collective-permute-start | bytes 786440 | tf_op jit(solution)/shard_map/ppermute | solution.py:24
  34.1 8.0 %collective-permute-start.5 = (bf16[2,512,128]{2,1,0:T(8,128)(2,1)S(1)}, bf16[2,512,128]{2,1,0:T(8,128)(2,1)S(1)}, u32[]{:S(2)}, u32[]{:S(2)}) collective-permute-start(bf16[2,512,128]{2,1,0:T(8,128)(2,1)S(1)} %collective-permute-done.3.refs_2_), channel_id=1, source_target_pairs={{0,7},{1,0},{2,1},{3,2},{4,3},{5,4},{6,5},{7,6},{8,15},{9,8},{10,9... | collective-permute-start | bytes 786440 | tf_op jit(solution)/shard_map/ppermute | solution.py:24
  42.0 28.5 %copy-start.11 = (bf16[2,512,128]{2,1,0:T(8,128)(2,1)}, bf16[2,512,128]{2,1,0:T(8,128)(2,1)S(1)}, u32[]{:S(2)}) copy-start(bf16[2,512,128]{2,1,0:T(8,128)(2,1)S(1)} %collective-permute-done.4.refs_3_) | copy-start | bytes 786436
  42.0 7.7 %copy-start.12 = (bf16[2,512,128]{2,1,0:T(8,128)(2,1)}, bf16[2,512,128]{2,1,0:T(8,128)(2,1)S(1)}, u32[]{:S(2)}) copy-start(bf16[2,512,128]{2,1,0:T(8,128)(2,1)S(1)} %collective-permute-done.5.refs_4_) | copy-start | bytes 786436
  42.0 7.7 %collective-permute-start.7 = (bf16[2,512,128]{2,1,0:T(8,128)(2,1)S(1)}, bf16[2,512,128]{2,1,0:T(8,128)(2,1)S(1)}, u32[]{:S(2)}, u32[]{:S(2)}) collective-permute-start(bf16[2,512,128]{2,1,0:T(8,128)(2,1)S(1)} %collective-permute-done.4.refs_3_), channel_id=1, source_target_pairs={{0,1},{1,2},{2,3},{3,4},{4,5},{5,6},{6,7},{7,0},{8,9},{9,10},{10,1... | collective-permute-start | bytes 786440 | tf_op jit(solution)/shard_map/ppermute | solution.py:24
  42.8 6.9 %collective-permute-start.8 = (bf16[2,512,128]{2,1,0:T(8,128)(2,1)S(1)}, bf16[2,512,128]{2,1,0:T(8,128)(2,1)}, u32[]{:S(2)}, u32[]{:S(2)}) collective-permute-start(bf16[2,512,128]{2,1,0:T(8,128)(2,1)S(1)} %collective-permute-done.5.refs_4_), channel_id=1, source_target_pairs={{0,7},{1,0},{2,1},{3,2},{4,3},{5,4},{6,5},{7,6},{8,15},{9,8},{10,9... | collective-permute-start | bytes 786440 | tf_op jit(solution)/shard_map/ppermute | solution.py:24
  49.7 0.7 copy-start.13
  50.4 20.1 %copy-start.5 = (bf16[4,1024,256]{2,1,0:T(8,128)(2,1)}, bf16[4,1024,256]{2,1,0:T(8,128)(2,1)S(1)}, u32[]{:S(2)}) copy-start(bf16[4,1024,256]{2,1,0:T(8,128)(2,1)S(1)} %all-to-all-done.refs_8_) | copy-start | bytes 6291460
  50.4 20.1 %collective-permute-start.11 = (bf16[4,1024,256]{2,1,0:T(8,128)(2,1)S(1)}, bf16[4,1024,256]{2,1,0:T(8,128)(2,1)}, u32[]{:S(2)}, u32[]{:S(2)}) collective-permute-start(bf16[4,1024,256]{2,1,0:T(8,128)(2,1)S(1)} %all-to-all-done.refs_8_), channel_id=1, source_target_pairs={{0,64},{64,0},{1,65},{65,1},{2,66},{66,2},{3,67},{67,3},{4,68},{68... | collective-permute-start | bytes 6291464 | tf_op jit(solution)/shard_map/ppermute | solution.py:24
  50.4 27.6 %collective-permute-start.6 = (bf16[2048,256]{1,0:T(8,128)(2,1)}, bf16[2048,256]{1,0:T(8,128)(2,1)S(1)}, u32[]{:S(2)}, u32[]{:S(2)}) collective-permute-start(bf16[2048,256]{1,0:T(8,128)(2,1)} %get-tuple-element.40), channel_id=1, source_target_pairs={{0,16},{16,32},{32,48},{48,0},{64,112},{80,64},{96,80},{112,96},{1... | collective-permute-start | bytes 3145736 | tf_op jit(solution)/shard_map/ppermute | solution.py:248
  52.1 27.0 %collective-permute-start.9 = (bf16[1024,256]{1,0:T(8,128)(2,1)}, bf16[1024,256]{1,0:T(8,128)(2,1)}, u32[]{:S(2)}, u32[]{:S(2)}) collective-permute-start(bf16[1024,256]{1,0:T(8,128)(2,1)} %get-tuple-element.45), channel_id=1, source_target_pairs={{0,32},{16,48},{32,0},{48,16},{1,33},{17,49},{33,1},{49,17},{2,34}... | collective-permute-start | bytes 1572872 | tf_op jit(solution)/shard_map/ppermute | solution.py:24
  54.8 15.7 %collective-permute-start.10 = (bf16[2,512,128]{2,1,0:T(8,128)(2,1)}, bf16[2,512,128]{2,1,0:T(8,128)(2,1)}, u32[]{:S(2)}, u32[]{:S(2)}) collective-permute-start(bf16[2,512,128]{2,1,0:T(8,128)(2,1)} %copy-done.13), channel_id=1, source_target_pairs={{0,1},{1,2},{2,3},{3,4},{4,5},{5,6},{6,7},{7,0},{8,9},{9,10},{10,1... | collective-permute-start | bytes 786440 | tf_op jit(solution)/shard_map/ppermute | solution.py:24
  78.0 10.8 %copy-start.1 = (s32[5]{0:T(128)S(1)}, s32[5]{0:T(128)}, u32[]{:S(2)}) copy-start(s32[5]{0:T(128)} %stack.41.at_ref) | copy-start | bytes 64
  78.0 10.8 %copy-start.2 = (bf16[2048,256]{1,0:T(8,128)(2,1)S(1)}, bf16[2048,256]{1,0:T(8,128)(2,1)}, u32[]{:S(2)}) copy-start(bf16[2048,256]{1,0:T(8,128)(2,1)} %get-tuple-element.54.refs_0_) | copy-start | bytes 3145732
  79.1 8.6 %collective-permute-start.12 = (bf16[2048,256]{1,0:T(8,128)(2,1)S(1)}, bf16[2048,256]{1,0:T(8,128)(2,1)S(1)}, u32[]{:S(2)}, u32[]{:S(2)}) collective-permute-start(bf16[2048,256]{1,0:T(8,128)(2,1)S(1)} %collective-permute-done.6.refs_1_), channel_id=1, source_target_pairs={{0,64},{64,0},{1,65},{65,1},{2,66},{66,2},{3,67},{67,3},{4,68},{68... | collective-permute-start | bytes 3145736 | tf_op jit(solution)/shard_map/ppermute | solution.py:24
  79.1 19.7 %all-to-all-start.1 = ((f32[16,32,512]{2,1,0:T(8,128)}), f32[16,32,512]{2,1,0:T(8,128)}, u32[]{:S(2)}, u32[]{:S(2)}) async-start(f32[16,32,512]{2,1,0:T(8,128)} %bitcast.22), calls=%async_computation.1 | async-start | bytes 2097152 | tf_op jit(solution)/shard_map/all_to_all | solution.py:275
  83.7 64.8 %all-gather.7.cloned.1.call-start = ((), (), s32[]{:S(2)}) async-start(), calls=%async_computation.6 | async-start | bytes 2359296 | tf_op jit(solution)/shard_map/all_gather | solution.py:281
  83.7 4.0 %collective-permute-start.13 = (bf16[1024,256]{1,0:T(8,128)(2,1)}, bf16[1024,256]{1,0:T(8,128)(2,1)}, u32[]{:S(2)}, u32[]{:S(2)}) collective-permute-start(bf16[1024,256]{1,0:T(8,128)(2,1)} %collective-permute-done.9.refs_3_), channel_id=1, source_target_pairs={{0,64},{64,0},{1,65},{65,1},{2,66},{66,2},{3,67},{67,3},{4,68},{68... | collective-permute-start | bytes 1572872 | tf_op jit(solution)/shard_map/ppermute | solution.py:24
  87.8 1.0 copy-start.3
  88.7 1.2 copy-start.4
  100.2 7.2 %collective-permute-start.14 = (bf16[1,4,32,512]{3,2,1,0:T(8,128)(2,1)S(1)}, bf16[1,4,32,512]{3,2,1,0:T(8,128)(2,1)S(1)}, u32[]{:S(2)}, u32[]{:S(2)}) collective-permute-start(bf16[1,4,32,512]{3,2,1,0:T(8,128)(2,1)S(1)} %bitcast.23), channel_id=1, source_target_pairs={{0,8},{8,0},{1,9},{9,1},{2,10},{10,2},{3,11},{11,3},{4,12},{12,4},... | collective-permute-start | bytes 393224 | tf_op jit(solution)/shard_map/ppermute | solution.py:24
  142.3 2.7 %collective-permute-start.15 = (bf16[2,4,128,512]{3,2,1,0:T(8,128)(2,1)S(1)}, bf16[2,4,128,512]{3,2,1,0:T(8,128)(2,1)S(1)}, u32[]{:S(2)}, u32[]{:S(2)}) collective-permute-start(bf16[2,4,128,512]{3,2,1,0:T(8,128)(2,1)S(1)} %bitcast.19), channel_id=1, source_target_pairs={{0,64},{64,0},{1,65},{65,1},{2,66},{66,2},{3,67},{67,3},{4,68},{68... | collective-permute-start | bytes 3145736 | tf_op jit(solution)/shard_map/ppermute | solution.py:24
  148.5 1.6 copy-start
Sparse Core Ops, SparseCore 0:
  42.2 45.5 all-gather.4
  108.3 40.1 all-gather.6

commit v13 on v12

--- a/solution.py
+++ b/solution.py
@@ -257,15 +257,14 @@
         [y * 2, y * 2 + 1, near_y * 2, near_y * 2 + 1, far_y * 2 + c]
     ).astype(jnp.int32)
 
-    a0, grads_pair, mine_in, basis_out = sync(
-        pair(activations), pair(gradients), split_basis(half, basis_in), basis_out
-    )
-    own_in = lax.all_to_all(mine_in, "y", 0, 0)
+    own_in = lax.all_to_all(split_basis(half, basis_in), "y", 0, 0)
+    a0, grads_pair, basis_out = sync(pair(activations), pair(gradients), basis_out)
     own_out, near_out, far_out = reach_basis(rows, basis_out)
     up1, down1, near_out, far_out = sync(*ring_step(a0, a0), near_out, far_out)
     up2, down2, near_out, far_out = sync(*ring_step(up1, down1), near_out, far_out)
-    near_out = shift_near(near_out)
-    up3, down3, own_in, far_out = sync(*ring_step(up2, down2), own_in, far_out)
+    up3, down3, own_in, near_out, far_out = sync(
+        *ring_step(up2, down2), own_in, shift_near(near_out), far_out
+    )
     grad_blocks = lax.all_gather(after(grads_pair, up2), "z")
     far_out = shift(far_out, "y", 2)
     up4, other_in = sync(shift(up3, "z", 1), shift(own_in, "c", 1))

time: 175 us -> 189 us (1.080)
  waiting for transfers between devices: 43 us -> 59.1 us
  starting transfers between devices: 35 us -> 31.5 us
    ppermute x1, waiting for transfers between devices: 0.01 us -> 11.1 us  [shift_near(): return lax.ppermute(x, ('c', 'y'), pairs)]
    ppermute x15, waiting for transfers between devices: 32.4 us -> 38.9 us  [shift(): return lax.ppermute(x, axis, [(i, (i + by) % n) for i in range(n)])]
    ppermute x15, starting transfers between devices: 24.2 us -> 20 us  [shift(): return lax.ppermute(x, axis, [(i, (i + by) % n) for i in range(n)])]
    all_gather x1, waiting for transfers between devices: 3.54 us -> 0.01 us  [body(): grad_blocks = lax.all_gather(after(grads_pair, up2), 'z')]
    unnamed x28 -> x20, local copies, waits for them, and re-layouts: 4.48 us -> 3.81 us
  transfers between devices with their start and end apart: 20 -> 20, of which waited for: 11 -> 12; matrix products, arithmetic and copies ran while one was open for 1% -> 1% of each run, Pallas kernels for 13% -> 12%
where the time goes in v13:
time: 189 us; the launch traced here: 188 us
  waiting for transfers between devices  59.1 us (31%)
  blocking collectives  45.9 us (24%)
  starting transfers between devices  31.5 us (17%)
  Pallas kernels  28.1 us (15%)
  between operations  13.6 us (7%)
  local copies, waits for them, and re-layouts  5.07 us (3%)
  other arithmetic  4.74 us (3%)
    ppermute x15, waiting for transfers between devices, shift(): return lax.ppermute(x, axis, [(i, (i + by) % n) for i in range(n)])  38.9 us
    ppermute x15, starting transfers between devices, shift(): return lax.ppermute(x, axis, [(i, (i + by) % n) for i in range(n)])  20 us
    all_to_all x1, blocking collectives, body(): grads_in = lax.all_to_all(grads_part, 'y', 0, 0)  17.4 us
    all_to_all x1, blocking collectives, body(): rot_own = lax.all_to_all(copies, ('xl', 'y'), 0, 0).reshape(2, 4, COLS, TOK)  16.4 us
    all_to_all x1, blocking collectives, body(): return weave(lax.all_to_all(part, 'y', 0, 0))  12.2 us
    ppermute x1, waiting for transfers between devices, shift_near(): return lax.ppermute(x, ('c', 'y'), pairs)  11.1 us
    pallas_call x1, Pallas kernels, rotate_ring(): pl.pallas_call(functools.partial(rotate_ring_kernel, [offset for _, offse...  7.45 us
    pallas_call x1, Pallas kernels, reach_basis(): pl.pallas_call(reach_kernel, grid_spec=pltpu.PrefetchScalarGridSpec(num_s...  5.78 us
  transfers between devices with their start and end apart: 20, of which 12 were waited for; matrix products, arithmetic and copies ran while one was open for 1% of the time, Pallas kernels for 12%

profile of v13, /device:TPU:2, one launch (start us, length us, event | category | flops | bytes accessed | tf_op | source)
XLA Modules:
  0.0 187.9 jit_solution(7741073189957456757)
XLA Ops:
  6.5 2.1 %collective-permute-start = (bf16[1,512,128]{2,1,0:T(8,128)(2,1)}, bf16[1,512,128]{2,1,0:T(8,128)(2,1)S(1)}, u32[]{:S(2)}, u32[]{:S(2)}) collective-permute-start(bf16[1,512,128]{2,1,0:T(8,128)(2,1)} %param.4), channel_id=1, source_target_pairs={{0,8},{8,0},{1,9},{9,1},{2,10},{10,2},{3,11},{11,3},{4,12},{12,4},... | collective-permute-start | bytes 393224 | tf_op jit(solution)/shard_map/ppermute | solution.py:24
  8.7 1.4 collective-permute-start.1
  10.1 4.4 %collective-permute-done = bf16[1,512,128]{2,1,0:T(8,128)(2,1)S(1)} collective-permute-done((bf16[1,512,128]{2,1,0:T(8,128)(2,1)}, bf16[1,512,128]{2,1,0:T(8,128)(2,1)S(1)}, u32[]{:S(2)}, u32[]{:S(2)}) %collective-permute-start) | collective-permute-done | bytes 131104 | tf_op jit(solution)/shard_map/ppermute | solution.py:24
  14.5 0.9 pad_maximum_fusion.refs_0_
  15.4 0.9 collective-permute-done.1
  16.3 1.7 pad_maximum_fusion.1
  17.9 1.9 %collective-permute-start.2 = (bf16[2,512,128]{2,1,0:T(8,128)(2,1)S(1)}, bf16[2,512,128]{2,1,0:T(8,128)(2,1)S(1)}, u32[]{:S(2)}, u32[]{:S(2)}) collective-permute-start(bf16[2,512,128]{2,1,0:T(8,128)(2,1)S(1)} %pad_maximum_fusion.refs_0_), channel_id=1, source_target_pairs={{0,1},{1,2},{2,3},{3,4},{4,5},{5,6},{6,7},{7,0},{8,9},{9,10},{10,1... | collective-permute-start | bytes 786440 | tf_op jit(solution)/shard_map/ppermute | solution.py:24
  19.9 3.9 %collective-permute-start.3 = (bf16[2,512,128]{2,1,0:T(8,128)(2,1)S(1)}, bf16[2,512,128]{2,1,0:T(8,128)(2,1)S(1)}, u32[]{:S(2)}, u32[]{:S(2)}) collective-permute-start(bf16[2,512,128]{2,1,0:T(8,128)(2,1)S(1)} %pad_maximum_fusion.refs_0_), channel_id=1, source_target_pairs={{0,7},{1,0},{2,1},{3,2},{4,3},{5,4},{6,5},{7,6},{8,15},{9,8},{10,9... | collective-permute-start | bytes 786440 | tf_op jit(solution)/shard_map/ppermute | solution.py:24
  23.8 3.9 %shard_map.47 = bf16[4,1024,256]{2,1,0:T(8,128)(2,1)} custom-call(s32[1]{0:T(128)} %bitcast.4.half_ref, f32[8192,128]{1,0:T(8,128)} %in_ref.2), custom_call_target="tpu_custom_call" | custom-call | flops 1048576 | bytes 4194304 | tf_op jit(solution)/shard_map/pallas_call | solution.py:44
  27.8 0.0 copy-done.6
  27.8 4.5 %all-to-all-start = ((bf16[4,1024,256]{2,1,0:T(8,128)(2,1)}), bf16[4,1024,256]{2,1,0:T(8,128)(2,1)S(1)}, u32[]{:S(2)}, u32[]{:S(2)}) async-start(bf16[4,1024,256]{2,1,0:T(8,128)(2,1)} %shard_map.47), calls=%async_computation | async-start | bytes 4194304 | tf_op jit(solution)/shard_map/all_to_all | solution.py:260
  32.2 0.0 all-gather.5.cloned.1.call-start
  32.2 0.6 stack.47.rows_ref
  32.8 5.8 %shard_map.46 = (bf16[2048,256]{1,0:T(8,128)(2,1)}, bf16[2048,256]{1,0:T(8,128)(2,1)}, bf16[1024,256]{1,0:T(8,128)(2,1)}) custom-call(s32[5]{0:T(128)} %stack.47.rows_ref, f32[8192,128]{1,0:T(8,128)} %in_ref.1), custom_call_target="tpu_custom_call" | custom-call | flops 1048576 | bytes 5242880 | tf_op jit(solution)/shard_map/pallas_call | solution.py:117
  38.6 0.0 collective-permute-done.2.refs_1_
  38.6 0.0 collective-permute-done.3.refs_2_
  38.6 0.0 copy-start.8
  38.6 0.1 collective-permute-start.4
  38.7 3.2 %collective-permute-start.5 = (bf16[2,512,128]{2,1,0:T(8,128)(2,1)S(1)}, bf16[2,512,128]{2,1,0:T(8,128)(2,1)}, u32[]{:S(2)}, u32[]{:S(2)}) collective-permute-start(bf16[2,512,128]{2,1,0:T(8,128)(2,1)S(1)} %collective-permute-done.3.refs_2_), channel_id=1, source_target_pairs={{0,7},{1,0},{2,1},{3,2},{4,3},{5,4},{6,5},{7,6},{8,15},{9,8},{10,9... | collective-permute-start | bytes 786440 | tf_op jit(solution)/shard_map/ppermute | solution.py:24
  41.9 4.7 %collective-permute-done.4.refs_3_ = bf16[2,512,128]{2,1,0:T(8,128)(2,1)S(1)} collective-permute-done((bf16[2,512,128]{2,1,0:T(8,128)(2,1)S(1)}, bf16[2,512,128]{2,1,0:T(8,128)(2,1)S(1)}, u32[]{:S(2)}, u32[]{:S(2)}) %collective-permute-start.4) | collective-permute-done | bytes 262176 | tf_op jit(solution)/shard_map/ppermute | solution.py:24
  46.7 0.0 copy-done.8
  46.7 0.0 collective-permute-done.5.refs_4_
  46.7 1.8 collective-permute-start.8
  48.5 0.0 all-gather.5.cloned.1.call-update
  48.5 0.1 collective-permute-start.6
  48.6 3.2 %collective-permute-start.7 = (bf16[2,512,128]{2,1,0:T(8,128)(2,1)}, bf16[2,512,128]{2,1,0:T(8,128)(2,1)}, u32[]{:S(2)}, u32[]{:S(2)}) collective-permute-start(bf16[2,512,128]{2,1,0:T(8,128)(2,1)} %collective-permute-done.5.refs_4_), channel_id=1, source_target_pairs={{0,7},{1,0},{2,1},{3,2},{4,3},{5,4},{6,5},{7,6},{8,15},{9,8},{10,9... | collective-permute-start | bytes 786440 | tf_op jit(solution)/shard_map/ppermute | solution.py:24
  51.8 4.6 %collective-permute-done.6.refs_5_ = bf16[2,512,128]{2,1,0:T(8,128)(2,1)} collective-permute-done((bf16[2,512,128]{2,1,0:T(8,128)(2,1)S(1)}, bf16[2,512,128]{2,1,0:T(8,128)(2,1)}, u32[]{:S(2)}, u32[]{:S(2)}) %collective-permute-start.6) | collective-permute-done | bytes 262176 | tf_op jit(solution)/shard_map/ppermute | solution.py:24
  56.4 0.0 collective-permute-done.7.refs_6_
  56.4 1.2 all-to-all-done.refs_8_
  57.7 11.1 %collective-permute-done.8.refs_1_ = bf16[2048,256]{1,0:T(8,128)(2,1)S(1)} collective-permute-done((bf16[2048,256]{1,0:T(8,128)(2,1)}, bf16[2048,256]{1,0:T(8,128)(2,1)S(1)}, u32[]{:S(2)}, u32[]{:S(2)}) %collective-permute-start.8) | collective-permute-done | bytes 1048608 | tf_op jit(solution)/shard_map/ppermute | solution.py:248
  68.8 0.0 collective-permute-start.11
  68.8 1.4 collective-permute-start.9
  70.2 0.0 collective-permute-start.10
  70.2 0.6 stack.41.at_ref
  70.8 15.0 %collective-permute-done.10.refs_7_ = bf16[2,512,128]{2,1,0:T(8,128)(2,1)} collective-permute-done((bf16[2,512,128]{2,1,0:T(8,128)(2,1)}, bf16[2,512,128]{2,1,0:T(8,128)(2,1)}, u32[]{:S(2)}, u32[]{:S(2)}) %collective-permute-start.10) | collective-permute-done | bytes 262176 | tf_op jit(solution)/shard_map/ppermute | solution.py:24
  85.8 0.0 collective-permute-done.11.refs_9_
  85.8 7.5 %shard_map.48 = f32[4,128,512]{2,1,0:T(8,128)} custom-call(s32[5]{0:T(128)} %stack.41.at_ref, bf16[2,512,128]{2,1,0:T(8,128)(2,1)} %copy-done.6, bf16[2,512,128]{2,1,0:T(8,128)(2,1)} %copy-done.7, bf16[2,512,128]{2,1,0:T(8,128)(2,1)} %copy-done.8, bf16[2,512,128]{2,1,0:T(8,128)(2,1)} %copy-done.9, bf16[2,512,128]{2,1,0:T(8,128)(2,1)} %collective-permute-done.5.refs_4_, ...), custom_call_target="tpu_custom_call" | custom-call | flops 2147483648 | bytes 7340032 | tf_op jit(solution)/shard_map/pallas_call | solution.py:87
  93.3 0.0 collective-permute-done.9.refs_3_
  93.3 0.1 collective-permute-start.12
  93.4 5.2 %all-to-all-start.1 = ((f32[16,32,512]{2,1,0:T(8,128)}), f32[16,32,512]{2,1,0:T(8,128)}, u32[]{:S(2)}, u32[]{:S(2)}) async-start(f32[16,32,512]{2,1,0:T(8,128)} %bitcast.22), calls=%async_computation.1 | async-start | bytes 2097152 | tf_op jit(solution)/shard_map/all_to_all | solution.py:274
  98.6 0.0 all-gather.7.cloned.1.call-start
  98.6 0.4 collective-permute-start.13
  99.1 2.1 %collective-permute-done.13.refs_4_ = bf16[1024,256]{1,0:T(8,128)(2,1)} collective-permute-done((bf16[1024,256]{1,0:T(8,128)(2,1)}, bf16[1024,256]{1,0:T(8,128)(2,1)}, u32[]{:S(2)}, u32[]{:S(2)}) %collective-permute-start.13) | collective-permute-done | bytes 524320 | tf_op jit(solution)/shard_map/ppermute | solution.py:24
  101.2 0.0 collective-permute-done.12.refs_2_
  101.2 1.0 copy-done.3
  102.1 1.2 copy-done.4
  103.4 5.4 %shard_map.49 = f32[4,128,512]{2,1,0:T(8,128)S(1)} custom-call(s32[5]{0:T(128)S(1)} %copy-done.1, bf16[8,2,512,128]{3,2,1,0:T(8,128)(2,1)} %bitcast.25, bf16[2048,256]{1,0:T(8,128)(2,1)S(1)} %copy-done.2, bf16[2048,256]{1,0:T(8,128)(2,1)S(1)} %collective-permute-done.8.refs_1_, bf16[2048,256]{1,0:T(8,128)(2,1)S(1)} %copy-done.4, ...), custom_call_target="tpu_custom_call" | custom-call | flops 2147483648 | bytes 7340032 | tf_op jit(solution)/shard_map/pallas_call | solution.py:165
  108.8 5.0 %all-to-all-done.1 = f32[16,32,512]{2,1,0:T(8,128)} async-done(((f32[16,32,512]{2,1,0:T(8,128)}), f32[16,32,512]{2,1,0:T(8,128)}, u32[]{:S(2)}, u32[]{:S(2)}) %all-to-all-start.1) | async-done | bytes 1048608 | tf_op jit(solution)/shard_map/all_to_all | solution.py:274
  113.8 1.3 bitcast_reduce_fusion
  115.2 2.1 %collective-permute-start.14 = (bf16[1,4,32,512]{3,2,1,0:T(8,128)(2,1)S(1)}, bf16[1,4,32,512]{3,2,1,0:T(8,128)(2,1)S(1)}, u32[]{:S(2)}, u32[]{:S(2)}) collective-permute-start(bf16[1,4,32,512]{3,2,1,0:T(8,128)(2,1)S(1)} %bitcast.23), channel_id=1, source_target_pairs={{0,8},{8,0},{1,9},{9,1},{2,10},{10,2},{3,11},{11,3},{4,12},{12,4},... | collective-permute-start | bytes 393224 | tf_op jit(solution)/shard_map/ppermute | solution.py:24
  117.2 4.5 %collective-permute-done.14 = bf16[1,4,32,512]{3,2,1,0:T(8,128)(2,1)S(1)} collective-permute-done((bf16[1,4,32,512]{3,2,1,0:T(8,128)(2,1)S(1)}, bf16[1,4,32,512]{3,2,1,0:T(8,128)(2,1)S(1)}, u32[]{:S(2)}, u32[]{:S(2)}) %collective-permute-start.14) | collective-permute-done | bytes 131104 | tf_op jit(solution)/shard_map/ppermute | solution.py:24
  121.7 0.7 pad_maximum_fusion.2
  122.4 0.0 all-gather.7.cloned.1.call-update
  122.5 17.4 %all_to_all.25 = f32[4,128,512]{2,1,0:T(8,128)S(1)} all-to-all(f32[4,128,512]{2,1,0:T(8,128)S(1)} %shard_map.49), channel_id=1, replica_groups=mesh['xl'=2,'c'=2,'y'=4,'xh'=2,'z'=8] {'y'}, dimensions={0} | all-to-all | bytes 2097152 | tf_op jit(solution)/shard_map/all_to_all | solution.py:282
  139.8 0.1 reduce_sum.19
  139.9 0.1 broadcast_in_dim.4
  140.0 16.4 %all_to_all.26 = bf16[8,128,512]{2,1,0:T(8,128)(2,1)S(1)} all-to-all(bf16[8,128,512]{2,1,0:T(8,128)(2,1)S(1)} %broadcast_in_dim.4), channel_id=1, replica_groups=mesh['xl'=2,'c'=2,'y'=4,'xh'=2,'z'=8] {'xl','y'}, dimensions={0} | all-to-all | bytes 2097152 | tf_op jit(solution)/shard_map/all_to_all | solution.py:285
  156.4 0.0 collective-permute-start.15
  156.4 2.7 %collective-permute-done.15.other_ref = bf16[2,4,128,512]{3,2,1,0:T(8,128)(2,1)S(1)} collective-permute-done((bf16[2,4,128,512]{3,2,1,0:T(8,128)(2,1)S(1)}, bf16[2,4,128,512]{3,2,1,0:T(8,128)(2,1)S(1)}, u32[]{:S(2)}, u32[]{:S(2)}) %collective-permute-start.15) | collective-permute-done | bytes 1048608 | tf_op jit(solution)/shard_map/ppermute | solution.py:24
  159.1 2.8 %all-gather.7.cloned.1.call-done = bf16[16,4,32,512]{3,2,1,0:T(8,128)(2,1)} async-done(((bf16[2,4,32,512]{3,2,1,0:T(8,128)(2,1)}), bf16[16,4,32,512]{3,2,1,0:T(8,128)(2,1)}) %all-gather.7.cloned.1.call-update) | async-done | bytes 2097168 | tf_op jit(solution)/shard_map/all_gather | solution.py:280
  161.8 1.6 copy-done
  163.4 3.5 %shard_map.50 = bf16[4,128,512]{2,1,0:T(8,128)(2,1)S(1)} custom-call(s32[5]{0:T(128)S(1)} %copy-done.1, bf16[8,2,4,32,512]{4,3,2,1,0:T(8,128)(2,1)S(1)} %bitcast.21, bf16[2,4,128,512]{3,2,1,0:T(8,128)(2,1)S(1)} %bitcast.20, bf16[2,4,128,512]{3,2,1,0:T(8,128)(2,1)S(1)} %collective-permute-done.15.other_ref), custom_call_target="tpu_custom_call" | custom-call | flops 1073741824 | bytes 5242880 | tf_op jit(solution)/shard_map/pallas_call | solution.py:201
  166.9 12.2 %all_to_all.27.in_ref = bf16[4,128,512]{2,1,0:T(8,128)(2,1)S(1)} all-to-all(bf16[4,128,512]{2,1,0:T(8,128)(2,1)S(1)} %shard_map.50), channel_id=1, replica_groups=mesh['xl'=2,'c'=2,'y'=4,'xh'=2,'z'=8] {'y'}, dimensions={0} | all-to-all | bytes 1048576 | tf_op jit(solution)/shard_map/all_to_all | solution.py:289
  179.1 2.0 %shard_map.51 = f32[128,2048]{1,0:T(8,128)} custom-call(bf16[4,128,512]{2,1,0:T(8,128)(2,1)S(1)} %all_to_all.27.in_ref), custom_call_target="tpu_custom_call" | custom-call | tf_op jit(solution)/shard_map/pallas_call | solution.py:224
  (15 shorter events, 0.0 us)
Async XLA Ops:
  6.5 8.0 %collective-permute-start = (bf16[1,512,128]{2,1,0:T(8,128)(2,1)}, bf16[1,512,128]{2,1,0:T(8,128)(2,1)S(1)}, u32[]{:S(2)}, u32[]{:S(2)}) collective-permute-start(bf16[1,512,128]{2,1,0:T(8,128)(2,1)} %param.4), channel_id=1, source_target_pairs={{0,8},{8,0},{1,9},{9,1},{2,10},{10,2},{3,11},{11,3},{4,12},{12,4},... | collective-permute-start | bytes 393224 | tf_op jit(solution)/shard_map/ppermute | solution.py:24
  8.7 7.6 %collective-permute-start.1 = (bf16[1,512,128]{2,1,0:T(8,128)(2,1)}, bf16[1,512,128]{2,1,0:T(8,128)(2,1)S(1)}, u32[]{:S(2)}, u32[]{:S(2)}) collective-permute-start(bf16[1,512,128]{2,1,0:T(8,128)(2,1)} %param.5), channel_id=1, source_target_pairs={{0,8},{8,0},{1,9},{9,1},{2,10},{10,2},{3,11},{11,3},{4,12},{12,4},... | collective-permute-start | bytes 393224 | tf_op jit(solution)/shard_map/ppermute | solution.py:24
  15.4 12.3 %copy-start.6 = (bf16[2,512,128]{2,1,0:T(8,128)(2,1)}, bf16[2,512,128]{2,1,0:T(8,128)(2,1)S(1)}, u32[]{:S(2)}) copy-start(bf16[2,512,128]{2,1,0:T(8,128)(2,1)S(1)} %pad_maximum_fusion.refs_0_) | copy-start | bytes 786436
  17.9 20.6 %collective-permute-start.2 = (bf16[2,512,128]{2,1,0:T(8,128)(2,1)S(1)}, bf16[2,512,128]{2,1,0:T(8,128)(2,1)S(1)}, u32[]{:S(2)}, u32[]{:S(2)}) collective-permute-start(bf16[2,512,128]{2,1,0:T(8,128)(2,1)S(1)} %pad_maximum_fusion.refs_0_), channel_id=1, source_target_pairs={{0,1},{1,2},{2,3},{3,4},{4,5},{5,6},{6,7},{7,0},{8,9},{9,10},{10,1... | collective-permute-start | bytes 786440 | tf_op jit(solution)/shard_map/ppermute | solution.py:24
  19.9 18.7 %collective-permute-start.3 = (bf16[2,512,128]{2,1,0:T(8,128)(2,1)S(1)}, bf16[2,512,128]{2,1,0:T(8,128)(2,1)S(1)}, u32[]{:S(2)}, u32[]{:S(2)}) collective-permute-start(bf16[2,512,128]{2,1,0:T(8,128)(2,1)S(1)} %pad_maximum_fusion.refs_0_), channel_id=1, source_target_pairs={{0,7},{1,0},{2,1},{3,2},{4,3},{5,4},{6,5},{7,6},{8,15},{9,8},{10,9... | collective-permute-start | bytes 786440 | tf_op jit(solution)/shard_map/ppermute | solution.py:24
  27.8 29.9 %all-to-all-start = ((bf16[4,1024,256]{2,1,0:T(8,128)(2,1)}), bf16[4,1024,256]{2,1,0:T(8,128)(2,1)S(1)}, u32[]{:S(2)}, u32[]{:S(2)}) async-start(bf16[4,1024,256]{2,1,0:T(8,128)(2,1)} %shard_map.47), calls=%async_computation | async-start | bytes 4194304 | tf_op jit(solution)/shard_map/all_to_all | solution.py:260
  32.2 66.8 %all-gather.5.cloned.1.call-start = ((), (), s32[]{:S(2)}) async-start(), calls=%async_computation.5 | async-start | bytes 2359296 | tf_op jit(solution)/shard_map/all_gather | solution.py:268
  38.6 8.1 %copy-start.7 = (bf16[2,512,128]{2,1,0:T(8,128)(2,1)}, bf16[2,512,128]{2,1,0:T(8,128)(2,1)S(1)}, u32[]{:S(2)}) copy-start(bf16[2,512,128]{2,1,0:T(8,128)(2,1)S(1)} %collective-permute-done.2.refs_1_) | copy-start | bytes 786436
  38.6 8.1 %copy-start.8 = (bf16[2,512,128]{2,1,0:T(8,128)(2,1)}, bf16[2,512,128]{2,1,0:T(8,128)(2,1)S(1)}, u32[]{:S(2)}) copy-start(bf16[2,512,128]{2,1,0:T(8,128)(2,1)S(1)} %collective-permute-done.3.refs_2_) | copy-start | bytes 786436
  38.6 8.0 %collective-permute-start.4 = (bf16[2,512,128]{2,1,0:T(8,128)(2,1)S(1)}, bf16[2,512,128]{2,1,0:T(8,128)(2,1)S(1)}, u32[]{:S(2)}, u32[]{:S(2)}) collective-permute-start(bf16[2,512,128]{2,1,0:T(8,128)(2,1)S(1)} %collective-permute-done.2.refs_1_), channel_id=1, source_target_pairs={{0,1},{1,2},{2,3},{3,4},{4,5},{5,6},{6,7},{7,0},{8,9},{9,10},{10,1... | collective-permute-start | bytes 786440 | tf_op jit(solution)/shard_map/ppermute | solution.py:24
  38.7 8.0 %collective-permute-start.5 = (bf16[2,512,128]{2,1,0:T(8,128)(2,1)S(1)}, bf16[2,512,128]{2,1,0:T(8,128)(2,1)}, u32[]{:S(2)}, u32[]{:S(2)}) collective-permute-start(bf16[2,512,128]{2,1,0:T(8,128)(2,1)S(1)} %collective-permute-done.3.refs_2_), channel_id=1, source_target_pairs={{0,7},{1,0},{2,1},{3,2},{4,3},{5,4},{6,5},{7,6},{8,15},{9,8},{10,9... | collective-permute-start | bytes 786440 | tf_op jit(solution)/shard_map/ppermute | solution.py:24
  46.7 39.2 %copy-start.9 = (bf16[2,512,128]{2,1,0:T(8,128)(2,1)}, bf16[2,512,128]{2,1,0:T(8,128)(2,1)S(1)}, u32[]{:S(2)}) copy-start(bf16[2,512,128]{2,1,0:T(8,128)(2,1)S(1)} %collective-permute-done.4.refs_3_) | copy-start | bytes 786436
  46.7 22.1 %collective-permute-start.8 = (bf16[2048,256]{1,0:T(8,128)(2,1)}, bf16[2048,256]{1,0:T(8,128)(2,1)S(1)}, u32[]{:S(2)}, u32[]{:S(2)}) collective-permute-start(bf16[2048,256]{1,0:T(8,128)(2,1)} %get-tuple-element.42), channel_id=1, source_target_pairs={{0,16},{16,32},{32,48},{48,0},{64,112},{80,64},{96,80},{112,96},{1... | collective-permute-start | bytes 3145736 | tf_op jit(solution)/shard_map/ppermute | solution.py:248
  48.5 7.9 %collective-permute-start.6 = (bf16[2,512,128]{2,1,0:T(8,128)(2,1)S(1)}, bf16[2,512,128]{2,1,0:T(8,128)(2,1)}, u32[]{:S(2)}, u32[]{:S(2)}) collective-permute-start(bf16[2,512,128]{2,1,0:T(8,128)(2,1)S(1)} %collective-permute-done.4.refs_3_), channel_id=1, source_target_pairs={{0,1},{1,2},{2,3},{3,4},{4,5},{5,6},{6,7},{7,0},{8,9},{9,10},{10,1... | collective-permute-start | bytes 786440 | tf_op jit(solution)/shard_map/ppermute | solution.py:24
  48.6 7.8 %collective-permute-start.7 = (bf16[2,512,128]{2,1,0:T(8,128)(2,1)}, bf16[2,512,128]{2,1,0:T(8,128)(2,1)}, u32[]{:S(2)}, u32[]{:S(2)}) collective-permute-start(bf16[2,512,128]{2,1,0:T(8,128)(2,1)} %collective-permute-done.5.refs_4_), channel_id=1, source_target_pairs={{0,7},{1,0},{2,1},{3,2},{4,3},{5,4},{6,5},{7,6},{8,15},{9,8},{10,9... | collective-permute-start | bytes 786440 | tf_op jit(solution)/shard_map/ppermute | solution.py:24
  57.6 28.2 %copy-start.5 = (bf16[4,1024,256]{2,1,0:T(8,128)(2,1)}, bf16[4,1024,256]{2,1,0:T(8,128)(2,1)S(1)}, u32[]{:S(2)}) copy-start(bf16[4,1024,256]{2,1,0:T(8,128)(2,1)S(1)} %all-to-all-done.refs_8_) | copy-start | bytes 6291460
  68.8 17.1 %collective-permute-start.11 = (bf16[4,1024,256]{2,1,0:T(8,128)(2,1)S(1)}, bf16[4,1024,256]{2,1,0:T(8,128)(2,1)}, u32[]{:S(2)}, u32[]{:S(2)}) collective-permute-start(bf16[4,1024,256]{2,1,0:T(8,128)(2,1)S(1)} %all-to-all-done.refs_8_), channel_id=1, source_target_pairs={{0,64},{64,0},{1,65},{65,1},{2,66},{66,2},{3,67},{67,3},{4,68},{68... | collective-permute-start | bytes 6291464 | tf_op jit(solution)/shard_map/ppermute | solution.py:24
  68.8 24.5 %collective-permute-start.9 = (bf16[1024,256]{1,0:T(8,128)(2,1)}, bf16[1024,256]{1,0:T(8,128)(2,1)}, u32[]{:S(2)}, u32[]{:S(2)}) collective-permute-start(bf16[1024,256]{1,0:T(8,128)(2,1)} %get-tuple-element.45), channel_id=1, source_target_pairs={{0,32},{16,48},{32,0},{48,16},{1,33},{17,49},{33,1},{49,17},{2,34}... | collective-permute-start | bytes 1572872 | tf_op jit(solution)/shard_map/ppermute | solution.py:24
  70.2 15.7 %collective-permute-start.10 = (bf16[2,512,128]{2,1,0:T(8,128)(2,1)}, bf16[2,512,128]{2,1,0:T(8,128)(2,1)}, u32[]{:S(2)}, u32[]{:S(2)}) collective-permute-start(bf16[2,512,128]{2,1,0:T(8,128)(2,1)} %collective-permute-done.6.refs_5_), channel_id=1, source_target_pairs={{0,1},{1,2},{2,3},{3,4},{4,5},{5,6},{6,7},{7,0},{8,9},{9,10},{10,1... | collective-permute-start | bytes 786440 | tf_op jit(solution)/shard_map/ppermute | solution.py:24
  93.3 8.8 %copy-start.1 = (s32[5]{0:T(128)S(1)}, s32[5]{0:T(128)}, u32[]{:S(2)}) copy-start(s32[5]{0:T(128)} %stack.41.at_ref) | copy-start | bytes 64
  93.3 8.8 %copy-start.2 = (bf16[2048,256]{1,0:T(8,128)(2,1)S(1)}, bf16[2048,256]{1,0:T(8,128)(2,1)}, u32[]{:S(2)}) copy-start(bf16[2048,256]{1,0:T(8,128)(2,1)} %get-tuple-element.54.refs_0_) | copy-start | bytes 3145732
  93.3 7.8 %collective-permute-start.12 = (bf16[2048,256]{1,0:T(8,128)(2,1)S(1)}, bf16[2048,256]{1,0:T(8,128)(2,1)S(1)}, u32[]{:S(2)}, u32[]{:S(2)}) collective-permute-start(bf16[2048,256]{1,0:T(8,128)(2,1)S(1)} %collective-permute-done.8.refs_1_), channel_id=1, source_target_pairs={{0,64},{64,0},{1,65},{65,1},{2,66},{66,2},{3,67},{67,3},{4,68},{68... | collective-permute-start | bytes 3145736 | tf_op jit(solution)/shard_map/ppermute | solution.py:24
  93.4 20.4 %all-to-all-start.1 = ((f32[16,32,512]{2,1,0:T(8,128)}), f32[16,32,512]{2,1,0:T(8,128)}, u32[]{:S(2)}, u32[]{:S(2)}) async-start(f32[16,32,512]{2,1,0:T(8,128)} %bitcast.22), calls=%async_computation.1 | async-start | bytes 2097152 | tf_op jit(solution)/shard_map/all_to_all | solution.py:274
  98.6 63.2 %all-gather.7.cloned.1.call-start = ((), (), s32[]{:S(2)}) async-start(), calls=%async_computation.6 | async-start | bytes 2359296 | tf_op jit(solution)/shard_map/all_gather | solution.py:280
  98.6 2.5 %collective-permute-start.13 = (bf16[1024,256]{1,0:T(8,128)(2,1)}, bf16[1024,256]{1,0:T(8,128)(2,1)}, u32[]{:S(2)}, u32[]{:S(2)}) collective-permute-start(bf16[1024,256]{1,0:T(8,128)(2,1)} %collective-permute-done.9.refs_3_), channel_id=1, source_target_pairs={{0,64},{64,0},{1,65},{65,1},{2,66},{66,2},{3,67},{67,3},{4,68},{68... | collective-permute-start | bytes 1572872 | tf_op jit(solution)/shard_map/ppermute | solution.py:24
  101.2 1.0 copy-start.3
  102.1 1.2 copy-start.4
  115.2 6.6 %collective-permute-start.14 = (bf16[1,4,32,512]{3,2,1,0:T(8,128)(2,1)S(1)}, bf16[1,4,32,512]{3,2,1,0:T(8,128)(2,1)S(1)}, u32[]{:S(2)}, u32[]{:S(2)}) collective-permute-start(bf16[1,4,32,512]{3,2,1,0:T(8,128)(2,1)S(1)} %bitcast.23), channel_id=1, source_target_pairs={{0,8},{8,0},{1,9},{9,1},{2,10},{10,2},{3,11},{11,3},{4,12},{12,4},... | collective-permute-start | bytes 393224 | tf_op jit(solution)/shard_map/ppermute | solution.py:24
  156.4 2.7 %collective-permute-start.15 = (bf16[2,4,128,512]{3,2,1,0:T(8,128)(2,1)S(1)}, bf16[2,4,128,512]{3,2,1,0:T(8,128)(2,1)S(1)}, u32[]{:S(2)}, u32[]{:S(2)}) collective-permute-start(bf16[2,4,128,512]{3,2,1,0:T(8,128)(2,1)S(1)} %bitcast.19), channel_id=1, source_target_pairs={{0,64},{64,0},{1,65},{65,1},{2,66},{66,2},{3,67},{67,3},{4,68},{68... | collective-permute-start | bytes 3145736 | tf_op jit(solution)/shard_map/ppermute | solution.py:24
  161.8 1.6 copy-start
Sparse Core Ops, SparseCore 0:
  48.6 44.7 all-gather.4
  122.6 39.1 all-gather.6

commit v14 on v12

--- a/solution.py
+++ b/solution.py
@@ -263,12 +263,14 @@
     own_in = lax.all_to_all(mine_in, "y", 0, 0)
     own_out, near_out, far_out = reach_basis(rows, basis_out)
     up1, down1, near_out, far_out = sync(*ring_step(a0, a0), near_out, far_out)
-    up2, down2, near_out, far_out = sync(*ring_step(up1, down1), near_out, far_out)
+    up2, down2, own_in, near_out, far_out = sync(
+        *ring_step(up1, down1), own_in, near_out, far_out
+    )
     near_out = shift_near(near_out)
-    up3, down3, own_in, far_out = sync(*ring_step(up2, down2), own_in, far_out)
+    up3, down3, other_in = sync(*ring_step(up2, down2), shift(own_in, "c", 1))
     grad_blocks = lax.all_gather(after(grads_pair, up2), "z")
     far_out = shift(far_out, "y", 2)
-    up4, other_in = sync(shift(up3, "z", 1), shift(own_in, "c", 1))
+    up4 = shift(up3, "z", 1)
     ring = [(a0, 0), (up1, -1), (down1, 1), (up2, -2), (down2, 2), (up3, -3), (down3, 3), (up4, -4)]
     acts_part = rotate_ring(at, ring, own_in, other_in)
     near_out, far_out, acts_part = sync(near_out, far_out, acts_part)

time: 175 us -> 181 us (1.034)
  local copies, waits for them, and re-layouts: 5.82 us -> 9.56 us
  waiting for transfers between devices: 43 us -> 45.6 us
    all_to_all x1, waiting for transfers between devices: 0.01 us -> 5.04 us  [body(): own_in = lax.all_to_all(mine_in, 'y', 0, 0)]
    unnamed x28 -> x38, local copies, waits for them, and re-layouts: 4.48 us -> 8.26 us
    ppermute x15, waiting for transfers between devices: 32.4 us -> 36.1 us  [shift(): return lax.ppermute(x, axis, [(i, (i + by) % n) for i in range(n)])]
    all_gather x1, waiting for transfers between devices: 3.54 us -> 0.01 us  [body(): grad_blocks = lax.all_gather(after(grads_pair, up2), 'z')]
  transfers between devices with their start and end apart: 20 -> 20, of which waited for: 11 -> 12; matrix products, arithmetic and copies ran while one was open for 1% -> 1% of each run, Pallas kernels for 13% -> 12%
where the time goes in v14:
time: 181 us; the launch traced here: 180 us
  blocking collectives  46.7 us (26%)
  waiting for transfers between devices  45.6 us (25%)
  starting transfers between devices  34.1 us (19%)
  Pallas kernels  27.5 us (15%)
  between operations  13.6 us (8%)
  local copies, waits for them, and re-layouts  9.56 us (5%)
  other arithmetic  2.9 us (2%)
    ppermute x15, waiting for transfers between devices, shift(): return lax.ppermute(x, axis, [(i, (i + by) % n) for i in range(n)])  36.1 us
    ppermute x15, starting transfers between devices, shift(): return lax.ppermute(x, axis, [(i, (i + by) % n) for i in range(n)])  24.6 us
    all_to_all x1, blocking collectives, body(): rot_own = lax.all_to_all(copies, ('xl', 'y'), 0, 0).reshape(2, 4, COLS, TOK)  17.3 us
    all_to_all x1, blocking collectives, body(): grads_in = lax.all_to_all(grads_part, 'y', 0, 0)  17.2 us
    all_to_all x1, blocking collectives, body(): return weave(lax.all_to_all(part, 'y', 0, 0))  12.2 us
    unnamed x38, local copies, waits for them, and re-layouts  8.26 us
    pallas_call x1, Pallas kernels, rotate_ring(): pl.pallas_call(functools.partial(rotate_ring_kernel, [offset for _, offse...  7.43 us
    pallas_call x1, Pallas kernels, reach_basis(): pl.pallas_call(reach_kernel, grid_spec=pltpu.PrefetchScalarGridSpec(num_s...  5.84 us
  transfers between devices with their start and end apart: 20, of which 12 were waited for; matrix products, arithmetic and copies ran while one was open for 1% of the time, Pallas kernels for 12%

profile of v14, /device:TPU:2, one launch (start us, length us, event | category | flops | bytes accessed | tf_op | source)
XLA Modules:
  0.0 180.0 jit_solution(7726763412062865498)
XLA Ops:
  6.5 2.1 %collective-permute-start = (bf16[1,512,128]{2,1,0:T(8,128)(2,1)}, bf16[1,512,128]{2,1,0:T(8,128)(2,1)S(1)}, u32[]{:S(2)}, u32[]{:S(2)}) collective-permute-start(bf16[1,512,128]{2,1,0:T(8,128)(2,1)} %param.4), channel_id=1, source_target_pairs={{0,8},{8,0},{1,9},{9,1},{2,10},{10,2},{3,11},{11,3},{4,12},{12,4},... | collective-permute-start | bytes 393224 | tf_op jit(solution)/shard_map/ppermute | solution.py:24
  8.7 1.4 collective-permute-start.1
  10.1 4.0 %shard_map.46 = bf16[4,1024,256]{2,1,0:T(8,128)(2,1)} custom-call(s32[1]{0:T(128)} %bitcast.4.half_ref, f32[8192,128]{1,0:T(8,128)} %in_ref.1), custom_call_target="tpu_custom_call" | custom-call | flops 1048576 | bytes 4194304 | tf_op jit(solution)/shard_map/pallas_call | solution.py:44
  14.1 0.4 collective-permute-done
  14.5 1.8 collective-permute-done.1
  16.3 0.7 pad_maximum_fusion.1
  17.0 4.5 %all-to-all-start = ((bf16[4,1024,256]{2,1,0:T(8,128)(2,1)}), bf16[4,1024,256]{2,1,0:T(8,128)(2,1)}, u32[]{:S(2)}, u32[]{:S(2)}) async-start(bf16[4,1024,256]{2,1,0:T(8,128)(2,1)} %shard_map.46), calls=%async_computation | async-start | bytes 4194304 | tf_op jit(solution)/shard_map/all_to_all | solution.py:263
  21.5 0.0 all-gather.5.cloned.1.call-start
  21.5 2.0 %collective-permute-start.2 = (bf16[2,512,128]{2,1,0:T(8,128)(2,1)S(1)}, bf16[2,512,128]{2,1,0:T(8,128)(2,1)S(1)}, u32[]{:S(2)}, u32[]{:S(2)}) collective-permute-start(bf16[2,512,128]{2,1,0:T(8,128)(2,1)S(1)} %pad_maximum_fusion.refs_0_), channel_id=1, source_target_pairs={{0,1},{1,2},{2,3},{3,4},{4,5},{5,6},{6,7},{7,0},{8,9},{9,10},{10,1... | collective-permute-start | bytes 786440 | tf_op jit(solution)/shard_map/ppermute | solution.py:24
  23.5 4.0 %collective-permute-start.3 = (bf16[2,512,128]{2,1,0:T(8,128)(2,1)S(1)}, bf16[2,512,128]{2,1,0:T(8,128)(2,1)S(1)}, u32[]{:S(2)}, u32[]{:S(2)}) collective-permute-start(bf16[2,512,128]{2,1,0:T(8,128)(2,1)S(1)} %pad_maximum_fusion.refs_0_), channel_id=1, source_target_pairs={{0,7},{1,0},{2,1},{3,2},{4,3},{5,4},{6,5},{7,6},{8,15},{9,8},{10,9... | collective-permute-start | bytes 786440 | tf_op jit(solution)/shard_map/ppermute | solution.py:24
  27.6 0.6 stack.47.rows_ref
  28.2 5.8 %shard_map.47 = (bf16[2048,256]{1,0:T(8,128)(2,1)}, bf16[2048,256]{1,0:T(8,128)(2,1)}, bf16[1024,256]{1,0:T(8,128)(2,1)}) custom-call(s32[5]{0:T(128)} %stack.47.rows_ref, f32[8192,128]{1,0:T(8,128)} %in_ref.2), custom_call_target="tpu_custom_call" | custom-call | flops 1048576 | bytes 5242880 | tf_op jit(solution)/shard_map/pallas_call | solution.py:117
  34.0 0.0 collective-permute-done.2.refs_1_
  34.0 0.0 collective-permute-done.3.refs_2_
  34.0 0.1 collective-permute-start.4
  34.1 3.2 %collective-permute-start.5 = (bf16[2,512,128]{2,1,0:T(8,128)(2,1)S(1)}, bf16[2,512,128]{2,1,0:T(8,128)(2,1)S(1)}, u32[]{:S(2)}, u32[]{:S(2)}) collective-permute-start(bf16[2,512,128]{2,1,0:T(8,128)(2,1)S(1)} %collective-permute-done.3.refs_2_), channel_id=1, source_target_pairs={{0,7},{1,0},{2,1},{3,2},{4,3},{5,4},{6,5},{7,6},{8,15},{9,8},{10,9... | collective-permute-start | bytes 786440 | tf_op jit(solution)/shard_map/ppermute | solution.py:24
  37.4 5.0 %collective-permute-done.4.refs_3_ = bf16[2,512,128]{2,1,0:T(8,128)(2,1)S(1)} collective-permute-done((bf16[2,512,128]{2,1,0:T(8,128)(2,1)S(1)}, bf16[2,512,128]{2,1,0:T(8,128)(2,1)S(1)}, u32[]{:S(2)}, u32[]{:S(2)}) %collective-permute-start.4) | collective-permute-done | bytes 262176 | tf_op jit(solution)/shard_map/ppermute | solution.py:24
  42.4 0.0 collective-permute-done.5.refs_4_
  42.4 5.0 %all-to-all-done.refs_8_ = bf16[4,1024,256]{2,1,0:T(8,128)(2,1)} async-done(((bf16[4,1024,256]{2,1,0:T(8,128)(2,1)}), bf16[4,1024,256]{2,1,0:T(8,128)(2,1)}, u32[]{:S(2)}, u32[]{:S(2)}) %all-to-all-start) | async-done | bytes 2097184 | tf_op jit(solution)/shard_map/all_to_all | solution.py:263
  47.4 0.0 all-gather.5.cloned.1.call-update
  47.4 0.1 collective-permute-start.10
  47.5 0.7 collective-permute-start.6
  48.3 1.9 %collective-permute-start.8 = (bf16[2,512,128]{2,1,0:T(8,128)(2,1)S(1)}, bf16[2,512,128]{2,1,0:T(8,128)(2,1)S(1)}, u32[]{:S(2)}, u32[]{:S(2)}) collective-permute-start(bf16[2,512,128]{2,1,0:T(8,128)(2,1)S(1)} %collective-permute-done.4.refs_3_), channel_id=1, source_target_pairs={{0,1},{1,2},{2,3},{3,4},{4,5},{5,6},{6,7},{7,0},{8,9},{9,10},{10,1... | collective-permute-start | bytes 786440 | tf_op jit(solution)/shard_map/ppermute | solution.py:24
  50.2 3.9 %collective-permute-start.9 = (bf16[2,512,128]{2,1,0:T(8,128)(2,1)S(1)}, bf16[2,512,128]{2,1,0:T(8,128)(2,1)S(1)}, u32[]{:S(2)}, u32[]{:S(2)}) collective-permute-start(bf16[2,512,128]{2,1,0:T(8,128)(2,1)S(1)} %collective-permute-done.5.refs_4_), channel_id=1, source_target_pairs={{0,7},{1,0},{2,1},{3,2},{4,3},{5,4},{6,5},{7,6},{8,15},{9,8},{10,9... | collective-permute-start | bytes 786440 | tf_op jit(solution)/shard_map/ppermute | solution.py:24
  54.1 2.0 %collective-permute-start.7 = (bf16[1024,256]{1,0:T(8,128)(2,1)}, bf16[1024,256]{1,0:T(8,128)(2,1)S(1)}, u32[]{:S(2)}, u32[]{:S(2)}) collective-permute-start(bf16[1024,256]{1,0:T(8,128)(2,1)} %get-tuple-element.40), channel_id=1, source_target_pairs={{0,32},{16,48},{32,0},{48,16},{1,33},{17,49},{33,1},{49,17},{2,34}... | collective-permute-start | bytes 1572872 | tf_op jit(solution)/shard_map/ppermute | solution.py:24
  56.1 5.1 %collective-permute-done.8.refs_5_ = bf16[2,512,128]{2,1,0:T(8,128)(2,1)S(1)} collective-permute-done((bf16[2,512,128]{2,1,0:T(8,128)(2,1)S(1)}, bf16[2,512,128]{2,1,0:T(8,128)(2,1)S(1)}, u32[]{:S(2)}, u32[]{:S(2)}) %collective-permute-start.8) | collective-permute-done | bytes 262176 | tf_op jit(solution)/shard_map/ppermute | solution.py:24
  61.3 0.5 collective-permute-done.9.refs_6_
  61.7 0.0 collective-permute-done.10.refs_9_
  61.8 0.0 collective-permute-start.11
  61.8 0.6 stack.41.at_ref
  62.4 15.0 %collective-permute-done.11.refs_7_ = bf16[2,512,128]{2,1,0:T(8,128)(2,1)S(1)} collective-permute-done((bf16[2,512,128]{2,1,0:T(8,128)(2,1)S(1)}, bf16[2,512,128]{2,1,0:T(8,128)(2,1)S(1)}, u32[]{:S(2)}, u32[]{:S(2)}) %collective-permute-start.11) | collective-permute-done | bytes 262176 | tf_op jit(solution)/shard_map/ppermute | solution.py:24
  77.4 0.7 copy-done.18
  78.1 7.4 %shard_map.48 = f32[4,128,512]{2,1,0:T(8,128)} custom-call(s32[5]{0:T(128)} %stack.41.at_ref, bf16[2,512,128]{2,1,0:T(8,128)(2,1)} %copy-done.9, bf16[2,512,128]{2,1,0:T(8,128)(2,1)} %copy-done.12, bf16[2,512,128]{2,1,0:T(8,128)(2,1)} %copy-done.13, bf16[2,512,128]{2,1,0:T(8,128)(2,1)} %copy-done.14, bf16[2,512,128]{2,1,0:T(8,128)(2,1)} %copy-done.15, ...), custom_call_target="tpu_custom_call" | custom-call | flops 2147483648 | bytes 7340032 | tf_op jit(solution)/shard_map/pallas_call | solution.py:87
  85.5 0.0 collective-permute-done.7.refs_3_
  85.6 0.8 copy-done.5
  86.3 0.0 collective-permute-done.6.refs_1_
  86.3 0.0 collective-permute-start.12
  86.3 4.2 %all-to-all-start.1 = ((f32[16,32,512]{2,1,0:T(8,128)}), f32[16,32,512]{2,1,0:T(8,128)}, u32[]{:S(2)}, u32[]{:S(2)}) async-start(f32[16,32,512]{2,1,0:T(8,128)} %bitcast.22), calls=%async_computation.1 | async-start | bytes 2097152 | tf_op jit(solution)/shard_map/all_to_all | solution.py:277
  90.6 0.0 all-gather.7.cloned.1.call-start
  90.7 0.8 collective-permute-start.13
  91.4 1.7 collective-permute-done.13.refs_4_
  93.2 0.8 copy-done.7
  94.0 0.0 collective-permute-done.12.refs_2_
  94.0 1.0 copy-done.3
  95.0 1.2 copy-done.4
  96.3 1.0 copy-done.6
  97.3 1.0 copy-done.8
  98.3 4.7 %shard_map.49 = f32[4,128,512]{2,1,0:T(8,128)S(1)} custom-call(s32[5]{0:T(128)S(1)} %copy-done.1, bf16[8,2,512,128]{3,2,1,0:T(8,128)(2,1)} %bitcast.25, bf16[2048,256]{1,0:T(8,128)(2,1)S(1)} %copy-done.2, bf16[2048,256]{1,0:T(8,128)(2,1)S(1)} %collective-permute-done.6.refs_1_, bf16[2048,256]{1,0:T(8,128)(2,1)S(1)} %copy-done.4, ...), custom_call_target="tpu_custom_call" | custom-call | flops 2147483648 | bytes 7340032 | tf_op jit(solution)/shard_map/pallas_call | solution.py:165
  103.1 2.2 %all-to-all-done.1 = f32[16,32,512]{2,1,0:T(8,128)} async-done(((f32[16,32,512]{2,1,0:T(8,128)}), f32[16,32,512]{2,1,0:T(8,128)}, u32[]{:S(2)}, u32[]{:S(2)}) %all-to-all-start.1) | async-done | bytes 1048608 | tf_op jit(solution)/shard_map/all_to_all | solution.py:277
  105.3 1.3 bitcast_reduce_fusion
  106.7 3.0 %collective-permute-start.14 = (bf16[1,4,32,512]{3,2,1,0:T(8,128)(2,1)S(1)}, bf16[1,4,32,512]{3,2,1,0:T(8,128)(2,1)S(1)}, u32[]{:S(2)}, u32[]{:S(2)}) collective-permute-start(bf16[1,4,32,512]{3,2,1,0:T(8,128)(2,1)S(1)} %bitcast.23), channel_id=1, source_target_pairs={{0,8},{8,0},{1,9},{9,1},{2,10},{10,2},{3,11},{11,3},{4,12},{12,4},... | collective-permute-start | bytes 393224 | tf_op jit(solution)/shard_map/ppermute | solution.py:24
  109.7 3.9 %collective-permute-done.14 = bf16[1,4,32,512]{3,2,1,0:T(8,128)(2,1)S(1)} collective-permute-done((bf16[1,4,32,512]{3,2,1,0:T(8,128)(2,1)S(1)}, bf16[1,4,32,512]{3,2,1,0:T(8,128)(2,1)S(1)}, u32[]{:S(2)}, u32[]{:S(2)}) %collective-permute-start.14) | collective-permute-done | bytes 131104 | tf_op jit(solution)/shard_map/ppermute | solution.py:24
  113.6 0.7 pad_maximum_fusion.2
  114.3 0.0 all-gather.7.cloned.1.call-update
  114.3 17.2 %all_to_all.25 = f32[4,128,512]{2,1,0:T(8,128)S(1)} all-to-all(f32[4,128,512]{2,1,0:T(8,128)S(1)} %shard_map.49), channel_id=1, replica_groups=mesh['xl'=2,'c'=2,'y'=4,'xh'=2,'z'=8] {'y'}, dimensions={0} | all-to-all | bytes 2097152 | tf_op jit(solution)/shard_map/all_to_all | solution.py:285
  131.5 0.1 reduce_sum.19
  131.6 0.1 broadcast_in_dim.4
  131.7 17.3 %all_to_all.26 = bf16[8,128,512]{2,1,0:T(8,128)(2,1)S(1)} all-to-all(bf16[8,128,512]{2,1,0:T(8,128)(2,1)S(1)} %broadcast_in_dim.4), channel_id=1, replica_groups=mesh['xl'=2,'c'=2,'y'=4,'xh'=2,'z'=8] {'xl','y'}, dimensions={0} | all-to-all | bytes 2097152 | tf_op jit(solution)/shard_map/all_to_all | solution.py:288
  149.0 2.7 %collective-permute-done.15.other_ref = bf16[2,4,128,512]{3,2,1,0:T(8,128)(2,1)S(1)} collective-permute-done((bf16[2,4,128,512]{3,2,1,0:T(8,128)(2,1)S(1)}, bf16[2,4,128,512]{3,2,1,0:T(8,128)(2,1)S(1)}, u32[]{:S(2)}, u32[]{:S(2)}) %collective-permute-start.15) | collective-permute-done | bytes 1048608 | tf_op jit(solution)/shard_map/ppermute | solution.py:24
  151.7 2.2 %all-gather.7.cloned.1.call-done = bf16[16,4,32,512]{3,2,1,0:T(8,128)(2,1)} async-done(((bf16[2,4,32,512]{3,2,1,0:T(8,128)(2,1)}), bf16[16,4,32,512]{3,2,1,0:T(8,128)(2,1)}) %all-gather.7.cloned.1.call-update) | async-done | bytes 2097168 | tf_op jit(solution)/shard_map/all_gather | solution.py:283
  153.9 1.6 copy-done
  155.5 3.5 %shard_map.50 = bf16[4,128,512]{2,1,0:T(8,128)(2,1)S(1)} custom-call(s32[5]{0:T(128)S(1)} %copy-done.1, bf16[8,2,4,32,512]{4,3,2,1,0:T(8,128)(2,1)S(1)} %bitcast.21, bf16[2,4,128,512]{3,2,1,0:T(8,128)(2,1)S(1)} %bitcast.20, bf16[2,4,128,512]{3,2,1,0:T(8,128)(2,1)S(1)} %collective-permute-done.15.other_ref), custom_call_target="tpu_custom_call" | custom-call | flops 1073741824 | bytes 5242880 | tf_op jit(solution)/shard_map/pallas_call | solution.py:201
  159.0 12.2 %all_to_all.27.in_ref = bf16[4,128,512]{2,1,0:T(8,128)(2,1)S(1)} all-to-all(bf16[4,128,512]{2,1,0:T(8,128)(2,1)S(1)} %shard_map.50), channel_id=1, replica_groups=mesh['xl'=2,'c'=2,'y'=4,'xh'=2,'z'=8] {'y'}, dimensions={0} | all-to-all | bytes 1048576 | tf_op jit(solution)/shard_map/all_to_all | solution.py:292
  171.2 2.0 %shard_map.51 = f32[128,2048]{1,0:T(8,128)} custom-call(bf16[4,128,512]{2,1,0:T(8,128)(2,1)S(1)} %all_to_all.27.in_ref), custom_call_target="tpu_custom_call" | custom-call | tf_op jit(solution)/shard_map/pallas_call | solution.py:224
  (33 shorter events, 0.1 us)
Async XLA Ops:
  6.5 8.0 %collective-permute-start = (bf16[1,512,128]{2,1,0:T(8,128)(2,1)}, bf16[1,512,128]{2,1,0:T(8,128)(2,1)S(1)}, u32[]{:S(2)}, u32[]{:S(2)}) collective-permute-start(bf16[1,512,128]{2,1,0:T(8,128)(2,1)} %param.4), channel_id=1, source_target_pairs={{0,8},{8,0},{1,9},{9,1},{2,10},{10,2},{3,11},{11,3},{4,12},{12,4},... | collective-permute-start | bytes 393224 | tf_op jit(solution)/shard_map/ppermute | solution.py:24
  8.7 7.6 %collective-permute-start.1 = (bf16[1,512,128]{2,1,0:T(8,128)(2,1)}, bf16[1,512,128]{2,1,0:T(8,128)(2,1)S(1)}, u32[]{:S(2)}, u32[]{:S(2)}) collective-permute-start(bf16[1,512,128]{2,1,0:T(8,128)(2,1)} %param.5), channel_id=1, source_target_pairs={{0,8},{8,0},{1,9},{9,1},{2,10},{10,2},{3,11},{11,3},{4,12},{12,4},... | collective-permute-start | bytes 393224 | tf_op jit(solution)/shard_map/ppermute | solution.py:24
  10.1 4.4 %copy-start.10 = (bf16[1,512,128]{2,1,0:T(8,128)(2,1)S(1)}, bf16[1,512,128]{2,1,0:T(8,128)(2,1)}, u32[]{:S(2)}) copy-start(bf16[1,512,128]{2,1,0:T(8,128)(2,1)} %param.4) | copy-start | bytes 393220
  10.1 6.2 %copy-start.11 = (bf16[1,512,128]{2,1,0:T(8,128)(2,1)S(1)}, bf16[1,512,128]{2,1,0:T(8,128)(2,1)}, u32[]{:S(2)}) copy-start(bf16[1,512,128]{2,1,0:T(8,128)(2,1)} %param.5) | copy-start | bytes 393220
  14.5 9.0 %copy-start.9 = (bf16[2,512,128]{2,1,0:T(8,128)(2,1)}, bf16[2,512,128]{2,1,0:T(8,128)(2,1)S(1)}, u32[]{:S(2)}) copy-start(bf16[2,512,128]{2,1,0:T(8,128)(2,1)S(1)} %pad_maximum_fusion.refs_0_) | copy-start | bytes 786436
  17.0 30.4 %all-to-all-start = ((bf16[4,1024,256]{2,1,0:T(8,128)(2,1)}), bf16[4,1024,256]{2,1,0:T(8,128)(2,1)}, u32[]{:S(2)}, u32[]{:S(2)}) async-start(bf16[4,1024,256]{2,1,0:T(8,128)(2,1)} %shard_map.46), calls=%async_computation | async-start | bytes 4194304 | tf_op jit(solution)/shard_map/all_to_all | solution.py:263
  21.5 73.5 %all-gather.5.cloned.1.call-start = ((), (), s32[]{:S(2)}) async-start(), calls=%async_computation.5 | async-start | bytes 2359296 | tf_op jit(solution)/shard_map/all_gather | solution.py:271
  21.5 12.5 %collective-permute-start.2 = (bf16[2,512,128]{2,1,0:T(8,128)(2,1)S(1)}, bf16[2,512,128]{2,1,0:T(8,128)(2,1)S(1)}, u32[]{:S(2)}, u32[]{:S(2)}) collective-permute-start(bf16[2,512,128]{2,1,0:T(8,128)(2,1)S(1)} %pad_maximum_fusion.refs_0_), channel_id=1, source_target_pairs={{0,1},{1,2},{2,3},{3,4},{4,5},{5,6},{6,7},{7,0},{8,9},{9,10},{10,1... | collective-permute-start | bytes 786440 | tf_op jit(solution)/shard_map/ppermute | solution.py:24
  23.5 10.5 %collective-permute-start.3 = (bf16[2,512,128]{2,1,0:T(8,128)(2,1)S(1)}, bf16[2,512,128]{2,1,0:T(8,128)(2,1)S(1)}, u32[]{:S(2)}, u32[]{:S(2)}) collective-permute-start(bf16[2,512,128]{2,1,0:T(8,128)(2,1)S(1)} %pad_maximum_fusion.refs_0_), channel_id=1, source_target_pairs={{0,7},{1,0},{2,1},{3,2},{4,3},{5,4},{6,5},{7,6},{8,15},{9,8},{10,9... | collective-permute-start | bytes 786440 | tf_op jit(solution)/shard_map/ppermute | solution.py:24
  34.0 43.3 %copy-start.12 = (bf16[2,512,128]{2,1,0:T(8,128)(2,1)}, bf16[2,512,128]{2,1,0:T(8,128)(2,1)S(1)}, u32[]{:S(2)}) copy-start(bf16[2,512,128]{2,1,0:T(8,128)(2,1)S(1)} %collective-permute-done.2.refs_1_) | copy-start | bytes 786436
  34.0 43.3 %copy-start.13 = (bf16[2,512,128]{2,1,0:T(8,128)(2,1)}, bf16[2,512,128]{2,1,0:T(8,128)(2,1)S(1)}, u32[]{:S(2)}) copy-start(bf16[2,512,128]{2,1,0:T(8,128)(2,1)S(1)} %collective-permute-done.3.refs_2_) | copy-start | bytes 786436
  34.0 8.3 %collective-permute-start.4 = (bf16[2,512,128]{2,1,0:T(8,128)(2,1)S(1)}, bf16[2,512,128]{2,1,0:T(8,128)(2,1)S(1)}, u32[]{:S(2)}, u32[]{:S(2)}) collective-permute-start(bf16[2,512,128]{2,1,0:T(8,128)(2,1)S(1)} %collective-permute-done.2.refs_1_), channel_id=1, source_target_pairs={{0,1},{1,2},{2,3},{3,4},{4,5},{5,6},{6,7},{7,0},{8,9},{9,10},{10,1... | collective-permute-start | bytes 786440 | tf_op jit(solution)/shard_map/ppermute | solution.py:24
  34.1 8.2 %collective-permute-start.5 = (bf16[2,512,128]{2,1,0:T(8,128)(2,1)S(1)}, bf16[2,512,128]{2,1,0:T(8,128)(2,1)S(1)}, u32[]{:S(2)}, u32[]{:S(2)}) collective-permute-start(bf16[2,512,128]{2,1,0:T(8,128)(2,1)S(1)} %collective-permute-done.3.refs_2_), channel_id=1, source_target_pairs={{0,7},{1,0},{2,1},{3,2},{4,3},{5,4},{6,5},{7,6},{8,15},{9,8},{10,9... | collective-permute-start | bytes 786440 | tf_op jit(solution)/shard_map/ppermute | solution.py:24
  42.4 35.0 %copy-start.14 = (bf16[2,512,128]{2,1,0:T(8,128)(2,1)}, bf16[2,512,128]{2,1,0:T(8,128)(2,1)S(1)}, u32[]{:S(2)}) copy-start(bf16[2,512,128]{2,1,0:T(8,128)(2,1)S(1)} %collective-permute-done.4.refs_3_) | copy-start | bytes 786436
  42.4 35.0 %copy-start.15 = (bf16[2,512,128]{2,1,0:T(8,128)(2,1)}, bf16[2,512,128]{2,1,0:T(8,128)(2,1)S(1)}, u32[]{:S(2)}) copy-start(bf16[2,512,128]{2,1,0:T(8,128)(2,1)S(1)} %collective-permute-done.5.refs_4_) | copy-start | bytes 786436
  47.4 14.3 %collective-permute-start.10 = (bf16[4,1024,256]{2,1,0:T(8,128)(2,1)}, bf16[4,1024,256]{2,1,0:T(8,128)(2,1)}, u32[]{:S(2)}, u32[]{:S(2)}) collective-permute-start(bf16[4,1024,256]{2,1,0:T(8,128)(2,1)} %all-to-all-done.refs_8_), channel_id=1, source_target_pairs={{0,64},{64,0},{1,65},{65,1},{2,66},{66,2},{3,67},{67,3},{4,68},{68... | collective-permute-start | bytes 6291464 | tf_op jit(solution)/shard_map/ppermute | solution.py:24
  47.5 38.8 %collective-permute-start.6 = (bf16[2048,256]{1,0:T(8,128)(2,1)}, bf16[2048,256]{1,0:T(8,128)(2,1)S(1)}, u32[]{:S(2)}, u32[]{:S(2)}) collective-permute-start(bf16[2048,256]{1,0:T(8,128)(2,1)} %get-tuple-element.39), channel_id=1, source_target_pairs={{0,16},{16,32},{32,48},{48,0},{64,112},{80,64},{96,80},{112,96},{1... | collective-permute-start | bytes 3145736 | tf_op jit(solution)/shard_map/ppermute | solution.py:248
  48.3 13.0 %collective-permute-start.8 = (bf16[2,512,128]{2,1,0:T(8,128)(2,1)S(1)}, bf16[2,512,128]{2,1,0:T(8,128)(2,1)S(1)}, u32[]{:S(2)}, u32[]{:S(2)}) collective-permute-start(bf16[2,512,128]{2,1,0:T(8,128)(2,1)S(1)} %collective-permute-done.4.refs_3_), channel_id=1, source_target_pairs={{0,1},{1,2},{2,3},{3,4},{4,5},{5,6},{6,7},{7,0},{8,9},{9,10},{10,1... | collective-permute-start | bytes 786440 | tf_op jit(solution)/shard_map/ppermute | solution.py:24
  50.2 11.6 %collective-permute-start.9 = (bf16[2,512,128]{2,1,0:T(8,128)(2,1)S(1)}, bf16[2,512,128]{2,1,0:T(8,128)(2,1)S(1)}, u32[]{:S(2)}, u32[]{:S(2)}) collective-permute-start(bf16[2,512,128]{2,1,0:T(8,128)(2,1)S(1)} %collective-permute-done.5.refs_4_), channel_id=1, source_target_pairs={{0,7},{1,0},{2,1},{3,2},{4,3},{5,4},{6,5},{7,6},{8,15},{9,8},{10,9... | collective-permute-start | bytes 786440 | tf_op jit(solution)/shard_map/ppermute | solution.py:24
  54.1 31.4 %collective-permute-start.7 = (bf16[1024,256]{1,0:T(8,128)(2,1)}, bf16[1024,256]{1,0:T(8,128)(2,1)S(1)}, u32[]{:S(2)}, u32[]{:S(2)}) collective-permute-start(bf16[1024,256]{1,0:T(8,128)(2,1)} %get-tuple-element.40), channel_id=1, source_target_pairs={{0,32},{16,48},{32,0},{48,16},{1,33},{17,49},{33,1},{49,17},{2,34}... | collective-permute-start | bytes 1572872 | tf_op jit(solution)/shard_map/ppermute | solution.py:24
  61.3 16.1 %copy-start.16 = (bf16[2,512,128]{2,1,0:T(8,128)(2,1)}, bf16[2,512,128]{2,1,0:T(8,128)(2,1)S(1)}, u32[]{:S(2)}) copy-start(bf16[2,512,128]{2,1,0:T(8,128)(2,1)S(1)} %collective-permute-done.8.refs_5_) | copy-start | bytes 786436
  61.7 15.6 %copy-start.17 = (bf16[2,512,128]{2,1,0:T(8,128)(2,1)}, bf16[2,512,128]{2,1,0:T(8,128)(2,1)S(1)}, u32[]{:S(2)}) copy-start(bf16[2,512,128]{2,1,0:T(8,128)(2,1)S(1)} %collective-permute-done.9.refs_6_) | copy-start | bytes 786436
  61.8 15.6 %collective-permute-start.11 = (bf16[2,512,128]{2,1,0:T(8,128)(2,1)S(1)}, bf16[2,512,128]{2,1,0:T(8,128)(2,1)S(1)}, u32[]{:S(2)}, u32[]{:S(2)}) collective-permute-start(bf16[2,512,128]{2,1,0:T(8,128)(2,1)S(1)} %collective-permute-done.8.refs_5_), channel_id=1, source_target_pairs={{0,1},{1,2},{2,3},{3,4},{4,5},{5,6},{6,7},{7,0},{8,9},{9,10},{10,1... | collective-permute-start | bytes 786440 | tf_op jit(solution)/shard_map/ppermute | solution.py:24
  77.4 0.7 copy-start.18
  85.5 9.5 %copy-start.1 = (s32[5]{0:T(128)S(1)}, s32[5]{0:T(128)}, u32[]{:S(2)}) copy-start(s32[5]{0:T(128)} %stack.41.at_ref) | copy-start | bytes 64
  85.5 9.5 %copy-start.2 = (bf16[2048,256]{1,0:T(8,128)(2,1)S(1)}, bf16[2048,256]{1,0:T(8,128)(2,1)}, u32[]{:S(2)}) copy-start(bf16[2048,256]{1,0:T(8,128)(2,1)} %get-tuple-element.50.refs_0_) | copy-start | bytes 3145732
  85.5 0.8 copy-start.5
  86.3 7.7 %collective-permute-start.12 = (bf16[2048,256]{1,0:T(8,128)(2,1)S(1)}, bf16[2048,256]{1,0:T(8,128)(2,1)S(1)}, u32[]{:S(2)}, u32[]{:S(2)}) collective-permute-start(bf16[2048,256]{1,0:T(8,128)(2,1)S(1)} %collective-permute-done.6.refs_1_), channel_id=1, source_target_pairs={{0,64},{64,0},{1,65},{65,1},{2,66},{66,2},{3,67},{67,3},{4,68},{68... | collective-permute-start | bytes 3145736 | tf_op jit(solution)/shard_map/ppermute | solution.py:24
  86.3 19.0 %all-to-all-start.1 = ((f32[16,32,512]{2,1,0:T(8,128)}), f32[16,32,512]{2,1,0:T(8,128)}, u32[]{:S(2)}, u32[]{:S(2)}) async-start(f32[16,32,512]{2,1,0:T(8,128)} %bitcast.22), calls=%async_computation.1 | async-start | bytes 2097152 | tf_op jit(solution)/shard_map/all_to_all | solution.py:277
  90.6 63.3 %all-gather.7.cloned.1.call-start = ((), (), s32[]{:S(2)}) async-start(), calls=%async_computation.6 | async-start | bytes 2359296 | tf_op jit(solution)/shard_map/all_gather | solution.py:283
  90.7 2.5 %collective-permute-start.13 = (bf16[1024,256]{1,0:T(8,128)(2,1)}, bf16[1024,256]{1,0:T(8,128)(2,1)S(1)}, u32[]{:S(2)}, u32[]{:S(2)}) collective-permute-start(bf16[1024,256]{1,0:T(8,128)(2,1)} %copy-done.5), channel_id=1, source_target_pairs={{0,64},{64,0},{1,65},{65,1},{2,66},{66,2},{3,67},{67,3},{4,68},{68... | collective-permute-start | bytes 1572872 | tf_op jit(solution)/shard_map/ppermute | solution.py:24
  93.2 0.8 copy-start.7
  94.0 1.0 copy-start.3
  95.0 1.2 copy-start.4
  96.3 1.0 copy-start.6
  97.3 1.0 copy-start.8
  106.7 6.9 %collective-permute-start.14 = (bf16[1,4,32,512]{3,2,1,0:T(8,128)(2,1)S(1)}, bf16[1,4,32,512]{3,2,1,0:T(8,128)(2,1)S(1)}, u32[]{:S(2)}, u32[]{:S(2)}) collective-permute-start(bf16[1,4,32,512]{3,2,1,0:T(8,128)(2,1)S(1)} %bitcast.23), channel_id=1, source_target_pairs={{0,8},{8,0},{1,9},{9,1},{2,10},{10,2},{3,11},{11,3},{4,12},{12,4},... | collective-permute-start | bytes 393224 | tf_op jit(solution)/shard_map/ppermute | solution.py:24
  149.0 2.7 %collective-permute-start.15 = (bf16[2,4,128,512]{3,2,1,0:T(8,128)(2,1)S(1)}, bf16[2,4,128,512]{3,2,1,0:T(8,128)(2,1)S(1)}, u32[]{:S(2)}, u32[]{:S(2)}) collective-permute-start(bf16[2,4,128,512]{3,2,1,0:T(8,128)(2,1)S(1)} %bitcast.19), channel_id=1, source_target_pairs={{0,64},{64,0},{1,65},{65,1},{2,66},{66,2},{3,67},{67,3},{4,68},{68... | collective-permute-start | bytes 3145736 | tf_op jit(solution)/shard_map/ppermute | solution.py:24
  153.9 1.6 copy-start
Sparse Core Ops, SparseCore 0:
  47.6 45.2 all-gather.4
  114.5 39.3 all-gather.6

commit v15 on v12

--- a/solution.py
+++ b/solution.py
@@ -257,12 +257,14 @@
         [y * 2, y * 2 + 1, near_y * 2, near_y * 2 + 1, far_y * 2 + c]
     ).astype(jnp.int32)
 
-    a0, grads_pair, mine_in, basis_out = sync(
-        pair(activations), pair(gradients), split_basis(half, basis_in), basis_out
+    a0, gradients, mine_in, basis_out = sync(
+        pair(activations), gradients, split_basis(half, basis_in), basis_out
     )
     own_in = lax.all_to_all(mine_in, "y", 0, 0)
     own_out, near_out, far_out = reach_basis(rows, basis_out)
-    up1, down1, near_out, far_out = sync(*ring_step(a0, a0), near_out, far_out)
+    up1, down1, grads_pair, near_out, far_out = sync(
+        *ring_step(a0, a0), pair(gradients), near_out, far_out
+    )
     up2, down2, near_out, far_out = sync(*ring_step(up1, down1), near_out, far_out)
     near_out = shift_near(near_out)
     up3, down3, own_in, far_out = sync(*ring_step(up2, down2), own_in, far_out)

time: 175 us -> 174 us (level)
    all_gather x1, waiting for transfers between devices: 3.54 us -> 1.62 us  [body(): grad_blocks = lax.all_gather(after(grads_pair, up2), 'z')]
where the time goes in v15:
time: 174 us; the launch traced here: 173 us
  blocking collectives  46.1 us (26%)
  waiting for transfers between devices  41.7 us (24%)
  starting transfers between devices  35.1 us (20%)
  Pallas kernels  28.2 us (16%)
  between operations  13.6 us (8%)
  local copies, waits for them, and re-layouts  5.83 us (3%)
  other arithmetic  2.91 us (2%)
    ppermute x15, waiting for transfers between devices, shift(): return lax.ppermute(x, axis, [(i, (i + by) % n) for i in range(n)])  33.1 us
    ppermute x15, starting transfers between devices, shift(): return lax.ppermute(x, axis, [(i, (i + by) % n) for i in range(n)])  22.9 us
    all_to_all x1, blocking collectives, body(): grads_in = lax.all_to_all(grads_part, 'y', 0, 0)  17.4 us
    all_to_all x1, blocking collectives, body(): rot_own = lax.all_to_all(copies, ('xl', 'y'), 0, 0).reshape(2, 4, COLS, TOK)  16.6 us
    all_to_all x1, blocking collectives, body(): return weave(lax.all_to_all(part, 'y', 0, 0))  12.2 us
    pallas_call x1, Pallas kernels, rotate_ring(): pl.pallas_call(functools.partial(rotate_ring_kernel, [offset for _, offse...  7.44 us
    pallas_call x1, Pallas kernels, reach_basis(): pl.pallas_call(reach_kernel, grid_spec=pltpu.PrefetchScalarGridSpec(num_s...  5.83 us
    all_to_all x1, starting transfers between devices, body(): lax.all_to_all(acts_part.reshape(16, 32, TOK), ('xl', 'c', 'y'), 0, 0)  5.55 us
  transfers between devices with their start and end apart: 20, of which 11 were waited for; matrix products, arithmetic and copies ran while one was open for 1% of the time, Pallas kernels for 13%

profile of v15, /device:TPU:2, one launch (start us, length us, event | category | flops | bytes accessed | tf_op | source)
XLA Modules:
  0.0 173.5 jit_solution(3008397471230179415)
XLA Ops:
  6.5 2.1 %collective-permute-start = (bf16[1,512,128]{2,1,0:T(8,128)(2,1)}, bf16[1,512,128]{2,1,0:T(8,128)(2,1)S(1)}, u32[]{:S(2)}, u32[]{:S(2)}) collective-permute-start(bf16[1,512,128]{2,1,0:T(8,128)(2,1)} %param.4), channel_id=1, source_target_pairs={{0,8},{8,0},{1,9},{9,1},{2,10},{10,2},{3,11},{11,3},{4,12},{12,4},... | collective-permute-start | bytes 393224 | tf_op jit(solution)/shard_map/ppermute | solution.py:24
  8.7 4.0 %shard_map.46 = bf16[4,1024,256]{2,1,0:T(8,128)(2,1)} custom-call(s32[1]{0:T(128)} %bitcast.4.half_ref, f32[8192,128]{1,0:T(8,128)} %in_ref.1), custom_call_target="tpu_custom_call" | custom-call | flops 1048576 | bytes 4194304 | tf_op jit(solution)/shard_map/pallas_call | solution.py:44
  12.7 0.8 collective-permute-done
  13.5 0.0 copy-start.8
  13.5 4.6 %all-to-all-start = ((bf16[4,1024,256]{2,1,0:T(8,128)(2,1)}), bf16[4,1024,256]{2,1,0:T(8,128)(2,1)S(1)}, u32[]{:S(2)}, u32[]{:S(2)}) async-start(bf16[4,1024,256]{2,1,0:T(8,128)(2,1)} %shard_map.46), calls=%async_computation | async-start | bytes 4194304 | tf_op jit(solution)/shard_map/all_to_all | solution.py:263
  18.1 0.0 all-gather.5.cloned.1.call-start
  18.2 1.9 %collective-permute-start.1 = (bf16[2,512,128]{2,1,0:T(8,128)(2,1)S(1)}, bf16[2,512,128]{2,1,0:T(8,128)(2,1)S(1)}, u32[]{:S(2)}, u32[]{:S(2)}) collective-permute-start(bf16[2,512,128]{2,1,0:T(8,128)(2,1)S(1)} %pad_maximum_fusion.refs_0_), channel_id=1, source_target_pairs={{0,1},{1,2},{2,3},{3,4},{4,5},{5,6},{6,7},{7,0},{8,9},{9,10},{10,1... | collective-permute-start | bytes 786440 | tf_op jit(solution)/shard_map/ppermute | solution.py:24
  20.1 4.0 %collective-permute-start.2 = (bf16[2,512,128]{2,1,0:T(8,128)(2,1)S(1)}, bf16[2,512,128]{2,1,0:T(8,128)(2,1)S(1)}, u32[]{:S(2)}, u32[]{:S(2)}) collective-permute-start(bf16[2,512,128]{2,1,0:T(8,128)(2,1)S(1)} %pad_maximum_fusion.refs_0_), channel_id=1, source_target_pairs={{0,7},{1,0},{2,1},{3,2},{4,3},{5,4},{6,5},{7,6},{8,15},{9,8},{10,9... | collective-permute-start | bytes 786440 | tf_op jit(solution)/shard_map/ppermute | solution.py:24
  24.1 0.0 copy-done.8
  24.1 2.1 %collective-permute-start.3 = (bf16[1,512,128]{2,1,0:T(8,128)(2,1)S(1)}, bf16[1,512,128]{2,1,0:T(8,128)(2,1)S(1)}, u32[]{:S(2)}, u32[]{:S(2)}) collective-permute-start(bf16[1,512,128]{2,1,0:T(8,128)(2,1)S(1)} %copy-done.8), channel_id=1, source_target_pairs={{0,8},{8,0},{1,9},{9,1},{2,10},{10,2},{3,11},{11,3},{4,12},{12,4},... | collective-permute-start | bytes 393224 | tf_op jit(solution)/shard_map/ppermute | solution.py:24
  26.2 0.7 stack.47.rows_ref
  26.9 5.8 %shard_map.47 = (bf16[2048,256]{1,0:T(8,128)(2,1)}, bf16[2048,256]{1,0:T(8,128)(2,1)}, bf16[1024,256]{1,0:T(8,128)(2,1)}) custom-call(s32[5]{0:T(128)} %stack.47.rows_ref, f32[8192,128]{1,0:T(8,128)} %in_ref.2), custom_call_target="tpu_custom_call" | custom-call | flops 1048576 | bytes 5242880 | tf_op jit(solution)/shard_map/pallas_call | solution.py:117
  32.7 0.0 collective-permute-done.3
  32.7 0.7 pad_maximum_fusion.1
  33.4 0.0 collective-permute-done.1.refs_1_
  33.5 0.0 collective-permute-done.2.refs_2_
  33.5 0.1 collective-permute-start.4
  33.6 3.2 %collective-permute-start.5 = (bf16[2,512,128]{2,1,0:T(8,128)(2,1)S(1)}, bf16[2,512,128]{2,1,0:T(8,128)(2,1)S(1)}, u32[]{:S(2)}, u32[]{:S(2)}) collective-permute-start(bf16[2,512,128]{2,1,0:T(8,128)(2,1)S(1)} %collective-permute-done.2.refs_2_), channel_id=1, source_target_pairs={{0,7},{1,0},{2,1},{3,2},{4,3},{5,4},{6,5},{7,6},{8,15},{9,8},{10,9... | collective-permute-start | bytes 786440 | tf_op jit(solution)/shard_map/ppermute | solution.py:24
  36.8 4.3 %collective-permute-done.4.refs_3_ = bf16[2,512,128]{2,1,0:T(8,128)(2,1)S(1)} collective-permute-done((bf16[2,512,128]{2,1,0:T(8,128)(2,1)S(1)}, bf16[2,512,128]{2,1,0:T(8,128)(2,1)S(1)}, u32[]{:S(2)}, u32[]{:S(2)}) %collective-permute-start.4) | collective-permute-done | bytes 262176 | tf_op jit(solution)/shard_map/ppermute | solution.py:24
  41.1 0.0 collective-permute-done.5.refs_4_
  41.1 0.0 all-gather.5.cloned.1.call-update
  41.2 0.1 collective-permute-start.7
  41.3 3.3 %collective-permute-start.8 = (bf16[2,512,128]{2,1,0:T(8,128)(2,1)S(1)}, bf16[2,512,128]{2,1,0:T(8,128)(2,1)}, u32[]{:S(2)}, u32[]{:S(2)}) collective-permute-start(bf16[2,512,128]{2,1,0:T(8,128)(2,1)S(1)} %collective-permute-done.5.refs_4_), channel_id=1, source_target_pairs={{0,7},{1,0},{2,1},{3,2},{4,3},{5,4},{6,5},{7,6},{8,15},{9,8},{10,9... | collective-permute-start | bytes 786440 | tf_op jit(solution)/shard_map/ppermute | solution.py:24
  44.6 4.3 %collective-permute-done.7.refs_5_ = bf16[2,512,128]{2,1,0:T(8,128)(2,1)S(1)} collective-permute-done((bf16[2,512,128]{2,1,0:T(8,128)(2,1)S(1)}, bf16[2,512,128]{2,1,0:T(8,128)(2,1)S(1)}, u32[]{:S(2)}, u32[]{:S(2)}) %collective-permute-start.7) | collective-permute-done | bytes 262176 | tf_op jit(solution)/shard_map/ppermute | solution.py:24
  48.8 0.0 collective-permute-done.8.refs_6_
  48.8 0.0 all-to-all-done.refs_8_
  48.9 0.6 copy-done.13
  49.5 0.0 collective-permute-start.11
  49.5 2.0 %collective-permute-start.6 = (bf16[2048,256]{1,0:T(8,128)(2,1)}, bf16[2048,256]{1,0:T(8,128)(2,1)S(1)}, u32[]{:S(2)}, u32[]{:S(2)}) collective-permute-start(bf16[2048,256]{1,0:T(8,128)(2,1)} %get-tuple-element.42), channel_id=1, source_target_pairs={{0,16},{16,32},{32,48},{48,0},{64,112},{80,64},{96,80},{112,96},{1... | collective-permute-start | bytes 3145736 | tf_op jit(solution)/shard_map/ppermute | solution.py:248
  51.5 2.7 %collective-permute-start.9 = (bf16[1024,256]{1,0:T(8,128)(2,1)}, bf16[1024,256]{1,0:T(8,128)(2,1)}, u32[]{:S(2)}, u32[]{:S(2)}) collective-permute-start(bf16[1024,256]{1,0:T(8,128)(2,1)} %get-tuple-element.47), channel_id=1, source_target_pairs={{0,32},{16,48},{32,0},{48,16},{1,33},{17,49},{33,1},{49,17},{2,34}... | collective-permute-start | bytes 1572872 | tf_op jit(solution)/shard_map/ppermute | solution.py:24
  54.2 2.6 %collective-permute-start.10 = (bf16[2,512,128]{2,1,0:T(8,128)(2,1)}, bf16[2,512,128]{2,1,0:T(8,128)(2,1)}, u32[]{:S(2)}, u32[]{:S(2)}) collective-permute-start(bf16[2,512,128]{2,1,0:T(8,128)(2,1)} %copy-done.13), channel_id=1, source_target_pairs={{0,1},{1,2},{2,3},{3,4},{4,5},{5,6},{6,7},{7,0},{8,9},{9,10},{10,1... | collective-permute-start | bytes 786440 | tf_op jit(solution)/shard_map/ppermute | solution.py:24
  56.8 0.6 stack.41.at_ref
  57.4 12.5 %collective-permute-done.10.refs_7_ = bf16[2,512,128]{2,1,0:T(8,128)(2,1)} collective-permute-done((bf16[2,512,128]{2,1,0:T(8,128)(2,1)}, bf16[2,512,128]{2,1,0:T(8,128)(2,1)}, u32[]{:S(2)}, u32[]{:S(2)}) %collective-permute-start.10) | collective-permute-done | bytes 262176 | tf_op jit(solution)/shard_map/ppermute | solution.py:24
  69.9 0.0 collective-permute-done.11.refs_9_
  69.9 7.4 %shard_map.48 = f32[4,128,512]{2,1,0:T(8,128)} custom-call(s32[5]{0:T(128)} %stack.41.at_ref, bf16[2,512,128]{2,1,0:T(8,128)(2,1)} %copy-done.6, bf16[2,512,128]{2,1,0:T(8,128)(2,1)} %copy-done.9, bf16[2,512,128]{2,1,0:T(8,128)(2,1)} %copy-done.10, bf16[2,512,128]{2,1,0:T(8,128)(2,1)} %copy-done.11, bf16[2,512,128]{2,1,0:T(8,128)(2,1)} %copy-done.12, ...), custom_call_target="tpu_custom_call" | custom-call | flops 2147483648 | bytes 7340032 | tf_op jit(solution)/shard_map/pallas_call | solution.py:87
  77.4 0.0 collective-permute-done.6.refs_1_
  77.4 1.2 collective-permute-done.9.refs_3_
  78.5 0.0 collective-permute-start.12
  78.5 5.5 %all-to-all-start.1 = ((f32[16,32,512]{2,1,0:T(8,128)}), f32[16,32,512]{2,1,0:T(8,128)}, u32[]{:S(2)}, u32[]{:S(2)}) async-start(f32[16,32,512]{2,1,0:T(8,128)} %bitcast.22), calls=%async_computation.1 | async-start | bytes 2097152 | tf_op jit(solution)/shard_map/all_to_all | solution.py:277
  84.1 0.0 all-gather.7.cloned.1.call-start
  84.1 0.4 collective-permute-start.13
  84.5 1.6 all-gather.5.cloned.1.call-done
  86.2 0.5 collective-permute-done.13.refs_4_
  86.6 0.0 collective-permute-done.12.refs_2_
  86.7 1.0 copy-done.3
  87.6 1.2 copy-done.4
  88.9 5.4 %shard_map.49 = f32[4,128,512]{2,1,0:T(8,128)S(1)} custom-call(s32[5]{0:T(128)S(1)} %copy-done.1, bf16[8,2,512,128]{3,2,1,0:T(8,128)(2,1)} %bitcast.25, bf16[2048,256]{1,0:T(8,128)(2,1)S(1)} %copy-done.2, bf16[2048,256]{1,0:T(8,128)(2,1)S(1)} %collective-permute-done.6.refs_1_, bf16[2048,256]{1,0:T(8,128)(2,1)S(1)} %copy-done.4, ...), custom_call_target="tpu_custom_call" | custom-call | flops 2147483648 | bytes 7340032 | tf_op jit(solution)/shard_map/pallas_call | solution.py:165
  94.3 5.0 %all-to-all-done.1 = f32[16,32,512]{2,1,0:T(8,128)} async-done(((f32[16,32,512]{2,1,0:T(8,128)}), f32[16,32,512]{2,1,0:T(8,128)}, u32[]{:S(2)}, u32[]{:S(2)}) %all-to-all-start.1) | async-done | bytes 1048608 | tf_op jit(solution)/shard_map/all_to_all | solution.py:277
  99.2 1.3 bitcast_reduce_fusion
  100.6 0.3 collective-permute-start.14
  100.9 6.9 %collective-permute-done.14 = bf16[1,4,32,512]{3,2,1,0:T(8,128)(2,1)S(1)} collective-permute-done((bf16[1,4,32,512]{3,2,1,0:T(8,128)(2,1)S(1)}, bf16[1,4,32,512]{3,2,1,0:T(8,128)(2,1)S(1)}, u32[]{:S(2)}, u32[]{:S(2)}) %collective-permute-start.14) | collective-permute-done | bytes 131104 | tf_op jit(solution)/shard_map/ppermute | solution.py:24
  107.8 0.7 pad_maximum_fusion.2
  108.5 0.0 all-gather.7.cloned.1.call-update
  108.6 17.4 %all_to_all.25 = f32[4,128,512]{2,1,0:T(8,128)S(1)} all-to-all(f32[4,128,512]{2,1,0:T(8,128)S(1)} %shard_map.49), channel_id=1, replica_groups=mesh['xl'=2,'c'=2,'y'=4,'xh'=2,'z'=8] {'y'}, dimensions={0} | all-to-all | bytes 2097152 | tf_op jit(solution)/shard_map/all_to_all | solution.py:285
  125.9 0.1 reduce_sum.19
  126.0 0.1 broadcast_in_dim.4
  126.1 16.6 %all_to_all.26 = bf16[8,128,512]{2,1,0:T(8,128)(2,1)S(1)} all-to-all(bf16[8,128,512]{2,1,0:T(8,128)(2,1)S(1)} %broadcast_in_dim.4), channel_id=1, replica_groups=mesh['xl'=2,'c'=2,'y'=4,'xh'=2,'z'=8] {'xl','y'}, dimensions={0} | all-to-all | bytes 2097152 | tf_op jit(solution)/shard_map/all_to_all | solution.py:288
  142.7 0.0 collective-permute-start.15
  142.7 2.7 %collective-permute-done.15.other_ref = bf16[2,4,128,512]{3,2,1,0:T(8,128)(2,1)S(1)} collective-permute-done((bf16[2,4,128,512]{3,2,1,0:T(8,128)(2,1)S(1)}, bf16[2,4,128,512]{3,2,1,0:T(8,128)(2,1)S(1)}, u32[]{:S(2)}, u32[]{:S(2)}) %collective-permute-start.15) | collective-permute-done | bytes 1048608 | tf_op jit(solution)/shard_map/ppermute | solution.py:24
  145.4 1.9 %all-gather.7.cloned.1.call-done = bf16[16,4,32,512]{3,2,1,0:T(8,128)(2,1)} async-done(((bf16[2,4,32,512]{3,2,1,0:T(8,128)(2,1)}), bf16[16,4,32,512]{3,2,1,0:T(8,128)(2,1)}) %all-gather.7.cloned.1.call-update) | async-done | bytes 2097168 | tf_op jit(solution)/shard_map/all_gather | solution.py:283
  147.3 1.6 copy-done
  148.9 3.5 %shard_map.50 = bf16[4,128,512]{2,1,0:T(8,128)(2,1)S(1)} custom-call(s32[5]{0:T(128)S(1)} %copy-done.1, bf16[8,2,4,32,512]{4,3,2,1,0:T(8,128)(2,1)S(1)} %bitcast.21, bf16[2,4,128,512]{3,2,1,0:T(8,128)(2,1)S(1)} %bitcast.20, bf16[2,4,128,512]{3,2,1,0:T(8,128)(2,1)S(1)} %collective-permute-done.15.other_ref), custom_call_target="tpu_custom_call" | custom-call | flops 1073741824 | bytes 5242880 | tf_op jit(solution)/shard_map/pallas_call | solution.py:201
  152.4 12.2 %all_to_all.27.in_ref = bf16[4,128,512]{2,1,0:T(8,128)(2,1)S(1)} all-to-all(bf16[4,128,512]{2,1,0:T(8,128)(2,1)S(1)} %shard_map.50), channel_id=1, replica_groups=mesh['xl'=2,'c'=2,'y'=4,'xh'=2,'z'=8] {'y'}, dimensions={0} | all-to-all | bytes 1048576 | tf_op jit(solution)/shard_map/all_to_all | solution.py:292
  164.6 2.0 %shard_map.51 = f32[128,2048]{1,0:T(8,128)} custom-call(bf16[4,128,512]{2,1,0:T(8,128)(2,1)S(1)} %all_to_all.27.in_ref), custom_call_target="tpu_custom_call" | custom-call | tf_op jit(solution)/shard_map/pallas_call | solution.py:224
  (23 shorter events, 0.1 us)
Async XLA Ops:
  6.5 7.0 %collective-permute-start = (bf16[1,512,128]{2,1,0:T(8,128)(2,1)}, bf16[1,512,128]{2,1,0:T(8,128)(2,1)S(1)}, u32[]{:S(2)}, u32[]{:S(2)}) collective-permute-start(bf16[1,512,128]{2,1,0:T(8,128)(2,1)} %param.4), channel_id=1, source_target_pairs={{0,8},{8,0},{1,9},{9,1},{2,10},{10,2},{3,11},{11,3},{4,12},{12,4},... | collective-permute-start | bytes 393224 | tf_op jit(solution)/shard_map/ppermute | solution.py:24
  8.7 4.8 %copy-start.7 = (bf16[1,512,128]{2,1,0:T(8,128)(2,1)S(1)}, bf16[1,512,128]{2,1,0:T(8,128)(2,1)}, u32[]{:S(2)}) copy-start(bf16[1,512,128]{2,1,0:T(8,128)(2,1)} %param.4) | copy-start | bytes 393220
  13.5 6.6 %copy-start.6 = (bf16[2,512,128]{2,1,0:T(8,128)(2,1)}, bf16[2,512,128]{2,1,0:T(8,128)(2,1)S(1)}, u32[]{:S(2)}) copy-start(bf16[2,512,128]{2,1,0:T(8,128)(2,1)S(1)} %pad_maximum_fusion.refs_0_) | copy-start | bytes 786436
  13.5 10.6 %copy-start.8 = (bf16[1,512,128]{2,1,0:T(8,128)(2,1)S(1)}, bf16[1,512,128]{2,1,0:T(8,128)(2,1)}, u32[]{:S(2)}) copy-start(bf16[1,512,128]{2,1,0:T(8,128)(2,1)} %param.5) | copy-start | bytes 393220
  13.5 35.3 %all-to-all-start = ((bf16[4,1024,256]{2,1,0:T(8,128)(2,1)}), bf16[4,1024,256]{2,1,0:T(8,128)(2,1)S(1)}, u32[]{:S(2)}, u32[]{:S(2)}) async-start(bf16[4,1024,256]{2,1,0:T(8,128)(2,1)} %shard_map.46), calls=%async_computation | async-start | bytes 4194304 | tf_op jit(solution)/shard_map/all_to_all | solution.py:263
  18.1 68.0 %all-gather.5.cloned.1.call-start = ((), (), s32[]{:S(2)}) async-start(), calls=%async_computation.5 | async-start | bytes 2359296 | tf_op jit(solution)/shard_map/all_gather | solution.py:271
  18.2 15.3 %collective-permute-start.1 = (bf16[2,512,128]{2,1,0:T(8,128)(2,1)S(1)}, bf16[2,512,128]{2,1,0:T(8,128)(2,1)S(1)}, u32[]{:S(2)}, u32[]{:S(2)}) collective-permute-start(bf16[2,512,128]{2,1,0:T(8,128)(2,1)S(1)} %pad_maximum_fusion.refs_0_), channel_id=1, source_target_pairs={{0,1},{1,2},{2,3},{3,4},{4,5},{5,6},{6,7},{7,0},{8,9},{9,10},{10,1... | collective-permute-start | bytes 786440 | tf_op jit(solution)/shard_map/ppermute | solution.py:24
  20.1 13.4 %collective-permute-start.2 = (bf16[2,512,128]{2,1,0:T(8,128)(2,1)S(1)}, bf16[2,512,128]{2,1,0:T(8,128)(2,1)S(1)}, u32[]{:S(2)}, u32[]{:S(2)}) collective-permute-start(bf16[2,512,128]{2,1,0:T(8,128)(2,1)S(1)} %pad_maximum_fusion.refs_0_), channel_id=1, source_target_pairs={{0,7},{1,0},{2,1},{3,2},{4,3},{5,4},{6,5},{7,6},{8,15},{9,8},{10,9... | collective-permute-start | bytes 786440 | tf_op jit(solution)/shard_map/ppermute | solution.py:24
  24.1 8.6 %collective-permute-start.3 = (bf16[1,512,128]{2,1,0:T(8,128)(2,1)S(1)}, bf16[1,512,128]{2,1,0:T(8,128)(2,1)S(1)}, u32[]{:S(2)}, u32[]{:S(2)}) collective-permute-start(bf16[1,512,128]{2,1,0:T(8,128)(2,1)S(1)} %copy-done.8), channel_id=1, source_target_pairs={{0,8},{8,0},{1,9},{9,1},{2,10},{10,2},{3,11},{11,3},{4,12},{12,4},... | collective-permute-start | bytes 393224 | tf_op jit(solution)/shard_map/ppermute | solution.py:24
  33.4 15.4 %copy-start.9 = (bf16[2,512,128]{2,1,0:T(8,128)(2,1)}, bf16[2,512,128]{2,1,0:T(8,128)(2,1)S(1)}, u32[]{:S(2)}) copy-start(bf16[2,512,128]{2,1,0:T(8,128)(2,1)S(1)} %collective-permute-done.1.refs_1_) | copy-start | bytes 786436
  33.5 15.4 %copy-start.10 = (bf16[2,512,128]{2,1,0:T(8,128)(2,1)}, bf16[2,512,128]{2,1,0:T(8,128)(2,1)S(1)}, u32[]{:S(2)}) copy-start(bf16[2,512,128]{2,1,0:T(8,128)(2,1)S(1)} %collective-permute-done.2.refs_2_) | copy-start | bytes 786436
  33.5 7.7 %collective-permute-start.4 = (bf16[2,512,128]{2,1,0:T(8,128)(2,1)S(1)}, bf16[2,512,128]{2,1,0:T(8,128)(2,1)S(1)}, u32[]{:S(2)}, u32[]{:S(2)}) collective-permute-start(bf16[2,512,128]{2,1,0:T(8,128)(2,1)S(1)} %collective-permute-done.1.refs_1_), channel_id=1, source_target_pairs={{0,1},{1,2},{2,3},{3,4},{4,5},{5,6},{6,7},{7,0},{8,9},{9,10},{10,1... | collective-permute-start | bytes 786440 | tf_op jit(solution)/shard_map/ppermute | solution.py:24
  33.6 7.6 %collective-permute-start.5 = (bf16[2,512,128]{2,1,0:T(8,128)(2,1)S(1)}, bf16[2,512,128]{2,1,0:T(8,128)(2,1)S(1)}, u32[]{:S(2)}, u32[]{:S(2)}) collective-permute-start(bf16[2,512,128]{2,1,0:T(8,128)(2,1)S(1)} %collective-permute-done.2.refs_2_), channel_id=1, source_target_pairs={{0,7},{1,0},{2,1},{3,2},{4,3},{5,4},{6,5},{7,6},{8,15},{9,8},{10,9... | collective-permute-start | bytes 786440 | tf_op jit(solution)/shard_map/ppermute | solution.py:24
  41.1 28.8 %copy-start.11 = (bf16[2,512,128]{2,1,0:T(8,128)(2,1)}, bf16[2,512,128]{2,1,0:T(8,128)(2,1)S(1)}, u32[]{:S(2)}) copy-start(bf16[2,512,128]{2,1,0:T(8,128)(2,1)S(1)} %collective-permute-done.4.refs_3_) | copy-start | bytes 786436
  41.1 7.7 %copy-start.12 = (bf16[2,512,128]{2,1,0:T(8,128)(2,1)}, bf16[2,512,128]{2,1,0:T(8,128)(2,1)S(1)}, u32[]{:S(2)}) copy-start(bf16[2,512,128]{2,1,0:T(8,128)(2,1)S(1)} %collective-permute-done.5.refs_4_) | copy-start | bytes 786436
  41.2 7.7 %collective-permute-start.7 = (bf16[2,512,128]{2,1,0:T(8,128)(2,1)S(1)}, bf16[2,512,128]{2,1,0:T(8,128)(2,1)S(1)}, u32[]{:S(2)}, u32[]{:S(2)}) collective-permute-start(bf16[2,512,128]{2,1,0:T(8,128)(2,1)S(1)} %collective-permute-done.4.refs_3_), channel_id=1, source_target_pairs={{0,1},{1,2},{2,3},{3,4},{4,5},{5,6},{6,7},{7,0},{8,9},{9,10},{10,1... | collective-permute-start | bytes 786440 | tf_op jit(solution)/shard_map/ppermute | solution.py:24
  41.3 7.6 %collective-permute-start.8 = (bf16[2,512,128]{2,1,0:T(8,128)(2,1)S(1)}, bf16[2,512,128]{2,1,0:T(8,128)(2,1)}, u32[]{:S(2)}, u32[]{:S(2)}) collective-permute-start(bf16[2,512,128]{2,1,0:T(8,128)(2,1)S(1)} %collective-permute-done.5.refs_4_), channel_id=1, source_target_pairs={{0,7},{1,0},{2,1},{3,2},{4,3},{5,4},{6,5},{7,6},{8,15},{9,8},{10,9... | collective-permute-start | bytes 786440 | tf_op jit(solution)/shard_map/ppermute | solution.py:24
  48.8 0.7 copy-start.13
  49.5 20.4 %copy-start.5 = (bf16[4,1024,256]{2,1,0:T(8,128)(2,1)}, bf16[4,1024,256]{2,1,0:T(8,128)(2,1)S(1)}, u32[]{:S(2)}) copy-start(bf16[4,1024,256]{2,1,0:T(8,128)(2,1)S(1)} %all-to-all-done.refs_8_) | copy-start | bytes 6291460
  49.5 20.4 %collective-permute-start.11 = (bf16[4,1024,256]{2,1,0:T(8,128)(2,1)S(1)}, bf16[4,1024,256]{2,1,0:T(8,128)(2,1)}, u32[]{:S(2)}, u32[]{:S(2)}) collective-permute-start(bf16[4,1024,256]{2,1,0:T(8,128)(2,1)S(1)} %all-to-all-done.refs_8_), channel_id=1, source_target_pairs={{0,64},{64,0},{1,65},{65,1},{2,66},{66,2},{3,67},{67,3},{4,68},{68... | collective-permute-start | bytes 6291464 | tf_op jit(solution)/shard_map/ppermute | solution.py:24
  49.5 27.8 %collective-permute-start.6 = (bf16[2048,256]{1,0:T(8,128)(2,1)}, bf16[2048,256]{1,0:T(8,128)(2,1)S(1)}, u32[]{:S(2)}, u32[]{:S(2)}) collective-permute-start(bf16[2048,256]{1,0:T(8,128)(2,1)} %get-tuple-element.42), channel_id=1, source_target_pairs={{0,16},{16,32},{32,48},{48,0},{64,112},{80,64},{96,80},{112,96},{1... | collective-permute-start | bytes 3145736 | tf_op jit(solution)/shard_map/ppermute | solution.py:248
  51.5 27.0 %collective-permute-start.9 = (bf16[1024,256]{1,0:T(8,128)(2,1)}, bf16[1024,256]{1,0:T(8,128)(2,1)}, u32[]{:S(2)}, u32[]{:S(2)}) collective-permute-start(bf16[1024,256]{1,0:T(8,128)(2,1)} %get-tuple-element.47), channel_id=1, source_target_pairs={{0,32},{16,48},{32,0},{48,16},{1,33},{17,49},{33,1},{49,17},{2,34}... | collective-permute-start | bytes 1572872 | tf_op jit(solution)/shard_map/ppermute | solution.py:24
  54.2 15.7 %collective-permute-start.10 = (bf16[2,512,128]{2,1,0:T(8,128)(2,1)}, bf16[2,512,128]{2,1,0:T(8,128)(2,1)}, u32[]{:S(2)}, u32[]{:S(2)}) collective-permute-start(bf16[2,512,128]{2,1,0:T(8,128)(2,1)} %copy-done.13), channel_id=1, source_target_pairs={{0,1},{1,2},{2,3},{3,4},{4,5},{5,6},{6,7},{7,0},{8,9},{9,10},{10,1... | collective-permute-start | bytes 786440 | tf_op jit(solution)/shard_map/ppermute | solution.py:24
  77.3 10.3 %copy-start.1 = (s32[5]{0:T(128)S(1)}, s32[5]{0:T(128)}, u32[]{:S(2)}) copy-start(s32[5]{0:T(128)} %stack.41.at_ref) | copy-start | bytes 64
  77.3 10.3 %copy-start.2 = (bf16[2048,256]{1,0:T(8,128)(2,1)S(1)}, bf16[2048,256]{1,0:T(8,128)(2,1)}, u32[]{:S(2)}) copy-start(bf16[2048,256]{1,0:T(8,128)(2,1)} %get-tuple-element.56.refs_0_) | copy-start | bytes 3145732
  78.5 8.1 %collective-permute-start.12 = (bf16[2048,256]{1,0:T(8,128)(2,1)S(1)}, bf16[2048,256]{1,0:T(8,128)(2,1)S(1)}, u32[]{:S(2)}, u32[]{:S(2)}) collective-permute-start(bf16[2048,256]{1,0:T(8,128)(2,1)S(1)} %collective-permute-done.6.refs_1_), channel_id=1, source_target_pairs={{0,64},{64,0},{1,65},{65,1},{2,66},{66,2},{3,67},{67,3},{4,68},{68... | collective-permute-start | bytes 3145736 | tf_op jit(solution)/shard_map/ppermute | solution.py:24
  78.5 20.7 %all-to-all-start.1 = ((f32[16,32,512]{2,1,0:T(8,128)}), f32[16,32,512]{2,1,0:T(8,128)}, u32[]{:S(2)}, u32[]{:S(2)}) async-start(f32[16,32,512]{2,1,0:T(8,128)} %bitcast.22), calls=%async_computation.1 | async-start | bytes 2097152 | tf_op jit(solution)/shard_map/all_to_all | solution.py:277
  84.1 63.2 %all-gather.7.cloned.1.call-start = ((), (), s32[]{:S(2)}) async-start(), calls=%async_computation.6 | async-start | bytes 2359296 | tf_op jit(solution)/shard_map/all_gather | solution.py:283
  84.1 2.5 %collective-permute-start.13 = (bf16[1024,256]{1,0:T(8,128)(2,1)}, bf16[1024,256]{1,0:T(8,128)(2,1)}, u32[]{:S(2)}, u32[]{:S(2)}) collective-permute-start(bf16[1024,256]{1,0:T(8,128)(2,1)} %collective-permute-done.9.refs_3_), channel_id=1, source_target_pairs={{0,64},{64,0},{1,65},{65,1},{2,66},{66,2},{3,67},{67,3},{4,68},{68... | collective-permute-start | bytes 1572872 | tf_op jit(solution)/shard_map/ppermute | solution.py:24
  86.6 1.0 copy-start.3
  87.6 1.2 copy-start.4
  100.6 7.2 %collective-permute-start.14 = (bf16[1,4,32,512]{3,2,1,0:T(8,128)(2,1)S(1)}, bf16[1,4,32,512]{3,2,1,0:T(8,128)(2,1)S(1)}, u32[]{:S(2)}, u32[]{:S(2)}) collective-permute-start(bf16[1,4,32,512]{3,2,1,0:T(8,128)(2,1)S(1)} %bitcast.23), channel_id=1, source_target_pairs={{0,8},{8,0},{1,9},{9,1},{2,10},{10,2},{3,11},{11,3},{4,12},{12,4},... | collective-permute-start | bytes 393224 | tf_op jit(solution)/shard_map/ppermute | solution.py:24
  142.7 2.7 %collective-permute-start.15 = (bf16[2,4,128,512]{3,2,1,0:T(8,128)(2,1)S(1)}, bf16[2,4,128,512]{3,2,1,0:T(8,128)(2,1)S(1)}, u32[]{:S(2)}, u32[]{:S(2)}) collective-permute-start(bf16[2,4,128,512]{3,2,1,0:T(8,128)(2,1)S(1)} %bitcast.19), channel_id=1, source_target_pairs={{0,64},{64,0},{1,65},{65,1},{2,66},{66,2},{3,67},{67,3},{4,68},{68... | collective-permute-start | bytes 3145736 | tf_op jit(solution)/shard_map/ppermute | solution.py:24
  147.3 1.6 copy-start
Sparse Core Ops, SparseCore 0:
  41.3 44.8 all-gather.4
  108.7 38.5 all-gather.6

commit v16 on v15

--- a/solution.py
+++ b/solution.py
@@ -100,38 +100,29 @@
     )(at, *[block for block, _ in ring], own, other)
 
 
-def reach_kernel(rows_ref, in_ref, own_ref, near_ref, far_ref):
-    def put(out_ref):
-        exact = in_ref[...]
-        high = exact.astype(BF16)
-        out_ref[:, :COLS] = high
-        out_ref[:, COLS:] = (exact - high.astype(F32)).astype(BF16)
-
-    step = pl.program_id(0)
-    pl.when(step < 2)(lambda: put(own_ref))
-    pl.when((step >= 2) & (step < 4))(lambda: put(near_ref))
-    pl.when(step == 4)(lambda: put(far_ref))
-
-
-def reach_basis(rows, basis):
-    return pl.pallas_call(
-        reach_kernel,
+def split_rows_kernel(rows_ref, in_ref, out_ref):
+    exact = in_ref[...]
+    high = exact.astype(BF16)
+    out_ref[:, :COLS] = high
+    out_ref[:, COLS:] = (exact - high.astype(F32)).astype(BF16)
+
+
+def split_rows(rows, basis):
+    count = len(rows)
+    return pl.pallas_call(
+        split_rows_kernel,
         grid_spec=pltpu.PrefetchScalarGridSpec(
             num_scalar_prefetch=1,
-            grid=(5,),
+            grid=(count,),
             in_specs=[pl.BlockSpec((1024, COLS), lambda g, rows: (rows[g], 0))],
-            out_specs=[
-                pl.BlockSpec((1024, 256), lambda g, rows: (jnp.minimum(g, 1), 0)),
-                pl.BlockSpec((1024, 256), lambda g, rows: (jnp.clip(g - 2, 0, 1), 0)),
-                pl.BlockSpec((1024, 256), lambda g, rows: (0, 0)),
-            ],
-        ),
-        out_shape=[jax.ShapeDtypeStruct((n, 256), BF16) for n in (2048, 2048, 1024)],
+            out_specs=pl.BlockSpec((1024, 256), lambda g, rows: (g, 0)),
+        ),
+        out_shape=jax.ShapeDtypeStruct((count * 1024, 256), BF16),
         compiler_params=ALL_VMEM,
         cost_estimate=pl.CostEstimate(
-            flops=1 << 20, bytes_accessed=5 << 20, transcendentals=0
-        ),
-    )(rows, basis)
+            flops=count << 18, bytes_accessed=count << 20, transcendentals=0
+        ),
+    )(jnp.stack(rows).astype(jnp.int32), basis)
 
 
 def rotate_kernel(at_ref, block_ref, *refs):
@@ -253,19 +244,20 @@
     at = jnp.stack([z, xh, y, xl, c]).astype(jnp.int32)
     half = c.astype(jnp.int32).reshape(1)
     near_y, far_y = (y + 1 + 2 * c) % 4, (y + 2) % 4
-    rows = jnp.stack(
-        [y * 2, y * 2 + 1, near_y * 2, near_y * 2 + 1, far_y * 2 + c]
-    ).astype(jnp.int32)
 
     a0, gradients, mine_in, basis_out = sync(
         pair(activations), gradients, split_basis(half, basis_in), basis_out
     )
     own_in = lax.all_to_all(mine_in, "y", 0, 0)
-    own_out, near_out, far_out = reach_basis(rows, basis_out)
-    up1, down1, grads_pair, near_out, far_out = sync(
-        *ring_step(a0, a0), pair(gradients), near_out, far_out
-    )
-    up2, down2, near_out, far_out = sync(*ring_step(up1, down1), near_out, far_out)
+    near_out = split_rows([near_y * 2, near_y * 2 + 1], basis_out)
+    up1, down1, grads_pair, near_out, basis_out = sync(
+        *ring_step(a0, a0), pair(gradients), near_out, basis_out
+    )
+    own_out = split_rows([y * 2, y * 2 + 1], basis_out)
+    far_out = split_rows([far_y * 2 + c], basis_out)
+    up2, down2, own_out, near_out, far_out = sync(
+        *ring_step(up1, down1), own_out, near_out, far_out
+    )
     near_out = shift_near(near_out)
     up3, down3, own_in, far_out = sync(*ring_step(up2, down2), own_in, far_out)
     grad_blocks = lax.all_gather(after(grads_pair, up2), "z")

time: 174 us -> 174 us (level)
  waiting for transfers between devices: 41.7 us -> 38.9 us
  Pallas kernels: 28.2 us -> 30.1 us
    ppermute x15, waiting for transfers between devices: 33.1 us -> 28.2 us  [shift(): return lax.ppermute(x, axis, [(i, (i + by) % n) for i in range(n)])]
    pallas_call x1 -> x3, Pallas kernels: 5.83 us -> 7.7 us  [split_rows(): pl.pallas_call(split_rows_kernel, grid_spec=pltpu.PrefetchScalarGridSpec(...]
    all_gather x1, waiting for transfers between devices: 1.92 us -> 3.66 us  [body(): rot_acts = lax.all_gather(pair(acts), 'z')]
    unnamed x28 -> x30, local copies, waits for them, and re-layouts: 4.49 us -> 4.6 us
  transfers between devices with their start and end apart: 20 -> 20, of which waited for: 11 -> 10; matrix products, arithmetic and copies ran while one was open for 1% -> 2% of each run, Pallas kernels for 13% -> 14%
where the time goes in v16:
time: 174 us; the launch traced here: 173 us
  blocking collectives  45.9 us (26%)
  waiting for transfers between devices  38.9 us (22%)
  starting transfers between devices  35.4 us (20%)
  Pallas kernels  30.1 us (17%)
  between operations  13.6 us (8%)
  local copies, waits for them, and re-layouts  5.29 us (3%)
  other arithmetic  4.16 us (2%)
    ppermute x15, waiting for transfers between devices, shift(): return lax.ppermute(x, axis, [(i, (i + by) % n) for i in range(n)])  28.2 us
    ppermute x15, starting transfers between devices, shift(): return lax.ppermute(x, axis, [(i, (i + by) % n) for i in range(n)])  24 us
    all_to_all x1, blocking collectives, body(): grads_in = lax.all_to_all(grads_part, 'y', 0, 0)  17.4 us
    all_to_all x1, blocking collectives, body(): rot_own = lax.all_to_all(copies, ('xl', 'y'), 0, 0).reshape(2, 4, COLS, TOK)  16.6 us
    all_to_all x1, blocking collectives, body(): return weave(lax.all_to_all(part, 'y', 0, 0))  11.9 us
    pallas_call x3, Pallas kernels, split_rows(): pl.pallas_call(split_rows_kernel, grid_spec=pltpu.PrefetchScalarGridSpec(...  7.7 us
    pallas_call x1, Pallas kernels, rotate_ring(): pl.pallas_call(functools.partial(rotate_ring_kernel, [offset for _, offse...  7.46 us
    pallas_call x1, Pallas kernels, rotate(): pl.pallas_call(rotate_kernel, out_shape=jax.ShapeDtypeStruct((4, COLS, TO...  5.41 us
  transfers between devices with their start and end apart: 20, of which 10 were waited for; matrix products, arithmetic and copies ran while one was open for 2% of the time, Pallas kernels for 14%

profile of v16, /device:TPU:2, one launch (start us, length us, event | category | flops | bytes accessed | tf_op | source)
XLA Modules:
  0.0 173.3 jit_solution(13609798577559715991)
XLA Ops:
  6.5 2.1 %collective-permute-start = (bf16[1,512,128]{2,1,0:T(8,128)(2,1)}, bf16[1,512,128]{2,1,0:T(8,128)(2,1)S(1)}, u32[]{:S(2)}, u32[]{:S(2)}) collective-permute-start(bf16[1,512,128]{2,1,0:T(8,128)(2,1)} %param.4), channel_id=1, source_target_pairs={{0,8},{8,0},{1,9},{9,1},{2,10},{10,2},{3,11},{11,3},{4,12},{12,4},... | collective-permute-start | bytes 393224 | tf_op jit(solution)/shard_map/ppermute | solution.py:24
  8.7 4.0 %shard_map.46 = bf16[4,1024,256]{2,1,0:T(8,128)(2,1)} custom-call(s32[1]{0:T(128)} %bitcast.4.half_ref, f32[8192,128]{1,0:T(8,128)} %in_ref.1), custom_call_target="tpu_custom_call" | custom-call | flops 1048576 | bytes 4194304 | tf_op jit(solution)/shard_map/pallas_call | solution.py:44
  12.7 0.8 collective-permute-done
  13.5 0.0 copy-start.8
  13.5 4.6 %all-to-all-start = ((bf16[4,1024,256]{2,1,0:T(8,128)(2,1)}), bf16[4,1024,256]{2,1,0:T(8,128)(2,1)S(1)}, u32[]{:S(2)}, u32[]{:S(2)}) async-start(bf16[4,1024,256]{2,1,0:T(8,128)(2,1)} %shard_map.46), calls=%async_computation | async-start | bytes 4194304 | tf_op jit(solution)/shard_map/all_to_all | solution.py:251
  18.2 1.9 %collective-permute-start.1 = (bf16[2,512,128]{2,1,0:T(8,128)(2,1)S(1)}, bf16[2,512,128]{2,1,0:T(8,128)(2,1)S(1)}, u32[]{:S(2)}, u32[]{:S(2)}) collective-permute-start(bf16[2,512,128]{2,1,0:T(8,128)(2,1)S(1)} %pad_maximum_fusion.refs_0_), channel_id=1, source_target_pairs={{0,1},{1,2},{2,3},{3,4},{4,5},{5,6},{6,7},{7,0},{8,9},{9,10},{10,1... | collective-permute-start | bytes 786440 | tf_op jit(solution)/shard_map/ppermute | solution.py:24
  20.1 4.0 %collective-permute-start.2 = (bf16[2,512,128]{2,1,0:T(8,128)(2,1)S(1)}, bf16[2,512,128]{2,1,0:T(8,128)(2,1)S(1)}, u32[]{:S(2)}, u32[]{:S(2)}) collective-permute-start(bf16[2,512,128]{2,1,0:T(8,128)(2,1)S(1)} %pad_maximum_fusion.refs_0_), channel_id=1, source_target_pairs={{0,7},{1,0},{2,1},{3,2},{4,3},{5,4},{6,5},{7,6},{8,15},{9,8},{10,9... | collective-permute-start | bytes 786440 | tf_op jit(solution)/shard_map/ppermute | solution.py:24
  24.1 2.1 %collective-permute-start.3 = (bf16[1,512,128]{2,1,0:T(8,128)(2,1)S(1)}, bf16[1,512,128]{2,1,0:T(8,128)(2,1)S(1)}, u32[]{:S(2)}, u32[]{:S(2)}) collective-permute-start(bf16[1,512,128]{2,1,0:T(8,128)(2,1)S(1)} %copy-done.8), channel_id=1, source_target_pairs={{0,8},{8,0},{1,9},{9,1},{2,10},{10,2},{3,11},{11,3},{4,12},{12,4},... | collective-permute-start | bytes 393224 | tf_op jit(solution)/shard_map/ppermute | solution.py:24
  26.2 0.6 pad_add_fusion.rows_ref
  26.8 2.8 %shard_map.47 = bf16[2048,256]{1,0:T(8,128)(2,1)} custom-call(s32[2]{0:T(128)} %pad_add_fusion.rows_ref, f32[8192,128]{1,0:T(8,128)} %in_ref.4), custom_call_target="tpu_custom_call" | custom-call | flops 524288 | bytes 2097152 | tf_op jit(solution)/shard_map/pallas_call | solution.py:112
  29.6 0.9 collective-permute-done.3
  30.6 0.7 pad_maximum_fusion.1
  31.3 0.0 collective-permute-done.1.refs_1_
  31.3 0.0 collective-permute-done.2.refs_2_
  31.3 0.1 collective-permute-start.4
  31.4 3.2 %collective-permute-start.5 = (bf16[2,512,128]{2,1,0:T(8,128)(2,1)S(1)}, bf16[2,512,128]{2,1,0:T(8,128)(2,1)S(1)}, u32[]{:S(2)}, u32[]{:S(2)}) collective-permute-start(bf16[2,512,128]{2,1,0:T(8,128)(2,1)S(1)} %collective-permute-done.2.refs_2_), channel_id=1, source_target_pairs={{0,7},{1,0},{2,1},{3,2},{4,3},{5,4},{6,5},{7,6},{8,15},{9,8},{10,9... | collective-permute-start | bytes 786440 | tf_op jit(solution)/shard_map/ppermute | solution.py:24
  34.6 0.6 pad_add_fusion.1.rows_ref
  35.3 2.0 %shard_map.49 = bf16[1024,256]{1,0:T(8,128)(2,1)} custom-call(s32[1]{0:T(128)} %bitcast.9.rows_ref, f32[8192,128]{1,0:T(8,128)} %in_ref.4), custom_call_target="tpu_custom_call" | custom-call | flops 262144 | bytes 1048576 | tf_op jit(solution)/shard_map/pallas_call | solution.py:112
  37.3 2.9 %shard_map.48.refs_0_ = bf16[2048,256]{1,0:T(8,128)(2,1)} custom-call(s32[2]{0:T(128)} %pad_add_fusion.1.rows_ref, f32[8192,128]{1,0:T(8,128)} %in_ref.4), custom_call_target="tpu_custom_call" | custom-call | flops 524288 | bytes 2097152 | tf_op jit(solution)/shard_map/pallas_call | solution.py:112
  40.2 0.0 collective-permute-done.4.refs_3_
  40.2 0.0 collective-permute-done.5.refs_4_
  40.2 0.0 all-gather.5.cloned.1.call-update
  40.2 0.1 collective-permute-start.7
  40.3 3.2 %collective-permute-start.8 = (bf16[2,512,128]{2,1,0:T(8,128)(2,1)S(1)}, bf16[2,512,128]{2,1,0:T(8,128)(2,1)S(1)}, u32[]{:S(2)}, u32[]{:S(2)}) collective-permute-start(bf16[2,512,128]{2,1,0:T(8,128)(2,1)S(1)} %collective-permute-done.5.refs_4_), channel_id=1, source_target_pairs={{0,7},{1,0},{2,1},{3,2},{4,3},{5,4},{6,5},{7,6},{8,15},{9,8},{10,9... | collective-permute-start | bytes 786440 | tf_op jit(solution)/shard_map/ppermute | solution.py:24
  43.6 4.3 %collective-permute-done.7.refs_5_ = bf16[2,512,128]{2,1,0:T(8,128)(2,1)S(1)} collective-permute-done((bf16[2,512,128]{2,1,0:T(8,128)(2,1)S(1)}, bf16[2,512,128]{2,1,0:T(8,128)(2,1)S(1)}, u32[]{:S(2)}, u32[]{:S(2)}) %collective-permute-start.7) | collective-permute-done | bytes 262176 | tf_op jit(solution)/shard_map/ppermute | solution.py:24
  47.9 0.0 collective-permute-done.8.refs_6_
  47.9 0.0 all-to-all-done.refs_8_
  47.9 0.7 copy-done.13
  48.6 0.1 copy-done.14
  48.7 0.0 collective-permute-start.11
  48.7 2.0 %collective-permute-start.6 = (bf16[2048,256]{1,0:T(8,128)(2,1)}, bf16[2048,256]{1,0:T(8,128)(2,1)S(1)}, u32[]{:S(2)}, u32[]{:S(2)}) collective-permute-start(bf16[2048,256]{1,0:T(8,128)(2,1)} %shard_map.47), channel_id=1, source_target_pairs={{0,16},{16,32},{32,48},{48,0},{64,112},{80,64},{96,80},{112,96},{1... | collective-permute-start | bytes 3145736 | tf_op jit(solution)/shard_map/ppermute | solution.py:239
  50.7 2.7 %collective-permute-start.9 = (bf16[1024,256]{1,0:T(8,128)(2,1)}, bf16[1024,256]{1,0:T(8,128)(2,1)}, u32[]{:S(2)}, u32[]{:S(2)}) collective-permute-start(bf16[1024,256]{1,0:T(8,128)(2,1)} %shard_map.49), channel_id=1, source_target_pairs={{0,32},{16,48},{32,0},{48,16},{1,33},{17,49},{33,1},{49,17},{2,34}... | collective-permute-start | bytes 1572872 | tf_op jit(solution)/shard_map/ppermute | solution.py:24
  53.4 1.6 collective-permute-start.10
  55.0 0.6 stack.44.at_ref
  55.6 13.5 %collective-permute-done.10.refs_7_ = bf16[2,512,128]{2,1,0:T(8,128)(2,1)} collective-permute-done((bf16[2,512,128]{2,1,0:T(8,128)(2,1)}, bf16[2,512,128]{2,1,0:T(8,128)(2,1)}, u32[]{:S(2)}, u32[]{:S(2)}) %collective-permute-start.10) | collective-permute-done | bytes 262176 | tf_op jit(solution)/shard_map/ppermute | solution.py:24
  69.1 0.0 collective-permute-done.11.refs_9_
  69.1 7.5 %shard_map.50 = f32[4,128,512]{2,1,0:T(8,128)} custom-call(s32[5]{0:T(128)} %stack.44.at_ref, bf16[2,512,128]{2,1,0:T(8,128)(2,1)} %copy-done.6, bf16[2,512,128]{2,1,0:T(8,128)(2,1)} %copy-done.9, bf16[2,512,128]{2,1,0:T(8,128)(2,1)} %copy-done.10, bf16[2,512,128]{2,1,0:T(8,128)(2,1)} %copy-done.11, bf16[2,512,128]{2,1,0:T(8,128)(2,1)} %copy-done.12, ...), custom_call_target="tpu_custom_call" | custom-call | flops 2147483648 | bytes 7340032 | tf_op jit(solution)/shard_map/pallas_call | solution.py:87
  76.6 0.0 collective-permute-done.6.refs_1_
  76.6 1.1 collective-permute-done.9.refs_3_
  77.7 0.0 collective-permute-start.12
  77.7 4.7 %all-to-all-start.1 = ((f32[16,32,512]{2,1,0:T(8,128)}), f32[16,32,512]{2,1,0:T(8,128)}, u32[]{:S(2)}, u32[]{:S(2)}) async-start(f32[16,32,512]{2,1,0:T(8,128)} %bitcast.22), calls=%async_computation.1 | async-start | bytes 2097152 | tf_op jit(solution)/shard_map/all_to_all | solution.py:269
  82.4 0.0 all-gather.7.cloned.1.call-start
  82.5 0.4 collective-permute-start.13
  82.9 2.8 %all-gather.5.cloned.1.call-done = bf16[16,512,128]{2,1,0:T(8,128)(2,1)} async-done(((bf16[2,512,128]{2,1,0:T(8,128)(2,1)}), bf16[16,512,128]{2,1,0:T(8,128)(2,1)}) %all-gather.5.cloned.1.call-update) | async-done | bytes 2097168 | tf_op jit(solution)/shard_map/all_gather | solution.py:263
  85.6 0.0 collective-permute-done.13.refs_4_
  85.7 1.0 copy-done.3
  86.6 1.2 copy-done.4
  87.9 5.4 %shard_map.51 = f32[4,128,512]{2,1,0:T(8,128)S(1)} custom-call(s32[5]{0:T(128)S(1)} %copy-done.2, bf16[8,2,512,128]{3,2,1,0:T(8,128)(2,1)} %bitcast.25, bf16[2048,256]{1,0:T(8,128)(2,1)S(1)} %copy-done.1, bf16[2048,256]{1,0:T(8,128)(2,1)S(1)} %collective-permute-done.6.refs_1_, bf16[2048,256]{1,0:T(8,128)(2,1)S(1)} %copy-done.4, ...), custom_call_target="tpu_custom_call" | custom-call | flops 2147483648 | bytes 7340032 | tf_op jit(solution)/shard_map/pallas_call | solution.py:156
  93.3 4.3 %all-to-all-done.1 = f32[16,32,512]{2,1,0:T(8,128)} async-done(((f32[16,32,512]{2,1,0:T(8,128)}), f32[16,32,512]{2,1,0:T(8,128)}, u32[]{:S(2)}, u32[]{:S(2)}) %all-to-all-start.1) | async-done | bytes 1048608 | tf_op jit(solution)/shard_map/all_to_all | solution.py:269
  97.6 1.3 bitcast_reduce_fusion
  98.9 2.4 %collective-permute-start.14 = (bf16[1,4,32,512]{3,2,1,0:T(8,128)(2,1)S(1)}, bf16[1,4,32,512]{3,2,1,0:T(8,128)(2,1)S(1)}, u32[]{:S(2)}, u32[]{:S(2)}) collective-permute-start(bf16[1,4,32,512]{3,2,1,0:T(8,128)(2,1)S(1)} %bitcast.23), channel_id=1, source_target_pairs={{0,8},{8,0},{1,9},{9,1},{2,10},{10,2},{3,11},{11,3},{4,12},{12,4},... | collective-permute-start | bytes 393224 | tf_op jit(solution)/shard_map/ppermute | solution.py:24
  101.4 4.8 %collective-permute-done.14 = bf16[1,4,32,512]{3,2,1,0:T(8,128)(2,1)S(1)} collective-permute-done((bf16[1,4,32,512]{3,2,1,0:T(8,128)(2,1)S(1)}, bf16[1,4,32,512]{3,2,1,0:T(8,128)(2,1)S(1)}, u32[]{:S(2)}, u32[]{:S(2)}) %collective-permute-start.14) | collective-permute-done | bytes 131104 | tf_op jit(solution)/shard_map/ppermute | solution.py:24
  106.2 0.7 pad_maximum_fusion.2
  106.9 0.0 all-gather.7.cloned.1.call-update
  106.9 17.4 %all_to_all.25 = f32[4,128,512]{2,1,0:T(8,128)S(1)} all-to-all(f32[4,128,512]{2,1,0:T(8,128)S(1)} %shard_map.51), channel_id=1, replica_groups=mesh['xl'=2,'c'=2,'y'=4,'xh'=2,'z'=8] {'y'}, dimensions={0} | all-to-all | bytes 2097152 | tf_op jit(solution)/shard_map/all_to_all | solution.py:277
  124.3 0.1 reduce_sum.19
  124.4 0.1 broadcast_in_dim.4
  124.5 16.6 %all_to_all.26 = bf16[8,128,512]{2,1,0:T(8,128)(2,1)S(1)} all-to-all(bf16[8,128,512]{2,1,0:T(8,128)(2,1)S(1)} %broadcast_in_dim.4), channel_id=1, replica_groups=mesh['xl'=2,'c'=2,'y'=4,'xh'=2,'z'=8] {'xl','y'}, dimensions={0} | all-to-all | bytes 2097152 | tf_op jit(solution)/shard_map/all_to_all | solution.py:280
  141.1 2.7 %collective-permute-done.15.other_ref = bf16[2,4,128,512]{3,2,1,0:T(8,128)(2,1)S(1)} collective-permute-done((bf16[2,4,128,512]{3,2,1,0:T(8,128)(2,1)S(1)}, bf16[2,4,128,512]{3,2,1,0:T(8,128)(2,1)S(1)}, u32[]{:S(2)}, u32[]{:S(2)}) %collective-permute-start.15) | collective-permute-done | bytes 1048608 | tf_op jit(solution)/shard_map/ppermute | solution.py:24
  143.7 3.7 %all-gather.7.cloned.1.call-done = bf16[16,4,32,512]{3,2,1,0:T(8,128)(2,1)} async-done(((bf16[2,4,32,512]{3,2,1,0:T(8,128)(2,1)}), bf16[16,4,32,512]{3,2,1,0:T(8,128)(2,1)}) %all-gather.7.cloned.1.call-update) | async-done | bytes 2097168 | tf_op jit(solution)/shard_map/all_gather | solution.py:275
  147.4 1.6 copy-done
  149.0 3.5 %shard_map.52 = bf16[4,128,512]{2,1,0:T(8,128)(2,1)S(1)} custom-call(s32[5]{0:T(128)S(1)} %copy-done.2, bf16[8,2,4,32,512]{4,3,2,1,0:T(8,128)(2,1)S(1)} %bitcast.21, bf16[2,4,128,512]{3,2,1,0:T(8,128)(2,1)S(1)} %bitcast.20, bf16[2,4,128,512]{3,2,1,0:T(8,128)(2,1)S(1)} %collective-permute-done.15.other_ref), custom_call_target="tpu_custom_call" | custom-call | flops 1073741824 | bytes 5242880 | tf_op jit(solution)/shard_map/pallas_call | solution.py:192
  152.5 11.9 %all_to_all.27.in_ref = bf16[4,128,512]{2,1,0:T(8,128)(2,1)S(1)} all-to-all(bf16[4,128,512]{2,1,0:T(8,128)(2,1)S(1)} %shard_map.52), channel_id=1, replica_groups=mesh['xl'=2,'c'=2,'y'=4,'xh'=2,'z'=8] {'y'}, dimensions={0} | all-to-all | bytes 1048576 | tf_op jit(solution)/shard_map/all_to_all | solution.py:284
  164.4 2.0 %shard_map.53 = f32[128,2048]{1,0:T(8,128)} custom-call(bf16[4,128,512]{2,1,0:T(8,128)(2,1)S(1)} %all_to_all.27.in_ref), custom_call_target="tpu_custom_call" | custom-call | tf_op jit(solution)/shard_map/pallas_call | solution.py:215
  (28 shorter events, 0.1 us)
Async XLA Ops:
  6.5 7.0 %collective-permute-start = (bf16[1,512,128]{2,1,0:T(8,128)(2,1)}, bf16[1,512,128]{2,1,0:T(8,128)(2,1)S(1)}, u32[]{:S(2)}, u32[]{:S(2)}) collective-permute-start(bf16[1,512,128]{2,1,0:T(8,128)(2,1)} %param.4), channel_id=1, source_target_pairs={{0,8},{8,0},{1,9},{9,1},{2,10},{10,2},{3,11},{11,3},{4,12},{12,4},... | collective-permute-start | bytes 393224 | tf_op jit(solution)/shard_map/ppermute | solution.py:24
  8.7 4.8 %copy-start.7 = (bf16[1,512,128]{2,1,0:T(8,128)(2,1)S(1)}, bf16[1,512,128]{2,1,0:T(8,128)(2,1)}, u32[]{:S(2)}) copy-start(bf16[1,512,128]{2,1,0:T(8,128)(2,1)} %param.4) | copy-start | bytes 393220
  13.5 6.6 %copy-start.6 = (bf16[2,512,128]{2,1,0:T(8,128)(2,1)}, bf16[2,512,128]{2,1,0:T(8,128)(2,1)S(1)}, u32[]{:S(2)}) copy-start(bf16[2,512,128]{2,1,0:T(8,128)(2,1)S(1)} %pad_maximum_fusion.refs_0_) | copy-start | bytes 786436
  13.5 10.6 %copy-start.8 = (bf16[1,512,128]{2,1,0:T(8,128)(2,1)S(1)}, bf16[1,512,128]{2,1,0:T(8,128)(2,1)}, u32[]{:S(2)}) copy-start(bf16[1,512,128]{2,1,0:T(8,128)(2,1)} %param.5) | copy-start | bytes 393220
  13.5 34.4 %all-to-all-start = ((bf16[4,1024,256]{2,1,0:T(8,128)(2,1)}), bf16[4,1024,256]{2,1,0:T(8,128)(2,1)S(1)}, u32[]{:S(2)}, u32[]{:S(2)}) async-start(bf16[4,1024,256]{2,1,0:T(8,128)(2,1)} %shard_map.46), calls=%async_computation | async-start | bytes 4194304 | tf_op jit(solution)/shard_map/all_to_all | solution.py:251
  18.1 67.5 %all-gather.5.cloned.1.call-start = ((), (), s32[]{:S(2)}) async-start(), calls=%async_computation.5 | async-start | bytes 2359296 | tf_op jit(solution)/shard_map/all_gather | solution.py:263
  18.2 13.2 %collective-permute-start.1 = (bf16[2,512,128]{2,1,0:T(8,128)(2,1)S(1)}, bf16[2,512,128]{2,1,0:T(8,128)(2,1)S(1)}, u32[]{:S(2)}, u32[]{:S(2)}) collective-permute-start(bf16[2,512,128]{2,1,0:T(8,128)(2,1)S(1)} %pad_maximum_fusion.refs_0_), channel_id=1, source_target_pairs={{0,1},{1,2},{2,3},{3,4},{4,5},{5,6},{6,7},{7,0},{8,9},{9,10},{10,1... | collective-permute-start | bytes 786440 | tf_op jit(solution)/shard_map/ppermute | solution.py:24
  20.1 11.2 %collective-permute-start.2 = (bf16[2,512,128]{2,1,0:T(8,128)(2,1)S(1)}, bf16[2,512,128]{2,1,0:T(8,128)(2,1)S(1)}, u32[]{:S(2)}, u32[]{:S(2)}) collective-permute-start(bf16[2,512,128]{2,1,0:T(8,128)(2,1)S(1)} %pad_maximum_fusion.refs_0_), channel_id=1, source_target_pairs={{0,7},{1,0},{2,1},{3,2},{4,3},{5,4},{6,5},{7,6},{8,15},{9,8},{10,9... | collective-permute-start | bytes 786440 | tf_op jit(solution)/shard_map/ppermute | solution.py:24
  24.1 6.5 %collective-permute-start.3 = (bf16[1,512,128]{2,1,0:T(8,128)(2,1)S(1)}, bf16[1,512,128]{2,1,0:T(8,128)(2,1)S(1)}, u32[]{:S(2)}, u32[]{:S(2)}) collective-permute-start(bf16[1,512,128]{2,1,0:T(8,128)(2,1)S(1)} %copy-done.8), channel_id=1, source_target_pairs={{0,8},{8,0},{1,9},{9,1},{2,10},{10,2},{3,11},{11,3},{4,12},{12,4},... | collective-permute-start | bytes 393224 | tf_op jit(solution)/shard_map/ppermute | solution.py:24
  31.3 6.0 %copy-start.9 = (bf16[2,512,128]{2,1,0:T(8,128)(2,1)}, bf16[2,512,128]{2,1,0:T(8,128)(2,1)S(1)}, u32[]{:S(2)}) copy-start(bf16[2,512,128]{2,1,0:T(8,128)(2,1)S(1)} %collective-permute-done.1.refs_1_) | copy-start | bytes 786436
  31.3 6.0 %copy-start.10 = (bf16[2,512,128]{2,1,0:T(8,128)(2,1)}, bf16[2,512,128]{2,1,0:T(8,128)(2,1)S(1)}, u32[]{:S(2)}) copy-start(bf16[2,512,128]{2,1,0:T(8,128)(2,1)S(1)} %collective-permute-done.2.refs_2_) | copy-start | bytes 786436
  31.3 8.9 %collective-permute-start.4 = (bf16[2,512,128]{2,1,0:T(8,128)(2,1)S(1)}, bf16[2,512,128]{2,1,0:T(8,128)(2,1)S(1)}, u32[]{:S(2)}, u32[]{:S(2)}) collective-permute-start(bf16[2,512,128]{2,1,0:T(8,128)(2,1)S(1)} %collective-permute-done.1.refs_1_), channel_id=1, source_target_pairs={{0,1},{1,2},{2,3},{3,4},{4,5},{5,6},{6,7},{7,0},{8,9},{9,10},{10,1... | collective-permute-start | bytes 786440 | tf_op jit(solution)/shard_map/ppermute | solution.py:24
  31.4 8.8 %collective-permute-start.5 = (bf16[2,512,128]{2,1,0:T(8,128)(2,1)S(1)}, bf16[2,512,128]{2,1,0:T(8,128)(2,1)S(1)}, u32[]{:S(2)}, u32[]{:S(2)}) collective-permute-start(bf16[2,512,128]{2,1,0:T(8,128)(2,1)S(1)} %collective-permute-done.2.refs_2_), channel_id=1, source_target_pairs={{0,7},{1,0},{2,1},{3,2},{4,3},{5,4},{6,5},{7,6},{8,15},{9,8},{10,9... | collective-permute-start | bytes 786440 | tf_op jit(solution)/shard_map/ppermute | solution.py:24
  40.2 28.9 %copy-start.11 = (bf16[2,512,128]{2,1,0:T(8,128)(2,1)}, bf16[2,512,128]{2,1,0:T(8,128)(2,1)S(1)}, u32[]{:S(2)}) copy-start(bf16[2,512,128]{2,1,0:T(8,128)(2,1)S(1)} %collective-permute-done.4.refs_3_) | copy-start | bytes 786436
  40.2 7.7 %copy-start.12 = (bf16[2,512,128]{2,1,0:T(8,128)(2,1)}, bf16[2,512,128]{2,1,0:T(8,128)(2,1)S(1)}, u32[]{:S(2)}) copy-start(bf16[2,512,128]{2,1,0:T(8,128)(2,1)S(1)} %collective-permute-done.5.refs_4_) | copy-start | bytes 786436
  40.2 7.7 %collective-permute-start.7 = (bf16[2,512,128]{2,1,0:T(8,128)(2,1)S(1)}, bf16[2,512,128]{2,1,0:T(8,128)(2,1)S(1)}, u32[]{:S(2)}, u32[]{:S(2)}) collective-permute-start(bf16[2,512,128]{2,1,0:T(8,128)(2,1)S(1)} %collective-permute-done.4.refs_3_), channel_id=1, source_target_pairs={{0,1},{1,2},{2,3},{3,4},{4,5},{5,6},{6,7},{7,0},{8,9},{9,10},{10,1... | collective-permute-start | bytes 786440 | tf_op jit(solution)/shard_map/ppermute | solution.py:24
  40.3 7.6 %collective-permute-start.8 = (bf16[2,512,128]{2,1,0:T(8,128)(2,1)S(1)}, bf16[2,512,128]{2,1,0:T(8,128)(2,1)S(1)}, u32[]{:S(2)}, u32[]{:S(2)}) collective-permute-start(bf16[2,512,128]{2,1,0:T(8,128)(2,1)S(1)} %collective-permute-done.5.refs_4_), channel_id=1, source_target_pairs={{0,7},{1,0},{2,1},{3,2},{4,3},{5,4},{6,5},{7,6},{8,15},{9,8},{10,9... | collective-permute-start | bytes 786440 | tf_op jit(solution)/shard_map/ppermute | solution.py:24
  47.9 0.7 copy-start.13
  47.9 0.8 copy-start.14
  48.7 20.4 %copy-start.5 = (bf16[4,1024,256]{2,1,0:T(8,128)(2,1)}, bf16[4,1024,256]{2,1,0:T(8,128)(2,1)S(1)}, u32[]{:S(2)}) copy-start(bf16[4,1024,256]{2,1,0:T(8,128)(2,1)S(1)} %all-to-all-done.refs_8_) | copy-start | bytes 6291460
  48.7 20.4 %collective-permute-start.11 = (bf16[4,1024,256]{2,1,0:T(8,128)(2,1)S(1)}, bf16[4,1024,256]{2,1,0:T(8,128)(2,1)}, u32[]{:S(2)}, u32[]{:S(2)}) collective-permute-start(bf16[4,1024,256]{2,1,0:T(8,128)(2,1)S(1)} %all-to-all-done.refs_8_), channel_id=1, source_target_pairs={{0,64},{64,0},{1,65},{65,1},{2,66},{66,2},{3,67},{67,3},{4,68},{68... | collective-permute-start | bytes 6291464 | tf_op jit(solution)/shard_map/ppermute | solution.py:24
  48.7 27.9 %collective-permute-start.6 = (bf16[2048,256]{1,0:T(8,128)(2,1)}, bf16[2048,256]{1,0:T(8,128)(2,1)S(1)}, u32[]{:S(2)}, u32[]{:S(2)}) collective-permute-start(bf16[2048,256]{1,0:T(8,128)(2,1)} %shard_map.47), channel_id=1, source_target_pairs={{0,16},{16,32},{32,48},{48,0},{64,112},{80,64},{96,80},{112,96},{1... | collective-permute-start | bytes 3145736 | tf_op jit(solution)/shard_map/ppermute | solution.py:239
  50.7 27.0 %collective-permute-start.9 = (bf16[1024,256]{1,0:T(8,128)(2,1)}, bf16[1024,256]{1,0:T(8,128)(2,1)}, u32[]{:S(2)}, u32[]{:S(2)}) collective-permute-start(bf16[1024,256]{1,0:T(8,128)(2,1)} %shard_map.49), channel_id=1, source_target_pairs={{0,32},{16,48},{32,0},{48,16},{1,33},{17,49},{33,1},{49,17},{2,34}... | collective-permute-start | bytes 1572872 | tf_op jit(solution)/shard_map/ppermute | solution.py:24
  53.4 15.7 %collective-permute-start.10 = (bf16[2,512,128]{2,1,0:T(8,128)(2,1)}, bf16[2,512,128]{2,1,0:T(8,128)(2,1)}, u32[]{:S(2)}, u32[]{:S(2)}) collective-permute-start(bf16[2,512,128]{2,1,0:T(8,128)(2,1)} %copy-done.13), channel_id=1, source_target_pairs={{0,1},{1,2},{2,3},{3,4},{4,5},{5,6},{6,7},{7,0},{8,9},{9,10},{10,1... | collective-permute-start | bytes 786440 | tf_op jit(solution)/shard_map/ppermute | solution.py:24
  76.6 10.0 %copy-start.1 = (bf16[2048,256]{1,0:T(8,128)(2,1)S(1)}, bf16[2048,256]{1,0:T(8,128)(2,1)}, u32[]{:S(2)}) copy-start(bf16[2048,256]{1,0:T(8,128)(2,1)} %shard_map.48.refs_0_) | copy-start | bytes 3145732
  76.6 10.0 %copy-start.2 = (s32[5]{0:T(128)S(1)}, s32[5]{0:T(128)}, u32[]{:S(2)}) copy-start(s32[5]{0:T(128)} %stack.44.at_ref) | copy-start | bytes 64
  77.7 7.9 %collective-permute-start.12 = (bf16[2048,256]{1,0:T(8,128)(2,1)S(1)}, bf16[2048,256]{1,0:T(8,128)(2,1)S(1)}, u32[]{:S(2)}, u32[]{:S(2)}) collective-permute-start(bf16[2048,256]{1,0:T(8,128)(2,1)S(1)} %collective-permute-done.6.refs_1_), channel_id=1, source_target_pairs={{0,64},{64,0},{1,65},{65,1},{2,66},{66,2},{3,67},{67,3},{4,68},{68... | collective-permute-start | bytes 3145736 | tf_op jit(solution)/shard_map/ppermute | solution.py:24
  77.7 19.9 %all-to-all-start.1 = ((f32[16,32,512]{2,1,0:T(8,128)}), f32[16,32,512]{2,1,0:T(8,128)}, u32[]{:S(2)}, u32[]{:S(2)}) async-start(f32[16,32,512]{2,1,0:T(8,128)} %bitcast.22), calls=%async_computation.1 | async-start | bytes 2097152 | tf_op jit(solution)/shard_map/all_to_all | solution.py:269
  82.4 65.0 %all-gather.7.cloned.1.call-start = ((), (), s32[]{:S(2)}) async-start(), calls=%async_computation.6 | async-start | bytes 2359296 | tf_op jit(solution)/shard_map/all_gather | solution.py:275
  82.5 3.2 %collective-permute-start.13 = (bf16[1024,256]{1,0:T(8,128)(2,1)}, bf16[1024,256]{1,0:T(8,128)(2,1)}, u32[]{:S(2)}, u32[]{:S(2)}) collective-permute-start(bf16[1024,256]{1,0:T(8,128)(2,1)} %collective-permute-done.9.refs_3_), channel_id=1, source_target_pairs={{0,64},{64,0},{1,65},{65,1},{2,66},{66,2},{3,67},{67,3},{4,68},{68... | collective-permute-start | bytes 1572872 | tf_op jit(solution)/shard_map/ppermute | solution.py:24
  85.7 1.0 copy-start.3
  86.6 1.2 copy-start.4
  98.9 7.2 %collective-permute-start.14 = (bf16[1,4,32,512]{3,2,1,0:T(8,128)(2,1)S(1)}, bf16[1,4,32,512]{3,2,1,0:T(8,128)(2,1)S(1)}, u32[]{:S(2)}, u32[]{:S(2)}) collective-permute-start(bf16[1,4,32,512]{3,2,1,0:T(8,128)(2,1)S(1)} %bitcast.23), channel_id=1, source_target_pairs={{0,8},{8,0},{1,9},{9,1},{2,10},{10,2},{3,11},{11,3},{4,12},{12,4},... | collective-permute-start | bytes 393224 | tf_op jit(solution)/shard_map/ppermute | solution.py:24
  141.1 2.7 %collective-permute-start.15 = (bf16[2,4,128,512]{3,2,1,0:T(8,128)(2,1)S(1)}, bf16[2,4,128,512]{3,2,1,0:T(8,128)(2,1)S(1)}, u32[]{:S(2)}, u32[]{:S(2)}) collective-permute-start(bf16[2,4,128,512]{3,2,1,0:T(8,128)(2,1)S(1)} %bitcast.19), channel_id=1, source_target_pairs={{0,64},{64,0},{1,65},{65,1},{2,66},{66,2},{3,67},{67,3},{4,68},{68... | collective-permute-start | bytes 3145736 | tf_op jit(solution)/shard_map/ppermute | solution.py:24
  147.4 1.6 copy-start
Sparse Core Ops, SparseCore 0:
  40.4 45.2 all-gather.4
  107.0 40.3 all-gather.6

commit v17 on v16

--- a/solution.py
+++ b/solution.py
@@ -77,21 +77,22 @@
         for copy in copies:
             copy.wait()
 
-    both = jnp.dot(lhs[:, :1024], own_ref[0], preferred_element_type=F32)
-    both += jnp.dot(lhs[:, 1024:], other_ref[0], preferred_element_type=F32)
-    out_ref[0] = (both[:, :COLS] + both[:, COLS:]).T
+    for i in range(2):
+        both = jnp.dot(lhs[:, :1024], own_ref[i], preferred_element_type=F32)
+        both += jnp.dot(lhs[:, 1024:], other_ref[i], preferred_element_type=F32)
+        out_ref[i] = (both[:, :COLS] + both[:, COLS:]).T
 
 
 def rotate_ring(at, ring, own, other):
-    slab = pl.BlockSpec((1, 1024, 256), lambda g: (g, 0, 0))
+    slab = pl.BlockSpec((2, 1024, 256), lambda g: (g, 0, 0))
     return pl.pallas_call(
         functools.partial(rotate_ring_kernel, [offset for _, offset in ring]),
-        grid=(4,),
+        grid=(2,),
         out_shape=jax.ShapeDtypeStruct((4, COLS, TOK), F32),
         in_specs=[pl.BlockSpec(memory_space=pltpu.SMEM)]
         + [pl.BlockSpec(memory_space=pltpu.HBM)] * len(ring)
         + [slab, slab],
-        out_specs=pl.BlockSpec((1, COLS, TOK), lambda g: (g, 0, 0)),
+        out_specs=pl.BlockSpec((2, COLS, TOK), lambda g: (g, 0, 0)),
         scratch_shapes=[pltpu.VMEM((TOK, 2048), BF16), pltpu.SemaphoreType.DMA((16,))],
         compiler_params=ALL_VMEM,
         cost_estimate=pl.CostEstimate(
@@ -204,7 +205,7 @@
 
 
 def weave_kernel(in_ref, out_ref):
-    for tile in range(4):
+    for tile in range(8):
         lanes = slice(tile * 32, tile * 32 + 32)
         out_ref[:, tile * COLS : (tile + 1) * COLS] = jnp.concatenate(
             [in_ref[q].astype(F32)[:, lanes] for q in range(4)], axis=1
@@ -214,10 +215,10 @@
 def weave(parts):
     return pl.pallas_call(
         weave_kernel,
-        grid=(4,),
+        grid=(2,),
         out_shape=jax.ShapeDtypeStruct((COLS, 2048), F32),
-        in_specs=[pl.BlockSpec((4, COLS, 128), lambda g: (0, 0, g))],
-        out_specs=pl.BlockSpec((COLS, 512), lambda g: (0, g)),
+        in_specs=[pl.BlockSpec((4, COLS, 256), lambda g: (0, 0, g))],
+        out_specs=pl.BlockSpec((COLS, 1024), lambda g: (0, g)),
         compiler_params=PARAMS,
     )(parts)
 

time: 174 us -> 173 us (level)
  no operation moved by 1% of the time
where the time goes in v17:
time: 173 us
  blocking collectives  45.9 us (27%)
  waiting for transfers between devices  39.4 us (23%)
  starting transfers between devices  35.4 us (20%)
  Pallas kernels  29 us (17%)
  between operations  13.6 us (8%)
  local copies, waits for them, and re-layouts  5.29 us (3%)
  other arithmetic  4.16 us (2%)
    ppermute x15, waiting for transfers between devices, shift(): return lax.ppermute(x, axis, [(i, (i + by) % n) for i in range(n)])  28.7 us
    ppermute x15, starting transfers between devices, shift(): return lax.ppermute(x, axis, [(i, (i + by) % n) for i in range(n)])  24 us
    all_to_all x1, blocking collectives, body(): grads_in = lax.all_to_all(grads_part, 'y', 0, 0)  17.4 us
    all_to_all x1, blocking collectives, body(): rot_own = lax.all_to_all(copies, ('xl', 'y'), 0, 0).reshape(2, 4, COLS, TOK)  16.6 us
    all_to_all x1, blocking collectives, body(): return weave(lax.all_to_all(part, 'y', 0, 0))  11.9 us
    pallas_call x3, Pallas kernels, split_rows(): pl.pallas_call(split_rows_kernel, grid_spec=pltpu.PrefetchScalarGridSpec(...  7.7 us
    pallas_call x1, Pallas kernels, rotate_ring(): pl.pallas_call(functools.partial(rotate_ring_kernel, [offset for _, offse...  6.94 us
    pallas_call x1, Pallas kernels, rotate(): pl.pallas_call(rotate_kernel, out_shape=jax.ShapeDtypeStruct((4, COLS, TO...  5.4 us
  transfers between devices with their start and end apart: 20, of which 10 were waited for; matrix products, arithmetic and copies ran while one was open for 2% of the time, Pallas kernels for 14%

profile of v17, /device:TPU:2, one launch (start us, length us, event | category | flops | bytes accessed | tf_op | source)
XLA Modules:
  0.0 172.7 jit_solution(13942554139430831854)
XLA Ops:
  6.5 2.1 %collective-permute-start = (bf16[1,512,128]{2,1,0:T(8,128)(2,1)}, bf16[1,512,128]{2,1,0:T(8,128)(2,1)S(1)}, u32[]{:S(2)}, u32[]{:S(2)}) collective-permute-start(bf16[1,512,128]{2,1,0:T(8,128)(2,1)} %param.4), channel_id=1, source_target_pairs={{0,8},{8,0},{1,9},{9,1},{2,10},{10,2},{3,11},{11,3},{4,12},{12,4},... | collective-permute-start | bytes 393224 | tf_op jit(solution)/shard_map/ppermute | solution.py:24
  8.7 4.0 %shard_map.46 = bf16[4,1024,256]{2,1,0:T(8,128)(2,1)} custom-call(s32[1]{0:T(128)} %bitcast.4.half_ref, f32[8192,128]{1,0:T(8,128)} %in_ref.1), custom_call_target="tpu_custom_call" | custom-call | flops 1048576 | bytes 4194304 | tf_op jit(solution)/shard_map/pallas_call | solution.py:44
  12.7 0.8 collective-permute-done
  13.5 0.0 copy-start.8
  13.5 4.6 %all-to-all-start = ((bf16[4,1024,256]{2,1,0:T(8,128)(2,1)}), bf16[4,1024,256]{2,1,0:T(8,128)(2,1)S(1)}, u32[]{:S(2)}, u32[]{:S(2)}) async-start(bf16[4,1024,256]{2,1,0:T(8,128)(2,1)} %shard_map.46), calls=%async_computation | async-start | bytes 4194304 | tf_op jit(solution)/shard_map/all_to_all | solution.py:252
  18.2 1.9 %collective-permute-start.1 = (bf16[2,512,128]{2,1,0:T(8,128)(2,1)S(1)}, bf16[2,512,128]{2,1,0:T(8,128)(2,1)S(1)}, u32[]{:S(2)}, u32[]{:S(2)}) collective-permute-start(bf16[2,512,128]{2,1,0:T(8,128)(2,1)S(1)} %pad_maximum_fusion.refs_0_), channel_id=1, source_target_pairs={{0,1},{1,2},{2,3},{3,4},{4,5},{5,6},{6,7},{7,0},{8,9},{9,10},{10,1... | collective-permute-start | bytes 786440 | tf_op jit(solution)/shard_map/ppermute | solution.py:24
  20.1 4.0 %collective-permute-start.2 = (bf16[2,512,128]{2,1,0:T(8,128)(2,1)S(1)}, bf16[2,512,128]{2,1,0:T(8,128)(2,1)S(1)}, u32[]{:S(2)}, u32[]{:S(2)}) collective-permute-start(bf16[2,512,128]{2,1,0:T(8,128)(2,1)S(1)} %pad_maximum_fusion.refs_0_), channel_id=1, source_target_pairs={{0,7},{1,0},{2,1},{3,2},{4,3},{5,4},{6,5},{7,6},{8,15},{9,8},{10,9... | collective-permute-start | bytes 786440 | tf_op jit(solution)/shard_map/ppermute | solution.py:24
  24.1 2.1 %collective-permute-start.3 = (bf16[1,512,128]{2,1,0:T(8,128)(2,1)S(1)}, bf16[1,512,128]{2,1,0:T(8,128)(2,1)S(1)}, u32[]{:S(2)}, u32[]{:S(2)}) collective-permute-start(bf16[1,512,128]{2,1,0:T(8,128)(2,1)S(1)} %copy-done.8), channel_id=1, source_target_pairs={{0,8},{8,0},{1,9},{9,1},{2,10},{10,2},{3,11},{11,3},{4,12},{12,4},... | collective-permute-start | bytes 393224 | tf_op jit(solution)/shard_map/ppermute | solution.py:24
  26.2 0.6 pad_add_fusion.rows_ref
  26.8 2.8 %shard_map.47 = bf16[2048,256]{1,0:T(8,128)(2,1)} custom-call(s32[2]{0:T(128)} %pad_add_fusion.rows_ref, f32[8192,128]{1,0:T(8,128)} %in_ref.4), custom_call_target="tpu_custom_call" | custom-call | flops 524288 | bytes 2097152 | tf_op jit(solution)/shard_map/pallas_call | solution.py:113
  29.6 0.9 collective-permute-done.3
  30.6 0.7 pad_maximum_fusion.1
  31.3 0.0 collective-permute-done.1.refs_1_
  31.3 0.0 collective-permute-done.2.refs_2_
  31.3 0.1 collective-permute-start.4
  31.4 3.2 %collective-permute-start.5 = (bf16[2,512,128]{2,1,0:T(8,128)(2,1)S(1)}, bf16[2,512,128]{2,1,0:T(8,128)(2,1)S(1)}, u32[]{:S(2)}, u32[]{:S(2)}) collective-permute-start(bf16[2,512,128]{2,1,0:T(8,128)(2,1)S(1)} %collective-permute-done.2.refs_2_), channel_id=1, source_target_pairs={{0,7},{1,0},{2,1},{3,2},{4,3},{5,4},{6,5},{7,6},{8,15},{9,8},{10,9... | collective-permute-start | bytes 786440 | tf_op jit(solution)/shard_map/ppermute | solution.py:24
  34.6 0.6 pad_add_fusion.1.rows_ref
  35.3 2.0 %shard_map.49 = bf16[1024,256]{1,0:T(8,128)(2,1)} custom-call(s32[1]{0:T(128)} %bitcast.9.rows_ref, f32[8192,128]{1,0:T(8,128)} %in_ref.4), custom_call_target="tpu_custom_call" | custom-call | flops 262144 | bytes 1048576 | tf_op jit(solution)/shard_map/pallas_call | solution.py:113
  37.3 2.9 %shard_map.48.refs_0_ = bf16[2048,256]{1,0:T(8,128)(2,1)} custom-call(s32[2]{0:T(128)} %pad_add_fusion.1.rows_ref, f32[8192,128]{1,0:T(8,128)} %in_ref.4), custom_call_target="tpu_custom_call" | custom-call | flops 524288 | bytes 2097152 | tf_op jit(solution)/shard_map/pallas_call | solution.py:113
  40.2 0.0 collective-permute-done.4.refs_3_
  40.2 0.0 collective-permute-done.5.refs_4_
  40.2 0.0 all-gather.5.cloned.1.call-update
  40.2 0.1 collective-permute-start.7
  40.3 3.2 %collective-permute-start.8 = (bf16[2,512,128]{2,1,0:T(8,128)(2,1)S(1)}, bf16[2,512,128]{2,1,0:T(8,128)(2,1)S(1)}, u32[]{:S(2)}, u32[]{:S(2)}) collective-permute-start(bf16[2,512,128]{2,1,0:T(8,128)(2,1)S(1)} %collective-permute-done.5.refs_4_), channel_id=1, source_target_pairs={{0,7},{1,0},{2,1},{3,2},{4,3},{5,4},{6,5},{7,6},{8,15},{9,8},{10,9... | collective-permute-start | bytes 786440 | tf_op jit(solution)/shard_map/ppermute | solution.py:24
  43.6 4.3 %collective-permute-done.7.refs_5_ = bf16[2,512,128]{2,1,0:T(8,128)(2,1)S(1)} collective-permute-done((bf16[2,512,128]{2,1,0:T(8,128)(2,1)S(1)}, bf16[2,512,128]{2,1,0:T(8,128)(2,1)S(1)}, u32[]{:S(2)}, u32[]{:S(2)}) %collective-permute-start.7) | collective-permute-done | bytes 262176 | tf_op jit(solution)/shard_map/ppermute | solution.py:24
  47.9 0.0 collective-permute-done.8.refs_6_
  47.9 0.0 all-to-all-done.refs_8_
  47.9 0.7 copy-done.13
  48.6 0.1 copy-done.14
  48.7 0.0 collective-permute-start.11
  48.7 2.0 %collective-permute-start.6 = (bf16[2048,256]{1,0:T(8,128)(2,1)}, bf16[2048,256]{1,0:T(8,128)(2,1)S(1)}, u32[]{:S(2)}, u32[]{:S(2)}) collective-permute-start(bf16[2048,256]{1,0:T(8,128)(2,1)} %shard_map.47), channel_id=1, source_target_pairs={{0,16},{16,32},{32,48},{48,0},{64,112},{80,64},{96,80},{112,96},{1... | collective-permute-start | bytes 3145736 | tf_op jit(solution)/shard_map/ppermute | solution.py:240
  50.7 2.7 %collective-permute-start.9 = (bf16[1024,256]{1,0:T(8,128)(2,1)}, bf16[1024,256]{1,0:T(8,128)(2,1)}, u32[]{:S(2)}, u32[]{:S(2)}) collective-permute-start(bf16[1024,256]{1,0:T(8,128)(2,1)} %shard_map.49), channel_id=1, source_target_pairs={{0,32},{16,48},{32,0},{48,16},{1,33},{17,49},{33,1},{49,17},{2,34}... | collective-permute-start | bytes 1572872 | tf_op jit(solution)/shard_map/ppermute | solution.py:24
  53.4 1.6 collective-permute-start.10
  55.0 0.6 stack.44.at_ref
  55.6 13.5 %collective-permute-done.10.refs_7_ = bf16[2,512,128]{2,1,0:T(8,128)(2,1)} collective-permute-done((bf16[2,512,128]{2,1,0:T(8,128)(2,1)}, bf16[2,512,128]{2,1,0:T(8,128)(2,1)}, u32[]{:S(2)}, u32[]{:S(2)}) %collective-permute-start.10) | collective-permute-done | bytes 262176 | tf_op jit(solution)/shard_map/ppermute | solution.py:24
  69.1 6.9 %shard_map.50 = f32[4,128,512]{2,1,0:T(8,128)} custom-call(s32[5]{0:T(128)} %stack.44.at_ref, bf16[2,512,128]{2,1,0:T(8,128)(2,1)} %copy-done.6, bf16[2,512,128]{2,1,0:T(8,128)(2,1)} %copy-done.9, bf16[2,512,128]{2,1,0:T(8,128)(2,1)} %copy-done.10, bf16[2,512,128]{2,1,0:T(8,128)(2,1)} %copy-done.11, bf16[2,512,128]{2,1,0:T(8,128)(2,1)} %copy-done.12, ...), custom_call_target="tpu_custom_call" | custom-call | flops 2147483648 | bytes 7340032 | tf_op jit(solution)/shard_map/pallas_call | solution.py:88
  76.1 0.0 collective-permute-done.6.refs_1_
  76.1 1.6 collective-permute-done.9.refs_3_
  77.7 0.0 collective-permute-start.12
  77.7 4.7 %all-to-all-start.1 = ((f32[16,32,512]{2,1,0:T(8,128)}), f32[16,32,512]{2,1,0:T(8,128)}, u32[]{:S(2)}, u32[]{:S(2)}) async-start(f32[16,32,512]{2,1,0:T(8,128)} %bitcast.22), calls=%async_computation.1 | async-start | bytes 2097152 | tf_op jit(solution)/shard_map/all_to_all | solution.py:270
  82.4 0.0 all-gather.7.cloned.1.call-start
  82.5 0.4 collective-permute-start.13
  82.9 2.8 %all-gather.5.cloned.1.call-done = bf16[16,512,128]{2,1,0:T(8,128)(2,1)} async-done(((bf16[2,512,128]{2,1,0:T(8,128)(2,1)}), bf16[16,512,128]{2,1,0:T(8,128)(2,1)}) %all-gather.5.cloned.1.call-update) | async-done | bytes 2097168 | tf_op jit(solution)/shard_map/all_gather | solution.py:264
  85.6 0.0 collective-permute-done.13.refs_4_
  85.7 0.0 collective-permute-done.12.refs_2_
  85.7 1.0 copy-done.3
  86.6 1.2 copy-done.4
  87.9 5.4 %shard_map.51 = f32[4,128,512]{2,1,0:T(8,128)S(1)} custom-call(s32[5]{0:T(128)S(1)} %copy-done.2, bf16[8,2,512,128]{3,2,1,0:T(8,128)(2,1)} %bitcast.25, bf16[2048,256]{1,0:T(8,128)(2,1)S(1)} %copy-done.1, bf16[2048,256]{1,0:T(8,128)(2,1)S(1)} %collective-permute-done.6.refs_1_, bf16[2048,256]{1,0:T(8,128)(2,1)S(1)} %copy-done.4, ...), custom_call_target="tpu_custom_call" | custom-call | flops 2147483648 | bytes 7340032 | tf_op jit(solution)/shard_map/pallas_call | solution.py:157
  93.3 4.3 %all-to-all-done.1 = f32[16,32,512]{2,1,0:T(8,128)} async-done(((f32[16,32,512]{2,1,0:T(8,128)}), f32[16,32,512]{2,1,0:T(8,128)}, u32[]{:S(2)}, u32[]{:S(2)}) %all-to-all-start.1) | async-done | bytes 1048608 | tf_op jit(solution)/shard_map/all_to_all | solution.py:270
  97.6 1.3 bitcast_reduce_fusion
  98.9 2.4 %collective-permute-start.14 = (bf16[1,4,32,512]{3,2,1,0:T(8,128)(2,1)S(1)}, bf16[1,4,32,512]{3,2,1,0:T(8,128)(2,1)S(1)}, u32[]{:S(2)}, u32[]{:S(2)}) collective-permute-start(bf16[1,4,32,512]{3,2,1,0:T(8,128)(2,1)S(1)} %bitcast.23), channel_id=1, source_target_pairs={{0,8},{8,0},{1,9},{9,1},{2,10},{10,2},{3,11},{11,3},{4,12},{12,4},... | collective-permute-start | bytes 393224 | tf_op jit(solution)/shard_map/ppermute | solution.py:24
  101.4 4.8 %collective-permute-done.14 = bf16[1,4,32,512]{3,2,1,0:T(8,128)(2,1)S(1)} collective-permute-done((bf16[1,4,32,512]{3,2,1,0:T(8,128)(2,1)S(1)}, bf16[1,4,32,512]{3,2,1,0:T(8,128)(2,1)S(1)}, u32[]{:S(2)}, u32[]{:S(2)}) %collective-permute-start.14) | collective-permute-done | bytes 131104 | tf_op jit(solution)/shard_map/ppermute | solution.py:24
  106.2 0.7 pad_maximum_fusion.2
  106.9 0.0 all-gather.7.cloned.1.call-update
  106.9 17.4 %all_to_all.25 = f32[4,128,512]{2,1,0:T(8,128)S(1)} all-to-all(f32[4,128,512]{2,1,0:T(8,128)S(1)} %shard_map.51), channel_id=1, replica_groups=mesh['xl'=2,'c'=2,'y'=4,'xh'=2,'z'=8] {'y'}, dimensions={0} | all-to-all | bytes 2097152 | tf_op jit(solution)/shard_map/all_to_all | solution.py:278
  124.3 0.1 reduce_sum.19
  124.4 0.1 broadcast_in_dim.4
  124.5 16.6 %all_to_all.26 = bf16[8,128,512]{2,1,0:T(8,128)(2,1)S(1)} all-to-all(bf16[8,128,512]{2,1,0:T(8,128)(2,1)S(1)} %broadcast_in_dim.4), channel_id=1, replica_groups=mesh['xl'=2,'c'=2,'y'=4,'xh'=2,'z'=8] {'xl','y'}, dimensions={0} | all-to-all | bytes 2097152 | tf_op jit(solution)/shard_map/all_to_all | solution.py:281
  141.1 2.7 %collective-permute-done.15.other_ref = bf16[2,4,128,512]{3,2,1,0:T(8,128)(2,1)S(1)} collective-permute-done((bf16[2,4,128,512]{3,2,1,0:T(8,128)(2,1)S(1)}, bf16[2,4,128,512]{3,2,1,0:T(8,128)(2,1)S(1)}, u32[]{:S(2)}, u32[]{:S(2)}) %collective-permute-start.15) | collective-permute-done | bytes 1048608 | tf_op jit(solution)/shard_map/ppermute | solution.py:24
  143.7 3.7 %all-gather.7.cloned.1.call-done = bf16[16,4,32,512]{3,2,1,0:T(8,128)(2,1)} async-done(((bf16[2,4,32,512]{3,2,1,0:T(8,128)(2,1)}), bf16[16,4,32,512]{3,2,1,0:T(8,128)(2,1)}) %all-gather.7.cloned.1.call-update) | async-done | bytes 2097168 | tf_op jit(solution)/shard_map/all_gather | solution.py:276
  147.4 1.6 copy-done
  149.0 3.5 %shard_map.52 = bf16[4,128,512]{2,1,0:T(8,128)(2,1)S(1)} custom-call(s32[5]{0:T(128)S(1)} %copy-done.2, bf16[8,2,4,32,512]{4,3,2,1,0:T(8,128)(2,1)S(1)} %bitcast.21, bf16[2,4,128,512]{3,2,1,0:T(8,128)(2,1)S(1)} %bitcast.20, bf16[2,4,128,512]{3,2,1,0:T(8,128)(2,1)S(1)} %collective-permute-done.15.other_ref), custom_call_target="tpu_custom_call" | custom-call | flops 1073741824 | bytes 5242880 | tf_op jit(solution)/shard_map/pallas_call | solution.py:193
  152.5 11.9 %all_to_all.27.in_ref = bf16[4,128,512]{2,1,0:T(8,128)(2,1)S(1)} all-to-all(bf16[4,128,512]{2,1,0:T(8,128)(2,1)S(1)} %shard_map.52), channel_id=1, replica_groups=mesh['xl'=2,'c'=2,'y'=4,'xh'=2,'z'=8] {'y'}, dimensions={0} | all-to-all | bytes 1048576 | tf_op jit(solution)/shard_map/all_to_all | solution.py:285
  164.4 1.4 shard_map.53
  (28 shorter events, 0.1 us)
Async XLA Ops:
  6.5 7.0 %collective-permute-start = (bf16[1,512,128]{2,1,0:T(8,128)(2,1)}, bf16[1,512,128]{2,1,0:T(8,128)(2,1)S(1)}, u32[]{:S(2)}, u32[]{:S(2)}) collective-permute-start(bf16[1,512,128]{2,1,0:T(8,128)(2,1)} %param.4), channel_id=1, source_target_pairs={{0,8},{8,0},{1,9},{9,1},{2,10},{10,2},{3,11},{11,3},{4,12},{12,4},... | collective-permute-start | bytes 393224 | tf_op jit(solution)/shard_map/ppermute | solution.py:24
  8.7 4.8 %copy-start.7 = (bf16[1,512,128]{2,1,0:T(8,128)(2,1)S(1)}, bf16[1,512,128]{2,1,0:T(8,128)(2,1)}, u32[]{:S(2)}) copy-start(bf16[1,512,128]{2,1,0:T(8,128)(2,1)} %param.4) | copy-start | bytes 393220
  13.5 6.6 %copy-start.6 = (bf16[2,512,128]{2,1,0:T(8,128)(2,1)}, bf16[2,512,128]{2,1,0:T(8,128)(2,1)S(1)}, u32[]{:S(2)}) copy-start(bf16[2,512,128]{2,1,0:T(8,128)(2,1)S(1)} %pad_maximum_fusion.refs_0_) | copy-start | bytes 786436
  13.5 10.6 %copy-start.8 = (bf16[1,512,128]{2,1,0:T(8,128)(2,1)S(1)}, bf16[1,512,128]{2,1,0:T(8,128)(2,1)}, u32[]{:S(2)}) copy-start(bf16[1,512,128]{2,1,0:T(8,128)(2,1)} %param.5) | copy-start | bytes 393220
  13.5 34.4 %all-to-all-start = ((bf16[4,1024,256]{2,1,0:T(8,128)(2,1)}), bf16[4,1024,256]{2,1,0:T(8,128)(2,1)S(1)}, u32[]{:S(2)}, u32[]{:S(2)}) async-start(bf16[4,1024,256]{2,1,0:T(8,128)(2,1)} %shard_map.46), calls=%async_computation | async-start | bytes 4194304 | tf_op jit(solution)/shard_map/all_to_all | solution.py:252
  18.1 67.5 %all-gather.5.cloned.1.call-start = ((), (), s32[]{:S(2)}) async-start(), calls=%async_computation.5 | async-start | bytes 2359296 | tf_op jit(solution)/shard_map/all_gather | solution.py:264
  18.2 13.2 %collective-permute-start.1 = (bf16[2,512,128]{2,1,0:T(8,128)(2,1)S(1)}, bf16[2,512,128]{2,1,0:T(8,128)(2,1)S(1)}, u32[]{:S(2)}, u32[]{:S(2)}) collective-permute-start(bf16[2,512,128]{2,1,0:T(8,128)(2,1)S(1)} %pad_maximum_fusion.refs_0_), channel_id=1, source_target_pairs={{0,1},{1,2},{2,3},{3,4},{4,5},{5,6},{6,7},{7,0},{8,9},{9,10},{10,1... | collective-permute-start | bytes 786440 | tf_op jit(solution)/shard_map/ppermute | solution.py:24
  20.1 11.2 %collective-permute-start.2 = (bf16[2,512,128]{2,1,0:T(8,128)(2,1)S(1)}, bf16[2,512,128]{2,1,0:T(8,128)(2,1)S(1)}, u32[]{:S(2)}, u32[]{:S(2)}) collective-permute-start(bf16[2,512,128]{2,1,0:T(8,128)(2,1)S(1)} %pad_maximum_fusion.refs_0_), channel_id=1, source_target_pairs={{0,7},{1,0},{2,1},{3,2},{4,3},{5,4},{6,5},{7,6},{8,15},{9,8},{10,9... | collective-permute-start | bytes 786440 | tf_op jit(solution)/shard_map/ppermute | solution.py:24
  24.1 6.5 %collective-permute-start.3 = (bf16[1,512,128]{2,1,0:T(8,128)(2,1)S(1)}, bf16[1,512,128]{2,1,0:T(8,128)(2,1)S(1)}, u32[]{:S(2)}, u32[]{:S(2)}) collective-permute-start(bf16[1,512,128]{2,1,0:T(8,128)(2,1)S(1)} %copy-done.8), channel_id=1, source_target_pairs={{0,8},{8,0},{1,9},{9,1},{2,10},{10,2},{3,11},{11,3},{4,12},{12,4},... | collective-permute-start | bytes 393224 | tf_op jit(solution)/shard_map/ppermute | solution.py:24
  31.3 6.0 %copy-start.9 = (bf16[2,512,128]{2,1,0:T(8,128)(2,1)}, bf16[2,512,128]{2,1,0:T(8,128)(2,1)S(1)}, u32[]{:S(2)}) copy-start(bf16[2,512,128]{2,1,0:T(8,128)(2,1)S(1)} %collective-permute-done.1.refs_1_) | copy-start | bytes 786436
  31.3 6.0 %copy-start.10 = (bf16[2,512,128]{2,1,0:T(8,128)(2,1)}, bf16[2,512,128]{2,1,0:T(8,128)(2,1)S(1)}, u32[]{:S(2)}) copy-start(bf16[2,512,128]{2,1,0:T(8,128)(2,1)S(1)} %collective-permute-done.2.refs_2_) | copy-start | bytes 786436
  31.3 8.9 %collective-permute-start.4 = (bf16[2,512,128]{2,1,0:T(8,128)(2,1)S(1)}, bf16[2,512,128]{2,1,0:T(8,128)(2,1)S(1)}, u32[]{:S(2)}, u32[]{:S(2)}) collective-permute-start(bf16[2,512,128]{2,1,0:T(8,128)(2,1)S(1)} %collective-permute-done.1.refs_1_), channel_id=1, source_target_pairs={{0,1},{1,2},{2,3},{3,4},{4,5},{5,6},{6,7},{7,0},{8,9},{9,10},{10,1... | collective-permute-start | bytes 786440 | tf_op jit(solution)/shard_map/ppermute | solution.py:24
  31.4 8.8 %collective-permute-start.5 = (bf16[2,512,128]{2,1,0:T(8,128)(2,1)S(1)}, bf16[2,512,128]{2,1,0:T(8,128)(2,1)S(1)}, u32[]{:S(2)}, u32[]{:S(2)}) collective-permute-start(bf16[2,512,128]{2,1,0:T(8,128)(2,1)S(1)} %collective-permute-done.2.refs_2_), channel_id=1, source_target_pairs={{0,7},{1,0},{2,1},{3,2},{4,3},{5,4},{6,5},{7,6},{8,15},{9,8},{10,9... | collective-permute-start | bytes 786440 | tf_op jit(solution)/shard_map/ppermute | solution.py:24
  40.2 28.9 %copy-start.11 = (bf16[2,512,128]{2,1,0:T(8,128)(2,1)}, bf16[2,512,128]{2,1,0:T(8,128)(2,1)S(1)}, u32[]{:S(2)}) copy-start(bf16[2,512,128]{2,1,0:T(8,128)(2,1)S(1)} %collective-permute-done.4.refs_3_) | copy-start | bytes 786436
  40.2 7.7 %copy-start.12 = (bf16[2,512,128]{2,1,0:T(8,128)(2,1)}, bf16[2,512,128]{2,1,0:T(8,128)(2,1)S(1)}, u32[]{:S(2)}) copy-start(bf16[2,512,128]{2,1,0:T(8,128)(2,1)S(1)} %collective-permute-done.5.refs_4_) | copy-start | bytes 786436
  40.2 7.7 %collective-permute-start.7 = (bf16[2,512,128]{2,1,0:T(8,128)(2,1)S(1)}, bf16[2,512,128]{2,1,0:T(8,128)(2,1)S(1)}, u32[]{:S(2)}, u32[]{:S(2)}) collective-permute-start(bf16[2,512,128]{2,1,0:T(8,128)(2,1)S(1)} %collective-permute-done.4.refs_3_), channel_id=1, source_target_pairs={{0,1},{1,2},{2,3},{3,4},{4,5},{5,6},{6,7},{7,0},{8,9},{9,10},{10,1... | collective-permute-start | bytes 786440 | tf_op jit(solution)/shard_map/ppermute | solution.py:24
  40.3 7.6 %collective-permute-start.8 = (bf16[2,512,128]{2,1,0:T(8,128)(2,1)S(1)}, bf16[2,512,128]{2,1,0:T(8,128)(2,1)S(1)}, u32[]{:S(2)}, u32[]{:S(2)}) collective-permute-start(bf16[2,512,128]{2,1,0:T(8,128)(2,1)S(1)} %collective-permute-done.5.refs_4_), channel_id=1, source_target_pairs={{0,7},{1,0},{2,1},{3,2},{4,3},{5,4},{6,5},{7,6},{8,15},{9,8},{10,9... | collective-permute-start | bytes 786440 | tf_op jit(solution)/shard_map/ppermute | solution.py:24
  47.9 0.7 copy-start.13
  47.9 0.8 copy-start.14
  48.7 20.4 %copy-start.5 = (bf16[4,1024,256]{2,1,0:T(8,128)(2,1)}, bf16[4,1024,256]{2,1,0:T(8,128)(2,1)S(1)}, u32[]{:S(2)}) copy-start(bf16[4,1024,256]{2,1,0:T(8,128)(2,1)S(1)} %all-to-all-done.refs_8_) | copy-start | bytes 6291460
  48.7 20.4 %collective-permute-start.11 = (bf16[4,1024,256]{2,1,0:T(8,128)(2,1)S(1)}, bf16[4,1024,256]{2,1,0:T(8,128)(2,1)}, u32[]{:S(2)}, u32[]{:S(2)}) collective-permute-start(bf16[4,1024,256]{2,1,0:T(8,128)(2,1)S(1)} %all-to-all-done.refs_8_), channel_id=1, source_target_pairs={{0,64},{64,0},{1,65},{65,1},{2,66},{66,2},{3,67},{67,3},{4,68},{68... | collective-permute-start | bytes 6291464 | tf_op jit(solution)/shard_map/ppermute | solution.py:24
  48.7 27.4 %collective-permute-start.6 = (bf16[2048,256]{1,0:T(8,128)(2,1)}, bf16[2048,256]{1,0:T(8,128)(2,1)S(1)}, u32[]{:S(2)}, u32[]{:S(2)}) collective-permute-start(bf16[2048,256]{1,0:T(8,128)(2,1)} %shard_map.47), channel_id=1, source_target_pairs={{0,16},{16,32},{32,48},{48,0},{64,112},{80,64},{96,80},{112,96},{1... | collective-permute-start | bytes 3145736 | tf_op jit(solution)/shard_map/ppermute | solution.py:240
  50.7 27.0 %collective-permute-start.9 = (bf16[1024,256]{1,0:T(8,128)(2,1)}, bf16[1024,256]{1,0:T(8,128)(2,1)}, u32[]{:S(2)}, u32[]{:S(2)}) collective-permute-start(bf16[1024,256]{1,0:T(8,128)(2,1)} %shard_map.49), channel_id=1, source_target_pairs={{0,32},{16,48},{32,0},{48,16},{1,33},{17,49},{33,1},{49,17},{2,34}... | collective-permute-start | bytes 1572872 | tf_op jit(solution)/shard_map/ppermute | solution.py:24
  53.4 15.7 %collective-permute-start.10 = (bf16[2,512,128]{2,1,0:T(8,128)(2,1)}, bf16[2,512,128]{2,1,0:T(8,128)(2,1)}, u32[]{:S(2)}, u32[]{:S(2)}) collective-permute-start(bf16[2,512,128]{2,1,0:T(8,128)(2,1)} %copy-done.13), channel_id=1, source_target_pairs={{0,1},{1,2},{2,3},{3,4},{4,5},{5,6},{6,7},{7,0},{8,9},{9,10},{10,1... | collective-permute-start | bytes 786440 | tf_op jit(solution)/shard_map/ppermute | solution.py:24
  76.1 10.6 %copy-start.1 = (bf16[2048,256]{1,0:T(8,128)(2,1)S(1)}, bf16[2048,256]{1,0:T(8,128)(2,1)}, u32[]{:S(2)}) copy-start(bf16[2048,256]{1,0:T(8,128)(2,1)} %shard_map.48.refs_0_) | copy-start | bytes 3145732
  76.1 10.6 %copy-start.2 = (s32[5]{0:T(128)S(1)}, s32[5]{0:T(128)}, u32[]{:S(2)}) copy-start(s32[5]{0:T(128)} %stack.44.at_ref) | copy-start | bytes 64
  77.7 7.9 %collective-permute-start.12 = (bf16[2048,256]{1,0:T(8,128)(2,1)S(1)}, bf16[2048,256]{1,0:T(8,128)(2,1)S(1)}, u32[]{:S(2)}, u32[]{:S(2)}) collective-permute-start(bf16[2048,256]{1,0:T(8,128)(2,1)S(1)} %collective-permute-done.6.refs_1_), channel_id=1, source_target_pairs={{0,64},{64,0},{1,65},{65,1},{2,66},{66,2},{3,67},{67,3},{4,68},{68... | collective-permute-start | bytes 3145736 | tf_op jit(solution)/shard_map/ppermute | solution.py:24
  77.7 19.9 %all-to-all-start.1 = ((f32[16,32,512]{2,1,0:T(8,128)}), f32[16,32,512]{2,1,0:T(8,128)}, u32[]{:S(2)}, u32[]{:S(2)}) async-start(f32[16,32,512]{2,1,0:T(8,128)} %bitcast.22), calls=%async_computation.1 | async-start | bytes 2097152 | tf_op jit(solution)/shard_map/all_to_all | solution.py:270
  82.4 65.0 %all-gather.7.cloned.1.call-start = ((), (), s32[]{:S(2)}) async-start(), calls=%async_computation.6 | async-start | bytes 2359296 | tf_op jit(solution)/shard_map/all_gather | solution.py:276
  82.5 3.2 %collective-permute-start.13 = (bf16[1024,256]{1,0:T(8,128)(2,1)}, bf16[1024,256]{1,0:T(8,128)(2,1)}, u32[]{:S(2)}, u32[]{:S(2)}) collective-permute-start(bf16[1024,256]{1,0:T(8,128)(2,1)} %collective-permute-done.9.refs_3_), channel_id=1, source_target_pairs={{0,64},{64,0},{1,65},{65,1},{2,66},{66,2},{3,67},{67,3},{4,68},{68... | collective-permute-start | bytes 1572872 | tf_op jit(solution)/shard_map/ppermute | solution.py:24
  85.7 1.0 copy-start.3
  86.6 1.2 copy-start.4
  98.9 7.2 %collective-permute-start.14 = (bf16[1,4,32,512]{3,2,1,0:T(8,128)(2,1)S(1)}, bf16[1,4,32,512]{3,2,1,0:T(8,128)(2,1)S(1)}, u32[]{:S(2)}, u32[]{:S(2)}) collective-permute-start(bf16[1,4,32,512]{3,2,1,0:T(8,128)(2,1)S(1)} %bitcast.23), channel_id=1, source_target_pairs={{0,8},{8,0},{1,9},{9,1},{2,10},{10,2},{3,11},{11,3},{4,12},{12,4},... | collective-permute-start | bytes 393224 | tf_op jit(solution)/shard_map/ppermute | solution.py:24
  141.1 2.7 %collective-permute-start.15 = (bf16[2,4,128,512]{3,2,1,0:T(8,128)(2,1)S(1)}, bf16[2,4,128,512]{3,2,1,0:T(8,128)(2,1)S(1)}, u32[]{:S(2)}, u32[]{:S(2)}) collective-permute-start(bf16[2,4,128,512]{3,2,1,0:T(8,128)(2,1)S(1)} %bitcast.19), channel_id=1, source_target_pairs={{0,64},{64,0},{1,65},{65,1},{2,66},{66,2},{3,67},{67,3},{4,68},{68... | collective-permute-start | bytes 3145736 | tf_op jit(solution)/shard_map/ppermute | solution.py:24
  147.4 1.6 copy-start
Sparse Core Ops, SparseCore 0:
  40.4 45.2 all-gather.4
  107.0 40.3 all-gather.6
